TPU v7x, 32 devices: a whole 2x2x4 slice. The times are simulated.
32 devices in a mesh: dp: 16 (over z, y, core), mp: 2 (over x).
Axes of the slice: x: 2, y: 2, z: 4, core: 2. Of those that a mesh axis runs over, the one named last changes fastest.
Arguments:
- pieces: bfloat16 [16384, 8, 512], P(('dp', 'mp')), may hold values from -6 to 6
- counts: int32 [16384], P(('dp', 'mp')), may hold values from 1 to 8
- token_index: int32 [16384], P('dp'), may hold values from 0 to 16383
- hyper_input: bfloat16 [512, 1536], P(('dp', 'mp')), may hold values from -0.25 to 0.25
- hyper_output: bfloat16 [512, 512], P(('dp', 'mp')), may hold values from -0.5 to 0.5
- hyper_expand: bfloat16 [512, 2048], P(('dp', 'mp')), may hold values from -0.25 to 0.25
- hyper_reduce: bfloat16 [2048, 512], P(('dp', 'mp')), may hold values from -0.125 to 0.125
- hyper_norms: bfloat16 [512, 4], P(('dp', 'mp')), may hold values from -0.5 to 1.5, as said below
- embed_weight: bfloat16 [512, 2048], P(('dp', 'mp')), may hold values from -0.25 to 0.25
- attention_gain: float32 [2048], replicated, may hold values from 0.5 to 1.5
- dense_gain: float32 [2048], replicated, may hold values from 0.1 to 1.9
- frozen_query_weight: bfloat16 [2048, 2048], P(None, 'mp'), may hold values from -0.125 to 0.125
- frozen_key_weight: bfloat16 [2048, 256], P(None, 'mp'), may hold values from -0.125 to 0.125
- frozen_value_weight: bfloat16 [2048, 256], P(None, 'mp'), may hold values from -0.125 to 0.125
- frozen_output_weight: bfloat16 [2048, 2048], P('mp'), may hold values from -0.5 to 0.5
- gate_weight: bfloat16 [2048, 5632], P(None, 'mp'), may hold values from -0.125 to 0.125
- up_weight: bfloat16 [2048, 5632], P(None, 'mp'), may hold values from -0.125 to 0.125
- down_weight: bfloat16 [5632, 2048], P('mp'), may hold values from -0.078125 to 0.078125
- upstream: bfloat16 [16384, 2048], P('dp'), may hold values from -6 to 6
Outputs:
- model_out: bfloat16 [16384, 2048], P('dp', 'mp')
- pieces_gradient: bfloat16 [16384, 8, 512], P(('dp', 'mp'))
- hyper_input_gradient: float32 [512, 1536], P(('dp', 'mp'))
- hyper_output_gradient: float32 [512, 512], P(('dp', 'mp'))
- hyper_expand_gradient: float32 [512, 2048], P(('dp', 'mp'))
- hyper_reduce_gradient: float32 [2048, 512], P(('dp', 'mp'))
- hyper_norms_gradient: float32 [512, 4], P(('dp', 'mp'))
- embed_weight_gradient: float32 [512, 2048], P(('dp', 'mp'))
Inputs may be any that keep to these rules, and one draw needn't show every extreme that they name: `counts`: the number of live slots of each entry; slots at or past it are padding. `hyper_norms`: columns 0 and 2 are the two norms' gains, columns 1 and 3 their shifts.
All inputs are finite; a program needn't handle non-finite values.
Results may differ from a plain program's by a relative error of at most 0.025.
Values may be sent and summed in bfloat16 or wider, within the bound.
No kernel may reach another device: no remote copies, remote signals or barrier semaphores. Data moves between devices by JAX's collectives and lax.ppermute only.
A program may use at most 448 MiB of HBM per device.

v0:
```python
import jax
import jax.numpy as jnp
from jax import lax
from jax.sharding import PartitionSpec as P

HEAD_WIDTH = 64
HHD = 64
MICRO = 2


EPS = 1e-05
NEGATIVE = -1000000000.0


def matmul(left, right):
    return jnp.dot(left, right, preferred_element_type=jnp.float32)


def matmul_first(left, right):
    return lax.dot_general(
        left, right, (((0,), (0,)), ((), ())), preferred_element_type=jnp.float32
    )


def matmul_last(left, right):
    return lax.dot_general(
        left, right, (((1,), (1,)), ((), ())), preferred_element_type=jnp.float32
    )


def layer_norm(value, gain, shift):
    centered = value - jnp.mean(value, axis=-1, keepdims=True)
    spread = jnp.mean(centered * centered, axis=-1, keepdims=True)
    return centered * lax.rsqrt(spread + EPS) * gain + shift


def rms_norm(value, gain):
    return value * lax.rsqrt(jnp.mean(value * value, axis=-1, keepdims=True) + EPS) * gain


def rotate(value, cosine, sine):
    half = value.shape[-1] // 2
    first = value[..., :half]
    second = value[..., half:]
    return jnp.concatenate(
        [first * cosine - second * sine, second * cosine + first * sine], axis=-1
    )


def rope_tables(length, head_size):
    positions = jnp.arange(length, dtype=jnp.float32)
    inverse = 10000.0 ** (-jnp.arange(0, head_size, 2, dtype=jnp.float32) / head_size)
    angles = positions[:, None] * inverse[None, :]
    return (jnp.cos(angles), jnp.sin(angles))


def exact_gelu(value):
    return jax.nn.gelu(value, approximate=False)


def gated_units(gate_pre, up_pre):
    return jax.nn.silu(gate_pre) * up_pre


def rounded(value):
    return lax.optimization_barrier(value.astype(jnp.bfloat16)).astype(jnp.float32)


def hyper_forward(rows_in, rows_count, weights):
    in_weight, out_weight, expand_weight, reduce_weight, norm_table = (
        weights[0],
        weights[1],
        weights[2],
        weights[3],
        weights[4],
    )
    entries, slots, width = rows_in.shape
    heads = width // HHD
    scale = HHD ** (-0.5)
    norm_values = norm_table.astype(jnp.float32)
    pieces_float = rows_in.astype(jnp.float32)
    first_normed, first_pull = jax.vjp(
        layer_norm, pieces_float, norm_values[:, 0], norm_values[:, 1]
    )
    first_low = first_normed.astype(jnp.bfloat16)
    flat_low = first_low.reshape(entries * slots, width)
    pair = (
        matmul(flat_low, in_weight[:, width:])
        .astype(jnp.bfloat16)
        .reshape(entries, slots, 2, heads, HHD)
    )
    keys = pair[:, :, 0]
    value_rows = pair[:, :, 1]
    lead_low = first_low[:, 0, :]
    query = matmul(lead_low, in_weight[:, :width]).astype(jnp.bfloat16).reshape(entries, heads, HHD)
    scores = jnp.einsum("vhd,vshd->vhs", query, keys, preferred_element_type=jnp.float32) * scale
    live = lax.broadcasted_iota(jnp.int32, (entries, slots), 1) < rows_count[:, None]
    scores = jnp.where(live[:, None, :], scores, NEGATIVE)
    probs = jax.nn.softmax(scores, axis=-1)
    probs_low = probs.astype(jnp.bfloat16)
    attended_rows = (
        jnp.einsum("vhs,vshd->vhd", probs_low, value_rows, preferred_element_type=jnp.float32)
        .astype(jnp.bfloat16)
        .reshape(entries, width)
    )
    hidden_state = pieces_float[:, 0, :] + matmul(attended_rows, out_weight)
    second, second_pull = jax.vjp(layer_norm, hidden_state, norm_values[:, 2], norm_values[:, 3])
    second_low = second.astype(jnp.bfloat16)
    expanded = matmul(second_low, expand_weight)
    active, gelu_pull = jax.vjp(exact_gelu, expanded)
    active_low = active.astype(jnp.bfloat16)
    pooled = (hidden_state + matmul(active_low, reduce_weight)).astype(jnp.bfloat16)
    saved = (
        first_pull,
        flat_low,
        lead_low,
        keys,
        value_rows,
        query,
        probs,
        probs_low,
        attended_rows,
        second_pull,
        second_low,
        gelu_pull,
        active_low,
    )
    return (pooled, saved)


def hyper_backward(saved, grad_pooled, weights):
    in_weight, out_weight, expand_weight, reduce_weight = (
        weights[0],
        weights[1],
        weights[2],
        weights[3],
    )
    (
        first_pull,
        flat_low,
        lead_low,
        keys,
        value_rows,
        query,
        probs,
        probs_low,
        attended_rows,
        second_pull,
        second_low,
        gelu_pull,
        active_low,
    ) = saved
    entries, heads, head_size = query.shape
    width = heads * head_size
    slots = keys.shape[1]
    scale = head_size ** (-0.5)
    grad_low = grad_pooled.astype(jnp.bfloat16)
    reduce_grad = matmul_first(active_low, grad_low)
    (grad_expanded,) = gelu_pull(matmul_last(grad_low, reduce_weight))
    grad_expanded = grad_expanded.astype(jnp.bfloat16)
    expand_grad = matmul_first(second_low, grad_expanded)
    grad_hidden_norm, gain_two, shift_two = second_pull(matmul_last(grad_expanded, expand_weight))
    grad_hidden = grad_pooled + grad_hidden_norm
    hidden_low = grad_hidden.astype(jnp.bfloat16)
    output_grad = matmul_first(attended_rows, hidden_low)
    grad_attended = (
        matmul_last(hidden_low, out_weight).astype(jnp.bfloat16).reshape(entries, heads, head_size)
    )
    grad_probs = jnp.einsum(
        "vhd,vshd->vhs", grad_attended, value_rows, preferred_element_type=jnp.float32
    )
    grad_scores = (
        probs * (grad_probs - jnp.sum(probs * grad_probs, axis=-1, keepdims=True))
    ).astype(jnp.bfloat16)
    grad_query = (
        (jnp.einsum("vhs,vshd->vhd", grad_scores, keys, preferred_element_type=jnp.float32) * scale)
        .astype(jnp.bfloat16)
        .reshape(entries, width)
    )
    grad_keys = (
        jnp.einsum("vhs,vhd->vshd", grad_scores, query, preferred_element_type=jnp.float32) * scale
    )
    grad_values = jnp.einsum(
        "vhs,vhd->vshd", probs_low, grad_attended, preferred_element_type=jnp.float32
    )
    grad_pair = (
        jnp.stack([grad_keys, grad_values], axis=2)
        .astype(jnp.bfloat16)
        .reshape(entries * slots, 2 * width)
    )
    input_grad = jnp.concatenate(
        [matmul_first(lead_low, grad_query), matmul_first(flat_low, grad_pair)], axis=1
    )
    grad_first = matmul_last(grad_pair, in_weight[:, width:]).reshape(entries, slots, width)
    grad_first = grad_first.at[:, 0, :].add(matmul_last(grad_query, in_weight[:, :width]))
    grad_pieces, gain_one, shift_one = first_pull(grad_first)
    grad_pieces = grad_pieces.at[:, 0, :].add(grad_hidden)
    norm_grad = jnp.stack([gain_one, shift_one, gain_two, shift_two], axis=1)
    return (grad_pieces, (input_grad, output_grad, expand_grad, reduce_grad, norm_grad))


def causal_mask(length):
    return lax.broadcasted_iota(jnp.int32, (length, length), 0) >= lax.broadcasted_iota(
        jnp.int32, (length, length), 1
    )


def attention_forward(queries, keys, value_rows, repeat):
    length, heads, head_size = queries.shape
    scale = head_size ** (-0.5)
    causal = causal_mask(length)
    outputs = []
    sums = []
    for group in range(keys.shape[1]):
        query_group = queries[:, group * repeat : (group + 1) * repeat, :]
        scores = (
            jnp.einsum(
                "qrd,kd->rqk", query_group, keys[:, group, :], preferred_element_type=jnp.float32
            )
            * scale
        )
        scores = jnp.where(causal, scores, NEGATIVE)
        highest = jnp.max(scores, axis=-1, keepdims=True)
        exponent = jnp.exp(scores - highest)
        total = jnp.sum(exponent, axis=-1, keepdims=True)
        probs_low = (exponent / total).astype(jnp.bfloat16)
        outputs.append(
            jnp.einsum(
                "rqk,kd->qrd",
                probs_low,
                value_rows[:, group, :],
                preferred_element_type=jnp.float32,
            )
        )
        sums.append(highest + jnp.log(total))
    return (jnp.concatenate(outputs, axis=1).astype(jnp.bfloat16), sums)


def attention_backward(queries, keys, value_rows, grad_out, sums, repeat):
    length, heads, head_size = queries.shape
    scale = head_size ** (-0.5)
    causal = causal_mask(length)
    grad_queries = []
    grad_keys = []
    grad_values = []
    for group in range(keys.shape[1]):
        query_group = queries[:, group * repeat : (group + 1) * repeat, :]
        key_group = keys[:, group, :]
        value_group = value_rows[:, group, :]
        grad_group = grad_out[:, group * repeat : (group + 1) * repeat, :]
        scores = (
            jnp.einsum("qrd,kd->rqk", query_group, key_group, preferred_element_type=jnp.float32)
            * scale
        )
        probs = jnp.exp(jnp.where(causal, scores, NEGATIVE) - sums[group])
        grad_probs = jnp.einsum(
            "qrd,kd->rqk", grad_group, value_group, preferred_element_type=jnp.float32
        )
        grad_scores = (
            probs * (grad_probs - jnp.sum(probs * grad_probs, axis=-1, keepdims=True))
        ).astype(jnp.bfloat16)
        grad_queries.append(
            jnp.einsum("rqk,kd->qrd", grad_scores, key_group, preferred_element_type=jnp.float32)
            * scale
        )
        grad_keys.append(
            jnp.einsum("rqk,qrd->kd", grad_scores, query_group, preferred_element_type=jnp.float32)
            * scale
        )
        grad_values.append(
            jnp.einsum(
                "rqk,qrd->kd",
                probs.astype(jnp.bfloat16),
                grad_group,
                preferred_element_type=jnp.float32,
            )
        )
    return (
        jnp.concatenate(grad_queries, axis=1),
        jnp.stack(grad_keys, axis=1),
        jnp.stack(grad_values, axis=1),
    )


def body(
    pieces,
    counts,
    token_index,
    hyper_input,
    hyper_output,
    hyper_expand,
    hyper_reduce,
    hyper_norms,
    embed_weight,
    attention_gain,
    dense_gain,
    frozen_query_weight,
    frozen_key_weight,
    frozen_value_weight,
    frozen_output_weight,
    gate_weight,
    up_weight,
    down_weight,
    upstream,
):
    local_vocab = pieces.shape[0]
    per_micro = local_vocab // MICRO
    mp_count = lax.axis_size("mp")
    mp_index = lax.axis_index("mp")
    pooled_parts = []
    saved_parts = []
    for step in range(MICRO):
        gathered = (
            lax.all_gather(hyper_input, ("dp", "mp"), axis=0, tiled=True),
            lax.all_gather(hyper_output, ("dp", "mp"), axis=0, tiled=True),
            lax.all_gather(hyper_expand, ("dp", "mp"), axis=0, tiled=True),
            lax.all_gather(hyper_reduce, ("dp", "mp"), axis=0, tiled=True),
            lax.all_gather(hyper_norms, ("dp", "mp"), axis=0, tiled=True),
            lax.all_gather(embed_weight, ("dp", "mp"), axis=0, tiled=True),
        )
        start = step * per_micro
        pooled, saved = hyper_forward(
            pieces[start : start + per_micro], counts[start : start + per_micro], gathered
        )
        pooled_parts.append(pooled)
        saved_parts.append(saved)
    pooled_own = jnp.concatenate(pooled_parts, axis=0)
    embed_full = gathered[5]
    pooled_all = lax.all_gather(pooled_own, ("dp", "mp"), axis=0, tiled=True)
    chosen = jnp.take(pooled_all, token_index, axis=0)
    embedded = rounded(matmul(chosen, embed_full))
    length = embedded.shape[0]
    cosine, sine = rope_tables(length, HEAD_WIDTH)
    heads_local = frozen_query_weight.shape[1] // HEAD_WIDTH
    kv_local = frozen_key_weight.shape[1] // HEAD_WIDTH
    repeat = heads_local // kv_local

    def turn(value):
        return rotate(value, cosine[:, None, :], sine[:, None, :])

    def first_norm(value):
        return rms_norm(value, attention_gain)

    def second_norm(value):
        return rms_norm(value, dense_gain)

    first_normed, first_pull = jax.vjp(first_norm, embedded)
    first_low = first_normed.astype(jnp.bfloat16)
    query_before_rotary = matmul(first_low, frozen_query_weight).reshape(
        length, heads_local, HEAD_WIDTH
    )
    key_before_rotary = matmul(first_low, frozen_key_weight).reshape(length, kv_local, HEAD_WIDTH)
    value_rows = (
        matmul(first_low, frozen_value_weight)
        .astype(jnp.bfloat16)
        .reshape(length, kv_local, HEAD_WIDTH)
    )
    queries, query_pull = jax.vjp(turn, query_before_rotary)
    keys, key_pull = jax.vjp(turn, key_before_rotary)
    queries = queries.astype(jnp.bfloat16)
    keys = keys.astype(jnp.bfloat16)
    attended_rows, sums = attention_forward(queries, keys, value_rows, repeat)
    attended_flat = attended_rows.reshape(length, heads_local * HEAD_WIDTH)
    hidden_state = embedded + lax.psum(
        matmul(attended_flat, frozen_output_weight).astype(jnp.bfloat16), "mp"
    ).astype(jnp.float32)
    second_normed, second_pull = jax.vjp(second_norm, hidden_state)
    second_low = second_normed.astype(jnp.bfloat16)
    gate_pre = matmul(second_low, gate_weight)
    up_pre = matmul(second_low, up_weight)
    active, active_pull = jax.vjp(gated_units, gate_pre, up_pre)
    active_low = active.astype(jnp.bfloat16)
    dense_share = lax.psum_scatter(
        matmul(active_low, down_weight).astype(jnp.bfloat16), "mp", scatter_dimension=1, tiled=True
    ).astype(jnp.float32)
    width_share = dense_share.shape[1]
    model_out = (
        lax.dynamic_slice_in_dim(hidden_state, mp_index * width_share, width_share, 1) + dense_share
    ).astype(jnp.bfloat16)
    grad_gate, grad_up = active_pull(matmul_last(upstream, down_weight))
    grad_second = matmul_last(grad_gate.astype(jnp.bfloat16), gate_weight) + matmul_last(
        grad_up.astype(jnp.bfloat16), up_weight
    )
    grad_second = lax.psum(grad_second.astype(jnp.bfloat16), "mp").astype(jnp.float32)
    (grad_hidden_norm,) = second_pull(grad_second)
    grad_hidden = upstream.astype(jnp.float32) + grad_hidden_norm
    grad_attended = (
        matmul_last(grad_hidden.astype(jnp.bfloat16), frozen_output_weight)
        .astype(jnp.bfloat16)
        .reshape(length, heads_local, HEAD_WIDTH)
    )
    grad_queries, grad_keys, grad_values = attention_backward(
        queries, keys, value_rows, grad_attended, sums, repeat
    )
    (grad_query_pre,) = query_pull(grad_queries)
    (grad_key_pre,) = key_pull(grad_keys)
    grad_first = matmul_last(
        grad_query_pre.reshape(length, heads_local * HEAD_WIDTH).astype(jnp.bfloat16),
        frozen_query_weight,
    )
    grad_first = grad_first + matmul_last(
        grad_key_pre.reshape(length, kv_local * HEAD_WIDTH).astype(jnp.bfloat16), frozen_key_weight
    )
    grad_first = grad_first + matmul_last(
        grad_values.reshape(length, kv_local * HEAD_WIDTH).astype(jnp.bfloat16), frozen_value_weight
    )
    grad_first = lax.psum(grad_first.astype(jnp.bfloat16), "mp").astype(jnp.float32)
    (grad_embed_norm,) = first_pull(grad_first)
    embedded_grad_low = (grad_hidden + grad_embed_norm).astype(jnp.bfloat16)
    half = length // mp_count
    row_start = mp_index * half
    my_index = lax.dynamic_slice_in_dim(token_index, row_start, half, 0)
    my_grad = lax.dynamic_slice_in_dim(embedded_grad_low, row_start, half, 0)
    chosen_mine = lax.dynamic_slice_in_dim(chosen, row_start, half, 0)
    dense_pool = (
        jnp.zeros((pooled_all.shape[0], pooled_all.shape[1]), jnp.float32)
        .at[my_index]
        .add(matmul_last(my_grad, embed_full))
    )
    grad_pooled, embed_grad = (
        lax.psum_scatter(dense_pool, ("dp", "mp"), scatter_dimension=0, tiled=True),
        lax.psum_scatter(
            matmul_first(chosen_mine, my_grad), ("dp", "mp"), scatter_dimension=0, tiled=True
        ),
    )
    piece_grads = []
    totals = None
    for step in range(MICRO):
        gathered_back = (
            lax.all_gather(hyper_input, ("dp", "mp"), axis=0, tiled=True),
            lax.all_gather(hyper_output, ("dp", "mp"), axis=0, tiled=True),
            lax.all_gather(hyper_expand, ("dp", "mp"), axis=0, tiled=True),
            lax.all_gather(hyper_reduce, ("dp", "mp"), axis=0, tiled=True),
            lax.all_gather(hyper_norms, ("dp", "mp"), axis=0, tiled=True),
        )
        start = step * per_micro
        grad_rows, grads = hyper_backward(
            saved_parts[step], grad_pooled[start : start + per_micro], gathered_back
        )
        piece_grads.append(grad_rows)
        if step == 0:
            totals = grads
        else:
            totals = jax.tree.map(jnp.add, totals, grads)
    reduced = (
        lax.psum_scatter(totals[0], ("dp", "mp"), scatter_dimension=0, tiled=True),
        lax.psum_scatter(totals[1], ("dp", "mp"), scatter_dimension=0, tiled=True),
        lax.psum_scatter(totals[2], ("dp", "mp"), scatter_dimension=0, tiled=True),
        lax.psum_scatter(totals[3], ("dp", "mp"), scatter_dimension=0, tiled=True),
        lax.psum_scatter(totals[4], ("dp", "mp"), scatter_dimension=0, tiled=True),
    )
    pieces_gradient = jnp.concatenate(piece_grads, axis=0).astype(jnp.bfloat16)
    return (
        model_out,
        pieces_gradient,
        reduced[0],
        reduced[1],
        reduced[2],
        reduced[3],
        reduced[4],
        embed_grad,
    )


def solution(mesh):
    return jax.shard_map(
        body,
        mesh=mesh,
        in_specs=(
            P(("dp", "mp"), None, None),
            P(("dp", "mp")),
            P("dp"),
            P(("dp", "mp"), None),
            P(("dp", "mp"), None),
            P(("dp", "mp"), None),
            P(("dp", "mp"), None),
            P(("dp", "mp"), None),
            P(("dp", "mp"), None),
            P(),
            P(),
            P(None, "mp"),
            P(None, "mp"),
            P(None, "mp"),
            P("mp", None),
            P(None, "mp"),
            P(None, "mp"),
            P("mp", None),
            P("dp", None),
        ),
        out_specs=(
            P("dp", "mp"),
            P(("dp", "mp"), None, None),
            P(("dp", "mp"), None),
            P(("dp", "mp"), None),
            P(("dp", "mp"), None),
            P(("dp", "mp"), None),
            P(("dp", "mp"), None),
            P(("dp", "mp"), None),
        ),
        check_vma=False,
    )
```

profile of v0, /device:TPU:0, one launch (start us, length us, event | category | flops | bytes accessed | tf_op | source)
XLA Modules:
  0.0 2753.3 jit_solution(14893653425243579655)
XLA Ops:
  19.1 69.8 %all-gather = bf16[32,16,4]{1,2,0:T(4,128)(2,1)S(1)} all-gather(bf16[1,16,4]{1,2,0:T(4,128)(2,1)S(1)} %bitcast.335), channel_id=1, replica_groups=mesh['dp'=16,'mp'=2] {'dp','mp'}, dimensions={0}, use_global_device_ids=true | all-gather | bytes 4224 | tf_op jit(solution)/shard_map/all_gather | solution.py:318
  89.2 67.6 %all_gather.16 = bf16[512,512]{1,0:T(8,128)(2,1)S(1)} all-gather(bf16[16,512]{1,0:T(8,128)(2,1)S(1)} %copy-done.128), channel_id=1, replica_groups=mesh['dp'=16,'mp'=2] {'dp','mp'}, dimensions={0}, use_global_device_ids=true | all-gather | bytes 540672 | tf_op jit(solution)/shard_map/all_gather | solution.py:315
  176.3 11.7 reshape.491
  210.5 11.6 reshape.495
  237.4 8.4 multiply_convert_fusion.10
  245.8 6.7 multiply_convert_fusion.11
  260.3 111.2 %all-gather.13.cloned.1.call-done = bf16[16384,512]{1,0:T(8,128)(2,1)} async-done(((bf16[512,512]{1,0:T(8,128)(2,1)}), bf16[16384,512]{1,0:T(8,128)(2,1)}) %all-gather.13.cloned.1.call-update) | async-done | bytes 16777232 | tf_op jit(solution)/shard_map/all_gather | solution.py:329
  371.5 12.3 gather_fusion
  385.0 44.1 %all-gather.15.cloned.1.call-done = bf16[512,2048]{1,0:T(8,128)(2,1)} async-done(((bf16[16,2048]{1,0:T(8,128)(2,1)}), bf16[512,2048]{1,0:T(8,128)(2,1)}) %all-gather.15.cloned.1.call-update) | async-done | bytes 2097168 | tf_op jit(solution)/shard_map/all_gather | solution.py:319
  442.9 13.7 fusion.179
  456.7 13.5 fusion.180
  471.8 13.1 fusion.7
  484.9 13.7 fusion.67
  498.7 13.1 fusion.6
  511.7 13.9 fusion.66
  534.1 18.8 fusion.181
  553.0 88.0 %all-reduce.8.cloned.1.call-done = bf16[1024,2048]{1,0:T(8,128)(2,1)} async-done(((bf16[1024,2048]{1,0:T(8,128)(2,1)}), bf16[1024,2048]{1,0:T(8,128)(2,1)}) %all-reduce.8.cloned.1.call-update) | async-done | bytes 4194320 | tf_op jit(solution)/shard_map/psum | solution.py:364
  646.9 17.7 fusion.167
  664.6 15.7 fusion.166
  680.3 24.8 fusion.27
  705.1 21.7 add_convert_fusion.1
  727.7 107.3 %all-reduce.10.cloned.1.call-done = bf16[1024,2048]{1,0:T(8,128)(2,1)} async-done(((bf16[1024,2048]{1,0:T(8,128)(2,1)}), bf16[1024,2048]{1,0:T(8,128)(2,1)}) %all-reduce.10.cloned.1.call-update) | async-done | bytes 4194320 | tf_op jit(solution)/shard_map/psum | solution.py:384
  834.9 6.8 multiply_reduce_fusion.9
  843.2 8.6 fusion.24
  851.8 10.0 fusion.55
  861.9 14.0 fusion.93
  876.0 21.6 fusion
  897.6 28.9 %fusion.2 = bf16[8,1024,1024]{1,2,0:T(8,128)(2,1)} fusion(f32[1024,1024,8]{1,0,2:T(8,128)} %get-tuple-element.152, f32[8,1024,1024]{1,2,0:T(8,128)} %get-tuple-element.148, f32[8,1024]{1,0:T(8,128)S(1)} %get-tuple-element.151, f32[8,1024]{1,0:T(8,128)S(1)} %log_add_fusion), kind=kLoop, calls=%fused_computation.6 | loop fusion | flops 33554432 | bytes 83951616 | tf_op jit(solution)/shard_map/convert_element_type | solution.py:261
  926.6 11.1 fusion.83
  942.0 16.0 fusion.90
  958.0 22.1 fusion.3
  980.1 28.1 %fusion.5 = bf16[8,1024,1024]{1,2,0:T(8,128)(2,1)} fusion(f32[1024,1024,8]{1,0,2:T(8,128)} %get-tuple-element.154, f32[8,1024,1024]{1,2,0:T(8,128)} %get-tuple-element.150, f32[8,1024]{1,0:T(8,128)S(1)} %get-tuple-element.153, f32[8,1024]{1,0:T(8,128)S(1)} %log_add_fusion.1), kind=kLoop, calls=%fused_computation.11 | loop fusion | flops 33554432 | bytes 83951616 | tf_op jit(solution)/shard_map/convert_element_type | solution.py:261
  1008.3 11.1 fusion.81
  1035.8 6.8 convert_element_type.253
  1042.6 100.4 %all-reduce.12.cloned.1.call-done = bf16[1024,2048]{1,0:T(8,128)(2,1)} async-done(((bf16[1024,2048]{1,0:T(8,128)(2,1)}), bf16[1024,2048]{1,0:T(8,128)(2,1)}) %all-reduce.12.cloned.1.call-update) | async-done | bytes 4194320 | tf_op jit(solution)/shard_map/psum | solution.py:407
  1155.7 17.4 scatter_custom_fusion
  1175.8 22.1 fusion.33
  1198.1 681.1 %reduce-scatter.13.cloned.1.call-done = f32[512,512]{1,0:T(8,128)} async-done(((f32[16384,512]{1,0:T(8,128)}), f32[512,512]{1,0:T(8,128)}) %reduce-scatter.13.cloned.1.call-update) | async-done | bytes 1048592 | tf_op jit(solution)/shard_map/reduce_scatter | solution.py:421
  1950.5 13.0 copy.114
  1963.5 13.0 copy.112
  1976.5 11.9 convert_element_type.302
  1988.4 11.9 convert_element_type.301
  2042.5 39.8 %reduce-scatter.25.cloned.1.call-done = f32[16,4]{1,0:T(8,128)} async-done(((f32[512,4]{1,0:T(8,128)}), f32[16,4]{1,0:T(8,128)}) %reduce-scatter.25.cloned.1.call-update) | async-done | bytes 272
  2083.6 139.4 %reduce-scatter.23.cloned.1.call-done = f32[16,2048]{1,0:T(8,128)} async-done(((f32[512,2048]{1,0:T(8,128)}), f32[16,2048]{1,0:T(8,128)}) %reduce-scatter.23.cloned.1.call-update) | async-done | bytes 131088 | tf_op jit(solution)/shard_map/reduce_scatter | solution.py:422
  2223.0 135.1 %reduce-scatter.17.cloned.1.call-done = f32[16,512]{1,0:T(8,128)} async-done(((f32[512,512]{1,0:T(8,128)}), f32[16,512]{1,0:T(8,128)}) %reduce-scatter.17.cloned.1.call-update) | async-done | bytes 32784 | tf_op jit(solution)/shard_map/reduce_scatter | solution.py:447
  2358.2 103.3 %reduce-scatter.15.cloned.1.call-done = f32[16,1536]{1,0:T(8,128)} async-done(((f32[512,1536]{1,0:T(8,128)}), f32[16,1536]{1,0:T(8,128)}) %reduce-scatter.15.cloned.1.call-update) | async-done | bytes 98320 | tf_op jit(solution)/shard_map/reduce_scatter | solution.py:446
  2461.5 143.8 %reduce-scatter.19.cloned.1.call-done = f32[16,2048]{1,0:T(8,128)} async-done(((f32[512,2048]{1,0:T(8,128)}), f32[16,2048]{1,0:T(8,128)}) %reduce-scatter.19.cloned.1.call-update) | async-done | bytes 131088 | tf_op jit(solution)/shard_map/reduce_scatter | solution.py:448
  2605.4 141.2 %reduce-scatter.21.cloned.1.call-done = f32[64,512]{1,0:T(8,128)} async-done(((f32[2048,512]{1,0:T(8,128)}), f32[64,512]{1,0:T(8,128)}) %reduce-scatter.21.cloned.1.call-update) | async-done | bytes 131088 | tf_op jit(solution)/shard_map/reduce_scatter | solution.py:449
  (511 shorter events, 259.8 us)
Async XLA Ops:
  7.2 427.1 %copy-start = (bf16[2048,128]{1,0:T(8,128)(2,1)S(1)}, bf16[2048,128]{1,0:T(8,128)(2,1)}, u32[]{:S(2)}) copy-start(bf16[2048,128]{1,0:T(8,128)(2,1)} %param.39) | copy-start | bytes 1572868
  7.2 158.7 %all-gather.7.cloned.1.call-start = ((), (), s32[]{:S(2)}) async-start(), calls=%async_computation.8 | async-start | bytes 1622016 | tf_op jit(solution)/shard_map/all_gather | solution.py:314
  7.9 229.4 %all-gather.9.cloned.1.call-start = ((), (), s32[]{:S(2)}) async-start(), calls=%async_computation.9 | async-start | bytes 2162688 | tf_op jit(solution)/shard_map/all_gather | solution.py:316
  8.7 243.9 %all-gather.11.cloned.1.call-start = ((), (), s32[]{:S(2)}) async-start(), calls=%async_computation.10 | async-start | bytes 2162688 | tf_op jit(solution)/shard_map/all_gather | solution.py:317
  9.4 362.1 %all-gather.13.cloned.1.call-start = ((), (), s32[]{:S(2)}) async-start(), calls=%async_computation.11 | async-start | bytes 17301504 | tf_op jit(solution)/shard_map/all_gather | solution.py:329
  12.0 149.0 %copy-start.6 = (bf16[256,8,512]{2,1,0:T(8,128)(2,1)}, bf16[256,8,512]{2,1,0:T(8,128)(2,1)S(1)}, u32[]{:S(2)}) copy-start(bf16[256,8,512]{2,1,0:T(8,128)(2,1)S(1)} %get-tuple-element.118) | copy-start | bytes 6291460
  14.3 74.8 %copy-start.128 = (bf16[16,512]{1,0:T(8,128)(2,1)S(1)}, bf16[16,512]{1,0:T(8,128)(2,1)}, u32[]{:S(2)}) copy-start(bf16[16,512]{1,0:T(8,128)(2,1)} %param.31) | copy-start | bytes 49156
  89.1 72.4 %copy-start.9 = (bf16[256,8,512]{2,1,0:T(8,128)(2,1)S(1)}, bf16[256,8,512]{2,1,0:T(8,128)(2,1)}, u32[]{:S(2)}) copy-start(bf16[256,8,512]{2,1,0:T(8,128)(2,1)} %copy-done.8) | copy-start | bytes 6291460
  89.1 76.7 %copy-start.115 = (f32[512,1]{0,1:T(1,128)}, f32[512,1]{0,1:T(1,128)S(1)}, u32[]{:S(2)}) copy-start(f32[512,1]{0,1:T(1,128)S(1)} %get-tuple-element.128) | copy-start | bytes 6148
  89.2 156.6 %copy-start.103 = (f32[512,1]{0,1:T(1,128)}, f32[512,1]{0,1:T(1,128)S(1)}, u32[]{:S(2)}) copy-start(f32[512,1]{0,1:T(1,128)S(1)} %get-tuple-element.125) | copy-start | bytes 6148
  89.2 156.6 %copy-start.105 = (f32[512,1]{0,1:T(1,128)}, f32[512,1]{0,1:T(1,128)S(1)}, u32[]{:S(2)}) copy-start(f32[512,1]{0,1:T(1,128)S(1)} %get-tuple-element.126) | copy-start | bytes 6148
  156.7 78.9 %copy-start.25 = (bf16[512,512]{1,0:T(8,128)(2,1)}, bf16[512,512]{1,0:T(8,128)(2,1)S(1)}, u32[]{:S(2)}) copy-start(bf16[512,512]{1,0:T(8,128)(2,1)S(1)} %all_gather.16) | copy-start | bytes 1572868
  160.9 34.1 %copy-start.109 = (pred[256,8]{0,1:T(8,128)(4,1)}, pred[256,8]{0,1:T(8,128)(4,1)S(1)}, u32[]{:S(2)}) copy-start(pred[256,8]{0,1:T(8,128)(4,1)S(1)} %get-tuple-element.161) | copy-start | bytes 6148
  160.9 66.1 %copy-start.107 = (pred[256,8]{0,1:T(8,128)(4,1)}, pred[256,8]{0,1:T(8,128)(4,1)S(1)}, u32[]{:S(2)}) copy-start(pred[256,8]{0,1:T(8,128)(4,1)S(1)} %get-tuple-element.160) | copy-start | bytes 6148
  203.8 30.0 %copy-start.48 = (bf16[256,8,64]{0,2,1:T(8,128)(2,1)}, bf16[256,8,64]{0,2,1:T(8,128)(2,1)S(1)}, u32[]{:S(2)}) copy-start(bf16[256,8,64]{0,2,1:T(8,128)(2,1)S(1)} %copy.129) | copy-start | bytes 786436
  235.3 20.2 copy-start.27
  237.0 15.5 copy-start.31
  258.7 170.3 %all-gather.15.cloned.1.call-start = ((), (), s32[]{:S(2)}) async-start(), calls=%async_computation.12 | async-start | bytes 2162688 | tf_op jit(solution)/shard_map/all_gather | solution.py:319
  259.3 381.6 %all-reduce.8.cloned.1.call-start = ((), (), s32[]{:S(2)}) async-start(), calls=%async_computation.13 | async-start | bytes 8388608 | tf_op jit(solution)/shard_map/psum | solution.py:364
  260.3 181.9 %copy-start.42 = (f32[1024,32]{0,1:T(8,128)}, f32[1024,32]{0,1:T(8,128)S(1)}, u32[]{:S(2)}) copy-start(f32[1024,32]{0,1:T(8,128)S(1)} %get-tuple-element.139) | copy-start | bytes 393220
  260.3 181.9 %copy-start.44 = (f32[1024,32]{0,1:T(8,128)}, f32[1024,32]{0,1:T(8,128)S(1)}, u32[]{:S(2)}) copy-start(f32[1024,32]{0,1:T(8,128)S(1)} %get-tuple-element.140) | copy-start | bytes 393220
  433.3 36.9 %copy-start.3 = (bf16[1024,2048]{1,0:T(8,128)(2,1)}, bf16[1024,2048]{1,0:T(8,128)(2,1)S(1)}, u32[]{:S(2)}) copy-start(bf16[1024,2048]{1,0:T(8,128)(2,1)S(1)} %convolution_convert_fusion) | copy-start | bytes 12582916
  434.2 35.9 %copy-start.135 = (f32[1024]{0:T(1024)}, f32[1024]{0:T(1024)S(1)}, u32[]{:S(2)}) copy-start(f32[1024]{0:T(1024)S(1)} %fusion.147) | copy-start | bytes 12292
  442.1 14.5 copy-start.62
  442.1 14.5 copy-start.64
  456.7 28.3 %copy-start.85 = (f32[8,1024]{1,0:T(8,128)}, f32[8,1024]{1,0:T(8,128)S(1)}, u32[]{:S(2)}) copy-start(f32[8,1024]{1,0:T(8,128)S(1)} %get-tuple-element.147) | copy-start | bytes 98308
  471.8 40.0 %copy-start.87 = (bf16[1024,128]{0,1:T(8,128)(2,1)}, bf16[1024,128]{0,1:T(8,128)(2,1)S(1)}, u32[]{:S(2)}) copy-start(bf16[1024,128]{0,1:T(8,128)(2,1)S(1)} %convolution_convert_fusion.8) | copy-start | bytes 786436
  534.1 300.8 %all-reduce.10.cloned.1.call-start = ((), (), s32[]{:S(2)}) async-start(), calls=%async_computation.15 | async-start | bytes 8388608 | tf_op jit(solution)/shard_map/psum | solution.py:384
  553.0 93.0 %copy-start.119 = (f32[2048]{0:T(1024)S(1)}, f32[2048]{0:T(1024)}, u32[]{:S(2)}) copy-start(f32[2048]{0:T(1024)} %param.37) | copy-start | bytes 24580
  640.9 23.7 slice-start
  646.9 17.8 slice-start.1
  646.9 17.8 slice-start.2
  726.9 416.2 %all-reduce.12.cloned.1.call-start = ((), (), s32[]{:S(2)}) async-start(), calls=%async_computation.16 | async-start | bytes 8388608 | tf_op jit(solution)/shard_map/psum | solution.py:407
  861.9 14.1 copy-start.29
  861.9 14.1 copy-start.88
  897.6 28.9 %copy-start.20 = (bf16[1024,16,32]{0,2,1:T(8,128)(2,1)S(1)}, bf16[1024,16,32]{0,2,1:T(8,128)(2,1)}, u32[]{:S(2)}) copy-start(bf16[1024,16,32]{0,2,1:T(8,128)(2,1)} %copy-done.19) | copy-start | bytes 3145732
  897.6 28.9 %copy-start.22 = (bf16[1024,16,32]{0,2,1:T(8,128)(2,1)S(1)}, bf16[1024,16,32]{0,2,1:T(8,128)(2,1)}, u32[]{:S(2)}) copy-start(bf16[1024,16,32]{0,2,1:T(8,128)(2,1)} %copy-done.21) | copy-start | bytes 3145732
  1035.0 844.2 %reduce-scatter.13.cloned.1.call-start = ((), (), s32[]{:S(2)}) async-start(), calls=%async_computation.17 | async-start | bytes 34603008 | tf_op jit(solution)/shard_map/reduce_scatter | solution.py:421
  1035.8 107.2 %copy-start.138 = (f32[2048]{0:T(1024)S(1)}, f32[2048]{0:T(1024)}, u32[]{:S(2)}) copy-start(f32[2048]{0:T(1024)} %param.36) | copy-start | bytes 24580
  1042.6 105.5 %copy-start.118 = (f32[1024]{0:T(1024)S(1)}, f32[1024]{0:T(1024)}, u32[]{:S(2)}) copy-start(f32[1024]{0:T(1024)} %copy-done.117) | copy-start | bytes 12292
  1173.2 854.7 %reduce-scatter.11.cloned.1.call-start = ((), (), s32[]{:S(2)}) async-start(), calls=%async_computation.14 | async-start | bytes 6291456 | tf_op jit(solution)/shard_map/reduce_scatter | solution.py:373
  1197.9 681.4 %copy-start.146 = (bf16[2048,512]{1,0:T(8,128)(2,1)S(1)}, bf16[2048,512]{1,0:T(8,128)(2,1)}, u32[]{:S(2)}) copy-start(bf16[2048,512]{1,0:T(8,128)(2,1)} %all-gather.11.cloned.1.call-done) | copy-start | bytes 6291460
  1197.9 884.4 %reduce-scatter.25.cloned.1.call-start = ((), (), s32[]{:S(2)}) async-start(), calls=%async_computation.23 | async-start | bytes 270336
  1945.3 277.7 %reduce-scatter.23.cloned.1.call-start = ((), (), s32[]{:S(2)}) async-start(), calls=%async_computation.22 | async-start | bytes 4325376 | tf_op jit(solution)/shard_map/reduce_scatter | solution.py:422
  1950.5 407.7 %reduce-scatter.17.cloned.1.call-start = ((), (), s32[]{:S(2)}) async-start(), calls=%async_computation.19 | async-start | bytes 1081344 | tf_op jit(solution)/shard_map/reduce_scatter | solution.py:447
  2004.1 457.4 %reduce-scatter.15.cloned.1.call-start = ((), (), s32[]{:S(2)}) async-start(), calls=%async_computation.18 | async-start | bytes 3244032 | tf_op jit(solution)/shard_map/reduce_scatter | solution.py:446
  2017.3 588.1 %reduce-scatter.19.cloned.1.call-start = ((), (), s32[]{:S(2)}) async-start(), calls=%async_computation.20 | async-start | bytes 4325376 | tf_op jit(solution)/shard_map/reduce_scatter | solution.py:448
  2022.5 724.1 %reduce-scatter.21.cloned.1.call-start = ((), (), s32[]{:S(2)}) async-start(), calls=%async_computation.21 | async-start | bytes 4325376 | tf_op jit(solution)/shard_map/reduce_scatter | solution.py:449
  (122 other events, 519.7 us)
Sparse Core Ops, SparseCore 0:
  10.9 57.7 all-gather.6
  71.7 56.2 all-gather.8
  131.1 55.8 all-gather.10
  258.8 112.5 all-gather.12
  374.3 54.6 all-gather.14
  534.2 106.6 all-reduce.7
  727.0 107.8 all-reduce.9
  1035.2 107.8 all-reduce.11
  1173.3 705.9 reduce-scatter.12
  1882.1 57.1 reduce-scatter.10
  1945.4 136.8 reduce-scatter.24
  2085.1 137.8 reduce-scatter.22
  2226.0 132.1 reduce-scatter.16
  2364.1 97.4 reduce-scatter.14
  2464.2 141.1 reduce-scatter.18
  2608.1 138.4 reduce-scatter.20
where the time goes:
time: 2760 us; the launch traced here: 2750 us
  waiting for transfers between devices  1840 us (67%)
  matrix products  401 us (15%)
  other arithmetic  230 us (8%)
  blocking collectives  137 us (5%)
  local copies, waits for them, and re-layouts  129 us (5%)
    reduce_scatter x1, waiting for transfers between devices, body(): lax.psum_scatter(dense_pool, ('dp', 'mp'), scatter_dimension=0, tiled=True)  681 us
    reduce_scatter x1, waiting for transfers between devices, body(): lax.psum_scatter(totals[2], ('dp', 'mp'), scatter_dimension=0, tiled=True)  144 us
    reduce_scatter x1, waiting for transfers between devices, body(): lax.psum_scatter(totals[3], ('dp', 'mp'), scatter_dimension=0, tiled=True)  141 us
    reduce_scatter x1, waiting for transfers between devices, body(): lax.psum_scatter(matmul_first(chosen_mine, my_grad), ('dp', 'mp'), scatte...  139 us
    reduce_scatter x1, waiting for transfers between devices, body(): lax.psum_scatter(totals[1], ('dp', 'mp'), scatter_dimension=0, tiled=True)  135 us
    dot_general x18, matrix products, matmul(): return jnp.dot(left, right, preferred_element_type=jnp.float32)  114 us
    all_gather x1, waiting for transfers between devices, body(): pooled_all = lax.all_gather(pooled_own, ('dp', 'mp'), axis=0, tiled=True)  111 us
    psum x1, waiting for transfers between devices, body(): lax.psum(grad_second.astype(jnp.bfloat16), 'mp').astype(jnp.float32)  107 us
  transfers between devices with their start and end apart: 16, of which 12 were waited for; matrix products, arithmetic and copies ran while one was open for 12% of the time, Pallas kernels for 0%

commit v1 on v0

--- a/solution.py
+++ b/solution.py
@@ -5,7 +5,8 @@
 
 HEAD_WIDTH = 64
 HHD = 64
-MICRO = 2
+BLOCK_PARTS = 4
+UNIT = 512
 
 
 EPS = 1e-05
@@ -205,18 +206,71 @@
     )
 
 
-def attention_forward(queries, keys, value_rows, repeat):
-    length, heads, head_size = queries.shape
+def log2_of(number):
+    return number.bit_length() - 1
+
+
+def swap(value, mask, devices):
+    return lax.ppermute(value, ("dp", "mp"), [(d, d ^ mask) for d in range(devices)])
+
+
+def gather_blocks(block, me, devices, order):
+    bits = log2_of(devices)
+    held = block.reshape((1,) * bits + block.shape)
+    for bit in order:
+        axis = bits - 1 - bit
+        arrived = swap(held, 1 << bit, devices)
+        upper = ((me >> bit) & 1) == 1
+        held = jnp.where(
+            upper,
+            jnp.concatenate([arrived, held], axis),
+            jnp.concatenate([held, arrived], axis),
+        )
+    return held.reshape((devices,) + block.shape)
+
+
+def scatter_blocks(blocks, me, devices, order):
+    bits = log2_of(devices)
+    held = blocks.reshape((2,) * bits + blocks.shape[1:])
+    for bit in order:
+        axis = bits - 1 - bit
+        mine = (me >> bit) & 1
+        leaving = lax.dynamic_slice_in_dim(held, 1 - mine, 1, axis).astype(jnp.bfloat16)
+        staying = lax.dynamic_slice_in_dim(held, mine, 1, axis)
+        held = staying + swap(leaving, 1 << bit, devices).astype(jnp.float32)
+    return held.reshape(blocks.shape[1:])
+
+
+def fold(value, devices):
+    rows, width = value.shape
+    parts = width // UNIT
+    each = rows // devices
+    return (
+        value.reshape(devices, each, parts, UNIT).transpose(0, 2, 1, 3).reshape(devices, parts * each, UNIT)
+    )
+
+
+def unfold(blocks, parts):
+    devices, total, unit = blocks.shape
+    each = total // parts
+    return blocks.reshape(devices, parts, each, unit).transpose(0, 2, 1, 3).reshape(devices * each, parts * unit)
+
+
+def attention_forward(queries, keys, value_rows, base):
+    rows, heads, head_size = queries.shape
+    groups = keys.shape[0]
+    repeat = heads // groups
+    length = keys.shape[1]
     scale = head_size ** (-0.5)
-    causal = causal_mask(length)
+    causal = base + lax.broadcasted_iota(jnp.int32, (rows, length), 0) >= lax.broadcasted_iota(
+        jnp.int32, (rows, length), 1
+    )
     outputs = []
     sums = []
-    for group in range(keys.shape[1]):
+    for group in range(groups):
         query_group = queries[:, group * repeat : (group + 1) * repeat, :]
         scores = (
-            jnp.einsum(
-                "qrd,kd->rqk", query_group, keys[:, group, :], preferred_element_type=jnp.float32
-            )
+            jnp.einsum("qrd,kd->rqk", query_group, keys[group], preferred_element_type=jnp.float32)
             * scale
         )
         scores = jnp.where(causal, scores, NEGATIVE)
@@ -226,27 +280,29 @@
         probs_low = (exponent / total).astype(jnp.bfloat16)
         outputs.append(
             jnp.einsum(
-                "rqk,kd->qrd",
-                probs_low,
-                value_rows[:, group, :],
-                preferred_element_type=jnp.float32,
+                "rqk,kd->qrd", probs_low, value_rows[group], preferred_element_type=jnp.float32
             )
         )
         sums.append(highest + jnp.log(total))
     return (jnp.concatenate(outputs, axis=1).astype(jnp.bfloat16), sums)
 
 
-def attention_backward(queries, keys, value_rows, grad_out, sums, repeat):
-    length, heads, head_size = queries.shape
+def attention_backward(queries, keys, value_rows, grad_out, sums, base):
+    rows, heads, head_size = queries.shape
+    groups = keys.shape[0]
+    repeat = heads // groups
+    length = keys.shape[1]
     scale = head_size ** (-0.5)
-    causal = causal_mask(length)
+    causal = base + lax.broadcasted_iota(jnp.int32, (rows, length), 0) >= lax.broadcasted_iota(
+        jnp.int32, (rows, length), 1
+    )
     grad_queries = []
     grad_keys = []
     grad_values = []
-    for group in range(keys.shape[1]):
+    for group in range(groups):
         query_group = queries[:, group * repeat : (group + 1) * repeat, :]
-        key_group = keys[:, group, :]
-        value_group = value_rows[:, group, :]
+        key_group = keys[group]
+        value_group = value_rows[group]
         grad_group = grad_out[:, group * repeat : (group + 1) * repeat, :]
         scores = (
             jnp.einsum("qrd,kd->rqk", query_group, key_group, preferred_element_type=jnp.float32)
@@ -277,8 +333,73 @@
         )
     return (
         jnp.concatenate(grad_queries, axis=1),
-        jnp.stack(grad_keys, axis=1),
-        jnp.stack(grad_values, axis=1),
+        jnp.stack(grad_keys, axis=0),
+        jnp.stack(grad_values, axis=0),
+    )
+
+
+def route(token_index, me, devices, local_vocab, capacity, mp_count):
+    groups = devices // mp_count
+    every = lax.all_gather(token_index, "dp", axis=0, tiled=True)
+    step = token_index.shape[0] // BLOCK_PARTS
+    cut = every.reshape(groups, BLOCK_PARTS, step)
+    asked = jnp.stack(
+        [
+            jnp.concatenate([cut[:, 0], cut[:, 3]], axis=1),
+            jnp.concatenate([cut[:, 1], cut[:, 2]], axis=1),
+        ],
+        axis=1,
+    ).reshape(devices, 2 * step)
+    count = 2 * step
+    places = jnp.arange(count, dtype=jnp.int32)
+    same = asked[:, :, None] == asked[:, None, :]
+    earlier = places[:, None] > places[None, :]
+    repeated = jnp.any(same & earlier[None], axis=2)
+    first = jnp.logical_not(repeated)
+    owner = asked // local_vocab
+    before = (
+        (owner[:, :, None] == owner[:, None, :])
+        & (asked[:, None, :] < asked[:, :, None])
+        & first[:, None, :]
+    )
+    rank = jnp.sum(before.astype(jnp.int32), axis=2)
+    rounds = jnp.max(rank) // capacity + 1
+    own_rank = lax.dynamic_index_in_dim(rank, me, 0, False)
+    own_owner = lax.dynamic_index_in_dim(owner, me, 0, False)
+    entries = me * local_vocab + jnp.arange(local_vocab, dtype=jnp.int32)
+    present = jnp.any(asked[:, :, None] == entries[None, None, :], axis=1)
+    lower = (
+        jnp.arange(local_vocab, dtype=jnp.int32)[:, None]
+        < jnp.arange(local_vocab, dtype=jnp.int32)[None, :]
+    )
+    standing = matmul(present.astype(jnp.bfloat16), lower.astype(jnp.bfloat16)).astype(jnp.int32)
+    return (rounds, own_rank, own_owner, present, standing)
+
+
+def sender_choice(present, standing, turn, capacity):
+    slot = turn * capacity + jnp.arange(capacity, dtype=jnp.int32)
+    chosen = present[:, None, :] & (standing[:, None, :] == slot[None, :, None])
+    return chosen.astype(jnp.bfloat16).reshape(present.shape[0] * capacity, present.shape[1])
+
+
+def taker_choice(own_rank, own_owner, turn, capacity, devices):
+    inside = own_rank - turn * capacity
+    valid = (inside >= 0) & (inside < capacity)
+    place = jnp.where(valid, own_owner * capacity + inside, -1)
+    return (place[:, None] == jnp.arange(devices * capacity, dtype=jnp.int32)[None, :]).astype(
+        jnp.bfloat16
+    )
+
+
+def exchange(value):
+    return lax.all_to_all(value, ("dp", "mp"), 0, 0, tiled=True)
+
+
+def ordered_blocks(first, own_two, other_two):
+    return jnp.where(
+        first,
+        jnp.concatenate([own_two[0], other_two[0], other_two[1], own_two[1]], axis=0),
+        jnp.concatenate([other_two[0], own_two[0], own_two[1], other_two[1]], axis=0),
     )
 
 
@@ -304,39 +425,102 @@
     upstream,
 ):
     local_vocab = pieces.shape[0]
-    per_micro = local_vocab // MICRO
     mp_count = lax.axis_size("mp")
+    devices = lax.axis_size("dp") * mp_count
     mp_index = lax.axis_index("mp")
-    pooled_parts = []
-    saved_parts = []
-    for step in range(MICRO):
-        gathered = (
-            lax.all_gather(hyper_input, ("dp", "mp"), axis=0, tiled=True),
-            lax.all_gather(hyper_output, ("dp", "mp"), axis=0, tiled=True),
-            lax.all_gather(hyper_expand, ("dp", "mp"), axis=0, tiled=True),
-            lax.all_gather(hyper_reduce, ("dp", "mp"), axis=0, tiled=True),
-            lax.all_gather(hyper_norms, ("dp", "mp"), axis=0, tiled=True),
-            lax.all_gather(embed_weight, ("dp", "mp"), axis=0, tiled=True),
-        )
-        start = step * per_micro
-        pooled, saved = hyper_forward(
-            pieces[start : start + per_micro], counts[start : start + per_micro], gathered
-        )
-        pooled_parts.append(pooled)
-        saved_parts.append(saved)
-    pooled_own = jnp.concatenate(pooled_parts, axis=0)
-    embed_full = gathered[5]
-    pooled_all = lax.all_gather(pooled_own, ("dp", "mp"), axis=0, tiled=True)
-    chosen = jnp.take(pooled_all, token_index, axis=0)
-    embedded = rounded(matmul(chosen, embed_full))
-    length = embedded.shape[0]
+    me = lax.axis_index("dp") * mp_count + mp_index
+    core = (me >> 1) & 1
+    lead = mp_index == 0
+    bits = log2_of(devices)
+    spread_order = list(range(bits - 1, 1, -1)) + [0, 1]
+    width = hyper_input.shape[0] * devices
+    own_rows = hyper_input.shape[0]
+    length = token_index.shape[0]
+    block = length // BLOCK_PARTS
+    capacity = max(16, 32 * length // (devices * 32))
+
+    norm_rows = jnp.pad(hyper_norms, ((0, 0), (0, UNIT - hyper_norms.shape[1])))
+    first_pack = jnp.concatenate([fold(hyper_input, 1)[0], norm_rows], axis=0)
+    second_pack = jnp.concatenate(
+        [
+            hyper_output,
+            fold(hyper_expand, 1)[0],
+            hyper_reduce,
+            fold(embed_weight, 1)[0],
+        ],
+        axis=0,
+    )
+    first_all = gather_blocks(first_pack, me, devices, spread_order)
+    second_all = gather_blocks(second_pack, me, devices, spread_order)
+    in_parts = hyper_input.shape[1] // UNIT
+    in_weight = unfold(first_all[:, : in_parts * own_rows], in_parts)
+    norm_table = first_all[:, in_parts * own_rows :, : hyper_norms.shape[1]].reshape(
+        width, hyper_norms.shape[1]
+    )
+    at = own_rows
+    out_weight = second_all[:, :at].reshape(width, UNIT)
+    expand_parts = hyper_expand.shape[1] // UNIT
+    expand_weight = unfold(second_all[:, at : at + expand_parts * own_rows], expand_parts)
+    at += expand_parts * own_rows
+    reduce_weight = second_all[:, at : at + hyper_reduce.shape[0]].reshape(
+        hyper_reduce.shape[0] * devices, UNIT
+    )
+    at += hyper_reduce.shape[0]
+    embed_parts = embed_weight.shape[1] // UNIT
+    embed_full = unfold(second_all[:, at:], embed_parts)
+    gathered = (in_weight, out_weight, expand_weight, reduce_weight, norm_table)
+
+    query_cut = frozen_query_weight.shape[1] // 2
+    key_pair = jnp.concatenate([frozen_key_weight, frozen_value_weight], axis=1)
+    query_near = swap(
+        lax.dynamic_slice_in_dim(frozen_query_weight, core * query_cut, query_cut, 1), 1, devices
+    )
+    output_near = swap(
+        lax.dynamic_slice_in_dim(frozen_output_weight, core * query_cut, query_cut, 0), 1, devices
+    )
+    key_other = swap(key_pair, 1, devices)
+    query_far = swap(query_near, 2, devices)
+    output_far = swap(output_near, 2, devices)
+    kv_local = frozen_key_weight.shape[1] // HEAD_WIDTH
+    span = frozen_key_weight.shape[1]
+
+    def whole_keys(own, other):
+        return jnp.where(
+            lead, jnp.concatenate([own, other], axis=1), jnp.concatenate([other, own], axis=1)
+        )
+
+    key_weight = whole_keys(frozen_key_weight, key_other[:, :span])
+    value_weight = whole_keys(frozen_value_weight, key_other[:, span:])
+    key_heads = key_weight.shape[1] // HEAD_WIDTH
+    other_base = (1 - mp_index) * kv_local
+    head_order = jnp.stack(
+        [mp_index * kv_local, mp_index * kv_local + 1, other_base + core, other_base + 1 - core]
+    )
+
+    rounds, own_rank, own_owner, present, standing = route(
+        token_index, me, devices, local_vocab, capacity, mp_count
+    )
+
+    pooled, saved = hyper_forward(pieces, counts, gathered)
+
+    def fetch(turn, chosen):
+        sent = matmul(sender_choice(present, standing, turn, capacity), pooled).astype(jnp.bfloat16)
+        came = exchange(sent)
+        picked = matmul(taker_choice(own_rank, own_owner, turn, capacity, devices), came)
+        return chosen + picked.astype(jnp.bfloat16)
+
+    chosen_own = fetch(0, jnp.zeros((2 * block, pooled.shape[1]), jnp.bfloat16))
+    chosen_own = lax.fori_loop(1, rounds, fetch, chosen_own)
+    chosen_other = swap(chosen_own, 1, devices)
+
     cosine, sine = rope_tables(length, HEAD_WIDTH)
-    heads_local = frozen_query_weight.shape[1] // HEAD_WIDTH
-    kv_local = frozen_key_weight.shape[1] // HEAD_WIDTH
-    repeat = heads_local // kv_local
-
-    def turn(value):
-        return rotate(value, cosine[:, None, :], sine[:, None, :])
+    own_base = (mp_index * block, (3 - mp_index) * block)
+    other_start = ((1 - mp_index) * block, (2 + mp_index) * block)
+
+    def own_blocks(value):
+        return jnp.concatenate(
+            [lax.dynamic_slice_in_dim(value, start, block, 0) for start in own_base], axis=0
+        )
 
     def first_norm(value):
         return rms_norm(value, attention_gain)
@@ -344,121 +528,201 @@
     def second_norm(value):
         return rms_norm(value, dense_gain)
 
+    embedded = rounded(matmul(chosen_own, embed_full))
     first_normed, first_pull = jax.vjp(first_norm, embedded)
     first_low = first_normed.astype(jnp.bfloat16)
-    query_before_rotary = matmul(first_low, frozen_query_weight).reshape(
-        length, heads_local, HEAD_WIDTH
-    )
-    key_before_rotary = matmul(first_low, frozen_key_weight).reshape(length, kv_local, HEAD_WIDTH)
-    value_rows = (
-        matmul(first_low, frozen_value_weight)
-        .astype(jnp.bfloat16)
-        .reshape(length, kv_local, HEAD_WIDTH)
-    )
-    queries, query_pull = jax.vjp(turn, query_before_rotary)
-    keys, key_pull = jax.vjp(turn, key_before_rotary)
+    query_weights = (frozen_query_weight, query_near, query_far)
+    output_weights = (frozen_output_weight, output_near, output_far)
+    query_pre = jnp.concatenate([matmul(first_low, part) for part in query_weights], axis=1)
+    heads = query_pre.shape[1] // HEAD_WIDTH
+    own_cosine, own_sine = own_blocks(cosine), own_blocks(sine)
+
+    def turn_own(value):
+        return rotate(value, own_cosine[:, None, :], own_sine[:, None, :])
+
+    queries, query_pull = jax.vjp(turn_own, query_pre.reshape(2 * block, heads, HEAD_WIDTH))
     queries = queries.astype(jnp.bfloat16)
-    keys = keys.astype(jnp.bfloat16)
-    attended_rows, sums = attention_forward(queries, keys, value_rows, repeat)
-    attended_flat = attended_rows.reshape(length, heads_local * HEAD_WIDTH)
-    hidden_state = embedded + lax.psum(
-        matmul(attended_flat, frozen_output_weight).astype(jnp.bfloat16), "mp"
+    other_low = first_norm(rounded(matmul(chosen_other, embed_full))).astype(jnp.bfloat16)
+
+    def in_order(own, other):
+        return ordered_blocks(lead, (own[:block], own[block:]), (other[:block], other[block:]))
+
+    key_pre = in_order(matmul(first_low, key_weight), matmul(other_low, key_weight))
+    values_low = in_order(
+        matmul(first_low, value_weight).astype(jnp.bfloat16),
+        matmul(other_low, value_weight).astype(jnp.bfloat16),
+    )
+    keys = rotate(
+        key_pre.reshape(length, key_heads, HEAD_WIDTH), cosine[:, None, :], sine[:, None, :]
+    ).astype(jnp.bfloat16)
+    keys_by = jnp.take(keys.transpose(1, 0, 2), head_order, axis=0)
+    values_by = jnp.take(
+        values_low.reshape(length, key_heads, HEAD_WIDTH).transpose(1, 0, 2), head_order, axis=0
+    )
+
+    sums = []
+    hidden_parts = []
+    second_pulls = []
+    second_rows = []
+    for part in range(2):
+        rows = slice(part * block, (part + 1) * block)
+        attended_rows, part_sums = attention_forward(
+            queries[rows], keys_by, values_by, own_base[part]
+        )
+        sums.append(part_sums)
+        flat = attended_rows.reshape(block, heads * HEAD_WIDTH)
+        mixed = 0.0
+        at = 0
+        for weight in output_weights:
+            mixed = mixed + matmul(flat[:, at : at + weight.shape[0]], weight)
+            at += weight.shape[0]
+        hidden_state = embedded[rows] + mixed
+        hidden_parts.append(hidden_state)
+        second_normed, pull = jax.vjp(second_norm, hidden_state)
+        second_pulls.append(pull)
+        second_low = second_normed.astype(jnp.bfloat16)
+        second_rows.append(jnp.concatenate([second_low, swap(second_low, 1, devices)], axis=0))
+
+    active_rows = []
+    grad_hidden = []
+    for part in range(2):
+        second_low = second_rows[part]
+        rising = jnp.concatenate(
+            [
+                lax.dynamic_slice_in_dim(upstream, own_base[part], block, 0),
+                lax.dynamic_slice_in_dim(upstream, other_start[part], block, 0),
+            ],
+            axis=0,
+        )
+        gate_pre = matmul(second_low, gate_weight)
+        up_pre = matmul(second_low, up_weight)
+        active, active_pull = jax.vjp(gated_units, gate_pre, up_pre)
+        active_rows.append(active.astype(jnp.bfloat16))
+        grad_gate, grad_up = active_pull(matmul_last(rising, down_weight))
+        grad_second = (
+            matmul_last(grad_gate.astype(jnp.bfloat16), gate_weight)
+            + matmul_last(grad_up.astype(jnp.bfloat16), up_weight)
+        ).astype(jnp.bfloat16)
+        total = grad_second[:block].astype(jnp.float32) + swap(
+            grad_second[block:], 1, devices
+        ).astype(jnp.float32)
+        (grad_hidden_norm,) = second_pulls[part](total)
+        grad_hidden.append(rising[:block].astype(jnp.float32) + grad_hidden_norm)
+
+    share = upstream.shape[1] // mp_count
+    own_out = []
+    other_out = []
+    for part in range(2):
+        dense = matmul(active_rows[part], down_weight)
+        dense_own = dense[:block] + hidden_parts[part]
+        dense_other = dense[block:]
+
+        def columns(value, index):
+            return lax.dynamic_slice_in_dim(value, index * share, share, 1)
+
+        leaving = jnp.concatenate(
+            [columns(dense_other, 1 - mp_index), columns(dense_own, 1 - mp_index)], axis=0
+        ).astype(jnp.bfloat16)
+        arrived = swap(leaving, 1, devices).astype(jnp.float32)
+        own_out.append((columns(dense_own, mp_index) + arrived[:block]).astype(jnp.bfloat16))
+        other_out.append((columns(dense_other, mp_index) + arrived[block:]).astype(jnp.bfloat16))
+    model_out = ordered_blocks(lead, own_out, other_out)
+
+    grad_queries = []
+    grad_keys = 0.0
+    grad_values = 0.0
+    for part in range(2):
+        rows = slice(part * block, (part + 1) * block)
+        hidden_low = grad_hidden[part].astype(jnp.bfloat16)
+        grad_attended = jnp.concatenate(
+            [matmul_last(hidden_low, weight).astype(jnp.bfloat16) for weight in output_weights],
+            axis=1,
+        ).reshape(block, heads, HEAD_WIDTH)
+        part_queries, part_keys, part_values = attention_backward(
+            queries[rows], keys_by, values_by, grad_attended, sums[part], own_base[part]
+        )
+        grad_queries.append(part_queries)
+        grad_keys = grad_keys + part_keys
+        grad_values = grad_values + part_values
+    back_order = jnp.argsort(head_order)
+    pair_grad = jnp.stack(
+        [jnp.take(grad_keys, back_order, axis=0), jnp.take(grad_values, back_order, axis=0)], axis=0
+    )
+
+    def pick_blocks(starts):
+        return jnp.concatenate(
+            [lax.dynamic_slice_in_dim(pair_grad, start, block, 2) for start in starts], axis=2
+        )
+
+    pair_total = pick_blocks(own_base) + swap(
+        pick_blocks(other_start).astype(jnp.bfloat16), 1, devices
     ).astype(jnp.float32)
-    second_normed, second_pull = jax.vjp(second_norm, hidden_state)
-    second_low = second_normed.astype(jnp.bfloat16)
-    gate_pre = matmul(second_low, gate_weight)
-    up_pre = matmul(second_low, up_weight)
-    active, active_pull = jax.vjp(gated_units, gate_pre, up_pre)
-    active_low = active.astype(jnp.bfloat16)
-    dense_share = lax.psum_scatter(
-        matmul(active_low, down_weight).astype(jnp.bfloat16), "mp", scatter_dimension=1, tiled=True
-    ).astype(jnp.float32)
-    width_share = dense_share.shape[1]
-    model_out = (
-        lax.dynamic_slice_in_dim(hidden_state, mp_index * width_share, width_share, 1) + dense_share
-    ).astype(jnp.bfloat16)
-    grad_gate, grad_up = active_pull(matmul_last(upstream, down_weight))
-    grad_second = matmul_last(grad_gate.astype(jnp.bfloat16), gate_weight) + matmul_last(
-        grad_up.astype(jnp.bfloat16), up_weight
-    )
-    grad_second = lax.psum(grad_second.astype(jnp.bfloat16), "mp").astype(jnp.float32)
-    (grad_hidden_norm,) = second_pull(grad_second)
-    grad_hidden = upstream.astype(jnp.float32) + grad_hidden_norm
-    grad_attended = (
-        matmul_last(grad_hidden.astype(jnp.bfloat16), frozen_output_weight)
-        .astype(jnp.bfloat16)
-        .reshape(length, heads_local, HEAD_WIDTH)
-    )
-    grad_queries, grad_keys, grad_values = attention_backward(
-        queries, keys, value_rows, grad_attended, sums, repeat
-    )
-    (grad_query_pre,) = query_pull(grad_queries)
-    (grad_key_pre,) = key_pull(grad_keys)
-    grad_first = matmul_last(
-        grad_query_pre.reshape(length, heads_local * HEAD_WIDTH).astype(jnp.bfloat16),
-        frozen_query_weight,
-    )
-    grad_first = grad_first + matmul_last(
-        grad_key_pre.reshape(length, kv_local * HEAD_WIDTH).astype(jnp.bfloat16), frozen_key_weight
-    )
-    grad_first = grad_first + matmul_last(
-        grad_values.reshape(length, kv_local * HEAD_WIDTH).astype(jnp.bfloat16), frozen_value_weight
-    )
-    grad_first = lax.psum(grad_first.astype(jnp.bfloat16), "mp").astype(jnp.float32)
+    (grad_query_pre,) = query_pull(jnp.concatenate(grad_queries, axis=0))
+    grad_query_low = grad_query_pre.reshape(2 * block, heads * HEAD_WIDTH).astype(jnp.bfloat16)
+    grad_key_own = pair_total[0].transpose(1, 0, 2)
+    grad_key_pre = rotate(grad_key_own, own_cosine[:, None, :], -own_sine[:, None, :])
+    grad_key_low = grad_key_pre.reshape(2 * block, key_heads * HEAD_WIDTH).astype(jnp.bfloat16)
+    grad_value_low = (
+        pair_total[1].transpose(1, 0, 2).reshape(2 * block, key_heads * HEAD_WIDTH).astype(jnp.bfloat16)
+    )
+    grad_first = matmul_last(grad_key_low, key_weight) + matmul_last(grad_value_low, value_weight)
+    at = 0
+    for weight in query_weights:
+        grad_first = grad_first + matmul_last(grad_query_low[:, at : at + weight.shape[1]], weight)
+        at += weight.shape[1]
     (grad_embed_norm,) = first_pull(grad_first)
-    embedded_grad_low = (grad_hidden + grad_embed_norm).astype(jnp.bfloat16)
-    half = length // mp_count
-    row_start = mp_index * half
-    my_index = lax.dynamic_slice_in_dim(token_index, row_start, half, 0)
-    my_grad = lax.dynamic_slice_in_dim(embedded_grad_low, row_start, half, 0)
-    chosen_mine = lax.dynamic_slice_in_dim(chosen, row_start, half, 0)
-    dense_pool = (
-        jnp.zeros((pooled_all.shape[0], pooled_all.shape[1]), jnp.float32)
-        .at[my_index]
-        .add(matmul_last(my_grad, embed_full))
-    )
-    grad_pooled, embed_grad = (
-        lax.psum_scatter(dense_pool, ("dp", "mp"), scatter_dimension=0, tiled=True),
-        lax.psum_scatter(
-            matmul_first(chosen_mine, my_grad), ("dp", "mp"), scatter_dimension=0, tiled=True
-        ),
-    )
-    piece_grads = []
-    totals = None
-    for step in range(MICRO):
-        gathered_back = (
-            lax.all_gather(hyper_input, ("dp", "mp"), axis=0, tiled=True),
-            lax.all_gather(hyper_output, ("dp", "mp"), axis=0, tiled=True),
-            lax.all_gather(hyper_expand, ("dp", "mp"), axis=0, tiled=True),
-            lax.all_gather(hyper_reduce, ("dp", "mp"), axis=0, tiled=True),
-            lax.all_gather(hyper_norms, ("dp", "mp"), axis=0, tiled=True),
-        )
-        start = step * per_micro
-        grad_rows, grads = hyper_backward(
-            saved_parts[step], grad_pooled[start : start + per_micro], gathered_back
-        )
-        piece_grads.append(grad_rows)
-        if step == 0:
-            totals = grads
-        else:
-            totals = jax.tree.map(jnp.add, totals, grads)
-    reduced = (
-        lax.psum_scatter(totals[0], ("dp", "mp"), scatter_dimension=0, tiled=True),
-        lax.psum_scatter(totals[1], ("dp", "mp"), scatter_dimension=0, tiled=True),
-        lax.psum_scatter(totals[2], ("dp", "mp"), scatter_dimension=0, tiled=True),
-        lax.psum_scatter(totals[3], ("dp", "mp"), scatter_dimension=0, tiled=True),
-        lax.psum_scatter(totals[4], ("dp", "mp"), scatter_dimension=0, tiled=True),
-    )
-    pieces_gradient = jnp.concatenate(piece_grads, axis=0).astype(jnp.bfloat16)
+    embedded_grad_low = (jnp.concatenate(grad_hidden, axis=0) + grad_embed_norm).astype(
+        jnp.bfloat16
+    )
+    token_grad = matmul_last(embedded_grad_low, embed_full).astype(jnp.bfloat16)
+    embed_grad = matmul_first(chosen_own, embedded_grad_low)
+
+    def give_back(turn, total):
+        taker = taker_choice(own_rank, own_owner, turn, capacity, devices)
+        leaving = matmul_first(taker, token_grad).astype(jnp.bfloat16)
+        came = exchange(leaving)
+        return total + matmul_first(sender_choice(present, standing, turn, capacity), came)
+
+    grad_pooled = give_back(0, jnp.zeros(pooled.shape, jnp.float32))
+    grad_pooled = lax.fori_loop(1, rounds, give_back, grad_pooled)
+
+    grad_rows, grads = hyper_backward(saved, grad_pooled, gathered)
+    input_grad, output_grad, expand_grad, reduce_grad, norm_grad = grads
+    final_order = spread_order[::-1]
+    packed = jnp.concatenate(
+        [
+            fold(input_grad, devices),
+            fold(output_grad, devices),
+            fold(expand_grad, devices),
+            reduce_grad.reshape(devices, hyper_reduce.shape[0], UNIT),
+            fold(jnp.pad(norm_grad, ((0, 0), (0, UNIT - norm_grad.shape[1]))), devices),
+        ],
+        axis=1,
+    )
+    embed_own = scatter_blocks(fold(embed_grad, devices), me, devices, final_order)
+    own = scatter_blocks(packed, me, devices, final_order)
+
+    def spread(rows, parts):
+        return unfold(rows[None], parts)
+
+    at = in_parts * own_rows
+    input_own = spread(own[:at], in_parts)
+    output_own = own[at : at + own_rows]
+    at += own_rows
+    expand_own = spread(own[at : at + expand_parts * own_rows], expand_parts)
+    at += expand_parts * own_rows
+    reduce_own = own[at : at + hyper_reduce.shape[0]]
+    at += hyper_reduce.shape[0]
+    norm_own = own[at:, : hyper_norms.shape[1]]
     return (
         model_out,
-        pieces_gradient,
-        reduced[0],
-        reduced[1],
-        reduced[2],
-        reduced[3],
-        reduced[4],
-        embed_grad,
+        grad_rows.astype(jnp.bfloat16),
+        input_own,
+        output_own,
+        expand_own,
+        reduce_own,
+        norm_own,
+        spread(embed_own, embed_parts),
     )
 
 

time: 2760 us -> 1170 us (0.42)
  waiting for transfers between devices: 1840 us -> 221 us
  blocking collectives: 137 us -> 21.8 us
  local copies, waits for them, and re-layouts: 129 us -> 226 us
  starting transfers between devices: 1.78 us -> 45 us
    reduce_scatter x7 -> x0, waiting for transfers between devices: 1340 us -> none  [the longest x1 681 us: body(): lax.psum_scatter(dense_pool, ('dp', 'mp'), scatter_dimension=0, tiled=True)]
    psum x3 -> x0, waiting for transfers between devices: 296 us -> none  [the longest x1 107 us: body(): lax.psum(grad_second.astype(jnp.bfloat16), 'mp').astype(jnp.float32)]
    ppermute x0 -> x33, waiting for transfers between devices: none -> 190 us  [swap(): lax.ppermute(value, ('dp', 'mp'), [(d, d ^ mask) for d in range(devices)])]
    all_gather x5 -> x0, waiting for transfers between devices: 155 us -> none  [the longest x1 111 us: body(): pooled_all = lax.all_gather(pooled_own, ('dp', 'mp'), axis=0, tiled=True)]
    all_gather x2 -> x1, blocking collectives: 137 us -> 21.8 us  [route(): every = lax.all_gather(token_index, 'dp', axis=0, tiled=True)]
    unnamed x17 -> x0, waiting for transfers between devices: 42.6 us -> none
    ppermute x0 -> x33, starting transfers between devices: none -> 33.2 us  [swap(): lax.ppermute(value, ('dp', 'mp'), [(d, d ^ mask) for d in range(devices)])]
    reshape x0 -> x14, local copies, waits for them, and re-layouts: none -> 32.8 us  [the longest x10 28.8 us: fold(): value.reshape(devices, each, parts, UNIT).transpose(0, 2, 1, 3)]
  transfers between devices with their start and end apart: 16 -> 35, of which waited for: 12 -> 18; matrix products, arithmetic and copies ran while one was open for 12% -> 43% of each run, Pallas kernels for 0% -> 0%
where the time goes in v1:
time: 1170 us; the launch traced here: 1160 us
  matrix products  410 us (35%)
  other arithmetic  229 us (20%)
  local copies, waits for them, and re-layouts  226 us (19%)
  waiting for transfers between devices  221 us (19%)
  starting transfers between devices  45 us (4%)
  blocking collectives  21.8 us (2%)
    ppermute x33, waiting for transfers between devices, swap(): lax.ppermute(value, ('dp', 'mp'), [(d, d ^ mask) for d in range(devices)])  190 us
    dot_general x23, matrix products, matmul_last(): lax.dot_general(left, right, (((1,), (1,)), ((), ())), preferred_element_...  132 us
    dot_general x29, matrix products, matmul(): return jnp.dot(left, right, preferred_element_type=jnp.float32)  127 us
    unnamed x492, local copies, waits for them, and re-layouts  58.9 us
    convert_element_type x2, local copies, waits for them, and re-layouts, hyper_backward(): grad_pair = jnp.stack([grad_keys, grad_values], axis=2).astype(jnp.bfloat...  46.9 us
    dot_general x8, matrix products, attention_backward(): jnp.einsum('qrd,kd->rqk', grad_group, value_group, preferred_element_type...  39.2 us
    unnamed x20, other arithmetic  38.3 us
    ppermute x33, starting transfers between devices, swap(): lax.ppermute(value, ('dp', 'mp'), [(d, d ^ mask) for d in range(devices)])  33.2 us
  transfers between devices with their start and end apart: 35, of which 18 were waited for; matrix products, arithmetic and copies ran while one was open for 43% of the time, Pallas kernels for 0%

profile of v1, /device:TPU:0, one launch (start us, length us, event | category | flops | bytes accessed | tf_op | source)
XLA Modules:
  0.0 1160.2 jit_solution(4935250834571195506)
XLA Ops:
  20.9 21.8 %all_gather.3 = s32[16384]{0:T(1024)S(1)} all-gather(s32[1024]{0:T(1024)S(1)} %copy-done.198), channel_id=1, replica_groups=mesh['dp'=16,'mp'=2] {'dp'}, dimensions={0}, use_global_device_ids=true | all-gather | bytes 69632 | tf_op jit(solution)/shard_map/all_gather | solution.py:343
  45.3 12.2 %and_reduce_fusion = (pred[32,512]{1,0:T(8,128)(4,1)S(1)}, pred[32,512]{1,0:T(8,128)(4,1)S(1)}) fusion(s32[32,512]{1,0:T(8,128)S(1)} %reshape.2097, pred[512,512]{1,0:T(8,128)(4,1)S(1)} %iota_compare_fusion.21, s32[512]{0:T(512)S(1)} %iota_add_fusion.2), kind=kLoop, calls=%fused_computation.30 | loop fusion | flops 41910272 | bytes 362496 | tf_op jit(solution)/shard_map/reduce_or | solution.py:357
  57.6 9.9 convert_reduce_fusion
  67.8 7.5 copy.351
  84.4 12.0 %fusion.124 = f32[512,2816]{1,0:T(8,128)} fusion(bf16[2816,2048]{1,0:T(8,128)(2,1)} %param.48, bf16[256,2048]{1,0:T(8,128)(2,1)S(1)} %get-tuple-element.259, bf16[256,2048]{1,0:T(8,128)(2,1)S(1)} %get-tuple-element.258), kind=kOutput, calls=%fused_computation.262 | convolution fusion | flops 5909774336 | bytes 19398656 | tf_op jit(solution)/shard_map/dot_general | solution.py:27
  104.0 6.8 collective-permute-done.2
  118.1 19.4 %collective-permute-done.3 = bf16[2,2,2,1,1,64,512]{6,5,0,1,2,4,3:T(8,128)(2,1)} collective-permute-done((bf16[2,2,2,1,1,64,512]{6,5,0,1,2,4,3:T(8,128)(2,1)}, bf16[2,2,2,1,1,64,512]{6,5,0,1,2,4,3:T(8,128)(2,1)}, u32[]{:S(2)}, u32[]{:S(2)}) %collective-permute-start.3) | collective-permute-done | bytes 524320 | tf_op jit(solution)/shard_map/ppermute | solution.py:214
  142.2 6.7 convert_element_type.401
  168.1 8.0 copy.358
  179.6 13.9 %collective-permute-done.8 = bf16[2,2,2,1,1,208,512]{6,5,4,3,2,1,0:T(8,128)(2,1)} collective-permute-done((bf16[2,2,2,1,1,208,512]{6,5,4,3,2,1,0:T(8,128)(2,1)}, bf16[2,2,2,1,1,208,512]{6,5,4,3,2,1,0:T(8,128)(2,1)}, u32[]{:S(2)}, u32[]{:S(2)}) %collective-permute-start.8) | collective-permute-done | bytes 1703968 | tf_op jit(solution)/shard_map/ppermute | solution.py:214
  197.1 7.1 convolution_convert_fusion.1
  204.2 22.2 %reshape.2104 = bf16[512,8,2,8,64]{4,3,2,1,0:T(8,128)(2,1)} reshape(bf16[4096,1024]{1,0:T(8,128)(2,1)} %convolution_convert_fusion.1) | data formatting | bytes 16777216 | tf_op jit(solution)/shard_map/reshape | solution.py:91
  226.5 9.9 multiply_reduce_fusion.3
  244.8 8.2 multiply_reduce_fusion.2
  266.5 12.2 %multiply_convert_fusion.5 = (bf16[512,2048]{1,0:T(8,128)(2,1)S(1)}, f32[512,2048]{1,0:T(8,128)}, f32[512,2048]{1,0:T(8,128)}) fusion(bf16[512,2048]{1,0:T(8,128)(2,1)S(1)} %bitcast.738, f32[512,512]{0,1:T(8,128)S(1)} %get-tuple-element.330, f32[512]{0:T(512)S(1)} %bitcast.788, f32[512]{0:T(512)S(1)} %bitcast.783, f32[512]{0:T(512)S(1)} %fusion.323, ...), kind=kOutput, calls=%fused_computation.192 | convolution fusion | flops 1143209984 | bytes 13639680 | tf_op jit(solution)/shard_map/dot_general | solution.py:17
  281.9 6.5 all-to-all-start.2
  289.0 12.7 %fusion.128 = f32[512,2816]{1,0:T(8,128)} fusion(bf16[2816,2048]{1,0:T(8,128)(2,1)} %param.48, bf16[256,2048]{1,0:T(8,128)(2,1)} %get-tuple-element.260, bf16[256,2048]{1,0:T(8,128)(2,1)S(1)} %copy-done.69), kind=kOutput, calls=%fused_computation.266 | convolution fusion | flops 5909774336 | bytes 19398656 | tf_op jit(solution)/shard_map/dot_general | solution.py:27
  435.0 41.8 %collective-permute-done.18 = bf16[256,2048]{1,0:T(8,128)(2,1)S(1)} collective-permute-done((bf16[256,2048]{1,0:T(8,128)(2,1)S(1)}, bf16[256,2048]{1,0:T(8,128)(2,1)S(1)}, u32[]{:S(2)}, u32[]{:S(2)}) %collective-permute-start.18) | collective-permute-done | bytes 1048608 | tf_op jit(solution)/shard_map/ppermute | solution.py:214
  476.8 8.8 fusion.144
  485.5 11.2 fusion.143
  496.7 17.3 %fusion.116 = f32[512,2048]{1,0:T(8,128)} fusion(bf16[2048,2816]{1,0:T(8,128)(2,1)} %param.46, f32[512,2816]{1,0:T(8,128)} %fusion.144, f32[512,2816]{1,0:T(8,128)} %fusion.128, f32[512,2816]{1,0:T(8,128)} %fusion.143), kind=kOutput, calls=%fused_computation.246 | convolution fusion | flops 5921439744 | bytes 33030144 | tf_op jit(solution)/shard_map/dot_general | solution.py:27
  514.0 13.1 %add_convert_fusion.3 = bf16[512,2048]{1,0:T(8,128)(2,1)S(1)} fusion(f32[512,2048]{1,0:T(8,128)} %fusion.116, bf16[2048,2816]{1,0:T(8,128)(2,1)} %param.47, f32[512,2816]{1,0:T(8,128)} %fusion.128, f32[512,2816]{1,0:T(8,128)} %fusion.144), kind=kOutput, calls=%fused_computation.188 | convolution fusion | flops 5916327936 | bytes 29360128 | tf_op jit(solution)/shard_map/dot_general | solution.py:27
  529.5 13.3 %fusion.115 = f32[512,2048]{1,0:T(8,128)} fusion(bf16[2816,2048]{1,0:T(8,128)(2,1)} %param.48, f32[512,2816]{1,0:T(8,128)S(1)} %copy-done.206, f32[512,2816]{1,0:T(8,128)} %fusion.144), kind=kOutput, calls=%fused_computation.245 | convolution fusion | flops 5914230784 | bytes 27262976 | tf_op jit(solution)/shard_map/dot_general | solution.py:17
  542.7 9.5 fusion.146
  552.2 11.8 %fusion.145 = f32[512,2816]{1,0:T(8,128)} fusion(bf16[2048,2816]{1,0:T(8,128)(2,1)} %param.47, bf16[256,2048]{1,0:T(8,128)(2,1)} %collective-permute-done.16, bf16[256,2048]{1,0:T(8,128)(2,1)} %get-tuple-element.321), kind=kOutput, calls=%fused_computation.306 | convolution fusion | flops 5909774336 | bytes 19398656 | tf_op jit(solution)/shard_map/dot_general | solution.py:17
  564.1 16.9 %fusion.118 = f32[512,2048]{1,0:T(8,128)} fusion(bf16[2048,2816]{1,0:T(8,128)(2,1)} %param.46, f32[512,2816]{1,0:T(8,128)} %fusion.146, f32[512,2816]{1,0:T(8,128)} %fusion.124, f32[512,2816]{1,0:T(8,128)} %fusion.145), kind=kOutput, calls=%fused_computation.247 | convolution fusion | flops 5921439744 | bytes 33030144 | tf_op jit(solution)/shard_map/dot_general | solution.py:27
  580.9 13.1 %add_convert_fusion.4 = bf16[512,2048]{1,0:T(8,128)(2,1)S(1)} fusion(f32[512,2048]{1,0:T(8,128)} %fusion.118, bf16[2048,2816]{1,0:T(8,128)(2,1)} %param.47, f32[512,2816]{1,0:T(8,128)} %fusion.124, f32[512,2816]{1,0:T(8,128)} %fusion.146), kind=kOutput, calls=%fused_computation.189 | convolution fusion | flops 5916327936 | bytes 29360128 | tf_op jit(solution)/shard_map/dot_general | solution.py:27
  595.1 13.0 %fusion.114 = f32[512,2048]{1,0:T(8,128)S(1)} fusion(bf16[2816,2048]{1,0:T(8,128)(2,1)} %param.48, f32[512,2816]{1,0:T(8,128)} %fusion.145, f32[512,2816]{1,0:T(8,128)} %fusion.146), kind=kOutput, calls=%fused_computation.244 | convolution fusion | flops 5914230784 | bytes 27262976 | tf_op jit(solution)/shard_map/dot_general | solution.py:17
  608.1 9.8 collective-permute-done.20
  634.0 8.2 fusion.32
  709.7 8.2 fusion.20
  787.5 6.6 multiply_reduce_fusion.7
  805.4 25.1 %all-to-all-done.3 = bf16[32,32,512]{2,1,0:T(8,128)(2,1)} async-done(((bf16[32,32,512]{2,1,0:T(8,128)(2,1)}), bf16[32,32,512]{2,1,0:T(8,128)(2,1)}, u32[]{:S(2)}, u32[]{:S(2)}) %all-to-all-start.3) | async-done | bytes 1048608 | tf_op jit(solution)/shard_map/all_to_all | solution.py:395
  855.1 6.4 reshape.2123
  867.4 9.2 multiply_reduce_fusion.1
  880.9 7.3 multiply_reduce_fusion
  896.3 6.3 maximum_convert_fusion
  902.7 24.1 %copy.417 = bf16[512,8,2,8,64]{4,3,2,1,0:T(8,128)(2,1)} copy(bf16[512,8,2,8,64]{0,4,3,2,1:T(8,128)(2,1)} %maximum_convert_fusion) | data formatting | bytes 16777216 | tf_op jit(solution)/shard_map/convert_element_type | solution.py:189
  926.8 7.2 fusion.225
  943.0 22.8 %convert_element_type.497 = bf16[4096,1024]{1,0:T(8,128)(2,1)} reshape(bf16[512,8,2,8,64]{4,3,2,1,0:T(8,128)(2,1)} %copy.417) | data formatting | bytes 16777216 | tf_op jit(solution)/shard_map/convert_element_type | solution.py:189
  965.8 8.3 fusion.90
  1034.2 6.6 collective-permute-done.17
  1041.1 22.3 %collective-permute-done.19 = bf16[512,1024]{1,0:T(8,128)(2,1)} collective-permute-done((bf16[512,1024]{1,0:T(8,128)(2,1)}, bf16[512,1024]{1,0:T(8,128)(2,1)}, u32[]{:S(2)}, u32[]{:S(2)}) %collective-permute-start.19) | collective-permute-done | bytes 1048608 | tf_op jit(solution)/shard_map/ppermute | solution.py:214
  1064.9 9.8 collective-permute-done.29
  1089.5 20.8 %collective-permute-done.24 = bf16[2,2,2,1,1,208,512]{6,5,4,3,2,1,0:T(8,128)(2,1)} collective-permute-done((bf16[2,2,2,1,1,208,512]{6,5,4,3,2,1,0:T(8,128)(2,1)}, bf16[2,2,2,1,1,208,512]{6,5,4,3,2,1,0:T(8,128)(2,1)}, u32[]{:S(2)}, u32[]{:S(2)}) %collective-permute-start.24) | collective-permute-done | bytes 1703968 | tf_op jit(solution)/shard_map/ppermute | solution.py:214
  1117.4 15.7 %collective-permute-done.25 = bf16[2,2,1,1,1,208,512]{6,5,4,3,2,1,0:T(8,128)(2,1)S(1)} collective-permute-done((bf16[2,2,1,1,1,208,512]{6,5,4,3,2,1,0:T(8,128)(2,1)S(1)}, bf16[2,2,1,1,1,208,512]{6,5,4,3,2,1,0:T(8,128)(2,1)S(1)}, u32[]{:S(2)}, u32[]{:S(2)}) %collective-permute-start.25) | collective-permute-done | bytes 852000 | tf_op jit(solution)/shard_map/ppermute | solution.py:214
  1138.1 6.3 collective-permute-done.26
  1148.2 8.0 copy.428
  (891 shorter events, 546.9 us)
Async XLA Ops:
  2.3 94.8 %collective-permute-start = (bf16[1,1,1,1,1,64,512]{6,5,0,1,2,4,3:T(8,128)(2,1)S(1)}, bf16[1,1,1,1,1,64,512]{6,5,0,1,2,4,3:T(8,128)(2,1)S(1)}, u32[]{:S(2)}, u32[]{:S(2)}) collective-permute-start(bf16[1,1,1,1,1,64,512]{6,5,0,1,2,4,3:T(8,128)(2,1)S(1)} %get-tuple-element.320), channel_id=1, source_target_pairs={{0,16},{1,17},{2,18},{3,19},{4,20},{5,21},{6,22},{7,23},{8,24},{9,... | collective-permute-start | bytes 196616 | tf_op jit(solution)/shard_map/ppermute | solution.py:214
  9.1 94.5 %collective-permute-start.5 = (bf16[1,1,1,1,1,208,512]{6,5,4,3,2,1,0:T(8,128)(2,1)S(1)}, bf16[1,1,1,1,1,208,512]{6,5,4,3,2,1,0:T(8,128)(2,1)S(1)}, u32[]{:S(2)}, u32[]{:S(2)}) collective-permute-start(bf16[1,1,1,1,1,208,512]{6,5,4,3,2,1,0:T(8,128)(2,1)S(1)} %get-tuple-element.306), channel_id=1, source_target_pairs={{0,16},{1,17},{2,18},{3,19},{4,20},{5,21},{6,22},{7,23},{8,24},{9,... | collective-permute-start | bytes 638984 | tf_op jit(solution)/shard_map/ppermute | solution.py:214
  11.4 290.3 %collective-permute-start.10 = (bf16[2048,256]{1,0:T(8,128)(2,1)}, bf16[2048,256]{1,0:T(8,128)(2,1)}, u32[]{:S(2)}, u32[]{:S(2)}) collective-permute-start(bf16[2048,256]{1,0:T(8,128)(2,1)} %pad_maximum_fusion.9), channel_id=1, source_target_pairs={{0,1},{1,0},{2,3},{3,2},{4,5},{5,4},{6,7},{7,6},{8,9},{9,8},{10,11... | collective-permute-start | bytes 3145736 | tf_op jit(solution)/shard_map/ppermute | solution.py:214
  16.6 287.5 %collective-permute-start.14 = (bf16[512,2048]{1,0:T(8,128)(2,1)}, bf16[512,2048]{1,0:T(8,128)(2,1)}, u32[]{:S(2)}, u32[]{:S(2)}) collective-permute-start(bf16[512,2048]{1,0:T(8,128)(2,1)} %constant_dynamic-slice_fusion.4), channel_id=1, source_target_pairs={{0,1},{1,0},{2,3},{3,2},{4,5},{5,4},{6,7},{7,6},{8,9},{9,8},{10,11... | collective-permute-start | bytes 6291464 | tf_op jit(solution)/shard_map/ppermute | solution.py:214
  18.3 286.0 %collective-permute-start.12 = (bf16[2048,512]{1,0:T(8,128)(2,1)}, bf16[2048,512]{1,0:T(8,128)(2,1)}, u32[]{:S(2)}, u32[]{:S(2)}) collective-permute-start(bf16[2048,512]{1,0:T(8,128)(2,1)} %constant_dynamic-slice_fusion.9), channel_id=1, source_target_pairs={{0,1},{1,0},{2,3},{3,2},{4,5},{5,4},{6,7},{7,6},{8,9},{9,8},{10,11... | collective-permute-start | bytes 6291464 | tf_op jit(solution)/shard_map/ppermute | solution.py:214
  45.3 67.6 %copy-start.130 = (f32[1024,32]{0,1:T(8,128)}, f32[1024,32]{0,1:T(8,128)S(1)}, u32[]{:S(2)}) copy-start(f32[1024,32]{0,1:T(8,128)S(1)} %get-tuple-element.327) | copy-start | bytes 393220
  45.3 67.6 %copy-start.132 = (f32[1024,32]{0,1:T(8,128)}, f32[1024,32]{0,1:T(8,128)S(1)}, u32[]{:S(2)}) copy-start(f32[1024,32]{0,1:T(8,128)S(1)} %get-tuple-element.328) | copy-start | bytes 393220
  67.7 82.0 %copy-start.81 = (s32[32,512]{1,0:T(8,128)}, s32[32,512]{1,0:T(8,128)S(1)}, u32[]{:S(2)}) copy-start(s32[32,512]{1,0:T(8,128)S(1)} %convolution_convert_fusion.16) | copy-start | bytes 196612
  78.7 84.7 %copy-start.138 = (f32[512,8]{0,1:T(8,128)}, f32[512,8]{0,1:T(8,128)S(1)}, u32[]{:S(2)}) copy-start(f32[512,8]{0,1:T(8,128)S(1)} %broadcast_multiply_fusion) | copy-start | bytes 49156
  97.1 5.8 collective-permute-start.1
  102.9 7.9 collective-permute-start.2
  103.6 11.4 collective-permute-start.6
  111.7 25.8 %collective-permute-start.3 = (bf16[2,2,2,1,1,64,512]{6,5,0,1,2,4,3:T(8,128)(2,1)}, bf16[2,2,2,1,1,64,512]{6,5,0,1,2,4,3:T(8,128)(2,1)}, u32[]{:S(2)}, u32[]{:S(2)}) collective-permute-start(bf16[2,2,2,1,1,64,512]{6,5,0,1,2,4,3:T(8,128)(2,1)} %maximum_select_fusion.9), channel_id=1, source_target_pairs={{0,1},{1,0},{2,3},{3,2},{4,5},{5,4},{6,7},{7,6},{8,9},{9,8},{10,11... | collective-permute-start | bytes 1572872 | tf_op jit(solution)/shard_map/ppermute | solution.py:214
  116.3 35.7 %collective-permute-start.7 = (bf16[2,2,1,1,1,208,512]{6,5,1,0,4,3,2:T(8,128)(2,1)}, bf16[2,2,1,1,1,208,512]{6,5,1,0,4,3,2:T(8,128)(2,1)S(1)}, u32[]{:S(2)}, u32[]{:S(2)}) collective-permute-start(bf16[2,2,1,1,1,208,512]{6,5,1,0,4,3,2:T(8,128)(2,1)} %maximum_select_fusion.8), channel_id=1, source_target_pairs={{0,4},{1,5},{2,6},{3,7},{4,0},{5,1},{6,2},{7,3},{8,12},{9,13},{10,... | collective-permute-start | bytes 2555912 | tf_op jit(solution)/shard_map/ppermute | solution.py:214
  138.9 18.2 %collective-permute-start.4 = (bf16[2,2,2,1,2,64,512]{6,5,0,1,2,4,3:T(8,128)(2,1)S(1)}, bf16[2,2,2,1,2,64,512]{6,5,0,1,2,4,3:T(8,128)(2,1)}, u32[]{:S(2)}, u32[]{:S(2)}) collective-permute-start(bf16[2,2,2,1,2,64,512]{6,5,0,1,2,4,3:T(8,128)(2,1)S(1)} %maximum_select_fusion.6), channel_id=1, source_target_pairs={{0,2},{1,3},{2,0},{3,1},{4,6},{5,7},{6,4},{7,5},{8,10},{9,11},{10,... | collective-permute-start | bytes 3145736 | tf_op jit(solution)/shard_map/ppermute | solution.py:214
  153.6 39.9 %collective-permute-start.8 = (bf16[2,2,2,1,1,208,512]{6,5,4,3,2,1,0:T(8,128)(2,1)}, bf16[2,2,2,1,1,208,512]{6,5,4,3,2,1,0:T(8,128)(2,1)}, u32[]{:S(2)}, u32[]{:S(2)}) collective-permute-start(bf16[2,2,2,1,1,208,512]{6,5,4,3,2,1,0:T(8,128)(2,1)} %copy.367), channel_id=1, source_target_pairs={{0,1},{1,0},{2,3},{3,2},{4,5},{5,4},{6,7},{7,6},{8,9},{9,8},{10,11... | collective-permute-start | bytes 5111816 | tf_op jit(solution)/shard_map/ppermute | solution.py:214
  197.0 58.7 %collective-permute-start.9 = (bf16[2,2,2,1,2,208,512]{6,5,4,3,2,1,0:T(8,128)(2,1)S(1)}, bf16[2,2,2,1,2,208,512]{6,5,4,3,2,1,0:T(8,128)(2,1)}, u32[]{:S(2)}, u32[]{:S(2)}) collective-permute-start(bf16[2,2,2,1,2,208,512]{6,5,4,3,2,1,0:T(8,128)(2,1)S(1)} %maximum_select_fusion.1), channel_id=1, source_target_pairs={{0,2},{1,3},{2,0},{3,1},{4,6},{5,7},{6,4},{7,5},{8,10},{9,11},{10,... | collective-permute-start | bytes 10223624 | tf_op jit(solution)/shard_map/ppermute | solution.py:214
  281.9 32.7 %all-to-all-start.2 = ((bf16[32,32,512]{2,1,0:T(8,128)(2,1)}), bf16[32,32,512]{2,1,0:T(8,128)(2,1)}, u32[]{:S(2)}, u32[]{:S(2)}) async-start(bf16[32,32,512]{2,1,0:T(8,128)(2,1)} %bitcast.750), calls=%async_computation.2 | async-start | bytes 2097152 | tf_op jit(solution)/shard_map/all_to_all | solution.py:395
  304.0 102.8 %collective-permute-start.15 = (bf16[512,2048]{1,0:T(8,128)(2,1)}, bf16[512,2048]{1,0:T(8,128)(2,1)}, u32[]{:S(2)}, u32[]{:S(2)}) collective-permute-start(bf16[512,2048]{1,0:T(8,128)(2,1)} %collective-permute-done.14), channel_id=1, source_target_pairs={{0,2},{1,3},{2,0},{3,1},{4,6},{5,7},{6,4},{7,5},{8,10},{9,11},{10,... | collective-permute-start | bytes 6291464 | tf_op jit(solution)/shard_map/ppermute | solution.py:214
  304.4 26.2 %collective-permute-start.13 = (bf16[2048,512]{1,0:T(8,128)(2,1)}, bf16[2048,512]{1,0:T(8,128)(2,1)}, u32[]{:S(2)}, u32[]{:S(2)}) collective-permute-start(bf16[2048,512]{1,0:T(8,128)(2,1)} %collective-permute-done.12), channel_id=1, source_target_pairs={{0,2},{1,3},{2,0},{3,1},{4,6},{5,7},{6,4},{7,5},{8,10},{9,11},{10,... | collective-permute-start | bytes 6291464 | tf_op jit(solution)/shard_map/ppermute | solution.py:214
  317.6 30.4 %collective-permute-start.11 = (bf16[512,512]{1,0:T(8,128)(2,1)}, bf16[512,512]{1,0:T(8,128)(2,1)}, u32[]{:S(2)}, u32[]{:S(2)}) collective-permute-start(bf16[512,512]{1,0:T(8,128)(2,1)} %get-tuple-element.121), channel_id=1, source_target_pairs={{0,1},{1,0},{2,3},{3,2},{4,5},{5,4},{6,7},{7,6},{8,9},{9,8},{10,11... | collective-permute-start | bytes 1572872 | tf_op jit(solution)/shard_map/ppermute | solution.py:214
  344.6 55.6 %copy-start.3 = (bf16[512,32,32]{0,2,1:T(8,128)(2,1)}, bf16[512,32,32]{0,2,1:T(8,128)(2,1)S(1)}, u32[]{:S(2)}) copy-start(bf16[512,32,32]{0,2,1:T(8,128)(2,1)S(1)} %get-tuple-element.256) | copy-start | bytes 3145732
  344.6 55.6 %copy-start.5 = (bf16[512,32,32]{0,2,1:T(8,128)(2,1)}, bf16[512,32,32]{0,2,1:T(8,128)(2,1)S(1)}, u32[]{:S(2)}) copy-start(bf16[512,32,32]{0,2,1:T(8,128)(2,1)S(1)} %get-tuple-element.257) | copy-start | bytes 3145732
  359.8 58.8 %copy-start.52 = (bf16[4,1024,64]{1,2,0:T(8,128)(2,1)}, bf16[4,1024,64]{1,2,0:T(8,128)(2,1)S(1)}, u32[]{:S(2)}) copy-start(bf16[4,1024,64]{1,2,0:T(8,128)(2,1)S(1)} %get-tuple-element.325) | copy-start | bytes 1572868
  420.8 55.9 %slice-start.22 = ((s8[11534336]{0:T(1024)(128)(4,1)}), s8[3145728]{0:T(1024)(128)(4,1)S(1)}, s32[]{:S(2)}) async-start(s8[11534336]{0:T(1024)(128)(4,1)} %bitcast.799), calls=%async_computation.26 | async-start | bytes 6291456
  422.1 54.6 %slice-start.23 = ((s8[11534336]{0:T(1024)(128)(4,1)}), s8[4194304]{0:T(1024)(128)(4,1)S(1)}, s32[]{:S(2)}) async-start(s8[11534336]{0:T(1024)(128)(4,1)} %bitcast.799), calls=%async_computation.27 | async-start | bytes 8388608
  424.6 52.1 %slice-start.24 = ((s8[11534336]{0:T(1024)(128)(4,1)}), s8[4194304]{0:T(1024)(128)(4,1)S(1)}, s32[]{:S(2)}) async-start(s8[11534336]{0:T(1024)(128)(4,1)} %bitcast.799), calls=%async_computation.28 | async-start | bytes 8388608
  427.3 58.3 %copy-start.185 = (f32[256]{0:T(256)}, f32[256]{0:T(256)S(1)}, u32[]{:S(2)}) copy-start(f32[256]{0:T(256)S(1)} %get-tuple-element.350) | copy-start | bytes 3076
  427.3 58.3 %copy-start.189 = (f32[256]{0:T(256)}, f32[256]{0:T(256)S(1)}, u32[]{:S(2)}) copy-start(f32[256]{0:T(256)S(1)} %fusion.326) | copy-start | bytes 3076
  429.9 112.8 %collective-permute-start.16 = (bf16[256,2048]{1,0:T(8,128)(2,1)}, bf16[256,2048]{1,0:T(8,128)(2,1)}, u32[]{:S(2)}, u32[]{:S(2)}) collective-permute-start(bf16[256,2048]{1,0:T(8,128)(2,1)} %get-tuple-element.321), channel_id=1, source_target_pairs={{0,1},{1,0},{2,3},{3,2},{4,5},{5,4},{6,7},{7,6},{8,9},{9,8},{10,11... | collective-permute-start | bytes 3145736 | tf_op jit(solution)/shard_map/ppermute | solution.py:214
  430.4 46.3 %collective-permute-start.18 = (bf16[256,2048]{1,0:T(8,128)(2,1)S(1)}, bf16[256,2048]{1,0:T(8,128)(2,1)S(1)}, u32[]{:S(2)}, u32[]{:S(2)}) collective-permute-start(bf16[256,2048]{1,0:T(8,128)(2,1)S(1)} %get-tuple-element.322), channel_id=1, source_target_pairs={{0,1},{1,0},{2,3},{3,2},{4,5},{5,4},{6,7},{7,6},{8,9},{9,8},{10,11... | collective-permute-start | bytes 3145736 | tf_op jit(solution)/shard_map/ppermute | solution.py:214
  527.2 90.7 %copy-start.62 = (bf16[512,2048]{1,0:T(8,128)(2,1)}, bf16[512,2048]{1,0:T(8,128)(2,1)S(1)}, u32[]{:S(2)}) copy-start(bf16[512,2048]{1,0:T(8,128)(2,1)S(1)} %add_convert_fusion.3) | copy-start | bytes 6291460
  528.3 79.8 %collective-permute-start.21 = (bf16[256,2048]{1,0:T(8,128)(2,1)}, bf16[256,2048]{1,0:T(8,128)(2,1)S(1)}, u32[]{:S(2)}, u32[]{:S(2)}) collective-permute-start(bf16[256,2048]{1,0:T(8,128)(2,1)} %slice.550), channel_id=1, source_target_pairs={{0,1},{1,0},{2,3},{3,2},{4,5},{5,4},{6,7},{7,6},{8,9},{9,8},{10,11... | collective-permute-start | bytes 3145736 | tf_op jit(solution)/shard_map/ppermute | solution.py:214
  594.2 23.7 %collective-permute-start.20 = (bf16[256,2048]{1,0:T(8,128)(2,1)S(1)}, bf16[256,2048]{1,0:T(8,128)(2,1)S(1)}, u32[]{:S(2)}, u32[]{:S(2)}) collective-permute-start(bf16[256,2048]{1,0:T(8,128)(2,1)S(1)} %slice.548), channel_id=1, source_target_pairs={{0,1},{1,0},{2,3},{3,2},{4,5},{5,4},{6,7},{7,6},{8,9},{9,8},{10,11... | collective-permute-start | bytes 3145736 | tf_op jit(solution)/shard_map/ppermute | solution.py:214
  771.6 11.6 collective-permute-start.22
  798.9 31.6 %all-to-all-start.3 = ((bf16[32,32,512]{2,1,0:T(8,128)(2,1)}), bf16[32,32,512]{2,1,0:T(8,128)(2,1)}, u32[]{:S(2)}, u32[]{:S(2)}) async-start(bf16[32,32,512]{2,1,0:T(8,128)(2,1)} %bitcast.188), calls=%async_computation.3 | async-start | bytes 2097152 | tf_op jit(solution)/shard_map/all_to_all | solution.py:395
  994.4 29.8 %collective-permute-start.23 = (bf16[2,2,2,1,2,208,512]{6,5,4,3,2,1,0:T(8,128)(2,1)}, bf16[2,2,2,1,2,208,512]{6,5,4,3,2,1,0:T(8,128)(2,1)}, u32[]{:S(2)}, u32[]{:S(2)}) collective-permute-start(bf16[2,2,2,1,2,208,512]{6,5,4,3,2,1,0:T(8,128)(2,1)} %dynamic-slice_convert_fusion), channel_id=1, source_target_pairs={{0,2},{1,3},{2,0},{3,1},{4,6},{5,7},{6,4},{7,5},{8,10},{9,11},{10,... | collective-permute-start | bytes 10223624 | tf_op jit(solution)/shard_map/ppermute | solution.py:214
  1010.1 10.2 collective-permute-start.28
  1014.6 26.2 %collective-permute-start.17 = (bf16[512,1024]{1,0:T(8,128)(2,1)}, bf16[512,1024]{1,0:T(8,128)(2,1)S(1)}, u32[]{:S(2)}, u32[]{:S(2)}) collective-permute-start(bf16[512,1024]{1,0:T(8,128)(2,1)} %pad_maximum_fusion.12), channel_id=1, source_target_pairs={{0,1},{1,0},{2,3},{3,2},{4,5},{5,4},{6,7},{7,6},{8,9},{9,8},{10,11... | collective-permute-start | bytes 3145736 | tf_op jit(solution)/shard_map/ppermute | solution.py:214
  1019.8 43.6 %collective-permute-start.19 = (bf16[512,1024]{1,0:T(8,128)(2,1)}, bf16[512,1024]{1,0:T(8,128)(2,1)}, u32[]{:S(2)}, u32[]{:S(2)}) collective-permute-start(bf16[512,1024]{1,0:T(8,128)(2,1)} %pad_maximum_fusion.14), channel_id=1, source_target_pairs={{0,1},{1,0},{2,3},{3,2},{4,5},{5,4},{6,7},{7,6},{8,9},{9,8},{10,11... | collective-permute-start | bytes 3145736 | tf_op jit(solution)/shard_map/ppermute | solution.py:214
  1022.8 51.9 %collective-permute-start.29 = (bf16[2,2,2,1,1,64,512]{6,5,4,3,2,1,0:T(8,128)(2,1)}, bf16[2,2,2,1,1,64,512]{6,5,4,3,2,1,0:T(8,128)(2,1)}, u32[]{:S(2)}, u32[]{:S(2)}) collective-permute-start(bf16[2,2,2,1,1,64,512]{6,5,4,3,2,1,0:T(8,128)(2,1)} %dynamic-slice_convert_fusion.4), channel_id=1, source_target_pairs={{0,1},{1,0},{2,3},{3,2},{4,5},{5,4},{6,7},{7,6},{8,9},{9,8},{10,11... | collective-permute-start | bytes 1572872 | tf_op jit(solution)/shard_map/ppermute | solution.py:214
  1033.7 76.6 %collective-permute-start.24 = (bf16[2,2,2,1,1,208,512]{6,5,4,3,2,1,0:T(8,128)(2,1)}, bf16[2,2,2,1,1,208,512]{6,5,4,3,2,1,0:T(8,128)(2,1)}, u32[]{:S(2)}, u32[]{:S(2)}) collective-permute-start(bf16[2,2,2,1,1,208,512]{6,5,4,3,2,1,0:T(8,128)(2,1)} %dynamic-slice_convert_fusion.1), channel_id=1, source_target_pairs={{0,1},{1,0},{2,3},{3,2},{4,5},{5,4},{6,7},{7,6},{8,9},{9,8},{10,11... | collective-permute-start | bytes 5111816 | tf_op jit(solution)/shard_map/ppermute | solution.py:214
  1076.0 7.0 collective-permute-start.30
  1083.1 5.2 collective-permute-start.31
  1088.3 28.3 %collective-permute-start.32 = (bf16[1,1,1,1,1,64,512]{6,5,4,3,2,1,0:T(8,128)(2,1)S(1)}, bf16[1,1,1,1,1,64,512]{6,5,4,3,2,1,0:T(8,128)(2,1)S(1)}, u32[]{:S(2)}, u32[]{:S(2)}) collective-permute-start(bf16[1,1,1,1,1,64,512]{6,5,4,3,2,1,0:T(8,128)(2,1)S(1)} %dynamic-slice_convert_fusion.13), channel_id=1, source_target_pairs={{0,16},{1,17},{2,18},{3,19},{4,20},{5,21},{6,22},{7,23},{8,24},{9,... | collective-permute-start | bytes 196616 | tf_op jit(solution)/shard_map/ppermute | solution.py:214
  1112.6 20.6 %collective-permute-start.25 = (bf16[2,2,1,1,1,208,512]{6,5,4,3,2,1,0:T(8,128)(2,1)S(1)}, bf16[2,2,1,1,1,208,512]{6,5,4,3,2,1,0:T(8,128)(2,1)S(1)}, u32[]{:S(2)}, u32[]{:S(2)}) collective-permute-start(bf16[2,2,1,1,1,208,512]{6,5,4,3,2,1,0:T(8,128)(2,1)S(1)} %dynamic-slice_convert_fusion.3), channel_id=1, source_target_pairs={{0,4},{1,5},{2,6},{3,7},{4,0},{5,1},{6,2},{7,3},{8,12},{9,13},{10,... | collective-permute-start | bytes 2555912 | tf_op jit(solution)/shard_map/ppermute | solution.py:214
  1133.6 10.8 collective-permute-start.26
  1144.6 11.6 %collective-permute-start.27 = (bf16[1,1,1,1,1,208,512]{6,5,4,3,2,1,0:T(8,128)(2,1)S(1)}, bf16[1,1,1,1,1,208,512]{6,5,4,3,2,1,0:T(8,128)(2,1)S(1)}, u32[]{:S(2)}, u32[]{:S(2)}) collective-permute-start(bf16[1,1,1,1,1,208,512]{6,5,4,3,2,1,0:T(8,128)(2,1)S(1)} %dynamic-slice_convert_fusion.11), channel_id=1, source_target_pairs={{0,16},{1,17},{2,18},{3,19},{4,20},{5,21},{6,22},{7,23},{8,24},{9,... | collective-permute-start | bytes 638984 | tf_op jit(solution)/shard_map/ppermute | solution.py:214
  (222 other events, 1738.2 us)

commit v2 on v1

v2 whole, which is shorter than its diff:
```python
import jax
import jax.numpy as jnp
import numpy as np
from jax import lax
from jax.experimental import pallas as pl
from jax.experimental.pallas import tpu as pltpu
from jax.sharding import PartitionSpec as P

HEAD_WIDTH = 64
HHD = 64
BLOCK_PARTS = 4
UNIT = 512
PAIR = 2 * HEAD_WIDTH
VMEM_LIMIT = 48 << 20
ENTRY_BLOCK = 64
UNIT_ROWS = 256


EPS = 1e-05
NEGATIVE = -1000000000.0


def matmul(left, right):
    return jnp.dot(left, right, preferred_element_type=jnp.float32)


def matmul_first(left, right):
    return lax.dot_general(
        left, right, (((0,), (0,)), ((), ())), preferred_element_type=jnp.float32
    )


def matmul_last(left, right):
    return lax.dot_general(
        left, right, (((1,), (1,)), ((), ())), preferred_element_type=jnp.float32
    )


def rms_norm(value, gain):
    return value * lax.rsqrt(jnp.mean(value * value, axis=-1, keepdims=True) + EPS) * gain


def gated_units(gate_pre, up_pre):
    return jax.nn.silu(gate_pre) * up_pre


def rounded(value):
    return lax.optimization_barrier(value.astype(jnp.bfloat16)).astype(jnp.float32)


def log2_of(number):
    return number.bit_length() - 1


def swap(value, mask, devices):
    return lax.ppermute(value, ("dp", "mp"), [(d, d ^ mask) for d in range(devices)])


def gather_blocks(block, me, devices, order):
    bits = log2_of(devices)
    held = block.reshape((1,) * bits + block.shape)
    begun = None
    for bit in order:
        axis = bits - 1 - bit
        arrived = swap(held, 1 << bit, devices)
        upper = ((me >> bit) & 1) == 1
        held = jnp.where(
            upper,
            jnp.concatenate([arrived, held], axis),
            jnp.concatenate([held, arrived], axis),
        )
        begun = held if begun is None else begun
    return (held.reshape((devices * block.shape[0],) + block.shape[1:]), begun)


def scatter_blocks(blocks, me, devices, order):
    bits = log2_of(devices)
    held = blocks.reshape((2,) * bits + (blocks.shape[0] // devices,) + blocks.shape[1:])
    for bit in order:
        axis = bits - 1 - bit
        mine = (me >> bit) & 1
        leaving = lax.dynamic_slice_in_dim(held, 1 - mine, 1, axis).astype(jnp.bfloat16)
        staying = lax.dynamic_slice_in_dim(held, mine, 1, axis)
        held = staying.astype(jnp.float32) + swap(leaving, 1 << bit, devices).astype(jnp.float32)
    return held.reshape(held.shape[bits:])


def lanes(shape):
    return lax.broadcasted_iota(jnp.int32, shape, len(shape) - 1)


def half_swap(value):
    quarter = HEAD_WIDTH // 2
    upper = (lanes(value.shape) & quarter) != 0
    return jnp.where(
        upper, pltpu.roll(value, quarter, 1), pltpu.roll(value, PAIR - quarter, 1)
    )


def to_low(value):
    return value.astype(jnp.bfloat16)


def causal_of(shape, block_at, rows):
    key_at = lax.broadcasted_iota(jnp.int32, shape, 0)
    query_at = lax.broadcasted_iota(jnp.int32, shape, 1) + block_at * rows
    return key_at <= query_at


def head_views(pair_ref, cos_ref, sin_ref):
    pair = pair_ref[...]
    turned = to_low(pair * cos_ref[...] + half_swap(pair) * sin_ref[...]).astype(jnp.float32)
    other = pltpu.roll(turned, HEAD_WIDTH, 1)
    left = lanes(turned.shape) < HEAD_WIDTH
    return (
        jnp.where(left, turned, 0.0),
        jnp.where(left, 0.0, other),
        jnp.where(left, other, 0.0),
        jnp.where(left, 0.0, turned),
    )


def attention_forward_kernel(
    info, near_ref, mid_ref, far_ref, pair_ref, cos_pair, sin_pair, cos_ref, sin_ref,
    out_ref, low_ref, lse_ref, even, odd, across, query_ref,
):
    group = pl.program_id(0)
    key_left, key_right, value_left, _ = head_views(pair_ref, cos_pair, sin_pair)
    even[...] = to_low(key_left)
    odd[...] = to_low(key_right)
    across[...] = to_low(value_left.T[:HEAD_WIDTH])

    @pl.when(group < 2)
    def take_near():
        query_ref[...] = near_ref[...]

    @pl.when(group == 2)
    def take_mid():
        query_ref[...] = mid_ref[...]

    @pl.when(group == 3)
    def take_far():
        query_ref[...] = far_ref[...]

    rows = query_ref.shape[0]
    length = pair_ref.shape[0]
    causal = causal_of((length, rows), info[0], rows)
    for pair in range(query_ref.shape[1] // PAIR):
        span = slice(pair * PAIR, (pair + 1) * PAIR)
        query = query_ref[:, span]
        turned = to_low(query * cos_ref[...] + half_swap(query) * sin_ref[...])
        low = to_low(turned.astype(jnp.float32) * HEAD_WIDTH ** (-0.5))
        low_ref[:, span] = low
        outs = []
        for at, keys in enumerate((even, odd)):
            scores = jnp.where(causal, matmul_last(keys[...], low), NEGATIVE)
            highest = jnp.max(scores, axis=0, keepdims=True)
            weight = jnp.exp(scores - highest)
            total = jnp.sum(weight, axis=0, keepdims=True)
            outs.append(matmul(across[...], to_low(weight)) / total)
            lse_ref[0, 2 * pair + at : 2 * pair + at + 1, :] = highest + jnp.log(total)
        out_ref[:, span] = to_low(jnp.concatenate(outs, axis=0).T)


def attention_backward_kernel(
    info, low_ref, near_ref, mid_ref, far_ref, lse_ref, pair_ref, cos_pair, sin_pair, cos_ref, sin_ref,
    query_ref, pair_grad_ref, even, odd, value_even, value_odd, across,
    key_even, key_odd, sum_even, sum_odd, grad_ref,
):
    group = pl.program_id(0)
    key_left, key_right, value_left, value_right = head_views(pair_ref, cos_pair, sin_pair)
    even[...] = to_low(key_left)
    odd[...] = to_low(key_right)
    value_even[...] = to_low(value_left)
    value_odd[...] = to_low(value_right)
    across[...] = to_low(key_left.T[:HEAD_WIDTH])
    for total in (key_even, key_odd, sum_even, sum_odd):
        total[...] = jnp.zeros_like(total)

    @pl.when(group < 2)
    def take_near():
        grad_ref[...] = near_ref[...]

    @pl.when(group == 2)
    def take_mid():
        grad_ref[...] = mid_ref[...]

    @pl.when(group == 3)
    def take_far():
        grad_ref[...] = far_ref[...]

    rows = low_ref.shape[0]
    length = pair_ref.shape[0]
    causal = causal_of((length, rows), info[0], rows)
    sides = ((even, value_even, key_even, sum_even), (odd, value_odd, key_odd, sum_odd))
    for pair in range(low_ref.shape[1] // PAIR):
        span = slice(pair * PAIR, (pair + 1) * PAIR)
        low = low_ref[:, span]
        grad = grad_ref[:, span]
        outs = []
        for at, (keys, values, key_total, value_total) in enumerate(sides):
            scores = jnp.where(causal, matmul_last(keys[...], low), NEGATIVE)
            probs = jnp.exp(scores - lse_ref[0, 2 * pair + at : 2 * pair + at + 1, :])
            value_total[...] += matmul(to_low(probs), grad)
            moved = probs * matmul_last(values[...], grad)
            mean = jnp.sum(moved, axis=0, keepdims=True)
            grad_scores = to_low(moved - probs * mean)
            key_total[...] += matmul(grad_scores, low)
            outs.append(matmul(across[...], grad_scores))
        turned = jnp.concatenate(outs, axis=0).T * HEAD_WIDTH ** (-0.5)
        query_ref[:, span] = to_low(turned * cos_ref[...] - half_swap(turned) * sin_ref[...])
    left = lanes((length, PAIR)) < HEAD_WIDTH
    pair_grad_ref[0] = jnp.where(
        left,
        key_even[...] + pltpu.roll(key_odd[...], HEAD_WIDTH, 1),
        pltpu.roll(sum_even[...], HEAD_WIDTH, 1) + sum_odd[...],
    )


def attention_specs(part, rows, length):
    span = (rows, 4 * PAIR)
    return {
        "table_pair": pl.BlockSpec((length, PAIR), lambda g, s: (0, 0)),
        "table": pl.BlockSpec((rows, PAIR), lambda g, s: (s[0], 0)),
        "pair": pl.BlockSpec((length, PAIR), lambda g, s: (0, s[1 + g])),
        "near": pl.BlockSpec(span, lambda g, s: (part, jnp.minimum(g, 1))),
        "one": pl.BlockSpec(span, lambda g, s: (part, 0)),
        "wide": pl.BlockSpec(span, lambda g, s: (0, g)),
        "sums": pl.BlockSpec((1, 8, rows), lambda g, s: (g, 0, 0)),
    }


def attention_cost(rows, length, heads, matmuls):
    work = rows * length * heads * HEAD_WIDTH * matmuls * 2
    return pl.CostEstimate(
        flops=work, bytes_accessed=16 * rows * heads * HEAD_WIDTH, transcendentals=rows * length * heads
    )


def attention_forward(info, queries, pair_pre, tables, part, length):
    cos_pair, sin_pair, cosine, sine = tables
    rows = cosine.shape[0] // BLOCK_PARTS
    heads = 4 * 4 * PAIR // HEAD_WIDTH
    spec = attention_specs(part, rows, length)
    half = pltpu.VMEM((length, PAIR), jnp.bfloat16)
    wide = (rows, heads * HEAD_WIDTH)
    return pl.pallas_call(
        attention_forward_kernel,
        grid_spec=pltpu.PrefetchScalarGridSpec(
            num_scalar_prefetch=1,
            grid=(4,),
            in_specs=[
                spec["near"], spec["one"], spec["one"], spec["pair"],
                spec["table_pair"], spec["table_pair"], spec["table"], spec["table"],
            ],
            out_specs=[spec["wide"], spec["wide"], spec["sums"]],
            scratch_shapes=[
                half, half,
                pltpu.VMEM((HEAD_WIDTH, length), jnp.bfloat16),
                pltpu.VMEM((rows, 4 * PAIR), jnp.float32),
            ],
        ),
        out_shape=[
            jax.ShapeDtypeStruct(wide, jnp.bfloat16),
            jax.ShapeDtypeStruct(wide, jnp.bfloat16),
            jax.ShapeDtypeStruct((4, 8, rows), jnp.float32),
        ],
        compiler_params=pltpu.CompilerParams(
            dimension_semantics=("arbitrary",), vmem_limit_bytes=VMEM_LIMIT
        ),
        cost_estimate=attention_cost(rows, length, heads, 2),
        name="attention_forward",
    )(info, *queries, pair_pre, cos_pair, sin_pair, cosine, sine)


def attention_backward(info, low, grads, sums, pair_pre, tables, length):
    cos_pair, sin_pair, cosine, sine = tables
    rows = cosine.shape[0] // BLOCK_PARTS
    heads = low.shape[1] // HEAD_WIDTH
    spec = attention_specs(0, rows, length)
    half = pltpu.VMEM((length, PAIR), jnp.bfloat16)
    full = pltpu.VMEM((length, PAIR), jnp.float32)
    return pl.pallas_call(
        attention_backward_kernel,
        grid_spec=pltpu.PrefetchScalarGridSpec(
            num_scalar_prefetch=1,
            grid=(4,),
            in_specs=[
                spec["wide"], spec["near"], spec["one"], spec["one"], spec["sums"], spec["pair"],
                spec["table_pair"], spec["table_pair"], spec["table"], spec["table"],
            ],
            out_specs=[spec["wide"], pl.BlockSpec((1, length, PAIR), lambda g, s: (s[1 + g], 0, 0))],
            scratch_shapes=[
                half, half, half, half,
                pltpu.VMEM((HEAD_WIDTH, length), jnp.bfloat16),
                full, full, full, full,
                pltpu.VMEM((rows, 4 * PAIR), jnp.bfloat16),
            ],
        ),
        out_shape=[
            jax.ShapeDtypeStruct(low.shape, jnp.bfloat16),
            jax.ShapeDtypeStruct((4, length, PAIR), jnp.float32),
        ],
        compiler_params=pltpu.CompilerParams(
            dimension_semantics=("arbitrary",), vmem_limit_bytes=VMEM_LIMIT
        ),
        cost_estimate=attention_cost(rows, length, heads, 5),
        name="attention_backward",
    )(info, low, *grads, sums, pair_pre, cos_pair, sin_pair, cosine, sine)


def pair_finish_kernel(info, own_ref, came_ref, cos_ref, sin_ref, out_ref):
    total = own_ref[0] + came_ref[0].astype(jnp.float32)
    out_ref[...] = to_low(total * cos_ref[...] - half_swap(total) * sin_ref[...])


def pair_finish(info, own, came, cos_pair, sin_pair):
    heads, both, _ = own.shape
    rows = both // 2
    part = pl.BlockSpec((1, rows, PAIR), lambda h, p, s: (h, p, 0))
    table = pl.BlockSpec((rows, PAIR), lambda h, p, s: (s[p], 0))
    return pl.pallas_call(
        pair_finish_kernel,
        grid_spec=pltpu.PrefetchScalarGridSpec(
            num_scalar_prefetch=1,
            grid=(heads, 2),
            in_specs=[part, part, table, table],
            out_specs=pl.BlockSpec((rows, PAIR), lambda h, p, s: (p, h)),
        ),
        out_shape=jax.ShapeDtypeStruct((both, heads * PAIR), jnp.bfloat16),
        name="pair_finish",
    )(info, own, came, cos_pair, sin_pair)


def rope_tables(length):
    positions = np.arange(length, dtype=np.float32)
    inverse = 10000.0 ** (-np.arange(0, HEAD_WIDTH, 2, dtype=np.float32) / HEAD_WIDTH)
    angles = positions[:, None] * inverse.astype(np.float32)[None, :]
    cosine, sine = np.cos(angles).astype(np.float32), np.sin(angles).astype(np.float32)
    head_cos = np.concatenate([cosine, cosine], axis=1)
    head_sin = np.concatenate([-sine, sine], axis=1)
    still = np.ones_like(head_cos)
    return tuple(
        jnp.asarray(np.concatenate(sides, axis=1))
        for sides in (
            (head_cos, still), (head_sin, 0 * still), (head_cos, head_cos), (head_sin, head_sin)
        )
    )


def head_marks(width, transposed):
    shape = (PAIR, width) if transposed else (width, PAIR)
    head_at, column_at = (0, 1) if transposed else (1, 0)
    head = lax.broadcasted_iota(jnp.int32, shape, head_at)
    column = lax.broadcasted_iota(jnp.int32, shape, column_at)
    return (column // HHD == head).astype(jnp.bfloat16)


def head_sums(value, marks):
    high = to_low(value)
    rest = to_low(value - high.astype(jnp.float32))
    return matmul(high, marks) + matmul(rest, marks)


def normalize(value):
    centered = value - jnp.mean(value, axis=-1, keepdims=True)
    inverse = lax.rsqrt(jnp.mean(centered * centered, axis=-1, keepdims=True) + EPS)
    return (centered * inverse, inverse)


def norm_back(grad, gain, hat, inverse):
    scaled = grad * gain
    mean = jnp.mean(scaled, axis=-1, keepdims=True)
    along = jnp.mean(scaled * hat, axis=-1, keepdims=True)
    return inverse * (scaled - mean - hat * along)


def slot_attention_kernel(
    pieces_ref, counts_ref, weight_ref, norm_ref, mixed_ref, probs_ref, attended_ref, lead_ref
):
    entries, slots, width = pieces_ref.shape
    rows = entries * slots
    tall = (entries, slots, width)
    pieces = pieces_ref[...].astype(jnp.float32)
    hat, _ = normalize(pieces.reshape(rows, width))
    low = to_low(hat * norm_ref[0:1, :] + norm_ref[1:2, :])
    mixed = []
    for part in range(3):
        span = slice(part * width, (part + 1) * width)
        value = to_low(matmul(low, weight_ref[:, span]))
        mixed_ref[:, span] = value
        mixed.append(value.astype(jnp.float32).reshape(tall))
    query, keys, values = mixed
    marks = head_marks(width, False)
    product = (keys * query[:, 0:1, :]).reshape(rows, width)
    scores = head_sums(product, marks).reshape(entries, slots, PAIR) * HHD ** (-0.5)
    live = lax.broadcasted_iota(jnp.int32, scores.shape, 1) < counts_ref[...]
    scores = jnp.where(live, scores, NEGATIVE)
    weight = jnp.exp(scores - jnp.max(scores, axis=1, keepdims=True))
    probs = weight / jnp.sum(weight, axis=1, keepdims=True)
    probs_ref[...] = probs
    spread = matmul(to_low(probs.reshape(rows, PAIR)), head_marks(width, True)).reshape(tall)
    attended_ref[...] = to_low(jnp.sum(spread * values, axis=1))
    lead_ref[...] = pieces[:, 0, :]


def slot_attention(pieces, counts, in_weight, norm_rows):
    entries, slots, width = pieces.shape
    part = min(ENTRY_BLOCK, entries)
    counts = jnp.broadcast_to(counts[:, None, None], (entries, 1, PAIR))
    whole = lambda shape: pl.BlockSpec(shape, lambda i: (0,) * len(shape))
    tall = pl.BlockSpec((part, slots, width), lambda i: (i, 0, 0))
    flat = pl.BlockSpec((part, width), lambda i: (i, 0))
    return pl.pallas_call(
        slot_attention_kernel,
        grid=(entries // part,),
        in_specs=[
            tall,
            pl.BlockSpec((part, 1, PAIR), lambda i: (i, 0, 0)),
            whole(in_weight.shape),
            whole(norm_rows.shape),
        ],
        out_specs=[
            pl.BlockSpec((part * slots, 3 * width), lambda i: (i, 0)),
            pl.BlockSpec((part, slots, PAIR), lambda i: (i, 0, 0)),
            flat,
            flat,
        ],
        out_shape=[
            jax.ShapeDtypeStruct((entries * slots, 3 * width), jnp.bfloat16),
            jax.ShapeDtypeStruct((entries, slots, PAIR), jnp.float32),
            jax.ShapeDtypeStruct((entries, width), jnp.bfloat16),
            jax.ShapeDtypeStruct((entries, width), jnp.float32),
        ],
        compiler_params=pltpu.CompilerParams(
            dimension_semantics=("arbitrary",), vmem_limit_bytes=VMEM_LIMIT
        ),
        cost_estimate=pl.CostEstimate(
            flops=8 * entries * slots * width * width, bytes_accessed=entries * slots * width * 8, transcendentals=0
        ),
        name="slot_attention",
    )(pieces, counts, in_weight, norm_rows)


def gelu_of(value):
    cdf = 0.5 * (1.0 + lax.erf(value * np.float32(0.5 ** 0.5)))
    return (value * cdf, cdf)


def gelu_slope(value, cdf):
    return cdf + value * (jnp.exp(-0.5 * value * value) * np.float32((2 * np.pi) ** -0.5))


def units_forward_kernel(
    attended_ref, lead_ref, wide_weight_ref, reduce_ref, norm_ref, pooled_ref, hidden_ref
):
    width = lead_ref.shape[1]
    hidden = lead_ref[...] + matmul(attended_ref[...], wide_weight_ref[:, :width])
    hidden_ref[...] = hidden
    hat, _ = normalize(hidden)
    second = to_low(hat * norm_ref[2:3, :] + norm_ref[3:4, :])
    total = hidden
    units = reduce_ref.shape[0]
    step = min(UNIT, units)
    for at in range(0, units, step):
        active, _ = gelu_of(matmul(second, wide_weight_ref[:, width + at : width + at + step]))
        total = total + matmul(to_low(active), reduce_ref[at : at + step, :])
    pooled_ref[...] = to_low(total)


def units_forward(attended, lead, wide_weight, reduce_weight, norm_rows):
    entries, width = attended.shape
    part = min(UNIT_ROWS, entries)
    whole = lambda shape: pl.BlockSpec(shape, lambda i: (0,) * len(shape))
    flat = pl.BlockSpec((part, width), lambda i: (i, 0))
    return pl.pallas_call(
        units_forward_kernel,
        grid=(entries // part,),
        in_specs=[flat, flat]
        + [whole(x.shape) for x in (wide_weight, reduce_weight, norm_rows)],
        out_specs=[flat, flat],
        out_shape=[
            jax.ShapeDtypeStruct((entries, width), jnp.bfloat16),
            jax.ShapeDtypeStruct((entries, width), jnp.float32),
        ],
        compiler_params=pltpu.CompilerParams(
            dimension_semantics=("arbitrary",), vmem_limit_bytes=VMEM_LIMIT
        ),
        cost_estimate=pl.CostEstimate(
            flops=2 * entries * width * (width + 2 * reduce_weight.shape[0]), bytes_accessed=8 << 20, transcendentals=0
        ),
        name="units_forward",
    )(attended, lead, wide_weight, reduce_weight, norm_rows)


def units_backward_kernel(
    grad_ref, hidden_ref, attended_ref, wide_weight_ref, reduce_ref, norm_ref,
    hidden_grad_ref, attended_grad_ref, wide_ref, reduce_grad_ref, norm_grad_ref,
    wide_total, reduce_total,
):
    step_at = pl.program_id(0)
    width = hidden_ref.shape[1]
    units = reduce_ref.shape[0]

    @pl.when(step_at == 0)
    def start():
        wide_total[...] = jnp.zeros_like(wide_total)
        reduce_total[...] = jnp.zeros_like(reduce_total)
        norm_grad_ref[...] = jnp.zeros_like(norm_grad_ref)

    grad = grad_ref[...]
    grad_low = to_low(grad)
    hat, inverse = normalize(hidden_ref[...])
    second = to_low(hat * norm_ref[2:3, :] + norm_ref[3:4, :])
    grad_normed = jnp.zeros_like(grad)
    step = min(UNIT, units)
    for at in range(0, units, step):
        span = slice(at, at + step)
        wide_span = slice(width + at, width + at + step)
        expanded = matmul(second, wide_weight_ref[:, wide_span])
        active, cdf = gelu_of(expanded)
        reduce_total[span, :] += matmul_first(to_low(active), grad_low)
        grad_active = matmul_last(grad_low, reduce_ref[span, :])
        grad_expanded = to_low(grad_active * gelu_slope(expanded, cdf))
        wide_total[:, wide_span] += matmul_first(second, grad_expanded)
        grad_normed = grad_normed + matmul_last(grad_expanded, wide_weight_ref[:, wide_span])
    norm_grad_ref[2:3, :] += jnp.sum(grad_normed * hat, axis=0, keepdims=True)
    norm_grad_ref[3:4, :] += jnp.sum(grad_normed, axis=0, keepdims=True)
    hidden_grad = grad + norm_back(grad_normed, norm_ref[2:3, :], hat, inverse)
    hidden_grad_ref[...] = hidden_grad
    hidden_low = to_low(hidden_grad)
    wide_total[:, :width] += matmul_first(attended_ref[...], hidden_low)
    attended_grad_ref[...] = to_low(matmul_last(hidden_low, wide_weight_ref[:, :width]))

    @pl.when(step_at == pl.num_programs(0) - 1)
    def finish():
        wide_ref[...] = to_low(wide_total[...])
        reduce_grad_ref[...] = to_low(reduce_total[...])


def units_backward(grad, hidden, attended, wide_weight, reduce_weight, norm_rows):
    entries, width = attended.shape
    part = min(UNIT_ROWS, entries)
    units = reduce_weight.shape[0]
    whole = lambda shape: pl.BlockSpec(shape, lambda i: (0,) * len(shape))
    flat = pl.BlockSpec((part, width), lambda i: (i, 0))
    wide = (width, width + units)
    return pl.pallas_call(
        units_backward_kernel,
        grid=(entries // part,),
        in_specs=[flat, flat, flat]
        + [whole(x.shape) for x in (wide_weight, reduce_weight, norm_rows)],
        out_specs=[flat, flat, whole(wide), whole((units, width)), whole((8, width))],
        out_shape=[
            jax.ShapeDtypeStruct((entries, width), jnp.float32),
            jax.ShapeDtypeStruct((entries, width), jnp.bfloat16),
            jax.ShapeDtypeStruct(wide, jnp.bfloat16),
            jax.ShapeDtypeStruct((units, width), jnp.bfloat16),
            jax.ShapeDtypeStruct((8, width), jnp.float32),
        ],
        scratch_shapes=[pltpu.VMEM(wide, jnp.float32), pltpu.VMEM((units, width), jnp.float32)],
        compiler_params=pltpu.CompilerParams(
            dimension_semantics=("arbitrary",), vmem_limit_bytes=VMEM_LIMIT
        ),
        cost_estimate=pl.CostEstimate(
            flops=2 * entries * width * (2 * width + 5 * units), bytes_accessed=16 << 20, transcendentals=0
        ),
        name="units_backward",
    )(grad, hidden, attended, wide_weight, reduce_weight, norm_rows)


def slot_backward_kernel(
    pieces_ref, mixed_ref, probs_ref, attended_grad_ref, hidden_grad_ref, weight_ref, norm_ref, later_ref,
    pieces_grad_ref, input_grad_ref, total, norm_total,
):
    step_at = pl.program_id(0)
    entries, slots, width = pieces_ref.shape
    rows = entries * slots
    tall = (entries, slots, width)

    @pl.when(step_at == 0)
    def start():
        total[...] = jnp.zeros_like(total)
        norm_total[...] = jnp.zeros_like(norm_total)
        norm_total[2:4, :] = later_ref[2:4, :]

    hat, inverse = normalize(pieces_ref[...].astype(jnp.float32).reshape(rows, width))
    low = to_low(hat * norm_ref[0:1, :] + norm_ref[1:2, :])
    scale = HHD ** (-0.5)
    query, keys, values = [
        mixed_ref[:, part * width : (part + 1) * width].astype(jnp.float32).reshape(tall) for part in range(3)
    ]
    probs = probs_ref[...]
    grad_attended = jnp.broadcast_to(attended_grad_ref[...].astype(jnp.float32)[:, None, :], tall)
    grad_probs = head_sums((grad_attended * values).reshape(rows, width), head_marks(width, False))
    moved = probs * grad_probs.reshape(probs.shape)
    grad_scores = to_low(moved - probs * jnp.sum(moved, axis=1, keepdims=True))
    marks = head_marks(width, True)
    spread = matmul(grad_scores.reshape(rows, PAIR), marks).reshape(tall) * scale
    first_slot = lax.broadcasted_iota(jnp.int32, tall, 1) == 0
    grad_query = jnp.where(first_slot, jnp.sum(spread * keys, axis=1, keepdims=True), 0.0)
    grad_keys = spread * query[:, 0:1, :]
    grad_values = matmul(to_low(probs.reshape(rows, PAIR)), marks).reshape(tall) * grad_attended
    grad_normed = jnp.zeros((rows, width), jnp.float32)
    for part, grad in enumerate((grad_query, grad_keys, grad_values)):
        span = slice(part * width, (part + 1) * width)
        grad_low = to_low(grad.reshape(rows, width))
        total[:, span] += matmul_first(low, grad_low)
        grad_normed = grad_normed + matmul_last(grad_low, weight_ref[:, span])
    norm_total[0:1, :] += jnp.sum(grad_normed * hat, axis=0, keepdims=True)
    norm_total[1:2, :] += jnp.sum(grad_normed, axis=0, keepdims=True)
    grad_pieces = norm_back(grad_normed, norm_ref[0:1, :], hat, inverse).reshape(tall)
    hidden_grad = jnp.broadcast_to(hidden_grad_ref[...][:, None, :], tall)
    pieces_grad_ref[...] = to_low(grad_pieces + jnp.where(first_slot, hidden_grad, 0.0))

    @pl.when(step_at == pl.num_programs(0) - 1)
    def finish():
        input_grad_ref[:, : 3 * width] = to_low(total[...])
        input_grad_ref[:, 3 * width :] = to_low(norm_total[...].T)


def slot_backward(
    pieces, mixed, probs, attended_grad, hidden_grad, in_weight, norm_rows, later_norms
):
    entries, slots, width = pieces.shape
    part = min(ENTRY_BLOCK, entries)
    whole = lambda shape: pl.BlockSpec(shape, lambda i: (0,) * len(shape))
    tall = pl.BlockSpec((part, slots, width), lambda i: (i, 0, 0))
    flat = pl.BlockSpec((part, width), lambda i: (i, 0))
    return pl.pallas_call(
        slot_backward_kernel,
        grid=(entries // part,),
        in_specs=[
            tall,
            pl.BlockSpec((part * slots, 3 * width), lambda i: (i, 0)),
            pl.BlockSpec((part, slots, PAIR), lambda i: (i, 0, 0)),
            flat,
            flat,
            whole(in_weight.shape),
            whole(norm_rows.shape),
            whole(later_norms.shape),
        ],
        out_specs=[tall, whole((width, 3 * width + PAIR))],
        out_shape=[
            jax.ShapeDtypeStruct(pieces.shape, jnp.bfloat16),
            jax.ShapeDtypeStruct((width, 3 * width + PAIR), jnp.bfloat16),
        ],
        scratch_shapes=[
            pltpu.VMEM((width, 3 * width), jnp.float32),
            pltpu.VMEM((PAIR, width), jnp.float32),
        ],
        compiler_params=pltpu.CompilerParams(
            dimension_semantics=("arbitrary",), vmem_limit_bytes=VMEM_LIMIT
        ),
        cost_estimate=pl.CostEstimate(
            flops=14 * entries * slots * width * width, bytes_accessed=entries * slots * width * 10, transcendentals=0
        ),
        name="slot_backward",
    )(pieces, mixed, probs, attended_grad, hidden_grad, in_weight, norm_rows, later_norms)


def route(token_index, me, devices, local_vocab, capacity, mp_count):
    step = token_index.shape[0] // BLOCK_PARTS
    cut = token_index.reshape(BLOCK_PARTS, step)
    own = jnp.where(me % mp_count == 0, cut[jnp.array([0, 3])], cut[jnp.array([1, 2])]).reshape(1, 2 * step)
    asked = exchange(jnp.broadcast_to(own, (devices, 2 * step)))
    count = 2 * step
    places = jnp.arange(count, dtype=jnp.int32)
    same = asked[:, :, None] == asked[:, None, :]
    earlier = places[:, None] > places[None, :]
    repeated = jnp.any(same & earlier[None], axis=2)
    first = jnp.logical_not(repeated)
    owner = asked // local_vocab
    before = (
        (owner[:, :, None] == owner[:, None, :])
        & (asked[:, None, :] < asked[:, :, None])
        & first[:, None, :]
    )
    rank = jnp.sum(before.astype(jnp.int32), axis=2)
    rounds = jnp.max(rank) // capacity + 1
    own_rank = lax.dynamic_index_in_dim(rank, me, 0, False)
    own_owner = lax.dynamic_index_in_dim(owner, me, 0, False)
    entries = me * local_vocab + jnp.arange(local_vocab, dtype=jnp.int32)
    present = jnp.any(asked[:, :, None] == entries[None, None, :], axis=1)
    lower = (
        jnp.arange(local_vocab, dtype=jnp.int32)[:, None]
        < jnp.arange(local_vocab, dtype=jnp.int32)[None, :]
    )
    standing = matmul(present.astype(jnp.bfloat16), lower.astype(jnp.bfloat16)).astype(jnp.int32)
    return (rounds, own_rank, own_owner, present, standing)


def sender_choice(present, standing, turn, capacity):
    slot = turn * capacity + jnp.arange(capacity, dtype=jnp.int32)
    chosen = present[:, None, :] & (standing[:, None, :] == slot[None, :, None])
    return chosen.astype(jnp.bfloat16).reshape(present.shape[0] * capacity, present.shape[1])


def taker_choice(own_rank, own_owner, turn, capacity, devices):
    inside = own_rank - turn * capacity
    valid = (inside >= 0) & (inside < capacity)
    place = jnp.where(valid, own_owner * capacity + inside, -1)
    return (place[:, None] == jnp.arange(devices * capacity, dtype=jnp.int32)[None, :]).astype(
        jnp.bfloat16
    )


def exchange(value):
    return lax.all_to_all(value, ("dp", "mp"), 0, 0, tiled=True)


def ordered_blocks(first, own_two, other_two):
    return jnp.where(
        first,
        jnp.concatenate([own_two[0], other_two[0], other_two[1], own_two[1]], axis=0),
        jnp.concatenate([other_two[0], own_two[0], own_two[1], other_two[1]], axis=0),
    )


def body(
    pieces,
    counts,
    token_index,
    hyper_input,
    hyper_output,
    hyper_expand,
    hyper_reduce,
    hyper_norms,
    embed_weight,
    attention_gain,
    dense_gain,
    frozen_query_weight,
    frozen_key_weight,
    frozen_value_weight,
    frozen_output_weight,
    gate_weight,
    up_weight,
    down_weight,
    upstream,
):
    local_vocab = pieces.shape[0]
    mp_count = lax.axis_size("mp")
    devices = lax.axis_size("dp") * mp_count
    mp_index = lax.axis_index("mp")
    me = lax.axis_index("dp") * mp_count + mp_index
    core = (me >> 1) & 1
    lead = mp_index == 0
    bits = log2_of(devices)
    far_bits = list(range(bits - 1, 1, -1))
    length = token_index.shape[0]
    block = length // BLOCK_PARTS
    capacity = max(16, length // devices)

    norm_count = hyper_norms.shape[1]
    in_width = hyper_input.shape[1]
    norm_lanes = jnp.pad(hyper_norms, ((0, 0), (0, PAIR - norm_count)))
    in_weight, begun = gather_blocks(
        jnp.concatenate([hyper_input, norm_lanes], axis=1), me, devices, [0] + far_bits + [1]
    )
    wide_weight, _ = gather_blocks(
        jnp.concatenate([hyper_output, hyper_expand], axis=1), me, devices, [0] + far_bits + [1]
    )
    reduce_weight, _ = gather_blocks(hyper_reduce, me, devices, far_bits + [0, 1])
    embed_full, _ = gather_blocks(embed_weight, me, devices, far_bits + [0, 1])
    norm_rows = in_weight[:, in_width : in_width + 8].astype(jnp.float32).T

    query_cut = frozen_query_weight.shape[1] // 2
    frozen_query_weight, frozen_output_weight, begun = lax.optimization_barrier(
        (frozen_query_weight, frozen_output_weight, begun)
    )
    kv_local = frozen_key_weight.shape[1] // HEAD_WIDTH
    key_own = jnp.concatenate(
        [
            weight[:, at * HEAD_WIDTH : (at + 1) * HEAD_WIDTH]
            for at in range(kv_local)
            for weight in (frozen_key_weight, frozen_value_weight)
        ],
        axis=1,
    )
    query_near = swap(
        lax.dynamic_slice_in_dim(frozen_query_weight, core * query_cut, query_cut, 1), 1, devices
    )
    output_near = swap(
        lax.dynamic_slice_in_dim(frozen_output_weight, core * query_cut, query_cut, 0), 1, devices
    )
    key_other = swap(key_own, 1, devices)
    query_far = swap(query_near, 2, devices)
    output_far = swap(output_near, 2, devices)
    pair_weight = jnp.where(
        lead,
        jnp.concatenate([key_own, key_other], axis=1),
        jnp.concatenate([key_other, key_own], axis=1),
    )
    other_base = (1 - mp_index) * kv_local
    head_order = [mp_index * kv_local, mp_index * kv_local + 1, other_base + core, other_base + 1 - core]

    rounds, own_rank, own_owner, present, standing = route(
        token_index, me, devices, local_vocab, capacity, mp_count
    )

    slot_mixed, slot_probs, hyper_attended, lead_rows = slot_attention(pieces, counts, in_weight, norm_rows)
    pooled, hyper_hidden = units_forward(
        hyper_attended, lead_rows, wide_weight, reduce_weight, norm_rows
    )

    def fetch(turn, chosen):
        sent = matmul(sender_choice(present, standing, turn, capacity), pooled).astype(jnp.bfloat16)
        came = exchange(sent)
        picked = matmul(taker_choice(own_rank, own_owner, turn, capacity, devices), came)
        return chosen + picked.astype(jnp.bfloat16)

    chosen_own = fetch(0, jnp.zeros((2 * block, pooled.shape[1]), jnp.bfloat16))
    chosen_own = lax.fori_loop(1, rounds, fetch, chosen_own)
    chosen_other = swap(chosen_own, 1, devices)

    tables = rope_tables(length)
    own_at = (mp_index, 3 - mp_index)
    own_base = tuple(at * block for at in own_at)
    other_start = ((1 - mp_index) * block, (2 + mp_index) * block)
    infos = [jnp.stack([at] + head_order).astype(jnp.int32) for at in own_at]

    def first_norm(value):
        return rms_norm(value, attention_gain)

    def second_norm(value):
        return rms_norm(value, dense_gain)

    embedded = rounded(matmul(chosen_own, embed_full))
    first_normed, first_pull = jax.vjp(first_norm, embedded)
    first_low = first_normed.astype(jnp.bfloat16)
    query_weights = (frozen_query_weight, query_near, query_far)
    output_weights = (frozen_output_weight, output_near, output_far)
    queries = [matmul(first_low, part) for part in query_weights]
    other_low = first_norm(rounded(matmul(chosen_other, embed_full))).astype(jnp.bfloat16)
    pair_own = matmul(first_low, pair_weight)
    pair_other = matmul(other_low, pair_weight)
    pair_pre = ordered_blocks(
        lead, (pair_own[:block], pair_own[block:]), (pair_other[:block], pair_other[block:])
    )
    spans = (2 * block, length)

    sums = []
    lows = []
    hidden_parts = []
    second_pulls = []
    second_rows = []
    for part in range(2):
        rows = slice(part * block, (part + 1) * block)
        flat, low, part_sums = attention_forward(
            infos[part], queries, pair_pre, tables, part, spans[part]
        )
        sums.append(part_sums)
        lows.append(low)
        mixed = 0.0
        at = 0
        for weight in output_weights:
            mixed = mixed + matmul(flat[:, at : at + weight.shape[0]], weight)
            at += weight.shape[0]
        hidden_state = embedded[rows] + mixed
        hidden_parts.append(hidden_state)
        second_normed, pull = jax.vjp(second_norm, hidden_state)
        second_pulls.append(pull)
        second_low = second_normed.astype(jnp.bfloat16)
        second_rows.append(jnp.concatenate([second_low, swap(second_low, 1, devices)], axis=0))

    active_rows = []
    grad_hidden = []
    for part in range(2):
        second_low = second_rows[part]
        rising = jnp.concatenate(
            [
                lax.dynamic_slice_in_dim(upstream, own_base[part], block, 0),
                lax.dynamic_slice_in_dim(upstream, other_start[part], block, 0),
            ],
            axis=0,
        )
        gate_pre = matmul(second_low, gate_weight)
        up_pre = matmul(second_low, up_weight)
        active, active_pull = jax.vjp(gated_units, gate_pre, up_pre)
        active_rows.append(active.astype(jnp.bfloat16))
        grad_gate, grad_up = active_pull(matmul_last(rising, down_weight))
        grad_second = (
            matmul_last(grad_gate.astype(jnp.bfloat16), gate_weight)
            + matmul_last(grad_up.astype(jnp.bfloat16), up_weight)
        ).astype(jnp.bfloat16)
        total = grad_second[:block].astype(jnp.float32) + swap(
            grad_second[block:], 1, devices
        ).astype(jnp.float32)
        (grad_hidden_norm,) = second_pulls[part](total)
        grad_hidden.append(rising[:block].astype(jnp.float32) + grad_hidden_norm)

    share = upstream.shape[1] // mp_count
    own_out = []
    other_out = []
    for part in range(2):
        dense = matmul(active_rows[part], down_weight)
        dense_own = dense[:block] + hidden_parts[part]
        dense_other = dense[block:]

        def columns(value, index):
            return lax.dynamic_slice_in_dim(value, index * share, share, 1)

        leaving = jnp.concatenate(
            [columns(dense_other, 1 - mp_index), columns(dense_own, 1 - mp_index)], axis=0
        ).astype(jnp.bfloat16)
        arrived = swap(leaving, 1, devices).astype(jnp.float32)
        own_out.append((columns(dense_own, mp_index) + arrived[:block]).astype(jnp.bfloat16))
        other_out.append((columns(dense_other, mp_index) + arrived[block:]).astype(jnp.bfloat16))
    model_out = ordered_blocks(lead, own_out, other_out)

    grad_queries = []
    pair_grads = []
    for part in range(2):
        hidden_low = grad_hidden[part].astype(jnp.bfloat16)
        grad_attended = [
            matmul_last(hidden_low, weight).astype(jnp.bfloat16) for weight in output_weights
        ]
        part_queries, part_pairs = attention_backward(
            infos[part], lows[part], grad_attended, sums[part], pair_pre, tables, spans[part]
        )
        grad_queries.append(part_queries)
        pair_grads.append(part_pairs)
    pair_grad = jnp.concatenate(
        [pair_grads[0] + pair_grads[1][:, : 2 * block], pair_grads[1][:, 2 * block :]], axis=1
    )

    def pick_blocks(starts):
        return jnp.concatenate(
            [lax.dynamic_slice_in_dim(pair_grad, start, block, 1) for start in starts], axis=1
        )

    pair_came = swap(pick_blocks(other_start).astype(jnp.bfloat16), 1, devices)
    pair_low = pair_finish(
        jnp.stack(own_at).astype(jnp.int32), pick_blocks(own_base), pair_came, tables[0], tables[1]
    )
    grad_first = matmul_last(pair_low, pair_weight)
    grad_query_low = jnp.concatenate(grad_queries, axis=0)
    at = 0
    for weight in query_weights:
        grad_first = grad_first + matmul_last(grad_query_low[:, at : at + weight.shape[1]], weight)
        at += weight.shape[1]
    (grad_embed_norm,) = first_pull(grad_first)
    embedded_grad_low = (jnp.concatenate(grad_hidden, axis=0) + grad_embed_norm).astype(
        jnp.bfloat16
    )
    token_grad = matmul_last(embedded_grad_low, embed_full).astype(jnp.bfloat16)
    embed_grad = to_low(matmul_first(chosen_own, embedded_grad_low))

    def give_back(turn, total):
        taker = taker_choice(own_rank, own_owner, turn, capacity, devices)
        leaving = matmul_first(taker, token_grad).astype(jnp.bfloat16)
        came = exchange(leaving)
        return total + matmul_first(sender_choice(present, standing, turn, capacity), came)

    grad_pooled = give_back(0, jnp.zeros(pooled.shape, jnp.float32))
    grad_pooled = lax.fori_loop(1, rounds, give_back, grad_pooled)

    back_order = [1, 0] + far_bits[::-1]
    embed_own = scatter_blocks(embed_grad, me, devices, back_order)
    hidden_grad, attended_grad, wide_grad, reduce_grad, later_norms = units_backward(
        grad_pooled, hyper_hidden, hyper_attended, wide_weight, reduce_weight, norm_rows
    )
    wide_own = scatter_blocks(wide_grad, me, devices, back_order)
    reduce_own = scatter_blocks(reduce_grad, me, devices, back_order)
    pieces_grad, input_grad = slot_backward(
        pieces, slot_mixed, slot_probs, attended_grad, hidden_grad, in_weight, norm_rows, later_norms
    )
    input_own = scatter_blocks(input_grad, me, devices, back_order)
    out_width = hyper_output.shape[1]
    return (
        model_out,
        pieces_grad,
        input_own[:, :in_width],
        wide_own[:, :out_width],
        wide_own[:, out_width:],
        reduce_own,
        input_own[:, in_width : in_width + norm_count],
        embed_own,
    )


def solution(mesh):
    return jax.shard_map(
        body,
        mesh=mesh,
        in_specs=(
            P(("dp", "mp"), None, None),
            P(("dp", "mp")),
            P("dp"),
            P(("dp", "mp"), None),
            P(("dp", "mp"), None),
            P(("dp", "mp"), None),
            P(("dp", "mp"), None),
            P(("dp", "mp"), None),
            P(("dp", "mp"), None),
            P(),
            P(),
            P(None, "mp"),
            P(None, "mp"),
            P(None, "mp"),
            P("mp", None),
            P(None, "mp"),
            P(None, "mp"),
            P("mp", None),
            P("dp", None),
        ),
        out_specs=(
            P("dp", "mp"),
            P(("dp", "mp"), None, None),
            P(("dp", "mp"), None),
            P(("dp", "mp"), None),
            P(("dp", "mp"), None),
            P(("dp", "mp"), None),
            P(("dp", "mp"), None),
            P(("dp", "mp"), None),
        ),
        check_vma=False,
    )
```

time: 1170 us -> 822 us (0.70)
  Pallas kernels: 0 us -> 186 us
  matrix products: 410 us -> 232 us
  local copies, waits for them, and re-layouts: 226 us -> 52.9 us
  other arithmetic: 229 us -> 74.4 us
  waiting for transfers between devices: 221 us -> 198 us
  blocking collectives: 21.8 us -> 0 us
  starting transfers between devices: 45 us -> 65.7 us
    pallas_call x0 -> x9, Pallas kernels: none -> 186 us  [the longest x2 60.3 us: attention_backward(): pl.pallas_call(attention_backward_kernel, grid_spec=pltpu.PrefetchScalarG...]
    dot_general x48 -> x0, matrix products: 124 us -> none  [the longest x8 39.2 us: attention_backward(): jnp.einsum('qrd,kd->rqk', grad_group, value_group, preferred_element_type...]
    reshape x15 -> x1, local copies, waits for them, and re-layouts: 55.1 us -> 0.01 us  [route(): cut = token_index.reshape(BLOCK_PARTS, step)]
    convert_element_type x3 -> x0, local copies, waits for them, and re-layouts: 54.9 us -> none  [the longest x2 46.9 us: hyper_backward(): grad_pair = jnp.stack([grad_keys, grad_values], axis=2).astype(jnp.bfloat...]
    convert_element_type x16 -> x0, other arithmetic: 52.6 us -> none  [the longest x8 31.6 us: attention_backward(): grad_scores = (probs * (grad_probs - jnp.sum(probs * grad_probs, axis=-1,...]
    unnamed x492 -> x221, local copies, waits for them, and re-layouts: 58.9 us -> 15.4 us
    unnamed x20 -> x3, other arithmetic: 38.3 us -> 0.01 us
    ppermute x33 -> x53, waiting for transfers between devices: 190 us -> 156 us  [swap(): lax.ppermute(value, ('dp', 'mp'), [(d, d ^ mask) for d in range(devices)])]
  transfers between devices with their start and end apart: 35 -> 56, of which waited for: 18 -> 21; matrix products, arithmetic and copies ran while one was open for 43% -> 36% of each run, Pallas kernels for 0% -> 14%
where the time goes in v2:
time: 822 us; the launch traced here: 815 us
  matrix products  232 us (28%)
  waiting for transfers between devices  198 us (24%)
  Pallas kernels  186 us (23%)
  other arithmetic  74.4 us (9%)
  starting transfers between devices  65.7 us (8%)
  local copies, waits for them, and re-layouts  52.9 us (6%)
    ppermute x53, waiting for transfers between devices, swap(): lax.ppermute(value, ('dp', 'mp'), [(d, d ^ mask) for d in range(devices)])  156 us
    dot_general x17, matrix products, matmul_last(): lax.dot_general(left, right, (((1,), (1,)), ((), ())), preferred_element_...  122 us
    dot_general x22, matrix products, matmul(): return jnp.dot(left, right, preferred_element_type=jnp.float32)  103 us
    pallas_call x2, Pallas kernels, attention_backward(): pl.pallas_call(attention_backward_kernel, grid_spec=pltpu.PrefetchScalarG...  60.3 us
    ppermute x53, starting transfers between devices, swap(): lax.ppermute(value, ('dp', 'mp'), [(d, d ^ mask) for d in range(devices)])  52.1 us
    pallas_call x2, Pallas kernels, attention_forward(): pl.pallas_call(attention_forward_kernel, grid_spec=pltpu.PrefetchScalarGr...  47.2 us
    all_to_all x3, waiting for transfers between devices, exchange(): return lax.all_to_all(value, ('dp', 'mp'), 0, 0, tiled=True)  42.8 us
    pallas_call x1, Pallas kernels, slot_backward(): pl.pallas_call(slot_backward_kernel, grid=(entries // part,), in_specs=[t...  31.2 us
  transfers between devices with their start and end apart: 56, of which 21 were waited for; matrix products, arithmetic and copies ran while one was open for 36% of the time, Pallas kernels for 14%

profile of v2, /device:TPU:0, one launch (start us, length us, event | category | flops | bytes accessed | tf_op | source)
XLA Modules:
  0.0 815.4 jit_solution(12292781628767641484)
XLA Ops:
  21.5 11.6 %fusion.45 = f32[512,2816]{1,0:T(8,128)} fusion(bf16[2816,2048]{1,0:T(8,128)(2,1)} %param.46, bf16[256,2048]{1,0:T(8,128)(2,1)S(1)} %get-tuple-element.223, bf16[256,2048]{1,0:T(8,128)(2,1)S(1)} %get-tuple-element.222), kind=kOutput, calls=%fused_computation.95 | convolution fusion | flops 5909774336 | bytes 19398656 | tf_op jit(solution)/shard_map/dot_general | solution.py:34
  49.2 39.6 %all-to-all-done.2 = s32[32,1,512]{2,1,0:T(1,128)S(1)} async-done(((s32[32,1,512]{2,1,0:T(1,128)}), s32[32,1,512]{2,1,0:T(1,128)S(1)}, u32[]{:S(2)}, u32[]{:S(2)}) %all-to-all-start.2) | async-done | bytes 65568 | tf_op jit(solution)/shard_map/all_to_all | solution.py:709
  89.8 12.4 %and_reduce_fusion = (pred[32,512]{1,0:T(8,128)(4,1)S(1)}, pred[32,512]{1,0:T(8,128)(4,1)S(1)}) fusion(s32[32,512]{1,0:T(8,128)S(1)} %get-tuple-element.281, pred[512,512]{1,0:T(8,128)(4,1)S(1)} %iota_compare_fusion.19, s32[512]{0:T(512)S(1)} %iota_add_fusion.2), kind=kLoop, calls=%fused_computation.28 | loop fusion | flops 41910272 | bytes 362496 | tf_op jit(solution)/shard_map/reduce_or | solution.py:671
  106.8 7.3 collective-permute-done.6
  115.4 5.8 collective-permute-done.17
  125.7 8.3 %collective-permute-done.3 = bf16[2,2,1,1,2,16,1664]{6,5,4,3,2,1,0:T(8,128)(2,1)S(1)} collective-permute-done((bf16[2,2,1,1,2,16,1664]{6,5,4,3,2,1,0:T(8,128)(2,1)S(1)}, bf16[2,2,1,1,2,16,1664]{6,5,4,3,2,1,0:T(8,128)(2,1)S(1)}, u32[]{:S(2)}, u32[]{:S(2)}) %collective-permute-start.3) | collective-permute-done | bytes 426016 | tf_op jit(solution)/shard_map/ppermute | solution.py:56
  136.9 8.0 collective-permute-done.8
  149.3 18.6 %slot_attention.1 = (bf16[4096,1536]{1,0:T(8,128)(2,1)}, f32[512,8,128]{2,1,0:T(8,128)S(1)}, bf16[512,512]{1,0:T(8,128)(2,1)S(1)}, f32[512,512]{1,0:T(8,128)S(1)}) custom-call(bf16[512,8,512]{2,1,0:T(8,128)(2,1)} %pieces_ref.3, s32[512,1,128]{2,1,0:T(1,128)S(1)} %broadcast_in_dim.29.counts_ref, bf16[512,1664]{1,0:T(8,128)(2,1)S(1)} %bitcast.233, ...), custom_call_target="tpu_custom_call" | custom-call | flops 8589934592 | bytes 16777216 | tf_op jit(solution)/shard_map/slot_attention/pallas_call | solution.py:414
  177.8 6.1 units_forward.1
  185.7 4.7 all-to-all-start.3
  190.4 10.0 %convert_reduce_fusion = s32[32,512]{1,0:T(8,128)S(1)} fusion(s32[32,512]{1,0:T(8,128)S(1)} %get-tuple-element.281, s32[32,512]{1,0:T(8,128)S(1)} %copy-done.73, s32[32,512]{1,0:T(8,128)S(1)} %add_select_fusion.2, pred[32,512]{1,0:T(8,128)(4,1)S(1)} %not.7), kind=kLoop, calls=%fused_computation.26 | loop fusion | flops 50315264 | bytes 278528 | tf_op jit(solution)/shard_map/reduce_sum | solution.py:679
  210.8 5.4 concatenate.1218
  249.3 18.7 %attention_forward.2 = (bf16[256,2048]{1,0:T(8,128)(2,1)S(1)}, bf16[256,2048]{1,0:T(8,128)(2,1)S(1)}, f32[4,8,256]{2,1,0:T(8,128)S(1)}) custom-call(s32[5]{0:T(128)S(1)} %stack.38.info, f32[512,1024]{1,0:T(8,128)} %fusion.156.near_ref, f32[512,512]{1,0:T(8,128)S(1)} %fusion.155.mid_ref, f32[512,512]{1,0:T(8,128)} %fusion.154.far_ref, ...), custom_call_target="tpu_custom_call" | custom-call | flops 1073741824 | bytes 8388608 | tf_op jit(solution)/shard_map/attention_forward/pallas_call | solution.py:247
  269.1 28.5 %attention_forward.3 = (bf16[256,2048]{1,0:T(8,128)(2,1)S(1)}, bf16[256,2048]{1,0:T(8,128)(2,1)S(1)}, f32[4,8,256]{2,1,0:T(8,128)S(1)}) custom-call(s32[5]{0:T(128)S(1)} %stack.40.info, f32[512,1024]{1,0:T(8,128)} %fusion.156.near_ref, f32[512,512]{1,0:T(8,128)S(1)} %fusion.155.mid_ref, f32[512,512]{1,0:T(8,128)} %fusion.154.far_ref, ...), custom_call_target="tpu_custom_call" | custom-call | flops 2147483648 | bytes 8388608 | tf_op jit(solution)/shard_map/attention_forward/pallas_call | solution.py:247
  317.2 11.3 %fusion.49 = f32[512,2816]{1,0:T(8,128)} fusion(bf16[2816,2048]{1,0:T(8,128)(2,1)} %param.46, bf16[256,2048]{1,0:T(8,128)(2,1)S(1)} %copy-done.57, bf16[256,2048]{1,0:T(8,128)(2,1)S(1)} %copy-done.42), kind=kOutput, calls=%fused_computation.99 | convolution fusion | flops 5909774336 | bytes 19398656 | tf_op jit(solution)/shard_map/dot_general | solution.py:34
  329.6 11.7 %collective-permute-done.28 = bf16[256,2048]{1,0:T(8,128)(2,1)S(1)} collective-permute-done((bf16[256,2048]{1,0:T(8,128)(2,1)S(1)}, bf16[256,2048]{1,0:T(8,128)(2,1)S(1)}, u32[]{:S(2)}, u32[]{:S(2)}) %collective-permute-start.28) | collective-permute-done | bytes 1048608 | tf_op jit(solution)/shard_map/ppermute | solution.py:56
  341.3 8.8 %fusion.66 = f32[512,2816]{1,0:T(8,128)} fusion(bf16[2048,2816]{1,0:T(8,128)(2,1)S(1)} %bitcast.278, bf16[256,2048]{1,0:T(8,128)(2,1)S(1)} %collective-permute-done.28, bf16[256,2048]{1,0:T(8,128)(2,1)S(1)} %get-tuple-element.273), kind=kOutput, calls=%fused_computation.130 | convolution fusion | flops 5909774336 | bytes 19398656 | tf_op jit(solution)/shard_map/dot_general | solution.py:24
  350.1 11.3 %fusion.65 = f32[512,2816]{1,0:T(8,128)} fusion(bf16[2048,2816]{1,0:T(8,128)(2,1)} %param.45, bf16[256,2048]{1,0:T(8,128)(2,1)S(1)} %collective-permute-done.28, bf16[256,2048]{1,0:T(8,128)(2,1)S(1)} %get-tuple-element.273), kind=kOutput, calls=%fused_computation.129 | convolution fusion | flops 5909774336 | bytes 19398656 | tf_op jit(solution)/shard_map/dot_general | solution.py:24
  361.4 16.9 %fusion.35 = f32[512,2048]{1,0:T(8,128)} fusion(bf16[2048,2816]{1,0:T(8,128)(2,1)} %param.44, f32[512,2816]{1,0:T(8,128)} %fusion.66, f32[512,2816]{1,0:T(8,128)} %fusion.49, f32[512,2816]{1,0:T(8,128)} %fusion.65), kind=kOutput, calls=%fused_computation.74 | convolution fusion | flops 5921439744 | bytes 33030144 | tf_op jit(solution)/shard_map/dot_general | solution.py:34
  378.2 13.2 %add_convert_fusion = bf16[512,2048]{1,0:T(8,128)(2,1)S(1)} fusion(f32[512,2048]{1,0:T(8,128)} %fusion.35, bf16[2048,2816]{1,0:T(8,128)(2,1)} %param.45, f32[512,2816]{1,0:T(8,128)} %fusion.49, f32[512,2816]{1,0:T(8,128)} %fusion.66), kind=kOutput, calls=%fused_computation.55 | convolution fusion | flops 5916327936 | bytes 29360128 | tf_op jit(solution)/shard_map/dot_general | solution.py:34
  394.5 13.1 %fusion.34 = f32[512,2048]{1,0:T(8,128)} fusion(bf16[2816,2048]{1,0:T(8,128)(2,1)} %param.46, f32[512,2816]{1,0:T(8,128)S(1)} %copy-done.99, f32[512,2816]{1,0:T(8,128)} %fusion.66), kind=kOutput, calls=%fused_computation.73 | convolution fusion | flops 5914230784 | bytes 27262976 | tf_op jit(solution)/shard_map/dot_general | solution.py:24
  407.6 9.7 %fusion.68 = f32[512,2816]{1,0:T(8,128)} fusion(bf16[2048,2816]{1,0:T(8,128)(2,1)S(1)} %bitcast.280, bf16[256,2048]{1,0:T(8,128)(2,1)} %collective-permute-done.26, bf16[256,2048]{1,0:T(8,128)(2,1)} %get-tuple-element.272), kind=kOutput, calls=%fused_computation.132 | convolution fusion | flops 5909774336 | bytes 19398656 | tf_op jit(solution)/shard_map/dot_general | solution.py:24
  417.3 11.7 %fusion.67 = f32[512,2816]{1,0:T(8,128)} fusion(bf16[2048,2816]{1,0:T(8,128)(2,1)} %param.45, bf16[256,2048]{1,0:T(8,128)(2,1)} %collective-permute-done.26, bf16[256,2048]{1,0:T(8,128)(2,1)} %get-tuple-element.272), kind=kOutput, calls=%fused_computation.131 | convolution fusion | flops 5909774336 | bytes 19398656 | tf_op jit(solution)/shard_map/dot_general | solution.py:24
  428.9 16.9 %fusion.37 = f32[512,2048]{1,0:T(8,128)} fusion(bf16[2048,2816]{1,0:T(8,128)(2,1)} %param.44, f32[512,2816]{1,0:T(8,128)} %fusion.68, f32[512,2816]{1,0:T(8,128)} %fusion.45, f32[512,2816]{1,0:T(8,128)} %fusion.67), kind=kOutput, calls=%fused_computation.75 | convolution fusion | flops 5921439744 | bytes 33030144 | tf_op jit(solution)/shard_map/dot_general | solution.py:34
  445.8 13.2 %add_convert_fusion.1 = bf16[512,2048]{1,0:T(8,128)(2,1)S(1)} fusion(f32[512,2048]{1,0:T(8,128)} %fusion.37, bf16[2048,2816]{1,0:T(8,128)(2,1)} %param.45, f32[512,2816]{1,0:T(8,128)} %fusion.45, f32[512,2816]{1,0:T(8,128)} %fusion.68), kind=kOutput, calls=%fused_computation.56 | convolution fusion | flops 5916327936 | bytes 29360128 | tf_op jit(solution)/shard_map/dot_general | solution.py:34
  459.2 11.8 %fusion.33 = f32[512,2048]{1,0:T(8,128)S(1)} fusion(bf16[2816,2048]{1,0:T(8,128)(2,1)} %param.46, f32[512,2816]{1,0:T(8,128)S(1)} %copy-done.100, f32[512,2816]{1,0:T(8,128)} %fusion.68), kind=kOutput, calls=%fused_computation.72 | convolution fusion | flops 5914230784 | bytes 27262976 | tf_op jit(solution)/shard_map/dot_general | solution.py:24
  471.1 10.8 %collective-permute-done.30 = bf16[256,2048]{1,0:T(8,128)(2,1)S(1)} collective-permute-done((bf16[256,2048]{1,0:T(8,128)(2,1)S(1)}, bf16[256,2048]{1,0:T(8,128)(2,1)S(1)}, u32[]{:S(2)}, u32[]{:S(2)}) %collective-permute-start.30) | collective-permute-done | bytes 1048608 | tf_op jit(solution)/shard_map/ppermute | solution.py:56
  484.4 4.4 fusion.158
  495.6 5.0 convolution_convert_fusion.7.near_ref
  505.5 22.1 %attention_backward.2 = (bf16[256,2048]{1,0:T(8,128)(2,1)S(1)}, f32[4,512,128]{2,1,0:T(8,128)S(1)}) custom-call(s32[5]{0:T(128)S(1)} %stack.38.info, bf16[256,2048]{1,0:T(8,128)(2,1)} %copy-done.13, bf16[256,1024]{1,0:T(8,128)(2,1)S(1)} %convolution_convert_fusion.7.near_ref, bf16[256,512]{1,0:T(8,128)(2,1)S(1)} %convolution_convert_fusion.11.mid_ref, ...), custom_call_target="tpu_custom_call" | custom-call | flops 2684354560 | bytes 8388608 | tf_op jit(solution)/shard_map/attention_backward/pallas_call | solution.py:283
  532.5 38.2 %attention_backward.3 = (bf16[256,2048]{1,0:T(8,128)(2,1)S(1)}, f32[4,1024,128]{2,1,0:T(8,128)}) custom-call(s32[5]{0:T(128)S(1)} %stack.40.info, bf16[256,2048]{1,0:T(8,128)(2,1)S(1)} %copy-done.17, bf16[256,1024]{1,0:T(8,128)(2,1)S(1)} %convolution_convert_fusion.6.near_ref, bf16[256,512]{1,0:T(8,128)(2,1)S(1)} %convolution_convert_fusion.9.mid_ref, ...), custom_call_target="tpu_custom_call" | custom-call | flops 5368709120 | bytes 8388608 | tf_op jit(solution)/shard_map/attention_backward/pallas_call | solution.py:283
  575.9 5.7 fusion.92
  585.9 7.4 pair_finish.1
  596.3 5.3 multiply_reduce_fusion
  617.6 14.3 %collective-permute-done.27 = bf16[512,1024]{1,0:T(8,128)(2,1)S(1)} collective-permute-done((bf16[512,1024]{1,0:T(8,128)(2,1)S(1)}, bf16[512,1024]{1,0:T(8,128)(2,1)S(1)}, u32[]{:S(2)}, u32[]{:S(2)}) %collective-permute-start.27) | collective-permute-done | bytes 1048608 | tf_op jit(solution)/shard_map/ppermute | solution.py:56
  632.2 22.2 %collective-permute-done.29 = bf16[512,1024]{1,0:T(8,128)(2,1)S(1)} collective-permute-done((bf16[512,1024]{1,0:T(8,128)(2,1)S(1)}, bf16[512,1024]{1,0:T(8,128)(2,1)S(1)}, u32[]{:S(2)}, u32[]{:S(2)}) %collective-permute-start.29) | collective-permute-done | bytes 1048608 | tf_op jit(solution)/shard_map/ppermute | solution.py:56
  656.0 7.7 collective-permute-done.49
  667.6 4.6 all-to-all-start.4
  678.3 14.3 %collective-permute-done.51 = bf16[2,1,1,1,1,16,2048]{6,5,4,3,2,1,0:T(8,128)(2,1)S(1)} collective-permute-done((bf16[2,1,1,1,1,16,2048]{6,5,4,3,2,1,0:T(8,128)(2,1)S(1)}, bf16[2,1,1,1,1,16,2048]{6,5,4,3,2,1,0:T(8,128)(2,1)S(1)}, u32[]{:S(2)}, u32[]{:S(2)}) %collective-permute-start.51) | collective-permute-done | bytes 131104 | tf_op jit(solution)/shard_map/ppermute | solution.py:56
  692.7 4.5 collective-permute-start.52
  704.3 15.1 %units_backward.1 = (f32[512,512]{1,0:T(8,128)S(1)}, bf16[512,512]{1,0:T(8,128)(2,1)S(1)}, bf16[512,2560]{1,0:T(8,128)(2,1)}, bf16[2048,512]{1,0:T(8,128)(2,1)S(1)}, f32[8,512]{1,0:T(8,128)S(1)}) custom-call(f32[512,512]{1,0:T(8,128)} %get-tuple-element.137.grad_ref, f32[512,512]{1,0:T(8,128)S(1)} %get-tuple-element.138.hidden_ref, ...), custom_call_target="tpu_custom_call" | custom-call | flops 5905580032 | bytes 16777216 | tf_op jit(solution)/shard_map/units_backward/pallas_call | solution.py:548
  719.5 31.2 %slot_backward.1 = (bf16[512,8,512]{2,1,0:T(8,128)(2,1)}, bf16[512,1664]{1,0:T(8,128)(2,1)S(1)}) custom-call(bf16[512,8,512]{2,1,0:T(8,128)(2,1)} %pieces_ref.3, bf16[4096,1536]{1,0:T(8,128)(2,1)} %get-tuple-element.127.mixed_ref, f32[512,8,128]{2,1,0:T(8,128)} %copy-done.18, bf16[512,512]{1,0:T(8,128)(2,1)S(1)} %get-tuple-element.139.attended_grad_ref, ...), custom_call_target="tpu_custom_call" | custom-call | flops 15032385536 | bytes 20971520 | tf_op jit(solution)/shard_map/slot_backward/pallas_call | solution.py:630
  756.7 9.6 %collective-permute-done.34 = bf16[2,2,2,1,1,16,1664]{6,5,4,3,2,1,0:T(8,128)(2,1)S(1)} collective-permute-done((bf16[2,2,2,1,1,16,1664]{6,5,4,3,2,1,0:T(8,128)(2,1)S(1)}, bf16[2,2,2,1,1,16,1664]{6,5,4,3,2,1,0:T(8,128)(2,1)S(1)}, u32[]{:S(2)}, u32[]{:S(2)}) %collective-permute-start.34) | collective-permute-done | bytes 426016 | tf_op jit(solution)/shard_map/ppermute | solution.py:56
  773.1 4.5 collective-permute-done.44
  784.4 6.9 collective-permute-done.39
  794.3 7.6 collective-permute-done.40
  802.6 5.7 collective-permute-done.41
  809.2 4.6 collective-permute-done.42
  (496 shorter events, 223.4 us)
Async XLA Ops:
  0.6 40.6 %collective-permute-start.10 = (bf16[1,1,1,1,1,64,512]{6,5,0,1,2,4,3:T(8,128)(2,1)}, bf16[1,1,1,1,1,64,512]{6,5,0,1,2,4,3:T(8,128)(2,1)S(1)}, u32[]{:S(2)}, u32[]{:S(2)}) collective-permute-start(bf16[1,1,1,1,1,64,512]{6,5,0,1,2,4,3:T(8,128)(2,1)} %bitcast.271), channel_id=1, source_target_pairs={{0,16},{1,17},{2,18},{3,19},{4,20},{5,21},{6,22},{7,23},{8,24},{9,... | collective-permute-start | bytes 196616 | tf_op jit(solution)/shard_map/ppermute | solution.py:56
  4.7 37.1 %collective-permute-start.15 = (bf16[1,1,1,1,1,16,2048]{6,5,4,3,2,1,0:T(8,128)(2,1)}, bf16[1,1,1,1,1,16,2048]{6,5,4,3,2,1,0:T(8,128)(2,1)S(1)}, u32[]{:S(2)}, u32[]{:S(2)}) collective-permute-start(bf16[1,1,1,1,1,16,2048]{6,5,4,3,2,1,0:T(8,128)(2,1)} %bitcast.267), channel_id=1, source_target_pairs={{0,16},{1,17},{2,18},{3,19},{4,20},{5,21},{6,22},{7,23},{8,24},{9,... | collective-permute-start | bytes 196616 | tf_op jit(solution)/shard_map/ppermute | solution.py:56
  6.4 37.2 %collective-permute-start.5 = (bf16[1,1,1,1,1,16,2560]{6,5,4,0,1,3,2:T(8,128)(2,1)S(1)}, bf16[1,1,1,1,1,16,2560]{6,5,4,0,1,3,2:T(8,128)(2,1)S(1)}, u32[]{:S(2)}, u32[]{:S(2)}) collective-permute-start(bf16[1,1,1,1,1,16,2560]{6,5,4,0,1,3,2:T(8,128)(2,1)S(1)} %bitcast.259), channel_id=1, source_target_pairs={{0,1},{1,0},{2,3},{3,2},{4,5},{5,4},{6,7},{7,6},{8,9},{9,8},{10,11... | collective-permute-start | bytes 245768 | tf_op jit(solution)/shard_map/ppermute | solution.py:56
  9.7 24.2 %collective-permute-start = (bf16[1,1,1,1,1,16,1664]{6,5,4,3,2,1,0:T(8,128)(2,1)S(1)}, bf16[1,1,1,1,1,16,1664]{6,5,4,3,2,1,0:T(8,128)(2,1)S(1)}, u32[]{:S(2)}, u32[]{:S(2)}) collective-permute-start(bf16[1,1,1,1,1,16,1664]{6,5,4,3,2,1,0:T(8,128)(2,1)S(1)} %get-tuple-element.271), channel_id=1, source_target_pairs={{0,1},{1,0},{2,3},{3,2},{4,5},{5,4},{6,7},{7,6},{8,9},{9,8},{10,11... | collective-permute-start | bytes 159752 | tf_op jit(solution)/shard_map/ppermute | solution.py:56
  14.5 192.0 %collective-permute-start.22 = (bf16[2048,256]{1,0:T(8,128)(2,1)}, bf16[2048,256]{1,0:T(8,128)(2,1)}, u32[]{:S(2)}, u32[]{:S(2)}) collective-permute-start(bf16[2048,256]{1,0:T(8,128)(2,1)} %pad_maximum_fusion.6), channel_id=1, source_target_pairs={{0,1},{1,0},{2,3},{3,2},{4,5},{5,4},{6,7},{7,6},{8,9},{9,8},{10,11... | collective-permute-start | bytes 3145736 | tf_op jit(solution)/shard_map/ppermute | solution.py:56
  34.0 69.7 %collective-permute-start.1 = (bf16[1,1,1,1,2,16,1664]{6,5,4,0,3,2,1:T(8,128)(2,1)S(1)}, bf16[1,1,1,1,2,16,1664]{6,5,4,0,3,2,1:T(8,128)(2,1)S(1)}, u32[]{:S(2)}, u32[]{:S(2)}) collective-permute-start(bf16[1,1,1,1,2,16,1664]{6,5,4,0,3,2,1:T(8,128)(2,1)S(1)} %fusion.218), channel_id=1, source_target_pairs={{0,16},{1,17},{2,18},{3,19},{4,20},{5,21},{6,22},{7,23},{8,24},{9,... | collective-permute-start | bytes 319496 | tf_op jit(solution)/shard_map/ppermute | solution.py:56
  41.2 182.2 %collective-permute-start.24 = (bf16[512,2048]{1,0:T(8,128)(2,1)}, bf16[512,2048]{1,0:T(8,128)(2,1)}, u32[]{:S(2)}, u32[]{:S(2)}) collective-permute-start(bf16[512,2048]{1,0:T(8,128)(2,1)} %constant_dynamic-slice_fusion.8), channel_id=1, source_target_pairs={{0,1},{1,0},{2,3},{3,2},{4,5},{5,4},{6,7},{7,6},{8,9},{9,8},{10,11... | collective-permute-start | bytes 6291464 | tf_op jit(solution)/shard_map/ppermute | solution.py:56
  41.8 62.4 %collective-permute-start.11 = (bf16[2,1,1,1,1,64,512]{6,5,0,1,2,4,3:T(8,128)(2,1)S(1)}, bf16[2,1,1,1,1,64,512]{6,5,0,1,2,4,3:T(8,128)(2,1)S(1)}, u32[]{:S(2)}, u32[]{:S(2)}) collective-permute-start(bf16[2,1,1,1,1,64,512]{6,5,0,1,2,4,3:T(8,128)(2,1)S(1)} %maximum_select_fusion.25), channel_id=1, source_target_pairs={{0,8},{1,9},{2,10},{3,11},{4,12},{5,13},{6,14},{7,15},{8,0},{9,1},... | collective-permute-start | bytes 393224 | tf_op jit(solution)/shard_map/ppermute | solution.py:56
  43.6 62.3 %collective-permute-start.16 = (bf16[2,1,1,1,1,16,2048]{6,5,1,0,4,3,2:T(8,128)(2,1)S(1)}, bf16[2,1,1,1,1,16,2048]{6,5,1,0,4,3,2:T(8,128)(2,1)S(1)}, u32[]{:S(2)}, u32[]{:S(2)}) collective-permute-start(bf16[2,1,1,1,1,16,2048]{6,5,1,0,4,3,2:T(8,128)(2,1)S(1)} %fusion.107), channel_id=1, source_target_pairs={{0,8},{1,9},{2,10},{3,11},{4,12},{5,13},{6,14},{7,15},{8,0},{9,1},... | collective-permute-start | bytes 393224 | tf_op jit(solution)/shard_map/ppermute | solution.py:56
  44.8 44.0 %all-to-all-start.2 = ((s32[32,1,512]{2,1,0:T(1,128)}), s32[32,1,512]{2,1,0:T(1,128)S(1)}, u32[]{:S(2)}, u32[]{:S(2)}) async-start(s32[32,1,512]{2,1,0:T(1,128)} %broadcast_in_dim.26), calls=%async_computation.2 | async-start | bytes 131072 | tf_op jit(solution)/shard_map/all_to_all | solution.py:709
  103.6 10.4 %collective-permute-start.6 = (bf16[1,1,1,1,2,16,2560]{6,5,4,0,1,3,2:T(8,128)(2,1)S(1)}, bf16[1,1,1,1,2,16,2560]{6,5,4,0,1,3,2:T(8,128)(2,1)S(1)}, u32[]{:S(2)}, u32[]{:S(2)}) collective-permute-start(bf16[1,1,1,1,2,16,2560]{6,5,4,0,1,3,2:T(8,128)(2,1)S(1)} %maximum_select_fusion.23), channel_id=1, source_target_pairs={{0,16},{1,17},{2,18},{3,19},{4,20},{5,21},{6,22},{7,23},{8,24},{9,... | collective-permute-start | bytes 491528 | tf_op jit(solution)/shard_map/ppermute | solution.py:56
  104.2 10.9 %collective-permute-start.2 = (bf16[2,1,1,1,2,16,1664]{6,5,4,0,3,2,1:T(8,128)(2,1)S(1)}, bf16[2,1,1,1,2,16,1664]{6,5,4,0,3,2,1:T(8,128)(2,1)S(1)}, u32[]{:S(2)}, u32[]{:S(2)}) collective-permute-start(bf16[2,1,1,1,2,16,1664]{6,5,4,0,3,2,1:T(8,128)(2,1)S(1)} %fusion.105), channel_id=1, source_target_pairs={{0,8},{1,9},{2,10},{3,11},{4,12},{5,13},{6,14},{7,15},{8,0},{9,1},... | collective-permute-start | bytes 638984 | tf_op jit(solution)/shard_map/ppermute | solution.py:56
  105.9 17.4 %collective-permute-start.12 = (bf16[2,2,1,1,1,64,512]{6,5,0,1,2,4,3:T(8,128)(2,1)S(1)}, bf16[2,2,1,1,1,64,512]{6,5,0,1,2,4,3:T(8,128)(2,1)S(1)}, u32[]{:S(2)}, u32[]{:S(2)}) collective-permute-start(bf16[2,2,1,1,1,64,512]{6,5,0,1,2,4,3:T(8,128)(2,1)S(1)} %maximum_select_fusion.20), channel_id=1, source_target_pairs={{0,4},{1,5},{2,6},{3,7},{4,0},{5,1},{6,2},{7,3},{8,12},{9,13},{10,... | collective-permute-start | bytes 786440 | tf_op jit(solution)/shard_map/ppermute | solution.py:56
  114.1 7.1 collective-permute-start.17
  115.1 9.0 %collective-permute-start.7 = (bf16[2,1,1,1,2,16,2560]{6,5,4,0,1,3,2:T(8,128)(2,1)S(1)}, bf16[2,1,1,1,2,16,2560]{6,5,4,0,1,3,2:T(8,128)(2,1)S(1)}, u32[]{:S(2)}, u32[]{:S(2)}) collective-permute-start(bf16[2,1,1,1,2,16,2560]{6,5,4,0,1,3,2:T(8,128)(2,1)S(1)} %maximum_select_fusion.18), channel_id=1, source_target_pairs={{0,8},{1,9},{2,10},{3,11},{4,12},{5,13},{6,14},{7,15},{8,0},{9,1},... | collective-permute-start | bytes 983048 | tf_op jit(solution)/shard_map/ppermute | solution.py:56
  121.2 12.8 %collective-permute-start.3 = (bf16[2,2,1,1,2,16,1664]{6,5,4,3,2,1,0:T(8,128)(2,1)S(1)}, bf16[2,2,1,1,2,16,1664]{6,5,4,3,2,1,0:T(8,128)(2,1)S(1)}, u32[]{:S(2)}, u32[]{:S(2)}) collective-permute-start(bf16[2,2,1,1,2,16,1664]{6,5,4,3,2,1,0:T(8,128)(2,1)S(1)} %copy.108), channel_id=1, source_target_pairs={{0,4},{1,5},{2,6},{3,7},{4,0},{5,1},{6,2},{7,3},{8,12},{9,13},{10,... | collective-permute-start | bytes 1277960 | tf_op jit(solution)/shard_map/ppermute | solution.py:56
  123.4 11.9 %collective-permute-start.13 = (bf16[2,2,2,1,1,64,512]{6,5,0,1,2,4,3:T(8,128)(2,1)S(1)}, bf16[2,2,2,1,1,64,512]{6,5,0,1,2,4,3:T(8,128)(2,1)S(1)}, u32[]{:S(2)}, u32[]{:S(2)}) collective-permute-start(bf16[2,2,2,1,1,64,512]{6,5,0,1,2,4,3:T(8,128)(2,1)S(1)} %maximum_select_fusion.12), channel_id=1, source_target_pairs={{0,1},{1,0},{2,3},{3,2},{4,5},{5,4},{6,7},{7,6},{8,9},{9,8},{10,11... | collective-permute-start | bytes 1572872 | tf_op jit(solution)/shard_map/ppermute | solution.py:56
  124.2 20.8 %collective-permute-start.8 = (bf16[2,2,1,1,2,16,2560]{6,5,4,0,1,3,2:T(8,128)(2,1)S(1)}, bf16[2,2,1,1,2,16,2560]{6,5,4,0,1,3,2:T(8,128)(2,1)S(1)}, u32[]{:S(2)}, u32[]{:S(2)}) collective-permute-start(bf16[2,2,1,1,2,16,2560]{6,5,4,0,1,3,2:T(8,128)(2,1)S(1)} %maximum_select_fusion.10), channel_id=1, source_target_pairs={{0,4},{1,5},{2,6},{3,7},{4,0},{5,1},{6,2},{7,3},{8,12},{9,13},{10,... | collective-permute-start | bytes 1966088 | tf_op jit(solution)/shard_map/ppermute | solution.py:56
  134.1 11.1 %collective-permute-start.4 = (bf16[2,2,2,1,2,16,1664]{6,5,4,3,2,1,0:T(8,128)(2,1)S(1)}, bf16[2,2,2,1,2,16,1664]{6,5,4,3,2,1,0:T(8,128)(2,1)S(1)}, u32[]{:S(2)}, u32[]{:S(2)}) collective-permute-start(bf16[2,2,2,1,2,16,1664]{6,5,4,3,2,1,0:T(8,128)(2,1)S(1)} %maximum_select_fusion.9), channel_id=1, source_target_pairs={{0,2},{1,3},{2,0},{3,1},{4,6},{5,7},{6,4},{7,5},{8,10},{9,11},{10,... | collective-permute-start | bytes 2555912 | tf_op jit(solution)/shard_map/ppermute | solution.py:56
  135.2 88.4 %collective-permute-start.20 = (bf16[2048,512]{1,0:T(8,128)(2,1)}, bf16[2048,512]{1,0:T(8,128)(2,1)}, u32[]{:S(2)}, u32[]{:S(2)}) collective-permute-start(bf16[2048,512]{1,0:T(8,128)(2,1)} %constant_dynamic-slice_fusion.9), channel_id=1, source_target_pairs={{0,1},{1,0},{2,3},{3,2},{4,5},{5,4},{6,7},{7,6},{8,9},{9,8},{10,11... | collective-permute-start | bytes 6291464 | tf_op jit(solution)/shard_map/ppermute | solution.py:56
  145.0 24.2 %collective-permute-start.14 = (bf16[2,2,2,1,2,64,512]{6,5,0,1,2,4,3:T(8,128)(2,1)}, bf16[2,2,2,1,2,64,512]{6,5,0,1,2,4,3:T(8,128)(2,1)}, u32[]{:S(2)}, u32[]{:S(2)}) collective-permute-start(bf16[2,2,2,1,2,64,512]{6,5,0,1,2,4,3:T(8,128)(2,1)} %maximum_select_fusion.7), channel_id=1, source_target_pairs={{0,2},{1,3},{2,0},{3,1},{4,6},{5,7},{6,4},{7,5},{8,10},{9,11},{10,... | collective-permute-start | bytes 3145736 | tf_op jit(solution)/shard_map/ppermute | solution.py:56
  145.2 28.3 %collective-permute-start.9 = (bf16[2,2,2,1,2,16,2560]{6,5,4,0,1,3,2:T(8,128)(2,1)S(1)}, bf16[2,2,2,1,2,16,2560]{6,5,4,0,1,3,2:T(8,128)(2,1)}, u32[]{:S(2)}, u32[]{:S(2)}) collective-permute-start(bf16[2,2,2,1,2,16,2560]{6,5,4,0,1,3,2:T(8,128)(2,1)S(1)} %maximum_select_fusion.6), channel_id=1, source_target_pairs={{0,2},{1,3},{2,0},{3,1},{4,6},{5,7},{6,4},{7,5},{8,10},{9,11},{10,... | collective-permute-start | bytes 3932168 | tf_op jit(solution)/shard_map/ppermute | solution.py:56
  169.2 34.6 %collective-permute-start.18 = (bf16[2,2,2,1,1,16,2048]{6,5,4,3,2,1,0:T(8,128)(2,1)}, bf16[2,2,2,1,1,16,2048]{6,5,4,3,2,1,0:T(8,128)(2,1)}, u32[]{:S(2)}, u32[]{:S(2)}) collective-permute-start(bf16[2,2,2,1,1,16,2048]{6,5,4,3,2,1,0:T(8,128)(2,1)} %copy.118), channel_id=1, source_target_pairs={{0,1},{1,0},{2,3},{3,2},{4,5},{5,4},{6,7},{7,6},{8,9},{9,8},{10,11... | collective-permute-start | bytes 1572872 | tf_op jit(solution)/shard_map/ppermute | solution.py:56
  185.7 38.3 %all-to-all-start.3 = ((bf16[32,32,512]{2,1,0:T(8,128)(2,1)}), bf16[32,32,512]{2,1,0:T(8,128)(2,1)}, u32[]{:S(2)}, u32[]{:S(2)}) async-start(bf16[32,32,512]{2,1,0:T(8,128)(2,1)} %bitcast.50), calls=%async_computation.3 | async-start | bytes 2097152 | tf_op jit(solution)/shard_map/all_to_all | solution.py:709
  206.1 13.4 %collective-permute-start.19 = (bf16[2,2,2,1,2,16,2048]{6,5,4,3,2,1,0:T(8,128)(2,1)}, bf16[2,2,2,1,2,16,2048]{6,5,4,3,2,1,0:T(8,128)(2,1)}, u32[]{:S(2)}, u32[]{:S(2)}) collective-permute-start(bf16[2,2,2,1,2,16,2048]{6,5,4,3,2,1,0:T(8,128)(2,1)} %maximum_select_fusion.8), channel_id=1, source_target_pairs={{0,2},{1,3},{2,0},{3,1},{4,6},{5,7},{6,4},{7,5},{8,10},{9,11},{10,... | collective-permute-start | bytes 3145736 | tf_op jit(solution)/shard_map/ppermute | solution.py:56
  223.5 82.0 %collective-permute-start.25 = (bf16[512,2048]{1,0:T(8,128)(2,1)}, bf16[512,2048]{1,0:T(8,128)(2,1)}, u32[]{:S(2)}, u32[]{:S(2)}) collective-permute-start(bf16[512,2048]{1,0:T(8,128)(2,1)} %collective-permute-done.24), channel_id=1, source_target_pairs={{0,2},{1,3},{2,0},{3,1},{4,6},{5,7},{6,4},{7,5},{8,10},{9,11},{10,... | collective-permute-start | bytes 6291464 | tf_op jit(solution)/shard_map/ppermute | solution.py:56
  223.6 16.6 %collective-permute-start.21 = (bf16[2048,512]{1,0:T(8,128)(2,1)}, bf16[2048,512]{1,0:T(8,128)(2,1)}, u32[]{:S(2)}, u32[]{:S(2)}) collective-permute-start(bf16[2048,512]{1,0:T(8,128)(2,1)} %collective-permute-done.20), channel_id=1, source_target_pairs={{0,2},{1,3},{2,0},{3,1},{4,6},{5,7},{6,4},{7,5},{8,10},{9,11},{10,... | collective-permute-start | bytes 6291464 | tf_op jit(solution)/shard_map/ppermute | solution.py:56
  226.0 18.3 %collective-permute-start.23 = (bf16[512,512]{1,0:T(8,128)(2,1)S(1)}, bf16[512,512]{1,0:T(8,128)(2,1)S(1)}, u32[]{:S(2)}, u32[]{:S(2)}) collective-permute-start(bf16[512,512]{1,0:T(8,128)(2,1)S(1)} %get-tuple-element.122), channel_id=1, source_target_pairs={{0,1},{1,0},{2,3},{3,2},{4,5},{5,4},{6,7},{7,6},{8,9},{9,8},{10,11... | collective-permute-start | bytes 1572872 | tf_op jit(solution)/shard_map/ppermute | solution.py:56
  315.3 26.0 %collective-permute-start.28 = (bf16[256,2048]{1,0:T(8,128)(2,1)S(1)}, bf16[256,2048]{1,0:T(8,128)(2,1)S(1)}, u32[]{:S(2)}, u32[]{:S(2)}) collective-permute-start(bf16[256,2048]{1,0:T(8,128)(2,1)S(1)} %get-tuple-element.273), channel_id=1, source_target_pairs={{0,1},{1,0},{2,3},{3,2},{4,5},{5,4},{6,7},{7,6},{8,9},{9,8},{10,11... | collective-permute-start | bytes 3145736 | tf_op jit(solution)/shard_map/ppermute | solution.py:56
  328.5 79.1 %collective-permute-start.26 = (bf16[256,2048]{1,0:T(8,128)(2,1)}, bf16[256,2048]{1,0:T(8,128)(2,1)}, u32[]{:S(2)}, u32[]{:S(2)}) collective-permute-start(bf16[256,2048]{1,0:T(8,128)(2,1)} %get-tuple-element.272), channel_id=1, source_target_pairs={{0,1},{1,0},{2,3},{3,2},{4,5},{5,4},{6,7},{7,6},{8,9},{9,8},{10,11... | collective-permute-start | bytes 3145736 | tf_op jit(solution)/shard_map/ppermute | solution.py:56
  392.5 78.5 %collective-permute-start.31 = (bf16[256,2048]{1,0:T(8,128)(2,1)}, bf16[256,2048]{1,0:T(8,128)(2,1)}, u32[]{:S(2)}, u32[]{:S(2)}) collective-permute-start(bf16[256,2048]{1,0:T(8,128)(2,1)} %slice.176), channel_id=1, source_target_pairs={{0,1},{1,0},{2,3},{3,2},{4,5},{5,4},{6,7},{7,6},{8,9},{9,8},{10,11... | collective-permute-start | bytes 3145736 | tf_op jit(solution)/shard_map/ppermute | solution.py:56
  459.1 22.8 %collective-permute-start.30 = (bf16[256,2048]{1,0:T(8,128)(2,1)S(1)}, bf16[256,2048]{1,0:T(8,128)(2,1)S(1)}, u32[]{:S(2)}, u32[]{:S(2)}) collective-permute-start(bf16[256,2048]{1,0:T(8,128)(2,1)S(1)} %slice.174), channel_id=1, source_target_pairs={{0,1},{1,0},{2,3},{3,2},{4,5},{5,4},{6,7},{7,6},{8,9},{9,8},{10,11... | collective-permute-start | bytes 3145736 | tf_op jit(solution)/shard_map/ppermute | solution.py:56
  572.9 13.0 %collective-permute-start.32 = (bf16[4,512,128]{2,1,0:T(8,128)(2,1)S(1)}, bf16[4,512,128]{2,1,0:T(8,128)(2,1)}, u32[]{:S(2)}, u32[]{:S(2)}) collective-permute-start(bf16[4,512,128]{2,1,0:T(8,128)(2,1)S(1)} %pad_maximum_fusion.10), channel_id=1, source_target_pairs={{0,1},{1,0},{2,3},{3,2},{4,5},{5,4},{6,7},{7,6},{8,9},{9,8},{10,11... | collective-permute-start | bytes 1572872 | tf_op jit(solution)/shard_map/ppermute | solution.py:56
  604.1 8.8 %collective-permute-start.48 = (bf16[2,2,2,1,2,16,2048]{6,5,4,3,2,1,0:T(8,128)(2,1)S(1)}, bf16[2,2,2,1,2,16,2048]{6,5,4,3,2,1,0:T(8,128)(2,1)S(1)}, u32[]{:S(2)}, u32[]{:S(2)}) collective-permute-start(bf16[2,2,2,1,2,16,2048]{6,5,4,3,2,1,0:T(8,128)(2,1)S(1)} %constant_dynamic-slice_fusion), channel_id=1, source_target_pairs={{0,2},{1,3},{2,0},{3,1},{4,6},{5,7},{6,4},{7,5},{8,10},{9,11},{10,... | collective-permute-start | bytes 3145736 | tf_op jit(solution)/shard_map/ppermute | solution.py:56
  605.8 26.2 %collective-permute-start.27 = (bf16[512,1024]{1,0:T(8,128)(2,1)S(1)}, bf16[512,1024]{1,0:T(8,128)(2,1)S(1)}, u32[]{:S(2)}, u32[]{:S(2)}) collective-permute-start(bf16[512,1024]{1,0:T(8,128)(2,1)S(1)} %pad_maximum_fusion.7), channel_id=1, source_target_pairs={{0,1},{1,0},{2,3},{3,2},{4,5},{5,4},{6,7},{7,6},{8,9},{9,8},{10,11... | collective-permute-start | bytes 3145736 | tf_op jit(solution)/shard_map/ppermute | solution.py:56
  610.0 44.4 %collective-permute-start.29 = (bf16[512,1024]{1,0:T(8,128)(2,1)S(1)}, bf16[512,1024]{1,0:T(8,128)(2,1)S(1)}, u32[]{:S(2)}, u32[]{:S(2)}) collective-permute-start(bf16[512,1024]{1,0:T(8,128)(2,1)S(1)} %pad_maximum_fusion.8), channel_id=1, source_target_pairs={{0,1},{1,0},{2,3},{3,2},{4,5},{5,4},{6,7},{7,6},{8,9},{9,8},{10,11... | collective-permute-start | bytes 3145736 | tf_op jit(solution)/shard_map/ppermute | solution.py:56
  613.4 50.3 %collective-permute-start.49 = (bf16[2,2,2,1,1,16,2048]{6,5,4,3,2,1,0:T(8,128)(2,1)S(1)}, bf16[2,2,2,1,1,16,2048]{6,5,4,3,2,1,0:T(8,128)(2,1)S(1)}, u32[]{:S(2)}, u32[]{:S(2)}) collective-permute-start(bf16[2,2,2,1,1,16,2048]{6,5,4,3,2,1,0:T(8,128)(2,1)S(1)} %dynamic-slice_convert_fusion.1), channel_id=1, source_target_pairs={{0,1},{1,0},{2,3},{3,2},{4,5},{5,4},{6,7},{7,6},{8,9},{9,8},{10,11... | collective-permute-start | bytes 1572872 | tf_op jit(solution)/shard_map/ppermute | solution.py:56
  665.5 8.7 %collective-permute-start.50 = (bf16[2,2,1,1,1,16,2048]{6,5,4,3,2,1,0:T(8,128)(2,1)}, bf16[2,2,1,1,1,16,2048]{6,5,4,3,2,1,0:T(8,128)(2,1)S(1)}, u32[]{:S(2)}, u32[]{:S(2)}) collective-permute-start(bf16[2,2,1,1,1,16,2048]{6,5,4,3,2,1,0:T(8,128)(2,1)} %dynamic-slice_convert_fusion.9), channel_id=1, source_target_pairs={{0,4},{1,5},{2,6},{3,7},{4,0},{5,1},{6,2},{7,3},{8,12},{9,13},{10,... | collective-permute-start | bytes 786440 | tf_op jit(solution)/shard_map/ppermute | solution.py:56
  667.6 32.7 %all-to-all-start.4 = ((bf16[32,32,512]{2,1,0:T(8,128)(2,1)}), bf16[32,32,512]{2,1,0:T(8,128)(2,1)}, u32[]{:S(2)}, u32[]{:S(2)}) async-start(bf16[32,32,512]{2,1,0:T(8,128)(2,1)} %bitcast.251), calls=%async_computation.4 | async-start | bytes 2097152 | tf_op jit(solution)/shard_map/all_to_all | solution.py:709
  674.4 18.2 %collective-permute-start.51 = (bf16[2,1,1,1,1,16,2048]{6,5,4,3,2,1,0:T(8,128)(2,1)S(1)}, bf16[2,1,1,1,1,16,2048]{6,5,4,3,2,1,0:T(8,128)(2,1)S(1)}, u32[]{:S(2)}, u32[]{:S(2)}) collective-permute-start(bf16[2,1,1,1,1,16,2048]{6,5,4,3,2,1,0:T(8,128)(2,1)S(1)} %dynamic-slice_convert_fusion.13), channel_id=1, source_target_pairs={{0,8},{1,9},{2,10},{3,11},{4,12},{5,13},{6,14},{7,15},{8,0},{9,1},... | collective-permute-start | bytes 393224 | tf_op jit(solution)/shard_map/ppermute | solution.py:56
  692.7 60.0 %collective-permute-start.52 = (bf16[1,1,1,1,1,16,2048]{6,5,4,3,2,1,0:T(8,128)(2,1)S(1)}, bf16[1,1,1,1,1,16,2048]{6,5,4,3,2,1,0:T(8,128)(2,1)S(1)}, u32[]{:S(2)}, u32[]{:S(2)}) collective-permute-start(bf16[1,1,1,1,1,16,2048]{6,5,4,3,2,1,0:T(8,128)(2,1)S(1)} %dynamic-slice_convert_fusion.17), channel_id=1, source_target_pairs={{0,16},{1,17},{2,18},{3,19},{4,20},{5,21},{6,22},{7,23},{8,24},{9,... | collective-permute-start | bytes 196616 | tf_op jit(solution)/shard_map/ppermute | solution.py:56
  752.6 15.4 %collective-permute-start.38 = (bf16[2,2,2,1,2,16,2560]{6,5,4,3,2,1,0:T(8,128)(2,1)S(1)}, bf16[2,2,2,1,2,16,2560]{6,5,4,3,2,1,0:T(8,128)(2,1)S(1)}, u32[]{:S(2)}, u32[]{:S(2)}) collective-permute-start(bf16[2,2,2,1,2,16,2560]{6,5,4,3,2,1,0:T(8,128)(2,1)S(1)} %constant_dynamic-slice_fusion.2), channel_id=1, source_target_pairs={{0,2},{1,3},{2,0},{3,1},{4,6},{5,7},{6,4},{7,5},{8,10},{9,11},{10,... | collective-permute-start | bytes 3932168 | tf_op jit(solution)/shard_map/ppermute | solution.py:56
  753.6 12.7 %collective-permute-start.34 = (bf16[2,2,2,1,1,16,1664]{6,5,4,3,2,1,0:T(8,128)(2,1)S(1)}, bf16[2,2,2,1,1,16,1664]{6,5,4,3,2,1,0:T(8,128)(2,1)S(1)}, u32[]{:S(2)}, u32[]{:S(2)}) collective-permute-start(bf16[2,2,2,1,1,16,1664]{6,5,4,3,2,1,0:T(8,128)(2,1)S(1)} %dynamic-slice_convert_fusion.7), channel_id=1, source_target_pairs={{0,1},{1,0},{2,3},{3,2},{4,5},{5,4},{6,7},{7,6},{8,9},{9,8},{10,11... | collective-permute-start | bytes 1277960 | tf_op jit(solution)/shard_map/ppermute | solution.py:56
  755.5 22.0 %collective-permute-start.44 = (bf16[2,2,2,1,1,64,512]{6,5,4,3,2,1,0:T(8,128)(2,1)S(1)}, bf16[2,2,2,1,1,64,512]{6,5,4,3,2,1,0:T(8,128)(2,1)S(1)}, u32[]{:S(2)}, u32[]{:S(2)}) collective-permute-start(bf16[2,2,2,1,1,64,512]{6,5,4,3,2,1,0:T(8,128)(2,1)S(1)} %dynamic-slice_convert_fusion.2), channel_id=1, source_target_pairs={{0,1},{1,0},{2,3},{3,2},{4,5},{5,4},{6,7},{7,6},{8,9},{9,8},{10,11... | collective-permute-start | bytes 1572872 | tf_op jit(solution)/shard_map/ppermute | solution.py:56
  768.4 22.8 %collective-permute-start.39 = (bf16[2,2,2,1,1,16,2560]{6,5,4,3,2,1,0:T(8,128)(2,1)S(1)}, bf16[2,2,2,1,1,16,2560]{6,5,4,3,2,1,0:T(8,128)(2,1)}, u32[]{:S(2)}, u32[]{:S(2)}) collective-permute-start(bf16[2,2,2,1,1,16,2560]{6,5,4,3,2,1,0:T(8,128)(2,1)S(1)} %dynamic-slice_convert_fusion), channel_id=1, source_target_pairs={{0,1},{1,0},{2,3},{3,2},{4,5},{5,4},{6,7},{7,6},{8,9},{9,8},{10,11... | collective-permute-start | bytes 1966088 | tf_op jit(solution)/shard_map/ppermute | solution.py:56
  779.4 14.7 %collective-permute-start.45 = (bf16[2,2,1,1,1,64,512]{6,5,4,3,2,1,0:T(8,128)(2,1)}, bf16[2,2,1,1,1,64,512]{6,5,4,3,2,1,0:T(8,128)(2,1)S(1)}, u32[]{:S(2)}, u32[]{:S(2)}) collective-permute-start(bf16[2,2,1,1,1,64,512]{6,5,4,3,2,1,0:T(8,128)(2,1)} %dynamic-slice_convert_fusion.10), channel_id=1, source_target_pairs={{0,4},{1,5},{2,6},{3,7},{4,0},{5,1},{6,2},{7,3},{8,12},{9,13},{10,... | collective-permute-start | bytes 786440 | tf_op jit(solution)/shard_map/ppermute | solution.py:56
  792.5 9.4 %collective-permute-start.40 = (bf16[2,2,1,1,1,16,2560]{6,5,4,3,2,1,0:T(8,128)(2,1)S(1)}, bf16[2,2,1,1,1,16,2560]{6,5,4,3,2,1,0:T(8,128)(2,1)S(1)}, u32[]{:S(2)}, u32[]{:S(2)}) collective-permute-start(bf16[2,2,1,1,1,16,2560]{6,5,4,3,2,1,0:T(8,128)(2,1)S(1)} %dynamic-slice_convert_fusion.8), channel_id=1, source_target_pairs={{0,4},{1,5},{2,6},{3,7},{4,0},{5,1},{6,2},{7,3},{8,12},{9,13},{10,... | collective-permute-start | bytes 983048 | tf_op jit(solution)/shard_map/ppermute | solution.py:56
  794.2 7.9 collective-permute-start.46
  (115 other events, 920.6 us)

commit v3 on v2

v3 whole, which is shorter than its diff:
```python
import functools

import jax
import jax.numpy as jnp
import numpy as np
from jax import lax
from jax.experimental import pallas as pl
from jax.experimental.pallas import tpu as pltpu
from jax.sharding import PartitionSpec as P

HEAD_WIDTH = 64
HHD = 64
BLOCK_PARTS = 4
UNIT = 512
PAIR = 2 * HEAD_WIDTH
VMEM_LIMIT = 48 << 20
ENTRY_BLOCK = 64
SLOT_PARTS = 2
UNIT_STEP = 256
COLUMN_STEP = 256
UNIT_ROWS = 256


EPS = 1e-05
NEGATIVE = -1000000000.0


def matmul(left, right):
    return jnp.dot(left, right, preferred_element_type=jnp.float32)


def matmul_first(left, right):
    return lax.dot_general(
        left, right, (((0,), (0,)), ((), ())), preferred_element_type=jnp.float32
    )


def matmul_last(left, right):
    return lax.dot_general(
        left, right, (((1,), (1,)), ((), ())), preferred_element_type=jnp.float32
    )


def log2_of(number):
    return number.bit_length() - 1


def swap(value, mask, devices):
    return lax.ppermute(value, ("dp", "mp"), [(d, d ^ mask) for d in range(devices)])


def gather_start(block, devices):
    return block.reshape((1,) * log2_of(devices) + block.shape)


def masks_of(bits):
    masks = [0]
    for bit in bits:
        masks += [mask | (1 << bit) for mask in masks]
    return masks


def gather_send(held, bits, devices):
    return [swap(held, mask, devices) for mask in masks_of(bits)[1:]]


def gather_join(held, came, bits, me, devices):
    blocks = [held, *came]
    for bit in bits:
        axis = log2_of(devices) - 1 - bit
        upper = ((me >> bit) & 1) == 1
        blocks = [
            jnp.where(
                upper,
                jnp.concatenate([other, own], axis),
                jnp.concatenate([own, other], axis),
            )
            for own, other in zip(blocks[::2], blocks[1::2])
        ]
    return blocks[0]


def gather_step(held, bits, me, devices):
    return gather_join(held, gather_send(held, bits, devices), bits, me, devices)


def gather_end(held):
    return held.reshape((-1, held.shape[-1]))


def scatter_start(blocks, devices):
    bits = log2_of(devices)
    return blocks.reshape((2,) * bits + (blocks.shape[0] // devices,) + blocks.shape[1:])


def scatter_send(held, bits, me, devices):
    def part(mask, value):
        for bit in bits:
            axis = log2_of(devices) - 1 - bit
            value = lax.dynamic_slice_in_dim(value, ((me ^ mask) >> bit) & 1, 1, axis)
        return value

    came = [swap(to_low(part(mask, held)), mask, devices) for mask in masks_of(bits)[1:]]
    return (part(0, held), came)


def scatter_add(staying, came):
    total = staying.astype(jnp.float32)
    for share in came:
        total = total + share.astype(jnp.float32)
    return total


def scatter_step(held, bits, me, devices):
    return scatter_add(*scatter_send(held, bits, me, devices))


def scatter_end(held):
    return held.reshape(held.shape[-2:])


def lanes(shape):
    return lax.broadcasted_iota(jnp.int32, shape, len(shape) - 1)


def half_swap(value):
    quarter = HEAD_WIDTH // 2
    upper = (lanes(value.shape) & quarter) != 0
    return jnp.where(
        upper, pltpu.roll(value, quarter, 1), pltpu.roll(value, PAIR - quarter, 1)
    )


def to_low(value):
    return value.astype(jnp.bfloat16)


def causal_of(shape, block_at, rows):
    key_at = lax.broadcasted_iota(jnp.int32, shape, 0)
    query_at = lax.broadcasted_iota(jnp.int32, shape, 1) + block_at * rows
    return key_at <= query_at


def head_views(pair_ref, cos_ref, sin_ref):
    pair = pair_ref[...]
    turned = to_low(pair * cos_ref[...] + half_swap(pair) * sin_ref[...]).astype(jnp.float32)
    other = pltpu.roll(turned, HEAD_WIDTH, 1)
    left = lanes(turned.shape) < HEAD_WIDTH
    return (
        jnp.where(left, turned, 0.0),
        jnp.where(left, 0.0, other),
        jnp.where(left, other, 0.0),
        jnp.where(left, 0.0, turned),
    )


def attention_forward_kernel(
    info, query_ref, pair_ref, cos_pair, sin_pair, cos_ref, sin_ref,
    out_ref, low_ref, lse_ref, even, odd, across,
):
    key_left, key_right, value_left, _ = head_views(pair_ref, cos_pair, sin_pair)
    even[...] = to_low(key_left)
    odd[...] = to_low(key_right)
    across[...] = to_low(value_left.T[:HEAD_WIDTH])

    rows = query_ref.shape[0]
    length = pair_ref.shape[0]
    causal = causal_of((length, rows), info[0], rows)
    for pair in range(query_ref.shape[1] // PAIR):
        span = slice(pair * PAIR, (pair + 1) * PAIR)
        query = query_ref[:, span]
        turned = to_low(query * cos_ref[...] + half_swap(query) * sin_ref[...])
        low = to_low(turned.astype(jnp.float32) * HEAD_WIDTH ** (-0.5))
        low_ref[:, span] = low
        outs = []
        for at, keys in enumerate((even, odd)):
            scores = jnp.where(causal, matmul_last(keys[...], low), NEGATIVE)
            highest = jnp.max(scores, axis=0, keepdims=True)
            weight = jnp.exp(scores - highest)
            total = jnp.sum(weight, axis=0, keepdims=True)
            outs.append(matmul(across[...], to_low(weight)) / total)
            lse_ref[0, 2 * pair + at : 2 * pair + at + 1, :] = highest + jnp.log(total)
        out_ref[:, span] = to_low(jnp.concatenate(outs, axis=0).T)


def attention_backward_kernel(
    info, low_ref, grad_ref, lse_ref, pair_ref, cos_pair, sin_pair, cos_ref, sin_ref, *refs,
):
    query_ref, pair_grad_ref, even, odd, value_even, value_odd, across = refs[-11:-4]
    key_even, key_odd, sum_even, sum_odd = refs[-4:]
    key_left, key_right, value_left, value_right = head_views(pair_ref, cos_pair, sin_pair)
    even[...] = to_low(key_left)
    odd[...] = to_low(key_right)
    value_even[...] = to_low(value_left)
    value_odd[...] = to_low(value_right)
    across[...] = to_low(key_left.T[:HEAD_WIDTH])
    for total in (key_even, key_odd, sum_even, sum_odd):
        total[...] = jnp.zeros_like(total)

    rows = low_ref.shape[0]
    length = pair_ref.shape[0]
    causal = causal_of((length, rows), info[0], rows)
    sides = ((even, value_even, key_even, sum_even), (odd, value_odd, key_odd, sum_odd))
    for pair in range(low_ref.shape[1] // PAIR):
        span = slice(pair * PAIR, (pair + 1) * PAIR)
        low = low_ref[:, span]
        grad = grad_ref[:, span]
        outs = []
        for at, (keys, values, key_total, value_total) in enumerate(sides):
            scores = jnp.where(causal, matmul_last(keys[...], low), NEGATIVE)
            probs = jnp.exp(scores - lse_ref[0, 2 * pair + at : 2 * pair + at + 1, :])
            value_total[...] += matmul(to_low(probs), grad)
            moved = probs * matmul_last(values[...], grad)
            mean = jnp.sum(moved, axis=0, keepdims=True)
            grad_scores = to_low(moved - probs * mean)
            key_total[...] += matmul(grad_scores, low)
            outs.append(matmul(across[...], grad_scores))
        turned = jnp.concatenate(outs, axis=0).T * HEAD_WIDTH ** (-0.5)
        query_ref[:, span] = to_low(turned * cos_ref[...] - half_swap(turned) * sin_ref[...])
    left = lanes((length, PAIR)) < HEAD_WIDTH
    pair_grad_ref[0] = jnp.where(
        left,
        key_even[...] + pltpu.roll(key_odd[...], HEAD_WIDTH, 1),
        pltpu.roll(sum_even[...], HEAD_WIDTH, 1) + sum_odd[...],
    )


def attention_specs(part, rows, length):
    span = (rows, 4 * PAIR)
    return {
        "table_pair": pl.BlockSpec((length, PAIR), lambda g, s: (0, 0)),
        "table": pl.BlockSpec((rows, PAIR), lambda g, s: (s[0], 0)),
        "pair": pl.BlockSpec((length, PAIR), lambda g, s: (0, s[1 + g])),
        "part": pl.BlockSpec(span, lambda g, s: (part, g)),
        "wide": pl.BlockSpec(span, lambda g, s: (0, g)),
        "sums": pl.BlockSpec((1, 8, rows), lambda g, s: (g, 0, 0)),
    }


def attention_cost(rows, length, heads, matmuls):
    work = 20 * rows * length * heads * HEAD_WIDTH * matmuls
    return pl.CostEstimate(
        flops=work, bytes_accessed=16 * rows * heads * HEAD_WIDTH, transcendentals=rows * length * heads
    )


def attention_forward(info, queries, pair_pre, tables, part, length):
    cos_pair, sin_pair, cosine, sine = tables
    rows = cosine.shape[0] // BLOCK_PARTS
    heads = 4 * 4 * PAIR // HEAD_WIDTH
    spec = attention_specs(part, rows, length)
    half = pltpu.VMEM((length, PAIR), jnp.bfloat16)
    wide = (rows, heads * HEAD_WIDTH)
    return pl.pallas_call(
        attention_forward_kernel,
        grid_spec=pltpu.PrefetchScalarGridSpec(
            num_scalar_prefetch=1,
            grid=(4,),
            in_specs=[
                spec["part"], spec["pair"],
                spec["table_pair"], spec["table_pair"], spec["table"], spec["table"],
            ],
            out_specs=[spec["wide"], spec["wide"], spec["sums"]],
            scratch_shapes=[
                half, half,
                pltpu.VMEM((HEAD_WIDTH, length), jnp.bfloat16),
            ],
        ),
        out_shape=[
            jax.ShapeDtypeStruct(wide, jnp.bfloat16),
            jax.ShapeDtypeStruct(wide, jnp.bfloat16),
            jax.ShapeDtypeStruct((4, 8, rows), jnp.float32),
        ],
        compiler_params=pltpu.CompilerParams(
            dimension_semantics=("arbitrary",), vmem_limit_bytes=VMEM_LIMIT
        ),
        cost_estimate=attention_cost(rows, length, heads, 2),
        name="attention_forward",
    )(info, queries, pair_pre, cos_pair, sin_pair, cosine, sine)


def attention_backward(info, low, grad, sums, pair_pre, tables, part, length, before):
    cos_pair, sin_pair, cosine, sine = tables
    rows = cosine.shape[0] // BLOCK_PARTS
    heads = low.shape[1] // HEAD_WIDTH
    spec = attention_specs(part, rows, length)
    before = [] if before is None else [before]
    half = pltpu.VMEM((length, PAIR), jnp.bfloat16)
    full = pltpu.VMEM((length, PAIR), jnp.float32)
    return pl.pallas_call(
        attention_backward_kernel,
        grid_spec=pltpu.PrefetchScalarGridSpec(
            num_scalar_prefetch=1,
            grid=(4,),
            in_specs=[
                spec["wide"], spec["wide"], spec["sums"], spec["pair"],
                spec["table_pair"], spec["table_pair"], spec["table"], spec["table"],
            ]
            + [pl.BlockSpec(memory_space=pl.ANY)] * len(before),
            out_specs=[spec["part"], pl.BlockSpec((1, length, PAIR), lambda g, s: (s[1 + g], 0, 0))],
            scratch_shapes=[
                half, half, half, half,
                pltpu.VMEM((HEAD_WIDTH, length), jnp.bfloat16),
                full, full, full, full,
            ],
        ),
        out_shape=[
            jax.ShapeDtypeStruct((2 * rows, low.shape[1]), jnp.bfloat16),
            jax.ShapeDtypeStruct((4, length, PAIR), jnp.float32),
        ],
        input_output_aliases={9: 0} if before else {},
        compiler_params=pltpu.CompilerParams(
            dimension_semantics=("arbitrary",), vmem_limit_bytes=VMEM_LIMIT
        ),
        cost_estimate=attention_cost(rows, length, heads, 5),
        name="attention_backward",
    )(info, low, grad, sums, pair_pre, cos_pair, sin_pair, cosine, sine, *before)


def rope_tables(length):
    positions = np.arange(length, dtype=np.float32)
    inverse = 10000.0 ** (-np.arange(0, HEAD_WIDTH, 2, dtype=np.float32) / HEAD_WIDTH)
    angles = positions[:, None] * inverse.astype(np.float32)[None, :]
    cosine, sine = np.cos(angles).astype(np.float32), np.sin(angles).astype(np.float32)
    head_cos = np.concatenate([cosine, cosine], axis=1)
    head_sin = np.concatenate([-sine, sine], axis=1)
    still = np.ones_like(head_cos)
    return tuple(
        jnp.asarray(np.concatenate(sides, axis=1))
        for sides in (
            (head_cos, still), (head_sin, 0 * still), (head_cos, head_cos), (head_sin, head_sin)
        )
    )


def head_marks(width, transposed):
    shape = (PAIR, width) if transposed else (width, PAIR)
    head_at, column_at = (0, 1) if transposed else (1, 0)
    head = lax.broadcasted_iota(jnp.int32, shape, head_at)
    column = lax.broadcasted_iota(jnp.int32, shape, column_at)
    return (column // HHD == head).astype(jnp.bfloat16)


def head_sums(value, marks):
    high = to_low(value)
    rest = to_low(value - high.astype(jnp.float32))
    return matmul(high, marks) + matmul(rest, marks)


def normalize(value):
    centered = value - jnp.mean(value, axis=-1, keepdims=True)
    inverse = lax.rsqrt(jnp.mean(centered * centered, axis=-1, keepdims=True) + EPS)
    return (centered * inverse, inverse)


def norm_back(grad, gain, hat, inverse):
    scaled = grad * gain
    mean = jnp.mean(scaled, axis=-1, keepdims=True)
    along = jnp.mean(scaled * hat, axis=-1, keepdims=True)
    return inverse * (scaled - mean - hat * along)


def slot_attention_kernel(pieces_ref, counts_ref, weight_ref, norm_ref, *refs):
    mixed_ref, probs_ref, attended_ref, lead_ref = refs[-4:]
    entries, slots, width = pieces_ref.shape
    rows = entries * slots
    tall = (entries, slots, width)
    pieces = pieces_ref[...].astype(jnp.float32)
    hat, _ = normalize(pieces.reshape(rows, width))
    low = to_low(hat * norm_ref[0:1, :] + norm_ref[1:2, :])
    mixed = []
    for part in range(3):
        span = slice(part * width, (part + 1) * width)
        value = to_low(matmul(low, weight_ref[:, span]))
        mixed_ref[:, span] = value
        mixed.append(value.astype(jnp.float32).reshape(tall))
    query, keys, values = mixed
    marks = head_marks(width, False)
    product = (keys * query[:, 0:1, :]).reshape(rows, width)
    scores = head_sums(product, marks).reshape(entries, slots, PAIR) * HHD ** (-0.5)
    live = lax.broadcasted_iota(jnp.int32, scores.shape, 1) < counts_ref[...]
    scores = jnp.where(live, scores, NEGATIVE)
    weight = jnp.exp(scores - jnp.max(scores, axis=1, keepdims=True))
    probs = weight / jnp.sum(weight, axis=1, keepdims=True)
    probs_ref[...] = probs
    spread = matmul(to_low(probs.reshape(rows, PAIR)), head_marks(width, True)).reshape(tall)
    attended_ref[...] = to_low(jnp.sum(spread * values, axis=1))
    lead_ref[...] = pieces[:, 0, :]


def slot_attention(at, before, pieces, counts, in_weight, norm_rows):
    entries, slots, width = pieces.shape
    part = min(ENTRY_BLOCK, entries // 2)
    steps = entries // 2 // part
    counts = jnp.broadcast_to(counts[:, None, None], (entries, 1, PAIR))
    whole = lambda shape: pl.BlockSpec(shape, lambda i: (0,) * len(shape))
    tall = pl.BlockSpec((part, slots, width), lambda i: (i + at * steps, 0, 0))
    flat = pl.BlockSpec((part, width), lambda i: (i + at * steps, 0))
    before = [] if before is None else list(before)
    return list(
        pl.pallas_call(
            slot_attention_kernel,
            grid=(steps,),
            in_specs=[
                tall,
                pl.BlockSpec((part, 1, PAIR), lambda i: (i + at * steps, 0, 0)),
                whole(in_weight.shape),
                whole(norm_rows.shape),
            ]
            + [pl.BlockSpec(memory_space=pl.ANY)] * len(before),
            out_specs=[
                pl.BlockSpec((part * slots, 3 * width), lambda i: (i + at * steps, 0)),
                pl.BlockSpec((part, slots, PAIR), lambda i: (i + at * steps, 0, 0)),
                flat,
                flat,
            ],
            out_shape=[
                jax.ShapeDtypeStruct((entries * slots, 3 * width), jnp.bfloat16),
                jax.ShapeDtypeStruct((entries, slots, PAIR), jnp.float32),
                jax.ShapeDtypeStruct((entries, width), jnp.bfloat16),
                jax.ShapeDtypeStruct((entries, width), jnp.float32),
            ],
            input_output_aliases={4 + i: i for i in range(len(before))},
            compiler_params=pltpu.CompilerParams(
                dimension_semantics=("arbitrary",), vmem_limit_bytes=VMEM_LIMIT
            ),
            cost_estimate=pl.CostEstimate(
                flops=entries * slots * width, bytes_accessed=entries * slots, transcendentals=0
            ),
            name="slot_attention",
        )(pieces, counts, in_weight, norm_rows, *before)
    )


def gelu_of(value):
    cdf = 0.5 * (1.0 + lax.erf(value * np.float32(0.5 ** 0.5)))
    return (value * cdf, cdf)


def gelu_slope(value, cdf):
    return cdf + value * (jnp.exp(-0.5 * value * value) * np.float32((2 * np.pi) ** -0.5))


def units_forward_kernel(
    attended_ref, lead_ref, wide_weight_ref, reduce_ref, norm_ref, pooled_ref, hidden_ref
):
    width = lead_ref.shape[1]
    hidden = lead_ref[...] + matmul(attended_ref[...], wide_weight_ref[:, :width])
    hidden_ref[...] = hidden
    hat, _ = normalize(hidden)
    second = to_low(hat * norm_ref[2:3, :] + norm_ref[3:4, :])
    total = hidden
    units = reduce_ref.shape[0]
    step = min(UNIT, units)
    for at in range(0, units, step):
        active, _ = gelu_of(matmul(second, wide_weight_ref[:, width + at : width + at + step]))
        total = total + matmul(to_low(active), reduce_ref[at : at + step, :])
    pooled_ref[...] = to_low(total)


def units_forward(attended, lead, wide_weight, reduce_weight, norm_rows):
    entries, width = attended.shape
    part = min(UNIT_ROWS, entries)
    whole = lambda shape: pl.BlockSpec(shape, lambda i: (0,) * len(shape))
    flat = pl.BlockSpec((part, width), lambda i: (i, 0))
    return pl.pallas_call(
        units_forward_kernel,
        grid=(entries // part,),
        in_specs=[flat, flat]
        + [whole(x.shape) for x in (wide_weight, reduce_weight, norm_rows)],
        out_specs=[flat, flat],
        out_shape=[
            jax.ShapeDtypeStruct((entries, width), jnp.bfloat16),
            jax.ShapeDtypeStruct((entries, width), jnp.float32),
        ],
        compiler_params=pltpu.CompilerParams(
            dimension_semantics=("arbitrary",), vmem_limit_bytes=VMEM_LIMIT
        ),
        cost_estimate=pl.CostEstimate(
            flops=entries * width, bytes_accessed=entries * width, transcendentals=0
        ),
        name="units_forward",
    )(attended, lead, wide_weight, reduce_weight, norm_rows)


def units_backward_kernel(
    grad_ref, hidden_ref, attended_ref, wide_weight_ref, reduce_ref, norm_ref,
    hidden_grad_ref, attended_grad_ref, wide_ref, reduce_grad_ref, norm_grad_ref,
    wide_total, reduce_total,
):
    step_at = pl.program_id(0)
    width = hidden_ref.shape[1]
    units = reduce_ref.shape[0]

    @pl.when(step_at == 0)
    def start():
        wide_total[...] = jnp.zeros_like(wide_total)
        reduce_total[...] = jnp.zeros_like(reduce_total)
        norm_grad_ref[...] = jnp.zeros_like(norm_grad_ref)

    grad = grad_ref[...]
    grad_low = to_low(grad)
    hat, inverse = normalize(hidden_ref[...])
    second = to_low(hat * norm_ref[2:3, :] + norm_ref[3:4, :])
    grad_normed = jnp.zeros_like(grad)
    step = min(UNIT, units)
    for at in range(0, units, step):
        span = slice(at, at + step)
        wide_span = slice(width + at, width + at + step)
        expanded = matmul(second, wide_weight_ref[:, wide_span])
        active, cdf = gelu_of(expanded)
        reduce_total[span, :] += matmul_first(to_low(active), grad_low)
        grad_active = matmul_last(grad_low, reduce_ref[span, :])
        grad_expanded = to_low(grad_active * gelu_slope(expanded, cdf))
        wide_total[:, wide_span] += matmul_first(second, grad_expanded)
        grad_normed = grad_normed + matmul_last(grad_expanded, wide_weight_ref[:, wide_span])
    norm_grad_ref[2:3, :] += jnp.sum(grad_normed * hat, axis=0, keepdims=True)
    norm_grad_ref[3:4, :] += jnp.sum(grad_normed, axis=0, keepdims=True)
    hidden_grad = grad + norm_back(grad_normed, norm_ref[2:3, :], hat, inverse)
    hidden_grad_ref[...] = hidden_grad
    hidden_low = to_low(hidden_grad)
    wide_total[:, :width] += matmul_first(attended_ref[...], hidden_low)
    attended_grad_ref[...] = to_low(matmul_last(hidden_low, wide_weight_ref[:, :width]))

    @pl.when(step_at == pl.num_programs(0) - 1)
    def finish():
        wide_ref[...] = to_low(wide_total[...])
        reduce_grad_ref[...] = to_low(reduce_total[...])


def units_backward(grad, hidden, attended, wide_weight, reduce_weight, norm_rows):
    entries, width = attended.shape
    part = min(UNIT_ROWS, entries)
    units = reduce_weight.shape[0]
    whole = lambda shape: pl.BlockSpec(shape, lambda i: (0,) * len(shape))
    flat = pl.BlockSpec((part, width), lambda i: (i, 0))
    wide = (width, width + units)
    return pl.pallas_call(
        units_backward_kernel,
        grid=(entries // part,),
        in_specs=[flat, flat, flat]
        + [whole(x.shape) for x in (wide_weight, reduce_weight, norm_rows)],
        out_specs=[flat, flat, whole(wide), whole((units, width)), whole((8, width))],
        out_shape=[
            jax.ShapeDtypeStruct((entries, width), jnp.float32),
            jax.ShapeDtypeStruct((entries, width), jnp.bfloat16),
            jax.ShapeDtypeStruct(wide, jnp.bfloat16),
            jax.ShapeDtypeStruct((units, width), jnp.bfloat16),
            jax.ShapeDtypeStruct((8, width), jnp.float32),
        ],
        scratch_shapes=[pltpu.VMEM(wide, jnp.float32), pltpu.VMEM((units, width), jnp.float32)],
        compiler_params=pltpu.CompilerParams(
            dimension_semantics=("arbitrary",), vmem_limit_bytes=VMEM_LIMIT
        ),
        cost_estimate=pl.CostEstimate(
            flops=6 * entries * width * (2 * width + 5 * units), bytes_accessed=16 << 20, transcendentals=0
        ),
        name="units_backward",
    )(grad, hidden, attended, wide_weight, reduce_weight, norm_rows)


def slot_backward_kernel(
    first, last, pieces_ref, mixed_ref, probs_ref, attended_grad_ref, hidden_grad_ref, weight_ref, norm_ref,
    later_ref, *refs,
):
    if first:
        pieces_grad_ref, input_grad_ref, norm_grad_ref, total, norm_total = refs
    else:
        _, total_ref, pieces_grad_ref, input_grad_ref, norm_grad_ref, total, norm_total = refs
    step_at = pl.program_id(0)
    entries, slots, width = pieces_ref.shape
    rows = entries * slots
    tall = (entries, slots, width)

    @pl.when(step_at == 0)
    def start():
        norm_total[...] = jnp.zeros_like(norm_total)
        norm_total[0:8, :] = later_ref[...]
        total[...] = jnp.zeros_like(total) if first else total_ref[...]

    hat, inverse = normalize(pieces_ref[...].astype(jnp.float32).reshape(rows, width))
    low = to_low(hat * norm_ref[0:1, :] + norm_ref[1:2, :])
    scale = HHD ** (-0.5)
    query, keys, values = [
        mixed_ref[:, part * width : (part + 1) * width].astype(jnp.float32).reshape(tall) for part in range(3)
    ]
    probs = probs_ref[...]
    grad_attended = jnp.broadcast_to(attended_grad_ref[...].astype(jnp.float32)[:, None, :], tall)
    grad_probs = head_sums((grad_attended * values).reshape(rows, width), head_marks(width, False))
    moved = probs * grad_probs.reshape(probs.shape)
    grad_scores = to_low(moved - probs * jnp.sum(moved, axis=1, keepdims=True))
    marks = head_marks(width, True)
    spread = matmul(grad_scores.reshape(rows, PAIR), marks).reshape(tall) * scale
    first_slot = lax.broadcasted_iota(jnp.int32, tall, 1) == 0
    grad_query = jnp.where(first_slot, jnp.sum(spread * keys, axis=1, keepdims=True), 0.0)
    grad_keys = spread * query[:, 0:1, :]
    grad_values = matmul(to_low(probs.reshape(rows, PAIR)), marks).reshape(tall) * grad_attended
    grad_normed = jnp.zeros((rows, width), jnp.float32)
    for part, grad in enumerate((grad_query, grad_keys, grad_values)):
        span = slice(part * width, (part + 1) * width)
        grad_low = to_low(grad.reshape(rows, width))
        total[:, span] += matmul_first(low, grad_low)
        grad_normed = grad_normed + matmul_last(grad_low, weight_ref[:, span])
    norm_total[0:1, :] += jnp.sum(grad_normed * hat, axis=0, keepdims=True)
    norm_total[1:2, :] += jnp.sum(grad_normed, axis=0, keepdims=True)
    grad_pieces = norm_back(grad_normed, norm_ref[0:1, :], hat, inverse).reshape(tall)
    hidden_grad = jnp.broadcast_to(hidden_grad_ref[...][:, None, :], tall)
    pieces_grad_ref[...] = to_low(grad_pieces + jnp.where(first_slot, hidden_grad, 0.0))

    @pl.when(step_at == pl.num_programs(0) - 1)
    def finish():
        norm_grad_ref[...] = norm_total[0:8, :]
        if last:
            input_grad_ref[:, : 3 * width] = to_low(total[...])
            input_grad_ref[:, 3 * width :] = to_low(norm_total[...].T)
        else:
            input_grad_ref[...] = total[...]


def slot_backward(at, parts, held, saved, grads, in_weight, norm_rows):
    pieces, mixed, probs = saved
    pieces_grad, total, norm_grad = held
    entries, slots, width = pieces.shape
    first, last = at == 0, at == parts - 1
    part = min(ENTRY_BLOCK, entries // parts)
    steps = entries // parts // part
    whole = lambda shape: pl.BlockSpec(shape, lambda i: (0,) * len(shape))
    tall = pl.BlockSpec((part, slots, width), lambda i: (i + at * steps, 0, 0))
    flat = pl.BlockSpec((part, width), lambda i: (i + at * steps, 0))
    total_shape = (
        jax.ShapeDtypeStruct((width, 3 * width + PAIR), jnp.bfloat16)
        if last
        else jax.ShapeDtypeStruct((width, 3 * width), jnp.float32)
    )
    in_specs = [
        tall,
        pl.BlockSpec((part * slots, 3 * width), lambda i: (i + at * steps, 0)),
        pl.BlockSpec((part, slots, PAIR), lambda i: (i + at * steps, 0, 0)),
        flat,
        flat,
        whole(in_weight.shape),
        whole(norm_rows.shape),
        whole(norm_grad.shape),
    ]
    operands = [pieces, mixed, probs, *grads, in_weight, norm_rows, norm_grad]
    if not first:
        in_specs += [pl.BlockSpec(memory_space=pl.ANY), whole(total.shape)]
        operands += [pieces_grad, total]
    return pl.pallas_call(
        functools.partial(slot_backward_kernel, first, last),
        grid=(steps,),
        in_specs=in_specs,
        out_specs=[tall, whole(total_shape.shape), whole(norm_grad.shape)],
        out_shape=[
            jax.ShapeDtypeStruct(pieces.shape, jnp.bfloat16),
            total_shape,
            jax.ShapeDtypeStruct(norm_grad.shape, jnp.float32),
        ],
        input_output_aliases={} if first else {len(operands) - 2: 0},
        scratch_shapes=[
            pltpu.VMEM((width, 3 * width), jnp.float32),
            pltpu.VMEM((PAIR, width), jnp.float32),
        ],
        compiler_params=pltpu.CompilerParams(
            dimension_semantics=("arbitrary",), vmem_limit_bytes=VMEM_LIMIT
        ),
        cost_estimate=pl.CostEstimate(
            flops=entries * slots * width // parts,
            bytes_accessed=entries * slots // parts,
            transcendentals=0,
        ),
        name="slot_backward",
    )(*operands)


def feed_forward_kernel(
    rows_ref, other_ref, rise_ref, rise_other_ref, hidden_ref, gate_ref, up_ref, down_ref,
    gate_rows, up_rows, down_columns, grad_ref, dense_ref, rows, rise, active, grad_gate, grad_up,
):
    at = pl.program_id(0)
    half = rows_ref.shape[0]
    step = gate_ref.shape[1]
    tiles = active.shape[1] // step

    @pl.when(at == 0)
    def start():
        rows[:half, :] = rows_ref[...]
        rows[half:, :] = other_ref[...]
        rise[:half, :] = rise_ref[...]
        rise[half:, :] = rise_other_ref[...]

    @pl.when(at < tiles)
    def units():
        gate = matmul(rows[...], gate_ref[...])
        up = matmul(rows[...], up_ref[...])
        rising = matmul_last(rise[...], down_ref[...])
        sign = 1.0 / (1.0 + jnp.exp(-gate))
        silu = gate * sign
        span = pl.ds(pl.multiple_of(at * step, step), step)
        active[:, span] = to_low(silu * up)
        grad_up[:, span] = to_low(rising * silu)
        grad_gate[:, span] = to_low(rising * up * (sign * (1.0 + gate * (1.0 - sign))))

    @pl.when(at >= tiles)
    def columns():
        dense = matmul(active[...], down_columns[...])
        grad = matmul_last(grad_gate[...], gate_rows[...]) + matmul_last(grad_up[...], up_rows[...])
        grad_ref[...] = to_low(grad)
        dense_ref[:half, :] = to_low(dense[:half] + hidden_ref[...])
        dense_ref[half:, :] = to_low(dense[half:])


def feed_forward(rows, other, upstream, hidden, info, gate_weight, up_weight, down_weight):
    half, width = rows.shape
    units = gate_weight.shape[1]
    step = UNIT_STEP
    tiles = units // step
    column = COLUMN_STEP
    fixed_rows = pl.BlockSpec((half, width), lambda i, s: (0, 0), pipeline_mode=pl.Buffered(1))
    early = lambda i: jnp.minimum(i, tiles - 1)
    late = lambda i: jnp.maximum(i - tiles, 0)
    tall = (2 * half, width)
    out = pl.BlockSpec((2 * half, column), lambda i, s: (0, late(i)))
    return pl.pallas_call(
        lambda info, *refs: feed_forward_kernel(*refs),
        grid_spec=pltpu.PrefetchScalarGridSpec(
            num_scalar_prefetch=1,
            grid=(tiles + width // column,),
            in_specs=[
                fixed_rows,
                fixed_rows,
                pl.BlockSpec((half, width), lambda i, s: (s[0], 0), pipeline_mode=pl.Buffered(1)),
                pl.BlockSpec((half, width), lambda i, s: (s[1], 0), pipeline_mode=pl.Buffered(1)),
                pl.BlockSpec((half, column), lambda i, s: (0, late(i))),
                pl.BlockSpec((width, step), lambda i, s: (0, early(i))),
                pl.BlockSpec((width, step), lambda i, s: (0, early(i))),
                pl.BlockSpec((step, width), lambda i, s: (early(i), 0)),
                pl.BlockSpec((column, units), lambda i, s: (late(i), 0)),
                pl.BlockSpec((column, units), lambda i, s: (late(i), 0)),
                pl.BlockSpec((units, column), lambda i, s: (0, late(i))),
            ],
            out_specs=[out, out],
            scratch_shapes=[
                pltpu.VMEM(tall, jnp.bfloat16),
                pltpu.VMEM(tall, jnp.bfloat16),
                *[pltpu.VMEM((2 * half, units), jnp.bfloat16)] * 3,
            ],
        ),
        out_shape=[jax.ShapeDtypeStruct(tall, jnp.bfloat16)] * 2,
        compiler_params=pltpu.CompilerParams(
            dimension_semantics=("arbitrary",), vmem_limit_bytes=VMEM_LIMIT
        ),
        cost_estimate=pl.CostEstimate(
            flops=34 * half * width * units, bytes_accessed=12 * width * units, transcendentals=0
        ),
        name="feed_forward",
    )(
        info, rows, other, upstream, upstream, hidden, gate_weight, up_weight, down_weight,
        gate_weight, up_weight, down_weight,
    )


def fixed(shape):
    return pl.BlockSpec(shape, lambda *_: (0,) * len(shape), pipeline_mode=pl.Buffered(1))


def root_mean(value):
    return lax.rsqrt(jnp.mean(value * value, axis=-1, keepdims=True) + EPS)


def root_mean_back(grad, gain, value):
    scaled = grad * gain
    inverse = root_mean(value)
    along = jnp.mean(value * scaled, axis=-1, keepdims=True)
    return inverse * scaled - value * (inverse * inverse * inverse * along)


def project_kernel(with_queries, info, chosen_ref, embed_ref, gain_ref, pair_weight_ref, *refs):
    embedded = to_low(matmul(chosen_ref[...], embed_ref[...]))
    value = embedded.astype(jnp.float32)
    low = to_low(value * root_mean(value) * gain_ref[...])
    if not with_queries:
        refs[-1][...] = matmul(low, pair_weight_ref[...])
        return
    near_ref, mid_a, mid_b, far_a, far_b, pair_ref, embedded_ref, query_ref = refs
    pair_ref[...] = matmul(low, pair_weight_ref[...])
    embedded_ref[...] = embedded
    near = near_ref.shape[1]
    step = mid_a.shape[1]
    half = mid_a.shape[0]
    query_ref[:, :near] = matmul(low, near_ref[...])
    for start, upper, lower in ((near, mid_a, mid_b), (near + step, far_a, far_b)):
        query_ref[:, start : start + step] = matmul(low[:, :half], upper[...]) + matmul(
            low[:, half:], lower[...]
        )


def project(info, chosen, embed, gain, pair_weight, query_weights, pair_before):
    rows, width = chosen.shape
    block = rows // 2
    wide = embed.shape[1]
    row = pl.BlockSpec((block, wide), lambda i, s: (i, 0))
    pairs = pair_weight.shape[1]
    before = [] if pair_before is None else [pair_before]
    more = bool(query_weights)
    return pl.pallas_call(
        functools.partial(project_kernel, more),
        grid_spec=pltpu.PrefetchScalarGridSpec(
            num_scalar_prefetch=1,
            grid=(2,),
            in_specs=[
                pl.BlockSpec((block, width), lambda i, s: (i, 0)),
                fixed(embed.shape),
                fixed((1, wide)),
                fixed(pair_weight.shape),
                *[fixed(weight.shape) for weight in query_weights],
                *[pl.BlockSpec(memory_space=pl.ANY)] * len(before),
            ],
            out_specs=[pl.BlockSpec((block, pairs), lambda i, s: (s[i], 0))] + [row, row] * more,
        ),
        out_shape=[jax.ShapeDtypeStruct((2 * rows, pairs), jnp.float32)]
        + [
            jax.ShapeDtypeStruct((rows, wide), jnp.bfloat16),
            jax.ShapeDtypeStruct((rows, wide), jnp.float32),
        ]
        * more,
        input_output_aliases={5: 0} if before else {},
        compiler_params=pltpu.CompilerParams(
            dimension_semantics=("arbitrary",), vmem_limit_bytes=VMEM_LIMIT
        ),
        cost_estimate=pl.CostEstimate(flops=1 << 30, bytes_accessed=1 << 20, transcendentals=0),
        name="project",
    )(info, chosen, embed, gain.reshape(1, -1), pair_weight, *query_weights, *before)


def output_kernel(rows_ref, embedded_ref, gain_ref, near_ref, mid_a, mid_b, far_a, far_b, hidden_ref, low_ref):
    total = embedded_ref[...].astype(jnp.float32)
    at = 0
    for ref in (near_ref, mid_a, mid_b, far_a, far_b):
        total = total + matmul(rows_ref[:, at : at + ref.shape[0]], ref[...])
        at += ref.shape[0]
    hidden_ref[...] = total
    low_ref[...] = to_low(total * root_mean(total) * gain_ref[...])


def output_project(part, rows, embedded, gain, weights):
    block, wide = rows.shape
    spec = pl.BlockSpec((block, wide), lambda i: (0, 0))
    return pl.pallas_call(
        output_kernel,
        grid=(1,),
        in_specs=[
            spec,
            pl.BlockSpec((block, wide), lambda i: (part, 0)),
            fixed((1, wide)),
            *[fixed(weight.shape) for weight in weights],
        ],
        out_specs=[spec, spec],
        out_shape=[
            jax.ShapeDtypeStruct((block, wide), jnp.float32),
            jax.ShapeDtypeStruct((block, wide), jnp.bfloat16),
        ],
        compiler_params=pltpu.CompilerParams(
            dimension_semantics=("arbitrary",), vmem_limit_bytes=VMEM_LIMIT
        ),
        cost_estimate=pl.CostEstimate(flops=4 << 30, bytes_accessed=12 << 20, transcendentals=0),
        name="output_project",
    )(rows, embedded, gain.reshape(1, -1), *weights)


def hidden_backward_kernel(
    info, here_ref, came_ref, hidden_ref, rising_ref, gain_ref, near_ref, mid_a, mid_b, far_a, far_b,
    grad_ref, rows_ref,
):
    grad = here_ref[...].astype(jnp.float32) + came_ref[...].astype(jnp.float32)
    total = rising_ref[...].astype(jnp.float32) + root_mean_back(grad, gain_ref[...], hidden_ref[...])
    grad_ref[...] = total
    low = to_low(total)
    at = 0
    for ref in (near_ref, mid_a, mid_b, far_a, far_b):
        rows_ref[:, at : at + ref.shape[0]] = to_low(matmul_last(low, ref[...]))
        at += ref.shape[0]


def hidden_backward(info, here, came, hidden, upstream, gain, weights):
    block, wide = hidden.shape
    spec = pl.BlockSpec((block, wide), lambda i, s: (0, 0))
    return pl.pallas_call(
        hidden_backward_kernel,
        grid_spec=pltpu.PrefetchScalarGridSpec(
            num_scalar_prefetch=1,
            grid=(1,),
            in_specs=[
                spec,
                spec,
                spec,
                pl.BlockSpec((block, wide), lambda i, s: (s[0], 0)),
                fixed((1, wide)),
                *[fixed(weight.shape) for weight in weights],
            ],
            out_specs=[spec, spec],
        ),
        out_shape=[
            jax.ShapeDtypeStruct((block, wide), jnp.float32),
            jax.ShapeDtypeStruct((block, wide), jnp.bfloat16),
        ],
        compiler_params=pltpu.CompilerParams(
            dimension_semantics=("arbitrary",), vmem_limit_bytes=VMEM_LIMIT
        ),
        cost_estimate=pl.CostEstimate(flops=4 << 30, bytes_accessed=14 << 20, transcendentals=0),
        name="hidden_backward",
    )(info, here, came, hidden, upstream, gain.reshape(1, -1), *weights)


def embed_backward_kernel(
    info, query_ref, own_ref, came_ref, short_ref, cos_ref, sin_ref, first_ref, second_ref, embedded_ref, gain_ref,
    embed_ref, near_ref, mid_a, mid_b, far_a, far_b, pair_weight_ref, grad_ref, token_ref,
):
    total = None
    for head in range(own_ref.shape[0]):
        short = jnp.where(pl.program_id(0) == 0, short_ref[head].astype(jnp.float32), 0.0)
        pair = own_ref[head] + came_ref[head].astype(jnp.float32) + short
        low = to_low(pair * cos_ref[...] - half_swap(pair) * sin_ref[...])
        term = matmul_last(low, pair_weight_ref[:, head * PAIR : (head + 1) * PAIR])
        total = term if total is None else total + term
    near = near_ref.shape[1]
    step = mid_a.shape[1]
    half = mid_a.shape[0]
    total = total + matmul_last(query_ref[:, :near], near_ref[...])
    mid = query_ref[:, near : near + step]
    far = query_ref[:, near + step : near + 2 * step]
    spread = jnp.concatenate(
        [
            matmul_last(mid, mid_a[...]) + matmul_last(far, far_a[...]),
            matmul_last(mid, mid_b[...]) + matmul_last(far, far_b[...]),
        ],
        axis=1,
    )
    value = embedded_ref[...].astype(jnp.float32)
    hidden = jnp.where(pl.program_id(0) == 0, first_ref[...], second_ref[...])
    grad = to_low(hidden + root_mean_back(total + spread, gain_ref[...], value))
    grad_ref[...] = grad
    token_ref[...] = to_low(matmul_last(grad, embed_ref[...]))


def embed_backward(
    info, query_grad, own, came, short, tables, hidden_grads, embedded, gain, embed, query_weights, pair_weight
):
    rows, wide = embedded.shape
    block = rows // 2
    heads = own.shape[0]
    row = pl.BlockSpec((block, wide), lambda i, s: (i, 0))
    once = pl.BlockSpec((block, wide), lambda i, s: (0, 0))
    pair = pl.BlockSpec((heads, block, PAIR), lambda i, s: (0, i, 0))
    table = pl.BlockSpec((block, PAIR), lambda i, s: (s[i], 0))
    return pl.pallas_call(
        embed_backward_kernel,
        grid_spec=pltpu.PrefetchScalarGridSpec(
            num_scalar_prefetch=1,
            grid=(2,),
            in_specs=[
                row, pair, pair, pl.BlockSpec((heads, block, PAIR), lambda i, s: (0, 0, 0)), table, table, once, once, row, fixed((1, wide)), fixed(embed.shape),
                *[fixed(weight.shape) for weight in query_weights],
                fixed(pair_weight.shape),
            ],
            out_specs=[row, pl.BlockSpec((block, embed.shape[0]), lambda i, s: (i, 0))],
        ),
        out_shape=[
            jax.ShapeDtypeStruct((rows, wide), jnp.bfloat16),
            jax.ShapeDtypeStruct((rows, embed.shape[0]), jnp.bfloat16),
        ],
        compiler_params=pltpu.CompilerParams(
            dimension_semantics=("arbitrary",), vmem_limit_bytes=VMEM_LIMIT
        ),
        cost_estimate=pl.CostEstimate(flops=12 << 30, bytes_accessed=20 << 20, transcendentals=0),
        name="embed_backward",
    )(
        info, query_grad, own, came, short, tables[0], tables[1], *hidden_grads, embedded, gain.reshape(1, -1), embed,
        *query_weights, pair_weight,
    )


def own_route(own, local_vocab):
    places = jnp.arange(own.shape[0], dtype=jnp.int32)
    same = own[:, None] == own[None, :]
    repeated = jnp.any(same & (places[:, None] > places[None, :]), axis=1)
    owner = own // local_vocab
    before = (owner[:, None] == owner[None, :]) & (own[None, :] < own[:, None])
    rank = jnp.sum((before & jnp.logical_not(repeated)[None, :]).astype(jnp.int32), axis=1)
    return (rank, owner)


def asked_of_me(asked, me, local_vocab):
    entries = me * local_vocab + jnp.arange(local_vocab, dtype=jnp.int32)
    present = jnp.any(asked[:, :, None] == entries[None, None, :], axis=1)
    places = jnp.arange(local_vocab, dtype=jnp.int32)
    lower = places[:, None] < places[None, :]
    standing = matmul(present.astype(jnp.bfloat16), lower.astype(jnp.bfloat16)).astype(jnp.int32)
    return (present, standing)


def sender_choice(present, standing, turn, capacity):
    place = jnp.arange(capacity, dtype=jnp.int32)
    slot = jnp.where(place < capacity - 1, turn * (capacity - 1) + place, -1)
    chosen = present[:, None, :] & (standing[:, None, :] == slot[None, :, None])
    return chosen.astype(jnp.bfloat16).reshape(present.shape[0] * capacity, present.shape[1])


def taker_choice(own_rank, own_owner, turn, capacity, devices):
    inside = own_rank - turn * (capacity - 1)
    valid = (inside >= 0) & (inside < capacity - 1)
    place = jnp.where(valid, own_owner * capacity + inside, -1)
    return (place[:, None] == jnp.arange(devices * capacity, dtype=jnp.int32)[None, :]).astype(
        jnp.bfloat16
    )


def exchange(value):
    return lax.all_to_all(value, ("dp", "mp"), 0, 0, tiled=True)


def ordered_blocks(first, own_two, other_two):
    return jnp.where(
        first,
        jnp.concatenate([own_two[0], other_two[0], other_two[1], own_two[1]], axis=0),
        jnp.concatenate([other_two[0], own_two[0], own_two[1], other_two[1]], axis=0),
    )


def body(
    pieces,
    counts,
    token_index,
    hyper_input,
    hyper_output,
    hyper_expand,
    hyper_reduce,
    hyper_norms,
    embed_weight,
    attention_gain,
    dense_gain,
    frozen_query_weight,
    frozen_key_weight,
    frozen_value_weight,
    frozen_output_weight,
    gate_weight,
    up_weight,
    down_weight,
    upstream,
):
    local_vocab = pieces.shape[0]
    mp_count = lax.axis_size("mp")
    devices = lax.axis_size("dp") * mp_count
    mp_index = lax.axis_index("mp")
    me = lax.axis_index("dp") * mp_count + mp_index
    core = (me >> 1) & 1
    lead = mp_index == 0
    bits = log2_of(devices)
    far_bits = list(range(bits - 1, 1, -1))
    length = token_index.shape[0]
    block = length // BLOCK_PARTS
    capacity = max(16, length // devices)

    norm_count = hyper_norms.shape[1]
    in_width = hyper_input.shape[1]
    norm_lanes = jnp.pad(hyper_norms, ((0, 0), (0, PAIR - norm_count)))
    cut = token_index.reshape(BLOCK_PARTS, block)
    own_tokens = jnp.where(
        lead, jnp.concatenate([cut[0], cut[3]]), jnp.concatenate([cut[1], cut[2]])
    )
    digits = jnp.concatenate([own_tokens // PAIR, own_tokens % PAIR]).astype(jnp.bfloat16)
    digits = digits.reshape(hyper_input.shape[0], -1)
    digit_width = digits.shape[1]
    digit_lanes = jnp.pad(digits, ((0, 0), (0, -digit_width % PAIR)))
    spread_order = [[bit] for bit in [0] + far_bits + [1]]
    in_held = gather_start(jnp.concatenate([hyper_input, norm_lanes, digit_lanes], axis=1), devices)
    later_held = [
        gather_start(jnp.concatenate([hyper_output, hyper_expand], axis=1), devices),
        gather_start(hyper_reduce, devices),
    ]
    for at, step in enumerate(spread_order):
        in_held = gather_step(in_held, step, me, devices)
        if at == 1:
            in_held, later_held = lax.optimization_barrier((in_held, later_held))
    in_weight = gather_end(in_held)
    for step in spread_order[:-3]:
        later_held = [gather_step(x, step, me, devices) for x in later_held]
        if step == spread_order[0]:
            begun = later_held
    later_came = [gather_send(x, spread_order[-3], devices) for x in later_held]
    embed_full = lax.all_gather(embed_weight, ("dp", "mp"), axis=0, tiled=True)
    norm_rows = in_weight[:, in_width : in_width + 8].astype(jnp.float32).T
    digit_at = in_width + PAIR
    all_digits = in_weight[:, digit_at : digit_at + digit_width].reshape(devices, 2, 2 * block)
    all_digits = all_digits.astype(jnp.int32)
    asked = all_digits[:, 0] * PAIR + all_digits[:, 1]

    query_cut = frozen_query_weight.shape[1] // 2
    kv_local = frozen_key_weight.shape[1] // HEAD_WIDTH
    key_own = jnp.concatenate(
        [
            weight[:, at * HEAD_WIDTH : (at + 1) * HEAD_WIDTH]
            for at in range(kv_local)
            for weight in (frozen_key_weight, frozen_value_weight)
        ],
        axis=1,
    )
    frozen_query_weight, key_own, *_ = lax.optimization_barrier((frozen_query_weight, key_own, *begun))
    query_near = lax.dynamic_slice_in_dim(frozen_query_weight, core * query_cut, query_cut, 1)
    half_in = query_near.shape[0] // 2
    query_near = [swap(query_near[:half_in], 1, devices), swap(query_near[half_in:], 1, devices)]
    key_other = swap(key_own, 1, devices)
    other_base = (1 - mp_index) * kv_local
    head_order = [mp_index * kv_local, mp_index * kv_local + 1, other_base + core, other_base + 1 - core]

    slots_done = slot_attention(0, None, pieces, counts, in_weight, norm_rows)
    slots_done[2], later_came, asked, key_other = lax.optimization_barrier(
        (slots_done[2], later_came, asked, key_other)
    )
    later_held = [
        gather_join(held, came, spread_order[-3], me, devices)
        for held, came in zip(later_held, later_came)
    ]
    later_came = [gather_send(x, spread_order[-2], devices) for x in later_held]
    slots_done = slot_attention(1, slots_done, pieces, counts, in_weight, norm_rows)
    slots_done[2], later_came, embed_full, query_near[0] = lax.optimization_barrier(
        (slots_done[2], later_came, embed_full, query_near[0])
    )
    later_held = [
        gather_join(held, came, spread_order[-2], me, devices)
        for held, came in zip(later_held, later_came)
    ]
    slot_mixed, slot_probs, hyper_attended, lead_rows = slots_done
    wide_weight, reduce_weight = [
        gather_end(gather_step(held, spread_order[-1], me, devices)) for held in later_held
    ]
    hyper_attended, query_near[1] = lax.optimization_barrier((hyper_attended, query_near[1]))
    query_far = [swap(x, 2, devices) for x in query_near]
    output_near, *_ = lax.optimization_barrier((frozen_output_weight, *query_near))
    output_near = lax.dynamic_slice_in_dim(output_near, core * query_cut, query_cut, 0)
    half_out = output_near.shape[0] // 2
    output_near = [swap(output_near[:half_out], 1, devices), swap(output_near[half_out:], 1, devices)]
    pooled, hyper_hidden = units_forward(
        hyper_attended, lead_rows, wide_weight, reduce_weight, norm_rows
    )
    pooled, output_near[0] = lax.optimization_barrier((pooled, output_near[0]))
    pair_weight = jnp.where(
        lead,
        jnp.concatenate([key_own, key_other], axis=1),
        jnp.concatenate([key_other, key_own], axis=1),
    )
    present, standing = asked_of_me(asked, me, local_vocab)
    own_rank, own_owner = own_route(lax.dynamic_index_in_dim(asked, me, 0, False), local_vocab)
    most = jnp.max(jnp.sum(present.astype(jnp.int32), axis=1))
    needed = ((most + capacity - 2) // (capacity - 1)).astype(jnp.float32)

    def fetch(turn):
        sent = matmul(sender_choice(present, standing, turn, capacity), pooled)
        sent = sent.reshape(devices, capacity, pooled.shape[1])
        free = lax.broadcasted_iota(jnp.int32, sent.shape, 1) == capacity - 1
        sent = to_low(jnp.where(free, needed, sent)).reshape(devices * capacity, pooled.shape[1])
        came = exchange(sent)
        picked = matmul(taker_choice(own_rank, own_owner, turn, capacity, devices), came)
        return (to_low(picked), came)

    chosen_own, came = fetch(0)
    chosen_own, came, pair_weight, output_near[1], query_far = lax.optimization_barrier(
        (chosen_own, came, pair_weight, output_near[1], query_far)
    )
    needs = came.reshape(devices, capacity, pooled.shape[1])[:, capacity - 1, 0]
    rounds = jnp.max(needs.astype(jnp.float32)).astype(jnp.int32)
    chosen_own = lax.fori_loop(1, rounds, lambda turn, chosen: chosen + fetch(turn)[0], chosen_own)
    chosen_other = swap(chosen_own, 1, devices)

    tables = rope_tables(length)
    own_at = (mp_index, 3 - mp_index)
    own_base = tuple(at * block for at in own_at)
    other_start = ((1 - mp_index) * block, (2 + mp_index) * block)
    infos = [jnp.stack([at] + head_order).astype(jnp.int32) for at in own_at]

    other_at = (1 - mp_index, 2 + mp_index)
    query_weights = (frozen_query_weight, *query_near, *query_far)
    own_info = jnp.stack(own_at).astype(jnp.int32)
    other_info = jnp.stack(other_at).astype(jnp.int32)
    pair_pre, embedded, queries = project(
        own_info, chosen_own, embed_full, attention_gain, pair_weight, query_weights, None
    )
    (pair_pre,) = project(
        other_info, chosen_other, embed_full, attention_gain, pair_weight, (), pair_pre
    )
    output_far = [swap(x, 2, devices) for x in output_near]
    output_weights = (frozen_output_weight, *output_near, *output_far)
    spans = (2 * block, length)

    sums = [None, None]
    lows = [None, None]
    hidden_parts = [None, None]
    second_low = [None, None]
    second_other = [None, None]
    for part in (1, 0):
        flat, lows[part], sums[part] = attention_forward(
            infos[part], queries, pair_pre, tables, part, spans[part]
        )
        if part == 0:
            flat, second_other[1] = lax.optimization_barrier((flat, second_other[1]))
        hidden_parts[part], second_low[part] = output_project(
            part, flat, embedded, dense_gain, output_weights
        )
        second_other[part] = swap(second_low[part], 1, devices)
        pair_pre, second_low[part] = lax.optimization_barrier((pair_pre, second_low[part]))

    second_low = list(lax.optimization_barrier(tuple(second_low)))
    dense_rows = [None, None]
    second_came = [None, None]
    for part in (1, 0):
        info = jnp.stack([own_at[part], other_at[part]]).astype(jnp.int32)
        grad_second, dense_rows[part] = feed_forward(
            second_low[part], second_other[part], upstream, hidden_parts[part], info,
            gate_weight, up_weight, down_weight,
        )
        second_came[part] = (grad_second[:block], swap(grad_second[block:], 1, devices))

    query_grad = None
    grad_hidden = [None, None]
    pair_grads = [None, None]
    for part in (1, 0):
        here, came = second_came[part]
        if part == 1:
            here, came, dense_rows[0] = lax.optimization_barrier((here, came, dense_rows[0]))
        else:
            here, came, query_grad = lax.optimization_barrier((here, came, query_grad))
        grad_hidden[part], grad_attended = hidden_backward(
            infos[part], here, came, hidden_parts[part], upstream, dense_gain, output_weights
        )
        query_grad, pair_grads[part] = attention_backward(
            infos[part], lows[part], grad_attended, sums[part], pair_pre, tables, part, spans[part], query_grad
        )

    def pick_block(value, at):
        return lax.dynamic_slice_in_dim(value, at * block, block, 1)

    came_long = swap(
        to_low(jnp.concatenate([pick_block(pair_grads[1], at) for at in other_at], axis=1)), 1, devices
    )
    pair_grads[0], came_long = lax.optimization_barrier((pair_grads[0], came_long))
    came_short = swap(to_low(pick_block(pair_grads[0], other_at[0])), 1, devices)
    pair_own = jnp.concatenate(
        [
            pick_block(pair_grads[1], own_at[0]) + pick_block(pair_grads[0], own_at[0]),
            pick_block(pair_grads[1], own_at[1]),
        ],
        axis=1,
    )

    share = upstream.shape[1] // mp_count

    def columns(value, index):
        return lax.dynamic_slice_in_dim(value, index * share, share, 1)

    dense_came = [swap(columns(dense_rows[part], 1 - mp_index), 1, devices) for part in range(2)]
    pair_grads[0], *dense_came = lax.optimization_barrier((pair_grads[0], *dense_came))

    embedded_grad_low, token_grad = embed_backward(
        own_info, query_grad, pair_own, came_long, came_short, tables, grad_hidden, embedded,
        attention_gain, embed_full, query_weights, pair_weight,
    )
    own_out = []
    other_out = []
    for part in range(2):
        kept = columns(dense_rows[part], mp_index).astype(jnp.float32)
        arrived = dense_came[part].astype(jnp.float32)
        own_out.append(to_low(kept[:block] + arrived[block:]))
        other_out.append(to_low(kept[block:] + arrived[:block]))
    model_out = ordered_blocks(lead, own_out, other_out)
    embed_grad = to_low(matmul_first(chosen_own, embedded_grad_low))

    def give_back(turn, total):
        taker = taker_choice(own_rank, own_owner, turn, capacity, devices)
        leaving = matmul_first(taker, token_grad).astype(jnp.bfloat16)
        came = exchange(leaving)
        return total + matmul_first(sender_choice(present, standing, turn, capacity), came)

    embed_start = scatter_start(embed_grad, devices)
    grad_pooled = give_back(0, jnp.zeros(pooled.shape, jnp.float32))
    grad_pooled = lax.fori_loop(1, rounds, give_back, grad_pooled)

    back_order = [[bit] for bit in [1, 0] + far_bits[::-1]]
    embed_held = scatter_step(embed_start, back_order[0], me, devices)
    embed_held, grad_pooled = lax.optimization_barrier((embed_held, grad_pooled))
    embed_held = scatter_step(embed_held, back_order[1], me, devices)
    hidden_grad, attended_grad, wide_grad, reduce_grad, later_norms = units_backward(
        grad_pooled, hyper_hidden, hyper_attended, wide_weight, reduce_weight, norm_rows
    )
    hidden_grad, embed_held = lax.optimization_barrier((hidden_grad, embed_held))
    held = [embed_held, scatter_start(wide_grad, devices), scatter_start(reduce_grad, devices)]
    turned_order = [back_order[0], back_order[2], back_order[1]] + back_order[3:]
    orders = [back_order[2:], back_order, turned_order]

    def depart(at):
        return [
            scatter_send(x, order[at], me, devices) if at < len(order) else (x, [])
            for x, order in zip(held, orders)
        ]

    def arrive(moving):
        return [scatter_add(*x) for x in moving]

    slots_saved = (pieces, slot_mixed, slot_probs)
    slots_held = (None, None, later_norms)
    for part in range(SLOT_PARTS):
        moving = depart(part)
        slots_held = slot_backward(
            part, SLOT_PARTS, slots_held, slots_saved, (attended_grad, hidden_grad), in_weight, norm_rows
        )
        slots_held, moving = lax.optimization_barrier((tuple(slots_held), moving))
        held = arrive(moving)
    pieces_grad, input_grad, _ = slots_held
    input_held = scatter_start(input_grad, devices)
    for at, step in enumerate(back_order):
        moving = depart(SLOT_PARTS + at)
        input_held = scatter_step(input_held, step, me, devices)
        _, moving = lax.optimization_barrier((input_held, moving))
        held = arrive(moving)
    embed_own, wide_own, reduce_own, input_own = [scatter_end(x) for x in (*held, input_held)]
    out_width = hyper_output.shape[1]
    return (
        model_out,
        pieces_grad,
        input_own[:, :in_width],
        wide_own[:, :out_width],
        wide_own[:, out_width:],
        reduce_own,
        input_own[:, in_width : in_width + norm_count],
        embed_own,
    )


def solution(mesh):
    return jax.shard_map(
        body,
        mesh=mesh,
        in_specs=(
            P(("dp", "mp"), None, None),
            P(("dp", "mp")),
            P("dp"),
            P(("dp", "mp"), None),
            P(("dp", "mp"), None),
            P(("dp", "mp"), None),
            P(("dp", "mp"), None),
            P(("dp", "mp"), None),
            P(("dp", "mp"), None),
            P(),
            P(),
            P(None, "mp"),
            P(None, "mp"),
            P(None, "mp"),
            P("mp", None),
            P(None, "mp"),
            P(None, "mp"),
            P("mp", None),
            P("dp", None),
        ),
        out_specs=(
            P("dp", "mp"),
            P(("dp", "mp"), None, None),
            P(("dp", "mp"), None),
            P(("dp", "mp"), None),
            P(("dp", "mp"), None),
            P(("dp", "mp"), None),
            P(("dp", "mp"), None),
            P(("dp", "mp"), None),
        ),
        check_vma=False,
    )
```

time: 822 us -> 645 us (0.78)
  matrix products: 232 us -> 11.7 us
  Pallas kernels: 186 us -> 343 us
  waiting for transfers between devices: 198 us -> 95 us
  other arithmetic: 74.4 us -> 58.3 us
  between operations: 5.77 us -> 17.1 us
    pallas_call x3 -> x13, Pallas kernels: 57.2 us -> 218 us  [the longest x2 95.8 us: feed_forward(): pl.pallas_call(lambda info, *refs: feed_forward_kernel(*refs), grid_spec=...]
    dot_general x17 -> x0, matrix products: 122 us -> none  [matmul_last(): lax.dot_general(left, right, (((1,), (1,)), ((), ())), preferred_element_...]
    dot_general x22 -> x3, matrix products: 103 us -> 3.9 us  [matmul(): return jnp.dot(left, right, preferred_element_type=jnp.float32)]
    ppermute x53, waiting for transfers between devices: 156 us -> 65.1 us  [swap(): lax.ppermute(value, ('dp', 'mp'), [(d, d ^ mask) for d in range(devices)])]
    all_to_all x3 -> x2, waiting for transfers between devices: 42.8 us -> 29.9 us  [exchange(): return lax.all_to_all(value, ('dp', 'mp'), 0, 0, tiled=True)]
    reduce_sum x4 -> x2, other arithmetic: 13.4 us -> 0.51 us  [the longest x1 0.4 us: own_route(): jnp.sum((before & jnp.logical_not(repeated)[None, :]).astype(jnp.int32),...]
    concatenate x4, local copies, waits for them, and re-layouts: 10.7 us -> 0.93 us  [the longest x2 0.77 us: body(): jnp.concatenate([cut[1], cut[2]])]
    unnamed x221 -> x156, local copies, waits for them, and re-layouts: 15.4 us -> 24.6 us
  transfers between devices with their start and end apart: 56 -> 56, of which waited for: 21 -> 19; matrix products, arithmetic and copies ran while one was open for 36% -> 12% of each run, Pallas kernels for 14% -> 51%
where the time goes in v3:
time: 645 us; the launch traced here: 640 us
  Pallas kernels  343 us (53%)
  waiting for transfers between devices  95 us (15%)
  starting transfers between devices  69.6 us (11%)
  other arithmetic  58.3 us (9%)
  local copies, waits for them, and re-layouts  45.4 us (7%)
  between operations  17.1 us (3%)
  matrix products  11.7 us (2%)
    pallas_call x2, Pallas kernels, feed_forward(): pl.pallas_call(lambda info, *refs: feed_forward_kernel(*refs), grid_spec=...  95.8 us
    ppermute x53, waiting for transfers between devices, swap(): lax.ppermute(value, ('dp', 'mp'), [(d, d ^ mask) for d in range(devices)])  65.1 us
    ppermute x53, starting transfers between devices, swap(): lax.ppermute(value, ('dp', 'mp'), [(d, d ^ mask) for d in range(devices)])  60.2 us
    pallas_call x2, Pallas kernels, attention_backward(): pl.pallas_call(attention_backward_kernel, grid_spec=pltpu.PrefetchScalarG...  59.6 us
    pallas_call x2, Pallas kernels, attention_forward(): pl.pallas_call(attention_forward_kernel, grid_spec=pltpu.PrefetchScalarGr...  43.5 us
    pallas_call x2, Pallas kernels, slot_backward(): pl.pallas_call(functools.partial(slot_backward_kernel, first, last), grid...  36.5 us
    all_to_all x2, waiting for transfers between devices, exchange(): return lax.all_to_all(value, ('dp', 'mp'), 0, 0, tiled=True)  29.9 us
    unnamed x156, local copies, waits for them, and re-layouts  24.6 us
  transfers between devices with their start and end apart: 56, of which 19 were waited for; matrix products, arithmetic and copies ran while one was open for 12% of the time, Pallas kernels for 51%

profile of v3, /device:TPU:0, one launch (start us, length us, event | category | flops | bytes accessed | tf_op | source)
XLA Modules:
  0.0 639.9 jit_solution(10835292590256959416)
XLA Ops:
  10.5 2.9 collective-permute-start
  18.7 2.7 collective-permute-start.1
  21.3 5.6 collective-permute-done.1
  31.7 2.4 collective-permute-start.9
  34.1 2.8 collective-permute-start.6
  42.3 9.5 %collective-permute-done.3 = bf16[2,2,1,1,2,16,1792]{6,5,4,3,2,1,0:T(8,128)(2,1)S(1)} collective-permute-done((bf16[2,2,1,1,2,16,1792]{6,5,4,3,2,1,0:T(8,128)(2,1)S(1)}, bf16[2,2,1,1,2,16,1792]{6,5,4,3,2,1,0:T(8,128)(2,1)S(1)}, u32[]{:S(2)}, u32[]{:S(2)}) %collective-permute-start.3) | collective-permute-done | bytes 458784 | tf_op jit(solution)/shard_map/ppermute | solution.py:49
  61.7 10.1 %slot_attention.2 = (bf16[4096,1536]{1,0:T(8,128)(2,1)}, f32[512,8,128]{2,1,0:T(8,128)S(1)}, bf16[512,512]{1,0:T(8,128)(2,1)S(1)}, f32[512,512]{1,0:T(8,128)S(1)}) custom-call(bf16[512,8,512]{2,1,0:T(8,128)(2,1)} %pieces_ref.7, s32[512,1,128]{2,1,0:T(1,128)S(1)} %broadcast_in_dim.28.counts_ref, bf16[512,1792]{1,0:T(8,128)(2,1)S(1)} %bitcast.120, ...), custom_call_target="tpu_custom_call" | custom-call | flops 2097152 | bytes 4096 | tf_op jit(solution)/shard_map/slot_attention/pallas_call | solution.py:401
  73.9 3.1 collective-permute-done.7
  86.1 10.4 %slot_attention.3 = (bf16[4096,1536]{1,0:T(8,128)(2,1)}, f32[512,8,128]{2,1,0:T(8,128)S(1)}, bf16[512,512]{1,0:T(8,128)(2,1)S(1)}, f32[512,512]{1,0:T(8,128)S(1)}) custom-call(bf16[512,8,512]{2,1,0:T(8,128)(2,1)} %pieces_ref.7, ...), custom_call_target="tpu_custom_call", output_to_operand_aliasing={{0}: (4, {}), {1}: (5, {}), {2}: (6, {}), {3}: (7, {})} | custom-call | flops 2097152 | bytes 4096 | tf_op jit(solution)/shard_map/slot_attention/pallas_call | solution.py:401
  102.1 4.9 collective-permute-done.13
  106.9 4.2 collective-permute-done.15.refs_2_.mid_b
  111.1 2.6 maximum_select_fusion.5
  113.7 2.4 maximum_select_fusion.6
  119.6 5.0 compare_reduce_fusion
  126.3 2.7 maximum_select_fusion.1
  129.3 3.5 maximum_select_fusion
  134.6 6.0 units_forward.1
  145.1 3.9 all-to-all-start.2
  152.1 4.2 maximum_select_fusion.2.pair_weight_ref
  156.3 18.9 %all-to-all-done.2 = bf16[32,32,512]{2,1,0:T(8,128)(2,1)} async-done(((bf16[32,32,512]{2,1,0:T(8,128)(2,1)}), bf16[32,32,512]{2,1,0:T(8,128)(2,1)}, u32[]{:S(2)}, u32[]{:S(2)}) %all-to-all-start.2) | async-done | bytes 1048608 | tf_op jit(solution)/shard_map/all_to_all | solution.py:1019
  177.2 8.2 %collective-permute-done.19.mid_b = bf16[256,2048]{1,0:T(8,128)(2,1)} collective-permute-done((bf16[256,2048]{1,0:T(8,128)(2,1)}, bf16[256,2048]{1,0:T(8,128)(2,1)}, u32[]{:S(2)}, u32[]{:S(2)}) %collective-permute-start.19) | collective-permute-done | bytes 1048608 | tf_op jit(solution)/shard_map/ppermute | solution.py:49
  188.9 14.0 %project.2 = (f32[1024,512]{1,0:T(8,128)}, bf16[512,2048]{1,0:T(8,128)(2,1)}, f32[512,2048]{1,0:T(8,128)}) custom-call(s32[2]{0:T(128)S(1)} %get-tuple-element.480.info, bf16[512,512]{1,0:T(8,128)(2,1)S(1)} %get-tuple-element.260.chosen_ref, bf16[512,2048]{1,0:T(8,128)(2,1)} %all-gather.2.cloned.1.call-done.embed_ref, f32[1,2048]{1,0:T(1,128)S(1)} %bitcast.133, ...), custom_call_target="tpu_custom_call" | custom-call | flops 1073741824 | bytes 1048576 | tf_op jit(solution)/shard_map/project/pallas_call | solution.py:806
  204.5 5.4 project.3.pair_ref
  211.2 26.4 %attention_forward.2 = (bf16[256,2048]{1,0:T(8,128)(2,1)S(1)}, bf16[256,2048]{1,0:T(8,128)(2,1)S(1)}, f32[4,8,256]{2,1,0:T(8,128)S(1)}) custom-call(s32[5]{0:T(128)S(1)} %stack.63.info, f32[512,2048]{1,0:T(8,128)} %get-tuple-element.266.query_ref, f32[1024,512]{1,0:T(8,128)} %copy-done.16, f32[1024,128]{1,0:T(8,128)S(1)} %copy-done.24, ...), custom_call_target="tpu_custom_call" | custom-call | flops 21474836480 | bytes 8388608 | tf_op jit(solution)/shard_map/attention_forward/pallas_call | solution.py:254
  238.7 7.2 %output_project.2 = (f32[256,2048]{1,0:T(8,128)}, bf16[256,2048]{1,0:T(8,128)(2,1)}) custom-call(bf16[256,2048]{1,0:T(8,128)(2,1)S(1)} %get-tuple-element.267.rows_ref, bf16[512,2048]{1,0:T(8,128)(2,1)} %get-tuple-element.268.embedded_ref, f32[1,2048]{1,0:T(1,128)S(1)} %bitcast.129, bf16[1024,2048]{1,0:T(8,128)(2,1)} %near_ref.7, ...), custom_call_target="tpu_custom_call" | custom-call | flops 4294967296 | bytes 12582912 | tf_op jit(solution)/shard_map/output_project/pallas_call | solution.py:849
  251.8 17.1 %attention_forward.3 = (bf16[256,2048]{1,0:T(8,128)(2,1)S(1)}, bf16[256,2048]{1,0:T(8,128)(2,1)S(1)}, f32[4,8,256]{2,1,0:T(8,128)S(1)}) custom-call(s32[5]{0:T(128)S(1)} %stack.64.info, f32[512,2048]{1,0:T(8,128)} %get-tuple-element.266.query_ref, f32[1024,512]{1,0:T(8,128)} %copy-done.16, f32[1024,128]{1,0:T(8,128)S(1)} %copy-done.25, ...), custom_call_target="tpu_custom_call" | custom-call | flops 10737418240 | bytes 8388608 | tf_op jit(solution)/shard_map/attention_forward/pallas_call | solution.py:254
  268.9 2.5 collective-permute-done.25.refs_1_
  271.4 6.8 %output_project.3 = (f32[256,2048]{1,0:T(8,128)}, bf16[256,2048]{1,0:T(8,128)(2,1)S(1)}) custom-call(bf16[256,2048]{1,0:T(8,128)(2,1)S(1)} %get-tuple-element.274.rows_ref, bf16[512,2048]{1,0:T(8,128)(2,1)} %get-tuple-element.268.embedded_ref, f32[1,2048]{1,0:T(1,128)S(1)} %bitcast.130, bf16[1024,2048]{1,0:T(8,128)(2,1)} %near_ref.7, ...), custom_call_target="tpu_custom_call" | custom-call | flops 4294967296 | bytes 12582912 | tf_op jit(solution)/shard_map/output_project/pallas_call | solution.py:849
  279.8 48.2 %feed_forward.2 = (bf16[512,2048]{1,0:T(8,128)(2,1)S(1)}, bf16[512,2048]{1,0:T(8,128)(2,1)}) custom-call(s32[2]{0:T(128)S(1)} %get-tuple-element.479.info, bf16[256,2048]{1,0:T(8,128)(2,1)} %get-tuple-element.278.refs_0_, bf16[256,2048]{1,0:T(8,128)(2,1)} %collective-permute-done.25.refs_1_, bf16[1024,2048]{1,0:T(8,128)(2,1)} %rising_ref.3, ...), custom_call_target="tpu_custom_call" | custom-call | flops 50197430272 | bytes 69206016 | tf_op jit(solution)/shard_map/feed_forward/pallas_call | solution.py:724
  332.3 47.6 %feed_forward.3 = (bf16[512,2048]{1,0:T(8,128)(2,1)S(1)}, bf16[512,2048]{1,0:T(8,128)(2,1)}) custom-call(s32[2]{0:T(128)S(1)} %pad_add_fusion.3.info, bf16[256,2048]{1,0:T(8,128)(2,1)S(1)} %get-tuple-element.282.refs_0_, bf16[256,2048]{1,0:T(8,128)(2,1)S(1)} %collective-permute-done.27.refs_1_, bf16[1024,2048]{1,0:T(8,128)(2,1)} %rising_ref.3, ...), custom_call_target="tpu_custom_call" | custom-call | flops 50197430272 | bytes 69206016 | tf_op jit(solution)/shard_map/feed_forward/pallas_call | solution.py:724
  381.5 7.9 %hidden_backward.2 = (f32[256,2048]{1,0:T(8,128)}, bf16[256,2048]{1,0:T(8,128)(2,1)S(1)}) custom-call(s32[5]{0:T(128)S(1)} %stack.63.info, bf16[256,2048]{1,0:T(8,128)(2,1)S(1)} %get-tuple-element.289.here_ref, bf16[256,2048]{1,0:T(8,128)(2,1)S(1)} %collective-permute-done.26.came_ref, f32[256,2048]{1,0:T(8,128)} %get-tuple-element.280.refs_4_.hidden_ref, ...), custom_call_target="tpu_custom_call" | custom-call | flops 4294967296 | bytes 14680064 | tf_op jit(solution)/shard_map/hidden_backward/pallas_call | solution.py:888
  389.4 37.3 %attention_backward.2 = (bf16[512,2048]{1,0:T(8,128)(2,1)}, f32[4,1024,128]{2,1,0:T(8,128)}) custom-call(s32[5]{0:T(128)S(1)} %stack.63.info, bf16[256,2048]{1,0:T(8,128)(2,1)S(1)} %copy-done.37, bf16[256,2048]{1,0:T(8,128)(2,1)S(1)} %get-tuple-element.291.grad_ref, f32[4,8,256]{2,1,0:T(8,128)S(1)} %get-tuple-element.292.lse_ref, f32[1024,512]{1,0:T(8,128)} %copy-done.16, ...), custom_call_target="tpu_custom_call" | custom-call | flops 53687091200 | bytes 8388608 | tf_op jit(solution)/shard_map/attention_backward/pallas_call | solution.py:290
  432.4 7.6 %hidden_backward.3 = (f32[256,2048]{1,0:T(8,128)}, bf16[256,2048]{1,0:T(8,128)(2,1)S(1)}) custom-call(s32[5]{0:T(128)S(1)} %stack.64.info, bf16[256,2048]{1,0:T(8,128)(2,1)S(1)} %get-tuple-element.295.here_ref, bf16[256,2048]{1,0:T(8,128)(2,1)S(1)} %collective-permute-done.28.came_ref, f32[256,2048]{1,0:T(8,128)} %get-tuple-element.283.refs_4_.hidden_ref, ...), custom_call_target="tpu_custom_call" | custom-call | flops 4294967296 | bytes 14680064 | tf_op jit(solution)/shard_map/hidden_backward/pallas_call | solution.py:888
  440.0 22.3 %attention_backward.3 = (bf16[512,2048]{1,0:T(8,128)(2,1)}, f32[4,512,128]{2,1,0:T(8,128)S(1)}) custom-call(s32[5]{0:T(128)S(1)} %stack.64.info, bf16[256,2048]{1,0:T(8,128)(2,1)S(1)} %get-tuple-element.286.low_ref, bf16[256,2048]{1,0:T(8,128)(2,1)S(1)} %get-tuple-element.297.grad_ref, ...), custom_call_target="tpu_custom_call", output_to_operand_aliasing={{0}: (9, {})} | custom-call | flops 26843545600 | bytes 8388608 | tf_op jit(solution)/shard_map/attention_backward/pallas_call | solution.py:290
  463.3 5.5 collective-permute-done.32.short_ref
  468.8 16.8 %embed_backward.1 = (bf16[512,2048]{1,0:T(8,128)(2,1)}, bf16[512,512]{1,0:T(8,128)(2,1)S(1)}) custom-call(s32[2]{0:T(128)S(1)} %copy-done.21, bf16[512,2048]{1,0:T(8,128)(2,1)} %get-tuple-element.308.query_ref, f32[4,512,128]{2,1,0:T(8,128)S(1)} %pad_maximum_fusion.1.own_ref, bf16[4,512,128]{2,1,0:T(8,128)(2,1)S(1)} %collective-permute-done.29.came_ref, ...), custom_call_target="tpu_custom_call" | custom-call | flops 12884901888 | bytes 20971520 | tf_op jit(solution)/shard_map/embed_backward/pallas_call | solution.py:956
  487.5 5.5 all-to-all-start.3
  493.0 2.9 convolution_convert_fusion
  505.4 2.9 convert_add_fusion.2
  508.3 11.0 %all-to-all-done.3 = bf16[32,32,512]{2,1,0:T(8,128)(2,1)} async-done(((bf16[32,32,512]{2,1,0:T(8,128)(2,1)}), bf16[32,32,512]{2,1,0:T(8,128)(2,1)}, u32[]{:S(2)}, u32[]{:S(2)}) %all-to-all-start.3) | async-done | bytes 1048608 | tf_op jit(solution)/shard_map/all_to_all | solution.py:1019
  519.2 3.1 fusion.33
  527.2 15.2 %units_backward.1 = (f32[512,512]{1,0:T(8,128)S(1)}, bf16[512,512]{1,0:T(8,128)(2,1)S(1)}, bf16[512,2560]{1,0:T(8,128)(2,1)}, bf16[2048,512]{1,0:T(8,128)(2,1)S(1)}, f32[8,512]{1,0:T(8,128)S(1)}) custom-call(f32[512,512]{1,0:T(8,128)} %get-tuple-element.315.grad_ref, f32[512,512]{1,0:T(8,128)S(1)} %copy-done.23, bf16[512,512]{1,0:T(8,128)(2,1)S(1)} %copy-done.14, ...), custom_call_target="tpu_custom_call" | custom-call | flops 17716740096 | bytes 16777216 | tf_op jit(solution)/shard_map/units_backward/pallas_call | solution.py:538
  550.9 17.9 %slot_backward.2 = (bf16[512,8,512]{2,1,0:T(8,128)(2,1)}, f32[512,1536]{1,0:T(8,128)}, f32[8,512]{1,0:T(8,128)S(1)}) custom-call(bf16[512,8,512]{2,1,0:T(8,128)(2,1)} %pieces_ref.7, bf16[4096,1536]{1,0:T(8,128)(2,1)} %get-tuple-element.306.mixed_ref, f32[512,8,128]{2,1,0:T(8,128)S(1)} %copy-done.3, ...), custom_call_target="tpu_custom_call" | custom-call | flops 1048576 | bytes 2048 | tf_op jit(solution)/shard_map/slot_backward/pallas_call | solution.py:649
  572.8 18.7 %slot_backward.3 = (bf16[512,8,512]{2,1,0:T(8,128)(2,1)}, bf16[512,1664]{1,0:T(8,128)(2,1)S(1)}, f32[8,512]{1,0:T(8,128)}) custom-call(bf16[512,8,512]{2,1,0:T(8,128)(2,1)} %pieces_ref.7, bf16[4096,1536]{1,0:T(8,128)(2,1)} %get-tuple-element.306.mixed_ref, f32[512,8,128]{2,1,0:T(8,128)} %copy-done.2, ...), custom_call_target="tpu_custom_call", output_to_operand_aliasing={{0}: (8, {})} | custom-call | flops 1048576 | bytes 2048 | tf_op jit(solution)/shard_map/slot_backward/pallas_call | solution.py:649
  596.3 2.3 collective-permute-done.46
  598.7 4.1 collective-permute-done.48
  607.1 6.8 %collective-permute-done.42 = bf16[2,2,2,1,1,16,1664]{6,5,4,3,2,1,0:T(8,128)(2,1)S(1)} collective-permute-done((bf16[2,2,2,1,1,16,1664]{6,5,4,3,2,1,0:T(8,128)(2,1)S(1)}, bf16[2,2,2,1,1,16,1664]{6,5,4,3,2,1,0:T(8,128)(2,1)S(1)}, u32[]{:S(2)}, u32[]{:S(2)}) %collective-permute-start.42) | collective-permute-done | bytes 426016 | tf_op jit(solution)/shard_map/ppermute | solution.py:49
  624.9 2.7 collective-permute-start.45
  (381 shorter events, 141.6 us)
Async XLA Ops:
  7.2 99.8 %all-gather.2.cloned.1.call-start = ((), (), s32[]{:S(2)}) async-start(), calls=%async_computation.4 | async-start | bytes 2162688 | tf_op jit(solution)/shard_map/all_gather | solution.py:1091
  10.5 8.1 %collective-permute-start = (bf16[1,1,1,1,1,16,1792]{6,5,4,3,2,1,0:T(8,128)(2,1)S(1)}, bf16[1,1,1,1,1,16,1792]{6,5,4,3,2,1,0:T(8,128)(2,1)S(1)}, u32[]{:S(2)}, u32[]{:S(2)}) collective-permute-start(bf16[1,1,1,1,1,16,1792]{6,5,4,3,2,1,0:T(8,128)(2,1)S(1)} %get-tuple-element.473), channel_id=1, source_target_pairs={{0,1},{1,0},{2,3},{3,2},{4,5},{5,4},{6,7},{7,6},{8,9},{9,8},{10,11... | collective-permute-start | bytes 172040 | tf_op jit(solution)/shard_map/ppermute | solution.py:49
  18.7 8.2 %collective-permute-start.1 = (bf16[1,1,1,1,2,16,1792]{6,5,4,0,3,2,1:T(8,128)(2,1)S(1)}, bf16[1,1,1,1,2,16,1792]{6,5,4,0,3,2,1:T(8,128)(2,1)S(1)}, u32[]{:S(2)}, u32[]{:S(2)}) collective-permute-start(bf16[1,1,1,1,2,16,1792]{6,5,4,0,3,2,1:T(8,128)(2,1)S(1)} %fusion.53), channel_id=1, source_target_pairs={{0,16},{1,17},{2,18},{3,19},{4,20},{5,21},{6,22},{7,23},{8,24},{9,... | collective-permute-start | bytes 344072 | tf_op jit(solution)/shard_map/ppermute | solution.py:49
  27.9 12.7 %collective-permute-start.2 = (bf16[2,1,1,1,2,16,1792]{6,5,4,0,3,2,1:T(8,128)(2,1)S(1)}, bf16[2,1,1,1,2,16,1792]{6,5,4,0,3,2,1:T(8,128)(2,1)S(1)}, u32[]{:S(2)}, u32[]{:S(2)}) collective-permute-start(bf16[2,1,1,1,2,16,1792]{6,5,4,0,3,2,1:T(8,128)(2,1)S(1)} %maximum_select_fusion.18), channel_id=1, source_target_pairs={{0,8},{1,9},{2,10},{3,11},{4,12},{5,13},{6,14},{7,15},{8,0},{9,1},... | collective-permute-start | bytes 688136 | tf_op jit(solution)/shard_map/ppermute | solution.py:49
  31.7 21.8 %collective-permute-start.9 = (bf16[1,1,1,1,2,64,512]{6,5,4,0,1,3,2:T(8,128)(2,1)S(1)}, bf16[1,1,1,1,2,64,512]{6,5,4,0,1,3,2:T(8,128)(2,1)S(1)}, u32[]{:S(2)}, u32[]{:S(2)}) collective-permute-start(bf16[1,1,1,1,2,64,512]{6,5,4,0,1,3,2:T(8,128)(2,1)S(1)} %maximum_select_fusion.21), channel_id=1, source_target_pairs={{0,16},{1,17},{2,18},{3,19},{4,20},{5,21},{6,22},{7,23},{8,24},{9,... | collective-permute-start | bytes 393224 | tf_op jit(solution)/shard_map/ppermute | solution.py:49
  34.1 21.0 %collective-permute-start.6 = (bf16[1,1,1,1,2,16,2560]{6,5,4,0,1,3,2:T(8,128)(2,1)S(1)}, bf16[1,1,1,1,2,16,2560]{6,5,4,0,1,3,2:T(8,128)(2,1)S(1)}, u32[]{:S(2)}, u32[]{:S(2)}) collective-permute-start(bf16[1,1,1,1,2,16,2560]{6,5,4,0,1,3,2:T(8,128)(2,1)S(1)} %maximum_select_fusion.19), channel_id=1, source_target_pairs={{0,16},{1,17},{2,18},{3,19},{4,20},{5,21},{6,22},{7,23},{8,24},{9,... | collective-permute-start | bytes 491528 | tf_op jit(solution)/shard_map/ppermute | solution.py:49
  37.0 40.0 %collective-permute-start.11 = (bf16[2048,256]{1,0:T(8,128)(2,1)}, bf16[2048,256]{1,0:T(8,128)(2,1)}, u32[]{:S(2)}, u32[]{:S(2)}) collective-permute-start(bf16[2048,256]{1,0:T(8,128)(2,1)} %pad_maximum_fusion), channel_id=1, source_target_pairs={{0,1},{1,0},{2,3},{3,2},{4,5},{5,4},{6,7},{7,6},{8,9},{9,8},{10,11... | collective-permute-start | bytes 3145736 | tf_op jit(solution)/shard_map/ppermute | solution.py:49
  40.1 62.0 %collective-permute-start.14 = (bf16[1024,512]{1,0:T(8,128)(2,1)}, bf16[1024,512]{1,0:T(8,128)(2,1)}, u32[]{:S(2)}, u32[]{:S(2)}) collective-permute-start(bf16[1024,512]{1,0:T(8,128)(2,1)} %get-tuple-element.444), channel_id=1, source_target_pairs={{0,1},{1,0},{2,3},{3,2},{4,5},{5,4},{6,7},{7,6},{8,9},{9,8},{10,11... | collective-permute-start | bytes 3145736 | tf_op jit(solution)/shard_map/ppermute | solution.py:49
  40.7 11.2 %collective-permute-start.3 = (bf16[2,2,1,1,2,16,1792]{6,5,4,3,2,1,0:T(8,128)(2,1)S(1)}, bf16[2,2,1,1,2,16,1792]{6,5,4,3,2,1,0:T(8,128)(2,1)S(1)}, u32[]{:S(2)}, u32[]{:S(2)}) collective-permute-start(bf16[2,2,1,1,2,16,1792]{6,5,4,3,2,1,0:T(8,128)(2,1)S(1)} %copy.88), channel_id=1, source_target_pairs={{0,4},{1,5},{2,6},{3,7},{4,0},{5,1},{6,2},{7,3},{8,12},{9,13},{10,... | collective-permute-start | bytes 1376264 | tf_op jit(solution)/shard_map/ppermute | solution.py:49
  51.9 59.3 %collective-permute-start.15 = (bf16[1024,512]{1,0:T(8,128)(2,1)}, bf16[1024,512]{1,0:T(8,128)(2,1)}, u32[]{:S(2)}, u32[]{:S(2)}) collective-permute-start(bf16[1024,512]{1,0:T(8,128)(2,1)} %get-tuple-element.443), channel_id=1, source_target_pairs={{0,1},{1,0},{2,3},{3,2},{4,5},{5,4},{6,7},{7,6},{8,9},{9,8},{10,11... | collective-permute-start | bytes 3145736 | tf_op jit(solution)/shard_map/ppermute | solution.py:49
  55.2 18.8 %collective-permute-start.10 = (bf16[2,1,1,1,2,64,512]{6,5,4,0,1,3,2:T(8,128)(2,1)}, bf16[2,1,1,1,2,64,512]{6,5,4,0,1,3,2:T(8,128)(2,1)}, u32[]{:S(2)}, u32[]{:S(2)}) collective-permute-start(bf16[2,1,1,1,2,64,512]{6,5,4,0,1,3,2:T(8,128)(2,1)} %maximum_select_fusion.16), channel_id=1, source_target_pairs={{0,8},{1,9},{2,10},{3,11},{4,12},{5,13},{6,14},{7,15},{8,0},{9,1},... | collective-permute-start | bytes 786440 | tf_op jit(solution)/shard_map/ppermute | solution.py:49
  57.0 20.0 %collective-permute-start.7 = (bf16[2,1,1,1,2,16,2560]{6,5,4,0,1,3,2:T(8,128)(2,1)}, bf16[2,1,1,1,2,16,2560]{6,5,4,0,1,3,2:T(8,128)(2,1)}, u32[]{:S(2)}, u32[]{:S(2)}) collective-permute-start(bf16[2,1,1,1,2,16,2560]{6,5,4,0,1,3,2:T(8,128)(2,1)} %maximum_select_fusion.14), channel_id=1, source_target_pairs={{0,8},{1,9},{2,10},{3,11},{4,12},{5,13},{6,14},{7,15},{8,0},{9,1},... | collective-permute-start | bytes 983048 | tf_op jit(solution)/shard_map/ppermute | solution.py:49
  79.0 27.9 %collective-permute-start.12 = (bf16[2,2,1,1,2,16,2560]{6,5,4,0,1,3,2:T(8,128)(2,1)}, bf16[2,2,1,1,2,16,2560]{6,5,4,0,1,3,2:T(8,128)(2,1)}, u32[]{:S(2)}, u32[]{:S(2)}) collective-permute-start(bf16[2,2,1,1,2,16,2560]{6,5,4,0,1,3,2:T(8,128)(2,1)} %maximum_select_fusion.8), channel_id=1, source_target_pairs={{0,4},{1,5},{2,6},{3,7},{4,0},{5,1},{6,2},{7,3},{8,12},{9,13},{10,... | collective-permute-start | bytes 1966088 | tf_op jit(solution)/shard_map/ppermute | solution.py:49
  82.1 24.8 %collective-permute-start.13 = (bf16[2,2,1,1,2,64,512]{6,5,4,0,1,3,2:T(8,128)(2,1)}, bf16[2,2,1,1,2,64,512]{6,5,4,0,1,3,2:T(8,128)(2,1)}, u32[]{:S(2)}, u32[]{:S(2)}) collective-permute-start(bf16[2,2,1,1,2,64,512]{6,5,4,0,1,3,2:T(8,128)(2,1)} %maximum_select_fusion.10), channel_id=1, source_target_pairs={{0,4},{1,5},{2,6},{3,7},{4,0},{5,1},{6,2},{7,3},{8,12},{9,13},{10,... | collective-permute-start | bytes 1572872 | tf_op jit(solution)/shard_map/ppermute | solution.py:49
  113.7 15.5 %collective-permute-start.16 = (bf16[2,2,2,1,2,16,2560]{6,5,4,0,1,3,2:T(8,128)(2,1)}, bf16[2,2,2,1,2,16,2560]{6,5,4,0,1,3,2:T(8,128)(2,1)}, u32[]{:S(2)}, u32[]{:S(2)}) collective-permute-start(bf16[2,2,2,1,2,16,2560]{6,5,4,0,1,3,2:T(8,128)(2,1)} %maximum_select_fusion.5), channel_id=1, source_target_pairs={{0,2},{1,3},{2,0},{3,1},{4,6},{5,7},{6,4},{7,5},{8,10},{9,11},{10,... | collective-permute-start | bytes 3932168 | tf_op jit(solution)/shard_map/ppermute | solution.py:49
  116.1 10.2 %collective-permute-start.17 = (bf16[2,2,2,1,2,64,512]{6,5,4,0,1,3,2:T(8,128)(2,1)}, bf16[2,2,2,1,2,64,512]{6,5,4,0,1,3,2:T(8,128)(2,1)}, u32[]{:S(2)}, u32[]{:S(2)}) collective-permute-start(bf16[2,2,2,1,2,64,512]{6,5,4,0,1,3,2:T(8,128)(2,1)} %maximum_select_fusion.6), channel_id=1, source_target_pairs={{0,2},{1,3},{2,0},{3,1},{4,6},{5,7},{6,4},{7,5},{8,10},{9,11},{10,... | collective-permute-start | bytes 3145736 | tf_op jit(solution)/shard_map/ppermute | solution.py:49
  118.1 25.3 %collective-permute-start.18 = (bf16[256,2048]{1,0:T(8,128)(2,1)}, bf16[256,2048]{1,0:T(8,128)(2,1)S(1)}, u32[]{:S(2)}, u32[]{:S(2)}) collective-permute-start(bf16[256,2048]{1,0:T(8,128)(2,1)} %get-tuple-element.442), channel_id=1, source_target_pairs={{0,1},{1,0},{2,3},{3,2},{4,5},{5,4},{6,7},{7,6},{8,9},{9,8},{10,11... | collective-permute-start | bytes 3145736 | tf_op jit(solution)/shard_map/ppermute | solution.py:49
  145.1 30.0 %all-to-all-start.2 = ((bf16[32,32,512]{2,1,0:T(8,128)(2,1)}), bf16[32,32,512]{2,1,0:T(8,128)(2,1)}, u32[]{:S(2)}, u32[]{:S(2)}) async-start(bf16[32,32,512]{2,1,0:T(8,128)(2,1)} %select_convert_fusion.1), calls=%async_computation.2 | async-start | bytes 2097152 | tf_op jit(solution)/shard_map/all_to_all | solution.py:1019
  149.3 36.1 %collective-permute-start.20 = (bf16[1024,512]{1,0:T(8,128)(2,1)}, bf16[1024,512]{1,0:T(8,128)(2,1)}, u32[]{:S(2)}, u32[]{:S(2)}) collective-permute-start(bf16[1024,512]{1,0:T(8,128)(2,1)} %collective-permute-done.14.refs_1_.mid_a), channel_id=1, source_target_pairs={{0,2},{1,3},{2,0},{3,1},{4,6},{5,7},{6,4},{7,5},{8,10},{9,11},{10,... | collective-permute-start | bytes 3145736 | tf_op jit(solution)/shard_map/ppermute | solution.py:49
  149.6 35.8 %collective-permute-start.21 = (bf16[1024,512]{1,0:T(8,128)(2,1)}, bf16[1024,512]{1,0:T(8,128)(2,1)}, u32[]{:S(2)}, u32[]{:S(2)}) collective-permute-start(bf16[1024,512]{1,0:T(8,128)(2,1)} %collective-permute-done.15.refs_2_.mid_b), channel_id=1, source_target_pairs={{0,2},{1,3},{2,0},{3,1},{4,6},{5,7},{6,4},{7,5},{8,10},{9,11},{10,... | collective-permute-start | bytes 3145736 | tf_op jit(solution)/shard_map/ppermute | solution.py:49
  149.9 35.5 %collective-permute-start.19 = (bf16[256,2048]{1,0:T(8,128)(2,1)}, bf16[256,2048]{1,0:T(8,128)(2,1)}, u32[]{:S(2)}, u32[]{:S(2)}) collective-permute-start(bf16[256,2048]{1,0:T(8,128)(2,1)} %get-tuple-element.441), channel_id=1, source_target_pairs={{0,1},{1,0},{2,3},{3,2},{4,5},{5,4},{6,7},{7,6},{8,9},{9,8},{10,11... | collective-permute-start | bytes 3145736 | tf_op jit(solution)/shard_map/ppermute | solution.py:49
  187.6 15.3 %collective-permute-start.22 = (bf16[512,512]{1,0:T(8,128)(2,1)S(1)}, bf16[512,512]{1,0:T(8,128)(2,1)}, u32[]{:S(2)}, u32[]{:S(2)}) collective-permute-start(bf16[512,512]{1,0:T(8,128)(2,1)S(1)} %get-tuple-element.260.chosen_ref), channel_id=1, source_target_pairs={{0,1},{1,0},{2,3},{3,2},{4,5},{5,4},{6,7},{7,6},{8,9},{9,8},{10,11... | collective-permute-start | bytes 1572872 | tf_op jit(solution)/shard_map/ppermute | solution.py:49
  188.4 49.3 %collective-permute-start.23 = (bf16[256,2048]{1,0:T(8,128)(2,1)S(1)}, bf16[256,2048]{1,0:T(8,128)(2,1)S(1)}, u32[]{:S(2)}, u32[]{:S(2)}) collective-permute-start(bf16[256,2048]{1,0:T(8,128)(2,1)S(1)} %collective-permute-done.18.mid_a), channel_id=1, source_target_pairs={{0,2},{1,3},{2,0},{3,1},{4,6},{5,7},{6,4},{7,5},{8,10},{9,11},{10,... | collective-permute-start | bytes 3145736 | tf_op jit(solution)/shard_map/ppermute | solution.py:49
  188.4 49.3 %collective-permute-start.24 = (bf16[256,2048]{1,0:T(8,128)(2,1)}, bf16[256,2048]{1,0:T(8,128)(2,1)S(1)}, u32[]{:S(2)}, u32[]{:S(2)}) collective-permute-start(bf16[256,2048]{1,0:T(8,128)(2,1)} %collective-permute-done.19.mid_b), channel_id=1, source_target_pairs={{0,2},{1,3},{2,0},{3,1},{4,6},{5,7},{6,4},{7,5},{8,10},{9,11},{10,... | collective-permute-start | bytes 3145736 | tf_op jit(solution)/shard_map/ppermute | solution.py:49
  246.0 25.5 %collective-permute-start.25 = (bf16[256,2048]{1,0:T(8,128)(2,1)}, bf16[256,2048]{1,0:T(8,128)(2,1)}, u32[]{:S(2)}, u32[]{:S(2)}) collective-permute-start(bf16[256,2048]{1,0:T(8,128)(2,1)} %get-tuple-element.278.refs_0_), channel_id=1, source_target_pairs={{0,1},{1,0},{2,3},{3,2},{4,5},{5,4},{6,7},{7,6},{8,9},{9,8},{10,11... | collective-permute-start | bytes 3145736 | tf_op jit(solution)/shard_map/ppermute | solution.py:49
  278.2 54.1 %collective-permute-start.27 = (bf16[256,2048]{1,0:T(8,128)(2,1)S(1)}, bf16[256,2048]{1,0:T(8,128)(2,1)S(1)}, u32[]{:S(2)}, u32[]{:S(2)}) collective-permute-start(bf16[256,2048]{1,0:T(8,128)(2,1)S(1)} %get-tuple-element.282.refs_0_), channel_id=1, source_target_pairs={{0,1},{1,0},{2,3},{3,2},{4,5},{5,4},{6,7},{7,6},{8,9},{9,8},{10,11... | collective-permute-start | bytes 3145736 | tf_op jit(solution)/shard_map/ppermute | solution.py:49
  328.2 53.3 %collective-permute-start.26 = (bf16[256,2048]{1,0:T(8,128)(2,1)S(1)}, bf16[256,2048]{1,0:T(8,128)(2,1)S(1)}, u32[]{:S(2)}, u32[]{:S(2)}) collective-permute-start(bf16[256,2048]{1,0:T(8,128)(2,1)S(1)} %get-tuple-element.457), channel_id=1, source_target_pairs={{0,1},{1,0},{2,3},{3,2},{4,5},{5,4},{6,7},{7,6},{8,9},{9,8},{10,11... | collective-permute-start | bytes 3145736 | tf_op jit(solution)/shard_map/ppermute | solution.py:49
  331.5 166.9 %collective-permute-start.31 = (bf16[512,1024]{1,0:T(8,128)(2,1)}, bf16[512,1024]{1,0:T(8,128)(2,1)}, u32[]{:S(2)}, u32[]{:S(2)}) collective-permute-start(bf16[512,1024]{1,0:T(8,128)(2,1)} %get-tuple-element.454), channel_id=1, source_target_pairs={{0,1},{1,0},{2,3},{3,2},{4,5},{5,4},{6,7},{7,6},{8,9},{9,8},{10,11... | collective-permute-start | bytes 3145736 | tf_op jit(solution)/shard_map/ppermute | solution.py:49
  380.1 52.3 %collective-permute-start.28 = (bf16[256,2048]{1,0:T(8,128)(2,1)S(1)}, bf16[256,2048]{1,0:T(8,128)(2,1)S(1)}, u32[]{:S(2)}, u32[]{:S(2)}) collective-permute-start(bf16[256,2048]{1,0:T(8,128)(2,1)S(1)} %get-tuple-element.459), channel_id=1, source_target_pairs={{0,1},{1,0},{2,3},{3,2},{4,5},{5,4},{6,7},{7,6},{8,9},{9,8},{10,11... | collective-permute-start | bytes 3145736 | tf_op jit(solution)/shard_map/ppermute | solution.py:49
  428.2 34.1 %collective-permute-start.29 = (bf16[4,512,128]{2,1,0:T(8,128)(2,1)S(1)}, bf16[4,512,128]{2,1,0:T(8,128)(2,1)S(1)}, u32[]{:S(2)}, u32[]{:S(2)}) collective-permute-start(bf16[4,512,128]{2,1,0:T(8,128)(2,1)S(1)} %pad_maximum_fusion.2), channel_id=1, source_target_pairs={{0,1},{1,0},{2,3},{3,2},{4,5},{5,4},{6,7},{7,6},{8,9},{9,8},{10,11... | collective-permute-start | bytes 1572872 | tf_op jit(solution)/shard_map/ppermute | solution.py:49
  431.1 67.3 %collective-permute-start.30 = (bf16[512,1024]{1,0:T(8,128)(2,1)}, bf16[512,1024]{1,0:T(8,128)(2,1)}, u32[]{:S(2)}, u32[]{:S(2)}) collective-permute-start(bf16[512,1024]{1,0:T(8,128)(2,1)} %get-tuple-element.452), channel_id=1, source_target_pairs={{0,1},{1,0},{2,3},{3,2},{4,5},{5,4},{6,7},{7,6},{8,9},{9,8},{10,11... | collective-permute-start | bytes 3145736 | tf_op jit(solution)/shard_map/ppermute | solution.py:49
  487.5 31.7 %all-to-all-start.3 = ((bf16[32,32,512]{2,1,0:T(8,128)(2,1)}), bf16[32,32,512]{2,1,0:T(8,128)(2,1)}, u32[]{:S(2)}, u32[]{:S(2)}) async-start(bf16[32,32,512]{2,1,0:T(8,128)(2,1)} %bitcast.58), calls=%async_computation.3 | async-start | bytes 2097152 | tf_op jit(solution)/shard_map/all_to_all | solution.py:1019
  498.2 6.6 %collective-permute-start.33 = (bf16[2,2,2,1,2,16,2048]{6,5,4,3,2,1,0:T(8,128)(2,1)}, bf16[2,2,2,1,2,16,2048]{6,5,4,3,2,1,0:T(8,128)(2,1)}, u32[]{:S(2)}, u32[]{:S(2)}) collective-permute-start(bf16[2,2,2,1,2,16,2048]{6,5,4,3,2,1,0:T(8,128)(2,1)} %constant_dynamic-slice_fusion.17), channel_id=1, source_target_pairs={{0,2},{1,3},{2,0},{3,1},{4,6},{5,7},{6,4},{7,5},{8,10},{9,11},{10,... | collective-permute-start | bytes 3145736 | tf_op jit(solution)/shard_map/ppermute | solution.py:49
  524.5 20.8 %collective-permute-start.34 = (bf16[2,2,2,1,1,16,2048]{6,5,4,3,2,1,0:T(8,128)(2,1)}, bf16[2,2,2,1,1,16,2048]{6,5,4,3,2,1,0:T(8,128)(2,1)}, u32[]{:S(2)}, u32[]{:S(2)}) collective-permute-start(bf16[2,2,2,1,1,16,2048]{6,5,4,3,2,1,0:T(8,128)(2,1)} %dynamic-slice_convert_fusion.2), channel_id=1, source_target_pairs={{0,1},{1,0},{2,3},{3,2},{4,5},{5,4},{6,7},{7,6},{8,9},{9,8},{10,11... | collective-permute-start | bytes 1572872 | tf_op jit(solution)/shard_map/ppermute | solution.py:49
  544.4 24.5 %collective-permute-start.36 = (bf16[2,2,2,1,2,16,2560]{6,5,4,3,2,1,0:T(8,128)(2,1)S(1)}, bf16[2,2,2,1,2,16,2560]{6,5,4,3,2,1,0:T(8,128)(2,1)S(1)}, u32[]{:S(2)}, u32[]{:S(2)}) collective-permute-start(bf16[2,2,2,1,2,16,2560]{6,5,4,3,2,1,0:T(8,128)(2,1)S(1)} %get-tuple-element.445), channel_id=1, source_target_pairs={{0,2},{1,3},{2,0},{3,1},{4,6},{5,7},{6,4},{7,5},{8,10},{9,11},{10,... | collective-permute-start | bytes 3932168 | tf_op jit(solution)/shard_map/ppermute | solution.py:49
  544.7 24.2 %collective-permute-start.37 = (bf16[2,2,2,1,2,64,512]{6,5,4,3,2,1,0:T(8,128)(2,1)S(1)}, bf16[2,2,2,1,2,64,512]{6,5,4,3,2,1,0:T(8,128)(2,1)S(1)}, u32[]{:S(2)}, u32[]{:S(2)}) collective-permute-start(bf16[2,2,2,1,2,64,512]{6,5,4,3,2,1,0:T(8,128)(2,1)S(1)} %get-tuple-element.447), channel_id=1, source_target_pairs={{0,2},{1,3},{2,0},{3,1},{4,6},{5,7},{6,4},{7,5},{8,10},{9,11},{10,... | collective-permute-start | bytes 3145736 | tf_op jit(solution)/shard_map/ppermute | solution.py:49
  547.2 21.6 %collective-permute-start.35 = (bf16[2,2,1,1,1,16,2048]{6,5,4,3,2,1,0:T(8,128)(2,1)S(1)}, bf16[2,2,1,1,1,16,2048]{6,5,4,3,2,1,0:T(8,128)(2,1)S(1)}, u32[]{:S(2)}, u32[]{:S(2)}) collective-permute-start(bf16[2,2,1,1,1,16,2048]{6,5,4,3,2,1,0:T(8,128)(2,1)S(1)} %dynamic-slice_convert_fusion.8), channel_id=1, source_target_pairs={{0,4},{1,5},{2,6},{3,7},{4,0},{5,1},{6,2},{7,3},{8,12},{9,13},{10,... | collective-permute-start | bytes 786440 | tf_op jit(solution)/shard_map/ppermute | solution.py:49
  569.4 22.3 %collective-permute-start.39 = (bf16[2,2,2,1,1,16,2560]{6,5,4,3,2,1,0:T(8,128)(2,1)S(1)}, bf16[2,2,2,1,1,16,2560]{6,5,4,3,2,1,0:T(8,128)(2,1)S(1)}, u32[]{:S(2)}, u32[]{:S(2)}) collective-permute-start(bf16[2,2,2,1,1,16,2560]{6,5,4,3,2,1,0:T(8,128)(2,1)S(1)} %dynamic-slice_convert_fusion), channel_id=1, source_target_pairs={{0,1},{1,0},{2,3},{3,2},{4,5},{5,4},{6,7},{7,6},{8,9},{9,8},{10,11... | collective-permute-start | bytes 1966088 | tf_op jit(solution)/shard_map/ppermute | solution.py:49
  570.4 21.2 %collective-permute-start.40 = (bf16[2,2,1,1,2,64,512]{6,5,4,3,2,1,0:T(8,128)(2,1)S(1)}, bf16[2,2,1,1,2,64,512]{6,5,4,3,2,1,0:T(8,128)(2,1)S(1)}, u32[]{:S(2)}, u32[]{:S(2)}) collective-permute-start(bf16[2,2,1,1,2,64,512]{6,5,4,3,2,1,0:T(8,128)(2,1)S(1)} %dynamic-slice_convert_fusion.1), channel_id=1, source_target_pairs={{0,4},{1,5},{2,6},{3,7},{4,0},{5,1},{6,2},{7,3},{8,12},{9,13},{10,... | collective-permute-start | bytes 1572872 | tf_op jit(solution)/shard_map/ppermute | solution.py:49
  571.1 20.5 %collective-permute-start.38 = (bf16[2,1,1,1,1,16,2048]{6,5,4,3,2,1,0:T(8,128)(2,1)S(1)}, bf16[2,1,1,1,1,16,2048]{6,5,4,3,2,1,0:T(8,128)(2,1)S(1)}, u32[]{:S(2)}, u32[]{:S(2)}) collective-permute-start(bf16[2,1,1,1,1,16,2048]{6,5,4,3,2,1,0:T(8,128)(2,1)S(1)} %dynamic-slice_convert_fusion.15), channel_id=1, source_target_pairs={{0,8},{1,9},{2,10},{3,11},{4,12},{5,13},{6,14},{7,15},{8,0},{9,1},... | collective-permute-start | bytes 393224 | tf_op jit(solution)/shard_map/ppermute | solution.py:49
  591.9 6.8 %collective-permute-start.46 = (bf16[1,1,1,1,1,16,2048]{6,5,4,3,2,1,0:T(8,128)(2,1)S(1)}, bf16[1,1,1,1,1,16,2048]{6,5,4,3,2,1,0:T(8,128)(2,1)S(1)}, u32[]{:S(2)}, u32[]{:S(2)}) collective-permute-start(bf16[1,1,1,1,1,16,2048]{6,5,4,3,2,1,0:T(8,128)(2,1)S(1)} %dynamic-slice_convert_fusion.19), channel_id=1, source_target_pairs={{0,16},{1,17},{2,18},{3,19},{4,20},{5,21},{6,22},{7,23},{8,24},{9,... | collective-permute-start | bytes 196616 | tf_op jit(solution)/shard_map/ppermute | solution.py:49
  592.5 10.3 %collective-permute-start.47 = (bf16[2,2,1,1,1,16,2560]{6,5,4,3,2,1,0:T(8,128)(2,1)S(1)}, bf16[2,2,1,1,1,16,2560]{6,5,4,3,2,1,0:T(8,128)(2,1)S(1)}, u32[]{:S(2)}, u32[]{:S(2)}) collective-permute-start(bf16[2,2,1,1,1,16,2560]{6,5,4,3,2,1,0:T(8,128)(2,1)S(1)} %dynamic-slice_convert_fusion.6), channel_id=1, source_target_pairs={{0,4},{1,5},{2,6},{3,7},{4,0},{5,1},{6,2},{7,3},{8,12},{9,13},{10,... | collective-permute-start | bytes 983048 | tf_op jit(solution)/shard_map/ppermute | solution.py:49
  594.5 8.2 %collective-permute-start.48 = (bf16[2,2,1,1,1,64,512]{6,5,4,3,2,1,0:T(8,128)(2,1)S(1)}, bf16[2,2,1,1,1,64,512]{6,5,4,3,2,1,0:T(8,128)(2,1)S(1)}, u32[]{:S(2)}, u32[]{:S(2)}) collective-permute-start(bf16[2,2,1,1,1,64,512]{6,5,4,3,2,1,0:T(8,128)(2,1)S(1)} %dynamic-slice_convert_fusion.7), channel_id=1, source_target_pairs={{0,1},{1,0},{2,3},{3,2},{4,5},{5,4},{6,7},{7,6},{8,9},{9,8},{10,11... | collective-permute-start | bytes 786440 | tf_op jit(solution)/shard_map/ppermute | solution.py:49
  603.0 10.9 %collective-permute-start.42 = (bf16[2,2,2,1,1,16,1664]{6,5,4,3,2,1,0:T(8,128)(2,1)S(1)}, bf16[2,2,2,1,1,16,1664]{6,5,4,3,2,1,0:T(8,128)(2,1)S(1)}, u32[]{:S(2)}, u32[]{:S(2)}) collective-permute-start(bf16[2,2,2,1,1,16,1664]{6,5,4,3,2,1,0:T(8,128)(2,1)S(1)} %dynamic-slice_convert_fusion.5), channel_id=1, source_target_pairs={{0,1},{1,0},{2,3},{3,2},{4,5},{5,4},{6,7},{7,6},{8,9},{9,8},{10,11... | collective-permute-start | bytes 1277960 | tf_op jit(solution)/shard_map/ppermute | solution.py:49
  604.4 9.6 %collective-permute-start.49 = (bf16[2,1,1,1,1,16,2560]{6,5,4,3,2,1,0:T(8,128)(2,1)S(1)}, bf16[2,1,1,1,1,16,2560]{6,5,4,3,2,1,0:T(8,128)(2,1)S(1)}, u32[]{:S(2)}, u32[]{:S(2)}) collective-permute-start(bf16[2,1,1,1,1,16,2560]{6,5,4,3,2,1,0:T(8,128)(2,1)S(1)} %dynamic-slice_convert_fusion.13), channel_id=1, source_target_pairs={{0,8},{1,9},{2,10},{3,11},{4,12},{5,13},{6,14},{7,15},{8,0},{9,1},... | collective-permute-start | bytes 491528 | tf_op jit(solution)/shard_map/ppermute | solution.py:49
  605.1 8.9 %collective-permute-start.50 = (bf16[2,1,1,1,1,64,512]{6,5,4,3,2,1,0:T(8,128)(2,1)S(1)}, bf16[2,1,1,1,1,64,512]{6,5,4,3,2,1,0:T(8,128)(2,1)S(1)}, u32[]{:S(2)}, u32[]{:S(2)}) collective-permute-start(bf16[2,1,1,1,1,64,512]{6,5,4,3,2,1,0:T(8,128)(2,1)S(1)} %dynamic-slice_convert_fusion.14), channel_id=1, source_target_pairs={{0,8},{1,9},{2,10},{3,11},{4,12},{5,13},{6,14},{7,15},{8,0},{9,1},... | collective-permute-start | bytes 393224 | tf_op jit(solution)/shard_map/ppermute | solution.py:49
  615.9 7.8 %collective-permute-start.51 = (bf16[1,1,1,1,1,16,2560]{6,5,4,3,2,1,0:T(8,128)(2,1)S(1)}, bf16[1,1,1,1,1,16,2560]{6,5,4,3,2,1,0:T(8,128)(2,1)S(1)}, u32[]{:S(2)}, u32[]{:S(2)}) collective-permute-start(bf16[1,1,1,1,1,16,2560]{6,5,4,3,2,1,0:T(8,128)(2,1)S(1)} %dynamic-slice_convert_fusion.17), channel_id=1, source_target_pairs={{0,16},{1,17},{2,18},{3,19},{4,20},{5,21},{6,22},{7,23},{8,24},{9,... | collective-permute-start | bytes 245768 | tf_op jit(solution)/shard_map/ppermute | solution.py:49
  617.2 6.4 %collective-permute-start.52 = (bf16[1,1,1,1,1,64,512]{6,5,4,3,2,1,0:T(8,128)(2,1)S(1)}, bf16[1,1,1,1,1,64,512]{6,5,4,3,2,1,0:T(8,128)(2,1)S(1)}, u32[]{:S(2)}, u32[]{:S(2)}) collective-permute-start(bf16[1,1,1,1,1,64,512]{6,5,4,3,2,1,0:T(8,128)(2,1)S(1)} %dynamic-slice_convert_fusion.18), channel_id=1, source_target_pairs={{0,16},{1,17},{2,18},{3,19},{4,20},{5,21},{6,22},{7,23},{8,24},{9,... | collective-permute-start | bytes 196616 | tf_op jit(solution)/shard_map/ppermute | solution.py:49
  (84 other events, 597.0 us)
Sparse Core Ops, SparseCore 0:
  13.6 61.8 all-gather.1

commit v4 on v3

--- a/solution.py
+++ b/solution.py
@@ -49,74 +49,32 @@
     return lax.ppermute(value, ("dp", "mp"), [(d, d ^ mask) for d in range(devices)])
 
 
-def gather_start(block, devices):
-    return block.reshape((1,) * log2_of(devices) + block.shape)
-
-
-def masks_of(bits):
-    masks = [0]
-    for bit in bits:
-        masks += [mask | (1 << bit) for mask in masks]
-    return masks
-
-
-def gather_send(held, bits, devices):
-    return [swap(held, mask, devices) for mask in masks_of(bits)[1:]]
-
-
-def gather_join(held, came, bits, me, devices):
-    blocks = [held, *came]
-    for bit in bits:
-        axis = log2_of(devices) - 1 - bit
-        upper = ((me >> bit) & 1) == 1
-        blocks = [
-            jnp.where(
-                upper,
-                jnp.concatenate([other, own], axis),
-                jnp.concatenate([own, other], axis),
-            )
-            for own, other in zip(blocks[::2], blocks[1::2])
-        ]
-    return blocks[0]
-
-
-def gather_step(held, bits, me, devices):
-    return gather_join(held, gather_send(held, bits, devices), bits, me, devices)
-
-
-def gather_end(held):
-    return held.reshape((-1, held.shape[-1]))
-
-
-def scatter_start(blocks, devices):
-    bits = log2_of(devices)
-    return blocks.reshape((2,) * bits + (blocks.shape[0] // devices,) + blocks.shape[1:])
-
-
-def scatter_send(held, bits, me, devices):
-    def part(mask, value):
-        for bit in bits:
-            axis = log2_of(devices) - 1 - bit
-            value = lax.dynamic_slice_in_dim(value, ((me ^ mask) >> bit) & 1, 1, axis)
-        return value
-
-    came = [swap(to_low(part(mask, held)), mask, devices) for mask in masks_of(bits)[1:]]
-    return (part(0, held), came)
+def gather_join(held, arrived, bit, done, me):
+    rows, width = held.shape
+    outer = 1 << sum(other > bit for other in done)
+    held, arrived = [x.reshape(outer, rows // outer, width) for x in (held, arrived)]
+    joined = jnp.where(
+        ((me >> bit) & 1) == 1,
+        jnp.concatenate([arrived, held], axis=1),
+        jnp.concatenate([held, arrived], axis=1),
+    )
+    return joined.reshape(2 * rows, width)
+
+
+def scatter_send(held, bit, left, me, devices):
+    rows, width = held.shape
+    outer = 1 << sum(other > bit for other in left)
+    parts = held.reshape(outer, 2, rows // outer // 2, width)
+    mine = (me >> bit) & 1
+
+    def part(at):
+        return lax.dynamic_slice_in_dim(parts, at, 1, 1).reshape(rows // 2, width)
+
+    return (part(mine), swap(to_low(part(1 - mine)), 1 << bit, devices))
 
 
 def scatter_add(staying, came):
-    total = staying.astype(jnp.float32)
-    for share in came:
-        total = total + share.astype(jnp.float32)
-    return total
-
-
-def scatter_step(held, bits, me, devices):
-    return scatter_add(*scatter_send(held, bits, me, devices))
-
-
-def scatter_end(held):
-    return held.reshape(held.shape[-2:])
+    return staying.astype(jnp.float32) + came.astype(jnp.float32)
 
 
 def lanes(shape):
@@ -135,15 +93,32 @@
     return value.astype(jnp.bfloat16)
 
 
-def causal_of(shape, block_at, rows):
-    key_at = lax.broadcasted_iota(jnp.int32, shape, 0)
-    query_at = lax.broadcasted_iota(jnp.int32, shape, 1) + block_at * rows
-    return key_at <= query_at
-
-
-def head_views(pair_ref, cos_ref, sin_ref):
-    pair = pair_ref[...]
-    turned = to_low(pair * cos_ref[...] + half_swap(pair) * sin_ref[...]).astype(jnp.float32)
+def causal_of(rows):
+    return lax.broadcasted_iota(jnp.int32, (rows, rows), 0) <= lax.broadcasted_iota(
+        jnp.int32, (rows, rows), 1
+    )
+
+
+def masked_scores(keys, low, causal):
+    rows = causal.shape[0]
+    length = keys.shape[0]
+    last = jnp.where(causal, matmul_last(keys[length - rows :, :], low), NEGATIVE)
+    return [matmul_last(keys[: length - rows, :], low), last] if length > rows else [last]
+
+
+def for_lengths(block_at, rows, length, work):
+    for count in (length - rows, length):
+        pl.when(block_at == count // rows - 1)(functools.partial(work, count))
+
+
+def turn_left(value, cosine, sine):
+    left = lanes(value.shape) < HEAD_WIDTH
+    return jnp.where(left, value * cosine + half_swap(value) * sine, value)
+
+
+def head_views(pair_ref, cos_ref, sin_ref, rows):
+    span = slice(0, rows)
+    turned = to_low(turn_left(pair_ref[span, :], cos_ref[span, :], sin_ref[span, :])).astype(jnp.float32)
     other = pltpu.roll(turned, HEAD_WIDTH, 1)
     left = lanes(turned.shape) < HEAD_WIDTH
     return (
@@ -158,29 +133,39 @@
     info, query_ref, pair_ref, cos_pair, sin_pair, cos_ref, sin_ref,
     out_ref, low_ref, lse_ref, even, odd, across,
 ):
-    key_left, key_right, value_left, _ = head_views(pair_ref, cos_pair, sin_pair)
-    even[...] = to_low(key_left)
-    odd[...] = to_low(key_right)
-    across[...] = to_low(value_left.T[:HEAD_WIDTH])
-
     rows = query_ref.shape[0]
-    length = pair_ref.shape[0]
-    causal = causal_of((length, rows), info[0], rows)
-    for pair in range(query_ref.shape[1] // PAIR):
-        span = slice(pair * PAIR, (pair + 1) * PAIR)
-        query = query_ref[:, span]
-        turned = to_low(query * cos_ref[...] + half_swap(query) * sin_ref[...])
-        low = to_low(turned.astype(jnp.float32) * HEAD_WIDTH ** (-0.5))
-        low_ref[:, span] = low
-        outs = []
-        for at, keys in enumerate((even, odd)):
-            scores = jnp.where(causal, matmul_last(keys[...], low), NEGATIVE)
-            highest = jnp.max(scores, axis=0, keepdims=True)
-            weight = jnp.exp(scores - highest)
-            total = jnp.sum(weight, axis=0, keepdims=True)
-            outs.append(matmul(across[...], to_low(weight)) / total)
-            lse_ref[0, 2 * pair + at : 2 * pair + at + 1, :] = highest + jnp.log(total)
-        out_ref[:, span] = to_low(jnp.concatenate(outs, axis=0).T)
+    causal = causal_of(rows)
+
+    def work(length):
+        span = slice(0, length)
+        key_left, key_right, value_left, _ = head_views(pair_ref, cos_pair, sin_pair, length)
+        even[span, :] = to_low(key_left)
+        odd[span, :] = to_low(key_right)
+        across[:, span] = to_low(value_left.T[:HEAD_WIDTH])
+        for pair in range(query_ref.shape[1] // PAIR):
+            columns = slice(pair * PAIR, (pair + 1) * PAIR)
+            query = query_ref[:, columns]
+            turned = to_low(query * cos_ref[...] + half_swap(query) * sin_ref[...])
+            low = to_low(turned.astype(jnp.float32) * HEAD_WIDTH ** (-0.5))
+            low_ref[:, columns] = low
+            outs = []
+            for at, keys in enumerate((even, odd)):
+                scores = masked_scores(keys[span, :], low, causal)
+                highest = functools.reduce(
+                    jnp.maximum, [jnp.max(x, axis=0, keepdims=True) for x in scores]
+                )
+                weights = [jnp.exp(x - highest) for x in scores]
+                total = sum(jnp.sum(x, axis=0, keepdims=True) for x in weights)
+                out = 0.0
+                start = 0
+                for x in weights:
+                    out = out + matmul(across[:, start : start + x.shape[0]], to_low(x))
+                    start += x.shape[0]
+                outs.append(out / total)
+                lse_ref[0, 2 * pair + at : 2 * pair + at + 1, :] = highest + jnp.log(total)
+            out_ref[:, columns] = to_low(jnp.concatenate(outs, axis=0).T)
+
+    for_lengths(info[0], rows, pair_ref.shape[0], work)
 
 
 def attention_backward_kernel(
@@ -188,41 +173,58 @@
 ):
     query_ref, pair_grad_ref, even, odd, value_even, value_odd, across = refs[-11:-4]
     key_even, key_odd, sum_even, sum_odd = refs[-4:]
-    key_left, key_right, value_left, value_right = head_views(pair_ref, cos_pair, sin_pair)
-    even[...] = to_low(key_left)
-    odd[...] = to_low(key_right)
-    value_even[...] = to_low(value_left)
-    value_odd[...] = to_low(value_right)
-    across[...] = to_low(key_left.T[:HEAD_WIDTH])
-    for total in (key_even, key_odd, sum_even, sum_odd):
-        total[...] = jnp.zeros_like(total)
-
     rows = low_ref.shape[0]
-    length = pair_ref.shape[0]
-    causal = causal_of((length, rows), info[0], rows)
-    sides = ((even, value_even, key_even, sum_even), (odd, value_odd, key_odd, sum_odd))
-    for pair in range(low_ref.shape[1] // PAIR):
-        span = slice(pair * PAIR, (pair + 1) * PAIR)
-        low = low_ref[:, span]
-        grad = grad_ref[:, span]
-        outs = []
-        for at, (keys, values, key_total, value_total) in enumerate(sides):
-            scores = jnp.where(causal, matmul_last(keys[...], low), NEGATIVE)
-            probs = jnp.exp(scores - lse_ref[0, 2 * pair + at : 2 * pair + at + 1, :])
-            value_total[...] += matmul(to_low(probs), grad)
-            moved = probs * matmul_last(values[...], grad)
-            mean = jnp.sum(moved, axis=0, keepdims=True)
-            grad_scores = to_low(moved - probs * mean)
-            key_total[...] += matmul(grad_scores, low)
-            outs.append(matmul(across[...], grad_scores))
-        turned = jnp.concatenate(outs, axis=0).T * HEAD_WIDTH ** (-0.5)
-        query_ref[:, span] = to_low(turned * cos_ref[...] - half_swap(turned) * sin_ref[...])
-    left = lanes((length, PAIR)) < HEAD_WIDTH
-    pair_grad_ref[0] = jnp.where(
-        left,
-        key_even[...] + pltpu.roll(key_odd[...], HEAD_WIDTH, 1),
-        pltpu.roll(sum_even[...], HEAD_WIDTH, 1) + sum_odd[...],
-    )
+    causal = causal_of(rows)
+
+    def work(length):
+        span = slice(0, length)
+        key_left, key_right, value_left, value_right = head_views(pair_ref, cos_pair, sin_pair, length)
+        even[span, :] = to_low(key_left)
+        odd[span, :] = to_low(key_right)
+        value_even[span, :] = to_low(value_left)
+        value_odd[span, :] = to_low(value_right)
+        across[:, span] = to_low(key_left.T[:HEAD_WIDTH])
+        sides = ((even, value_even, key_even, sum_even), (odd, value_odd, key_odd, sum_odd))
+        for total in (key_even, key_odd, sum_even, sum_odd):
+            total[span, :] = jnp.zeros((length, PAIR), jnp.float32)
+        for pair in range(low_ref.shape[1] // PAIR):
+            columns = slice(pair * PAIR, (pair + 1) * PAIR)
+            low = low_ref[:, columns]
+            grad = grad_ref[:, columns]
+            outs = []
+            for at, (keys, values, key_total, value_total) in enumerate(sides):
+                lse = lse_ref[0, 2 * pair + at : 2 * pair + at + 1, :]
+                probs = [jnp.exp(x - lse) for x in masked_scores(keys[span, :], low, causal)]
+                moved = []
+                start = 0
+                for x in probs:
+                    part = slice(start, start + x.shape[0])
+                    value_total[part, :] += matmul(to_low(x), grad)
+                    moved.append(x * matmul_last(values[part, :], grad))
+                    start += x.shape[0]
+                mean = sum(jnp.sum(x, axis=0, keepdims=True) for x in moved)
+                out = 0.0
+                start = 0
+                for x, y in zip(probs, moved):
+                    part = slice(start, start + x.shape[0])
+                    grad_scores = to_low(y - x * mean)
+                    key_total[part, :] += matmul(grad_scores, low)
+                    out = out + matmul(across[:, part], grad_scores)
+                    start += x.shape[0]
+                outs.append(out)
+            turned = jnp.concatenate(outs, axis=0).T * HEAD_WIDTH ** (-0.5)
+            query_ref[:, columns] = to_low(turned * cos_ref[...] - half_swap(turned) * sin_ref[...])
+        left = lanes((length, PAIR)) < HEAD_WIDTH
+        pair_grad_ref[0, span, :] = jnp.where(
+            left,
+            key_even[span, :] + pltpu.roll(key_odd[span, :], HEAD_WIDTH, 1),
+            pltpu.roll(sum_even[span, :], HEAD_WIDTH, 1) + sum_odd[span, :],
+        )
+        if length < pair_ref.shape[0]:
+            rest = (pair_ref.shape[0] - length, PAIR)
+            pair_grad_ref[0, length:, :] = jnp.zeros(rest, jnp.float32)
+
+    for_lengths(info[0], rows, pair_ref.shape[0], work)
 
 
 def attention_specs(part, rows, length):
@@ -230,7 +232,7 @@
     return {
         "table_pair": pl.BlockSpec((length, PAIR), lambda g, s: (0, 0)),
         "table": pl.BlockSpec((rows, PAIR), lambda g, s: (s[0], 0)),
-        "pair": pl.BlockSpec((length, PAIR), lambda g, s: (0, s[1 + g])),
+        "pair": pl.BlockSpec((length, PAIR), lambda g, s: (0, g)),
         "part": pl.BlockSpec(span, lambda g, s: (part, g)),
         "wide": pl.BlockSpec(span, lambda g, s: (0, g)),
         "sums": pl.BlockSpec((1, 8, rows), lambda g, s: (g, 0, 0)),
@@ -245,7 +247,7 @@
 
 
 def attention_forward(info, queries, pair_pre, tables, part, length):
-    cos_pair, sin_pair, cosine, sine = tables
+    cosine, sine = tables
     rows = cosine.shape[0] // BLOCK_PARTS
     heads = 4 * 4 * PAIR // HEAD_WIDTH
     spec = attention_specs(part, rows, length)
@@ -276,11 +278,11 @@
         ),
         cost_estimate=attention_cost(rows, length, heads, 2),
         name="attention_forward",
-    )(info, queries, pair_pre, cos_pair, sin_pair, cosine, sine)
+    )(info, queries, pair_pre, cosine, sine, cosine, sine)
 
 
 def attention_backward(info, low, grad, sums, pair_pre, tables, part, length, before):
-    cos_pair, sin_pair, cosine, sine = tables
+    cosine, sine = tables
     rows = cosine.shape[0] // BLOCK_PARTS
     heads = low.shape[1] // HEAD_WIDTH
     spec = attention_specs(part, rows, length)
@@ -314,7 +316,7 @@
         ),
         cost_estimate=attention_cost(rows, length, heads, 5),
         name="attention_backward",
-    )(info, low, grad, sums, pair_pre, cos_pair, sin_pair, cosine, sine, *before)
+    )(info, low, grad, sums, pair_pre, cosine, sine, cosine, sine, *before)
 
 
 def rope_tables(length):
@@ -322,14 +324,9 @@
     inverse = 10000.0 ** (-np.arange(0, HEAD_WIDTH, 2, dtype=np.float32) / HEAD_WIDTH)
     angles = positions[:, None] * inverse.astype(np.float32)[None, :]
     cosine, sine = np.cos(angles).astype(np.float32), np.sin(angles).astype(np.float32)
-    head_cos = np.concatenate([cosine, cosine], axis=1)
-    head_sin = np.concatenate([-sine, sine], axis=1)
-    still = np.ones_like(head_cos)
-    return tuple(
-        jnp.asarray(np.concatenate(sides, axis=1))
-        for sides in (
-            (head_cos, still), (head_sin, 0 * still), (head_cos, head_cos), (head_sin, head_sin)
-        )
+    return (
+        jnp.asarray(np.concatenate([cosine] * 4, axis=1)),
+        jnp.asarray(np.concatenate([-sine, sine, -sine, sine], axis=1)),
     )
 
 
@@ -360,8 +357,9 @@
     return inverse * (scaled - mean - hat * along)
 
 
-def slot_attention_kernel(pieces_ref, counts_ref, weight_ref, norm_ref, *refs):
-    mixed_ref, probs_ref, attended_ref, lead_ref = refs[-4:]
+def slot_attention_kernel(
+    pieces_ref, counts_ref, weight_ref, norm_ref, mixed_ref, probs_ref, attended_ref, lead_ref
+):
     entries, slots, width = pieces_ref.shape
     rows = entries * slots
     tall = (entries, slots, width)
@@ -388,48 +386,41 @@
     lead_ref[...] = pieces[:, 0, :]
 
 
-def slot_attention(at, before, pieces, counts, in_weight, norm_rows):
+def slot_attention(pieces, counts, in_weight, norm_rows):
     entries, slots, width = pieces.shape
-    part = min(ENTRY_BLOCK, entries // 2)
-    steps = entries // 2 // part
-    counts = jnp.broadcast_to(counts[:, None, None], (entries, 1, PAIR))
+    part = min(ENTRY_BLOCK, entries)
     whole = lambda shape: pl.BlockSpec(shape, lambda i: (0,) * len(shape))
-    tall = pl.BlockSpec((part, slots, width), lambda i: (i + at * steps, 0, 0))
-    flat = pl.BlockSpec((part, width), lambda i: (i + at * steps, 0))
-    before = [] if before is None else list(before)
-    return list(
-        pl.pallas_call(
-            slot_attention_kernel,
-            grid=(steps,),
-            in_specs=[
-                tall,
-                pl.BlockSpec((part, 1, PAIR), lambda i: (i + at * steps, 0, 0)),
-                whole(in_weight.shape),
-                whole(norm_rows.shape),
-            ]
-            + [pl.BlockSpec(memory_space=pl.ANY)] * len(before),
-            out_specs=[
-                pl.BlockSpec((part * slots, 3 * width), lambda i: (i + at * steps, 0)),
-                pl.BlockSpec((part, slots, PAIR), lambda i: (i + at * steps, 0, 0)),
-                flat,
-                flat,
-            ],
-            out_shape=[
-                jax.ShapeDtypeStruct((entries * slots, 3 * width), jnp.bfloat16),
-                jax.ShapeDtypeStruct((entries, slots, PAIR), jnp.float32),
-                jax.ShapeDtypeStruct((entries, width), jnp.bfloat16),
-                jax.ShapeDtypeStruct((entries, width), jnp.float32),
-            ],
-            input_output_aliases={4 + i: i for i in range(len(before))},
-            compiler_params=pltpu.CompilerParams(
-                dimension_semantics=("arbitrary",), vmem_limit_bytes=VMEM_LIMIT
-            ),
-            cost_estimate=pl.CostEstimate(
-                flops=entries * slots * width, bytes_accessed=entries * slots, transcendentals=0
-            ),
-            name="slot_attention",
-        )(pieces, counts, in_weight, norm_rows, *before)
-    )
+    tall = pl.BlockSpec((part, slots, width), lambda i: (i, 0, 0))
+    flat = pl.BlockSpec((part, width), lambda i: (i, 0))
+    return pl.pallas_call(
+        slot_attention_kernel,
+        grid=(entries // part,),
+        in_specs=[
+            tall,
+            pl.BlockSpec((part, 1, PAIR), lambda i: (i, 0, 0)),
+            whole(in_weight.shape),
+            whole(norm_rows.shape),
+        ],
+        out_specs=[
+            pl.BlockSpec((part * slots, 3 * width), lambda i: (i, 0)),
+            pl.BlockSpec((part, slots, PAIR), lambda i: (i, 0, 0)),
+            flat,
+            flat,
+        ],
+        out_shape=[
+            jax.ShapeDtypeStruct((entries * slots, 3 * width), jnp.bfloat16),
+            jax.ShapeDtypeStruct((entries, slots, PAIR), jnp.float32),
+            jax.ShapeDtypeStruct((entries, width), jnp.bfloat16),
+            jax.ShapeDtypeStruct((entries, width), jnp.float32),
+        ],
+        compiler_params=pltpu.CompilerParams(
+            dimension_semantics=("arbitrary",), vmem_limit_bytes=VMEM_LIMIT
+        ),
+        cost_estimate=pl.CostEstimate(
+            flops=entries * slots * width, bytes_accessed=entries * slots, transcendentals=0
+        ),
+        name="slot_attention",
+    )(pieces, counts, in_weight, norm_rows)
 
 
 def gelu_of(value):
@@ -442,8 +433,26 @@
 
 
 def units_forward_kernel(
-    attended_ref, lead_ref, wide_weight_ref, reduce_ref, norm_ref, pooled_ref, hidden_ref
+    split, places, attended_ref, lead_ref, *refs
 ):
+    *weights, norm_ref, pooled_ref, hidden_ref = refs[: 11 if split else 5]
+    if not split:
+        wide_weight_ref, reduce_ref = weights
+    else:
+        wide_weight_ref, reduce_ref = refs[11:]
+
+        @pl.when(pl.program_id(0) == 0)
+        def join():
+            core = places[0]
+            for whole, parts in ((wide_weight_ref, weights[:4]), (reduce_ref, weights[4:])):
+                rows = parts[0].shape[0] // split
+                for at, part in enumerate(parts):
+                    side = places[1] if at % 2 == 0 else 1 - places[1]
+                    place = 2 * side + (core if at < 2 else 1 - core)
+                    for group in range(split):
+                        start = pl.multiple_of((4 * group + place) * rows, rows)
+                        whole[pl.ds(start, rows), :] = part[group * rows : (group + 1) * rows, :]
+
     width = lead_ref.shape[1]
     hidden = lead_ref[...] + matmul(attended_ref[...], wide_weight_ref[:, :width])
     hidden_ref[...] = hidden
@@ -458,17 +467,26 @@
     pooled_ref[...] = to_low(total)
 
 
-def units_forward(attended, lead, wide_weight, reduce_weight, norm_rows):
+def units_forward(groups, places, attended, lead, wide_weight, reduce_weight, norm_rows):
     entries, width = attended.shape
     part = min(UNIT_ROWS, entries)
-    whole = lambda shape: pl.BlockSpec(shape, lambda i: (0,) * len(shape))
-    flat = pl.BlockSpec((part, width), lambda i: (i, 0))
+    split = groups if len(wide_weight) == 4 else 0
+    whole = lambda shape: pl.BlockSpec(shape, lambda i, s: (0,) * len(shape))
+    flat = pl.BlockSpec((part, width), lambda i, s: (i, 0))
+    weights = [*wide_weight, *reduce_weight]
+    joined = [
+        pltpu.VMEM((4 * parts[0].shape[0], parts[0].shape[1]), jnp.bfloat16)
+        for parts in (wide_weight, reduce_weight)
+    ]
     return pl.pallas_call(
-        units_forward_kernel,
-        grid=(entries // part,),
-        in_specs=[flat, flat]
-        + [whole(x.shape) for x in (wide_weight, reduce_weight, norm_rows)],
-        out_specs=[flat, flat],
+        functools.partial(units_forward_kernel, split),
+        grid_spec=pltpu.PrefetchScalarGridSpec(
+            num_scalar_prefetch=1,
+            grid=(entries // part,),
+            in_specs=[flat, flat] + [whole(x.shape) for x in (*weights, norm_rows)],
+            out_specs=[flat, flat],
+            scratch_shapes=joined if split else [],
+        ),
         out_shape=[
             jax.ShapeDtypeStruct((entries, width), jnp.bfloat16),
             jax.ShapeDtypeStruct((entries, width), jnp.float32),
@@ -480,7 +498,7 @@
             flops=entries * width, bytes_accessed=entries * width, transcendentals=0
         ),
         name="units_forward",
-    )(attended, lead, wide_weight, reduce_weight, norm_rows)
+    )(places.astype(jnp.int32), attended, lead, *weights, norm_rows)
 
 
 def units_backward_kernel(
@@ -775,15 +793,18 @@
     return inverse * scaled - value * (inverse * inverse * inverse * along)
 
 
-def project_kernel(with_queries, info, chosen_ref, embed_ref, gain_ref, pair_weight_ref, *refs):
+def project_kernel(with_queries, info, chosen_ref, embed_ref, gain_ref, pair_own, pair_near, pair_far, *refs):
     embedded = to_low(matmul(chosen_ref[...], embed_ref[...]))
     value = embedded.astype(jnp.float32)
     low = to_low(value * root_mean(value) * gain_ref[...])
+    pair_ref = refs[-3] if with_queries else refs[-1]
+    at = 0
+    for ref in (pair_own, pair_near, pair_far):
+        pair_ref[:, at : at + ref.shape[1]] = matmul(low, ref[...])
+        at += ref.shape[1]
     if not with_queries:
-        refs[-1][...] = matmul(low, pair_weight_ref[...])
         return
-    near_ref, mid_a, mid_b, far_a, far_b, pair_ref, embedded_ref, query_ref = refs
-    pair_ref[...] = matmul(low, pair_weight_ref[...])
+    near_ref, mid_a, mid_b, far_a, far_b, _, embedded_ref, query_ref = refs
     embedded_ref[...] = embedded
     near = near_ref.shape[1]
     step = mid_a.shape[1]
@@ -795,12 +816,12 @@
         )
 
 
-def project(info, chosen, embed, gain, pair_weight, query_weights, pair_before):
+def project(info, chosen, embed, gain, pair_weights, query_weights, pair_before):
     rows, width = chosen.shape
     block = rows // 2
     wide = embed.shape[1]
     row = pl.BlockSpec((block, wide), lambda i, s: (i, 0))
-    pairs = pair_weight.shape[1]
+    pairs = sum(weight.shape[1] for weight in pair_weights)
     before = [] if pair_before is None else [pair_before]
     more = bool(query_weights)
     return pl.pallas_call(
@@ -812,7 +833,7 @@
                 pl.BlockSpec((block, width), lambda i, s: (i, 0)),
                 fixed(embed.shape),
                 fixed((1, wide)),
-                fixed(pair_weight.shape),
+                *[fixed(weight.shape) for weight in pair_weights],
                 *[fixed(weight.shape) for weight in query_weights],
                 *[pl.BlockSpec(memory_space=pl.ANY)] * len(before),
             ],
@@ -824,13 +845,13 @@
             jax.ShapeDtypeStruct((rows, wide), jnp.float32),
         ]
         * more,
-        input_output_aliases={5: 0} if before else {},
+        input_output_aliases={7: 0} if before else {},
         compiler_params=pltpu.CompilerParams(
             dimension_semantics=("arbitrary",), vmem_limit_bytes=VMEM_LIMIT
         ),
         cost_estimate=pl.CostEstimate(flops=1 << 30, bytes_accessed=1 << 20, transcendentals=0),
         name="project",
-    )(info, chosen, embed, gain.reshape(1, -1), pair_weight, *query_weights, *before)
+    )(info, chosen, embed, gain.reshape(1, -1), *pair_weights, *query_weights, *before)
 
 
 def output_kernel(rows_ref, embedded_ref, gain_ref, near_ref, mid_a, mid_b, far_a, far_b, hidden_ref, low_ref):
@@ -914,14 +935,16 @@
 
 def embed_backward_kernel(
     info, query_ref, own_ref, came_ref, short_ref, cos_ref, sin_ref, first_ref, second_ref, embedded_ref, gain_ref,
-    embed_ref, near_ref, mid_a, mid_b, far_a, far_b, pair_weight_ref, grad_ref, token_ref,
+    embed_ref, near_ref, mid_a, mid_b, far_a, far_b, pair_own, pair_near, pair_far, grad_ref, token_ref,
 ):
     total = None
-    for head in range(own_ref.shape[0]):
+    weights = [pair_own[:, :PAIR], pair_own[:, PAIR:], pair_near[...], pair_far[...]]
+    for group, weight in enumerate(weights):
+        head = info[2 + group]
         short = jnp.where(pl.program_id(0) == 0, short_ref[head].astype(jnp.float32), 0.0)
         pair = own_ref[head] + came_ref[head].astype(jnp.float32) + short
-        low = to_low(pair * cos_ref[...] - half_swap(pair) * sin_ref[...])
-        term = matmul_last(low, pair_weight_ref[:, head * PAIR : (head + 1) * PAIR])
+        low = to_low(turn_left(pair, cos_ref[...], -sin_ref[...]))
+        term = matmul_last(low, weight)
         total = term if total is None else total + term
     near = near_ref.shape[1]
     step = mid_a.shape[1]
@@ -944,7 +967,7 @@
 
 
 def embed_backward(
-    info, query_grad, own, came, short, tables, hidden_grads, embedded, gain, embed, query_weights, pair_weight
+    info, query_grad, own, came, short, tables, hidden_grads, embedded, gain, embed, query_weights, pair_weights
 ):
     rows, wide = embedded.shape
     block = rows // 2
@@ -960,8 +983,7 @@
             grid=(2,),
             in_specs=[
                 row, pair, pair, pl.BlockSpec((heads, block, PAIR), lambda i, s: (0, 0, 0)), table, table, once, once, row, fixed((1, wide)), fixed(embed.shape),
-                *[fixed(weight.shape) for weight in query_weights],
-                fixed(pair_weight.shape),
+                *[fixed(weight.shape) for weight in (*query_weights, *pair_weights)],
             ],
             out_specs=[row, pl.BlockSpec((block, embed.shape[0]), lambda i, s: (i, 0))],
         ),
@@ -976,7 +998,7 @@
         name="embed_backward",
     )(
         info, query_grad, own, came, short, tables[0], tables[1], *hidden_grads, embedded, gain.reshape(1, -1), embed,
-        *query_weights, pair_weight,
+        *query_weights, *pair_weights,
     )
 
 
@@ -1072,30 +1094,6 @@
     digits = digits.reshape(hyper_input.shape[0], -1)
     digit_width = digits.shape[1]
     digit_lanes = jnp.pad(digits, ((0, 0), (0, -digit_width % PAIR)))
-    spread_order = [[bit] for bit in [0] + far_bits + [1]]
-    in_held = gather_start(jnp.concatenate([hyper_input, norm_lanes, digit_lanes], axis=1), devices)
-    later_held = [
-        gather_start(jnp.concatenate([hyper_output, hyper_expand], axis=1), devices),
-        gather_start(hyper_reduce, devices),
-    ]
-    for at, step in enumerate(spread_order):
-        in_held = gather_step(in_held, step, me, devices)
-        if at == 1:
-            in_held, later_held = lax.optimization_barrier((in_held, later_held))
-    in_weight = gather_end(in_held)
-    for step in spread_order[:-3]:
-        later_held = [gather_step(x, step, me, devices) for x in later_held]
-        if step == spread_order[0]:
-            begun = later_held
-    later_came = [gather_send(x, spread_order[-3], devices) for x in later_held]
-    embed_full = lax.all_gather(embed_weight, ("dp", "mp"), axis=0, tiled=True)
-    norm_rows = in_weight[:, in_width : in_width + 8].astype(jnp.float32).T
-    digit_at = in_width + PAIR
-    all_digits = in_weight[:, digit_at : digit_at + digit_width].reshape(devices, 2, 2 * block)
-    all_digits = all_digits.astype(jnp.int32)
-    asked = all_digits[:, 0] * PAIR + all_digits[:, 1]
-
-    query_cut = frozen_query_weight.shape[1] // 2
     kv_local = frozen_key_weight.shape[1] // HEAD_WIDTH
     key_own = jnp.concatenate(
         [
@@ -1105,50 +1103,97 @@
         ],
         axis=1,
     )
-    frozen_query_weight, key_own, *_ = lax.optimization_barrier((frozen_query_weight, key_own, *begun))
-    query_near = lax.dynamic_slice_in_dim(frozen_query_weight, core * query_cut, query_cut, 1)
-    half_in = query_near.shape[0] // 2
-    query_near = [swap(query_near[:half_in], 1, devices), swap(query_near[half_in:], 1, devices)]
-    key_other = swap(key_own, 1, devices)
+    key_near = swap(lax.dynamic_slice_in_dim(key_own, core * PAIR, PAIR, 1), 1, devices)
+    query_cut = frozen_query_weight.shape[1] // 2
+    side = (me >> 2) & 1
+    half_in = frozen_query_weight.shape[0] // 2
+    query_slice = lax.dynamic_slice(
+        frozen_query_weight, (side * half_in, core * query_cut), (half_in, query_cut)
+    )
+    half_out = query_cut // 2
+    output_slice = lax.dynamic_slice_in_dim(
+        frozen_output_weight, core * query_cut + side * half_out, half_out, 0
+    )
+    count_rows = jnp.broadcast_to(counts[:, None, None], (counts.shape[0], 1, PAIR))
+    early_x = far_bits[:1] + [0] + far_bits[1:] + [1]
+    late_y = far_bits[:-1] + [0] + far_bits[-1:] + [1]
+    gathers = [
+        (jnp.concatenate([hyper_input, norm_lanes, digit_lanes], axis=1), late_y),
+        (jnp.concatenate([hyper_output, hyper_expand], axis=1), late_y),
+        (hyper_reduce, early_x),
+    ]
+    gather_held = [x for x, _ in gathers]
+
+    def send(which, at):
+        return swap(gather_held[which], 1 << gathers[which][1][at], devices)
+
+    def join(which, came, at):
+        order = gathers[which][1]
+        return gather_join(gather_held[which], came, order[at], order[:at], me)
+
+    for at in range(bits - 3):
+        gather_held = [join(which, send(which, at), at) for which in range(3)]
+        if at == bits - 4:
+            gather_held, key_near, query_slice, output_slice, count_rows = lax.optimization_barrier(
+                (gather_held, key_near, query_slice, output_slice, count_rows)
+            )
+            key_far = swap(key_near, 2, devices)
+    later_came = [send(which, bits - 3) for which in (1, 2)]
+    gather_held[0] = join(0, send(0, bits - 3), bits - 3)
+    begun = gather_held[:1]
+    in_held = join(0, send(0, bits - 2), bits - 2)
+    in_held, later_came = lax.optimization_barrier((in_held, later_came))
+    gather_held = [in_held] + [join(which, came, bits - 3) for which, came in zip((1, 2), later_came)]
+    later_came = [send(which, bits - 2) for which in (1, 2)]
+    in_came = send(0, bits - 1)
+    in_weight = join(0, in_came, bits - 1)
+    small = gather_join(
+        in_held[:, in_width:], in_came[:, in_width:], late_y[-1], late_y[:-1], me
+    )
+    embed_full = lax.all_gather(embed_weight, ("dp", "mp"), axis=0, tiled=True)
+    norm_rows = small[:, :8].astype(jnp.float32).T
+    digit_at = PAIR
+    all_digits = small[:, digit_at : digit_at + digit_width].reshape(devices, 2, 2 * block)
+    all_digits = all_digits.astype(jnp.int32)
+    asked = all_digits[:, 0] * PAIR + all_digits[:, 1]
+
+    query_slice, *_ = lax.optimization_barrier((query_slice, *begun))
+    query_near = swap(query_slice, 1, devices)
+
+    def by_side(own, other):
+        return [jnp.where(side == 0, own, other), jnp.where(side == 0, other, own)]
+
     other_base = (1 - mp_index) * kv_local
     head_order = [mp_index * kv_local, mp_index * kv_local + 1, other_base + core, other_base + 1 - core]
 
-    slots_done = slot_attention(0, None, pieces, counts, in_weight, norm_rows)
-    slots_done[2], later_came, asked, key_other = lax.optimization_barrier(
-        (slots_done[2], later_came, asked, key_other)
-    )
-    later_held = [
-        gather_join(held, came, spread_order[-3], me, devices)
-        for held, came in zip(later_held, later_came)
-    ]
-    later_came = [gather_send(x, spread_order[-2], devices) for x in later_held]
-    slots_done = slot_attention(1, slots_done, pieces, counts, in_weight, norm_rows)
-    slots_done[2], later_came, embed_full, query_near[0] = lax.optimization_barrier(
-        (slots_done[2], later_came, embed_full, query_near[0])
-    )
-    later_held = [
-        gather_join(held, came, spread_order[-2], me, devices)
-        for held, came in zip(later_held, later_came)
-    ]
-    slot_mixed, slot_probs, hyper_attended, lead_rows = slots_done
-    wide_weight, reduce_weight = [
-        gather_end(gather_step(held, spread_order[-1], me, devices)) for held in later_held
-    ]
-    hyper_attended, query_near[1] = lax.optimization_barrier((hyper_attended, query_near[1]))
-    query_far = [swap(x, 2, devices) for x in query_near]
-    output_near, *_ = lax.optimization_barrier((frozen_output_weight, *query_near))
-    output_near = lax.dynamic_slice_in_dim(output_near, core * query_cut, query_cut, 0)
-    half_out = output_near.shape[0] // 2
-    output_near = [swap(output_near[:half_out], 1, devices), swap(output_near[half_out:], 1, devices)]
+    slot_mixed, slot_probs, hyper_attended, lead_rows = slot_attention(
+        pieces, count_rows, in_weight, norm_rows
+    )
+    asked, _ = lax.optimization_barrier((asked, hyper_attended))
+    hyper_attended, embed_full, later_came, query_near = lax.optimization_barrier(
+        (hyper_attended, embed_full, later_came, query_near)
+    )
+    last = late_y[-1]
+
+    def joined(which, parts):
+        order = gathers[which][1]
+        halves = [gather_join(*parts[at : at + 2], order[-2], order[:-2], me) for at in (0, 2)]
+        return gather_join(*halves, last, order[:-1], me)
+
+    later_parts = [(gather_held[which], came) for which, came in zip((1, 2), later_came)]
+    later_parts = [(*own, *[swap(x, 1 << last, devices) for x in own]) for own in later_parts]
+    together = hyper_input.shape[0] * 2 % 16 == 0
+    if together:
+        forward_weights = later_parts
+    else:
+        forward_weights = [[joined(which, later_parts[which - 1])] for which in (1, 2)]
+    query_far_row = swap(query_near, 4, devices)
+    output_slice, _ = lax.optimization_barrier((output_slice, query_near))
+    output_near = swap(output_slice, 1, devices)
     pooled, hyper_hidden = units_forward(
-        hyper_attended, lead_rows, wide_weight, reduce_weight, norm_rows
-    )
-    pooled, output_near[0] = lax.optimization_barrier((pooled, output_near[0]))
-    pair_weight = jnp.where(
-        lead,
-        jnp.concatenate([key_own, key_other], axis=1),
-        jnp.concatenate([key_other, key_own], axis=1),
-    )
+        devices // 8, jnp.stack([core, side]), hyper_attended, lead_rows, *forward_weights, norm_rows
+    )
+    _, query_far_row = lax.optimization_barrier((pooled, query_far_row))
     present, standing = asked_of_me(asked, me, local_vocab)
     own_rank, own_owner = own_route(lax.dynamic_index_in_dim(asked, me, 0, False), local_vocab)
     most = jnp.max(jnp.sum(present.astype(jnp.int32), axis=1))
@@ -1164,9 +1209,12 @@
         return (to_low(picked), came)
 
     chosen_own, came = fetch(0)
-    chosen_own, came, pair_weight, output_near[1], query_far = lax.optimization_barrier(
-        (chosen_own, came, pair_weight, output_near[1], query_far)
-    )
+    query_near = by_side(query_near, query_far_row)
+    query_far = [swap(x, 2, devices) for x in query_near]
+    chosen_own, came, query_far, output_near = lax.optimization_barrier(
+        (chosen_own, came, query_far, output_near)
+    )
+    output_far_row = swap(output_near, 4, devices)
     needs = came.reshape(devices, capacity, pooled.shape[1])[:, capacity - 1, 0]
     rounds = jnp.max(needs.astype(jnp.float32)).astype(jnp.int32)
     chosen_own = lax.fori_loop(1, rounds, lambda turn, chosen: chosen + fetch(turn)[0], chosen_own)
@@ -1180,14 +1228,17 @@
 
     other_at = (1 - mp_index, 2 + mp_index)
     query_weights = (frozen_query_weight, *query_near, *query_far)
+    pair_weights = (key_own, key_near, key_far)
     own_info = jnp.stack(own_at).astype(jnp.int32)
     other_info = jnp.stack(other_at).astype(jnp.int32)
     pair_pre, embedded, queries = project(
-        own_info, chosen_own, embed_full, attention_gain, pair_weight, query_weights, None
+        own_info, chosen_own, embed_full, attention_gain, pair_weights, query_weights, None
     )
     (pair_pre,) = project(
-        other_info, chosen_other, embed_full, attention_gain, pair_weight, (), pair_pre
-    )
+        other_info, chosen_other, embed_full, attention_gain, pair_weights, (), pair_pre
+    )
+    pair_pre, output_far_row = lax.optimization_barrier((pair_pre, output_far_row))
+    output_near = by_side(output_near, output_far_row)
     output_far = [swap(x, 2, devices) for x in output_near]
     output_weights = (frozen_output_weight, *output_near, *output_far)
     spans = (2 * block, length)
@@ -1201,15 +1252,13 @@
         flat, lows[part], sums[part] = attention_forward(
             infos[part], queries, pair_pre, tables, part, spans[part]
         )
-        if part == 0:
-            flat, second_other[1] = lax.optimization_barrier((flat, second_other[1]))
         hidden_parts[part], second_low[part] = output_project(
             part, flat, embedded, dense_gain, output_weights
         )
         second_other[part] = swap(second_low[part], 1, devices)
         pair_pre, second_low[part] = lax.optimization_barrier((pair_pre, second_low[part]))
 
-    second_low = list(lax.optimization_barrier(tuple(second_low)))
+    second_low, second_other[1] = lax.optimization_barrier((second_low, second_other[1]))
     dense_rows = [None, None]
     second_came = [None, None]
     for part in (1, 0):
@@ -1261,8 +1310,8 @@
     pair_grads[0], *dense_came = lax.optimization_barrier((pair_grads[0], *dense_came))
 
     embedded_grad_low, token_grad = embed_backward(
-        own_info, query_grad, pair_own, came_long, came_short, tables, grad_hidden, embedded,
-        attention_gain, embed_full, query_weights, pair_weight,
+        jnp.stack([*own_at, *head_order]).astype(jnp.int32), query_grad, pair_own, came_long, came_short, tables, grad_hidden, embedded,
+        attention_gain, embed_full, query_weights, pair_weights,
     )
     own_out = []
     other_out = []
@@ -1273,6 +1322,8 @@
         other_out.append(to_low(kept[block:] + arrived[:block]))
     model_out = ordered_blocks(lead, own_out, other_out)
     embed_grad = to_low(matmul_first(chosen_own, embedded_grad_low))
+    _, later_parts = lax.optimization_barrier((token_grad, later_parts))
+    wide_weight, reduce_weight = [joined(which, later_parts[which - 1]) for which in (1, 2)]
 
     def give_back(turn, total):
         taker = taker_choice(own_rank, own_owner, turn, capacity, devices)
@@ -1280,30 +1331,34 @@
         came = exchange(leaving)
         return total + matmul_first(sender_choice(present, standing, turn, capacity), came)
 
-    embed_start = scatter_start(embed_grad, devices)
     grad_pooled = give_back(0, jnp.zeros(pooled.shape, jnp.float32))
     grad_pooled = lax.fori_loop(1, rounds, give_back, grad_pooled)
 
-    back_order = [[bit] for bit in [1, 0] + far_bits[::-1]]
-    embed_held = scatter_step(embed_start, back_order[0], me, devices)
+    back_order = [1, 0] + far_bits[::-1]
+
+    def scatter(held, order, at):
+        return scatter_send(held, order[at], order[at + 1 :], me, devices)
+
+    embed_held = scatter_add(*scatter(embed_grad, back_order, 0))
     embed_held, grad_pooled = lax.optimization_barrier((embed_held, grad_pooled))
-    embed_held = scatter_step(embed_held, back_order[1], me, devices)
+    embed_held = scatter_add(*scatter(embed_held, back_order, 1))
     hidden_grad, attended_grad, wide_grad, reduce_grad, later_norms = units_backward(
         grad_pooled, hyper_hidden, hyper_attended, wide_weight, reduce_weight, norm_rows
     )
     hidden_grad, embed_held = lax.optimization_barrier((hidden_grad, embed_held))
-    held = [embed_held, scatter_start(wide_grad, devices), scatter_start(reduce_grad, devices)]
-    turned_order = [back_order[0], back_order[2], back_order[1]] + back_order[3:]
-    orders = [back_order[2:], back_order, turned_order]
+    held = [embed_held, wide_grad, reduce_grad]
+    turned_order = [back_order[0], back_order[2], back_order[3], back_order[1]] + back_order[4:]
+    orders = [back_order, back_order, turned_order]
+    ahead = [2, 0, 0]
 
     def depart(at):
         return [
-            scatter_send(x, order[at], me, devices) if at < len(order) else (x, [])
-            for x, order in zip(held, orders)
+            scatter(x, order, at + skip) if at + skip < bits else (x, None)
+            for x, order, skip in zip(held, orders, ahead)
         ]
 
     def arrive(moving):
-        return [scatter_add(*x) for x in moving]
+        return [x if came is None else scatter_add(x, came) for x, came in moving]
 
     slots_saved = (pieces, slot_mixed, slot_probs)
     slots_held = (None, None, later_norms)
@@ -1315,13 +1370,16 @@
         slots_held, moving = lax.optimization_barrier((tuple(slots_held), moving))
         held = arrive(moving)
     pieces_grad, input_grad, _ = slots_held
-    input_held = scatter_start(input_grad, devices)
-    for at, step in enumerate(back_order):
-        moving = depart(SLOT_PARTS + at)
-        input_held = scatter_step(input_held, step, me, devices)
-        _, moving = lax.optimization_barrier((input_held, moving))
-        held = arrive(moving)
-    embed_own, wide_own, reduce_own, input_own = [scatter_end(x) for x in (*held, input_held)]
+    input_held = input_grad
+    moving = depart(SLOT_PARTS)
+    for at in range(bits):
+        input_held = scatter_add(*scatter(input_held, back_order, at))
+        if at > 0:
+            _, moving = lax.optimization_barrier((input_held, moving))
+            held = arrive(moving)
+            moving = depart(SLOT_PARTS + at)
+    held = arrive(moving)
+    embed_own, wide_own, reduce_own, input_own = (*held, input_held)
     out_width = hyper_output.shape[1]
     return (
         model_out,

time: 645 us -> 613 us (0.950)
  Pallas kernels: 343 us -> 321 us
  waiting for transfers between devices: 95 us -> 81.3 us
    all_to_all x2, waiting for transfers between devices: 29.9 us -> 11.9 us  [exchange(): return lax.all_to_all(value, ('dp', 'mp'), 0, 0, tiled=True)]
    pallas_call x2, Pallas kernels: 43.5 us -> 33.3 us  [attention_forward(): pl.pallas_call(attention_forward_kernel, grid_spec=pltpu.PrefetchScalarGr...]
    pallas_call x2, Pallas kernels: 59.6 us -> 49.6 us  [attention_backward(): pl.pallas_call(attention_backward_kernel, grid_spec=pltpu.PrefetchScalarG...]
    unnamed x156 -> x123, local copies, waits for them, and re-layouts: 24.6 us -> 15.5 us
    dynamic_slice x15 -> x19, local copies, waits for them, and re-layouts: 3.67 us -> 11.2 us  [the longest x16 6.54 us: part(): return lax.dynamic_slice_in_dim(parts, at, 1, 1).reshape(rows // 2, width)]
    select_n x16 -> x23, other arithmetic: 21.2 us -> 27.9 us  [the longest x21 22.4 us: gather_join(): jnp.where(me >> bit & 1 == 1, jnp.concatenate([arrived, held], axis=1), j...]
    ppermute x53 -> x56, waiting for transfers between devices: 65.1 us -> 69.4 us  [swap(): lax.ppermute(value, ('dp', 'mp'), [(d, d ^ mask) for d in range(devices)])]
    ppermute x53 -> x56, starting transfers between devices: 60.2 us -> 63.9 us  [swap(): lax.ppermute(value, ('dp', 'mp'), [(d, d ^ mask) for d in range(devices)])]
  transfers between devices with their start and end apart: 56 -> 59, of which waited for: 19 -> 17; matrix products, arithmetic and copies ran while one was open for 12% -> 14% of each run, Pallas kernels for 51% -> 52%
where the time goes in v4:
time: 613 us; the launch traced here: 603 us
  Pallas kernels  321 us (52%)
  waiting for transfers between devices  81.3 us (13%)
  starting transfers between devices  72.2 us (12%)
  other arithmetic  57.8 us (9%)
  local copies, waits for them, and re-layouts  40.5 us (7%)
  between operations  16.9 us (3%)
  matrix products  12.6 us (2%)
    pallas_call x2, Pallas kernels, feed_forward(): pl.pallas_call(lambda info, *refs: feed_forward_kernel(*refs), grid_spec=...  95.1 us
    ppermute x56, waiting for transfers between devices, swap(): lax.ppermute(value, ('dp', 'mp'), [(d, d ^ mask) for d in range(devices)])  69.4 us
    ppermute x56, starting transfers between devices, swap(): lax.ppermute(value, ('dp', 'mp'), [(d, d ^ mask) for d in range(devices)])  63.9 us
    pallas_call x2, Pallas kernels, attention_backward(): pl.pallas_call(attention_backward_kernel, grid_spec=pltpu.PrefetchScalarG...  49.6 us
    pallas_call x2, Pallas kernels, slot_backward(): pl.pallas_call(functools.partial(slot_backward_kernel, first, last), grid...  36.5 us
    pallas_call x2, Pallas kernels, attention_forward(): pl.pallas_call(attention_forward_kernel, grid_spec=pltpu.PrefetchScalarGr...  33.3 us
    select_n x21, other arithmetic, gather_join(): jnp.where(me >> bit & 1 == 1, jnp.concatenate([arrived, held], axis=1), j...  22.4 us
    pallas_call x2, Pallas kernels, project(): pl.pallas_call(functools.partial(project_kernel, more), grid_spec=pltpu.P...  19.9 us
  transfers between devices with their start and end apart: 59, of which 17 were waited for; matrix products, arithmetic and copies ran while one was open for 14% of the time, Pallas kernels for 52%

profile of v4, /device:TPU:0, one launch (start us, length us, event | category | flops | bytes accessed | tf_op | source)
XLA Modules:
  0.0 603.0 jit_solution(6377385471629245047)
XLA Ops:
  11.2 4.0 collective-permute-start
  16.8 2.9 collective-permute-start.4
  24.0 2.4 constant_dynamic-slice_fusion.24
  26.3 2.3 dynamic_slice.164
  31.6 3.3 collective-permute-done.1
  34.9 3.6 collective-permute-done.5
  43.2 4.5 collective-permute-done.7
  52.5 5.7 collective-permute-done.8
  62.1 2.3 maximum_select_fusion.9
  72.0 18.9 %slot_attention.1 = (bf16[4096,1536]{1,0:T(8,128)(2,1)}, f32[512,8,128]{2,1,0:T(8,128)S(1)}, bf16[512,512]{1,0:T(8,128)(2,1)S(1)}, f32[512,512]{1,0:T(8,128)S(1)}) custom-call(bf16[512,8,512]{2,1,0:T(8,128)(2,1)} %pieces_ref.5, s32[512,1,128]{2,1,0:T(1,128)S(1)} %broadcast_in_dim.30.counts_ref, bf16[512,1792]{1,0:T(8,128)(2,1)S(1)} %bitcast.182, ...), custom_call_target="tpu_custom_call" | custom-call | flops 2097152 | bytes 4096 | tf_op jit(solution)/shard_map/slot_attention/pallas_call | solution.py:395
  92.7 3.3 collective-permute-done.13.refs_5_
  96.6 5.0 compare_reduce_fusion
  104.7 7.6 %units_forward.1 = (bf16[512,512]{1,0:T(8,128)(2,1)S(1)}, f32[512,512]{1,0:T(8,128)}) custom-call(s32[2]{0:T(128)S(1)} %pad_add_fusion.2.places, bf16[512,512]{1,0:T(8,128)(2,1)S(1)} %copy-done.15, f32[512,512]{1,0:T(8,128)} %copy-done.13, bf16[128,2560]{1,0:T(8,128)(2,1)} %bitcast.40.refs_0_, bf16[128,2560]{1,0:T(8,128)(2,1)} %collective-permute-done.12.refs_1_, ...), custom_call_target="tpu_custom_call" | custom-call | flops 262144 | bytes 262144 | tf_op jit(solution)/shard_map/units_forward/pallas_call | solution.py:481
  114.8 3.9 all-to-all-start.2
  121.1 16.8 %collective-permute-done.19 = bf16[1024,512]{1,0:T(8,128)(2,1)} collective-permute-done((bf16[1024,512]{1,0:T(8,128)(2,1)}, bf16[1024,512]{1,0:T(8,128)(2,1)}, u32[]{:S(2)}, u32[]{:S(2)}) %collective-permute-start.19) | collective-permute-done | bytes 1048608 | tf_op jit(solution)/shard_map/ppermute | solution.py:49
  137.9 3.0 broadcast_select_fusion.2
  142.1 2.8 all-to-all-done.2
  144.9 2.8 fusion.34
  147.7 7.6 %collective-permute-done.22 = bf16[256,2048]{1,0:T(8,128)(2,1)} collective-permute-done((bf16[256,2048]{1,0:T(8,128)(2,1)}, bf16[256,2048]{1,0:T(8,128)(2,1)}, u32[]{:S(2)}, u32[]{:S(2)}) %collective-permute-start.22) | collective-permute-done | bytes 1048608 | tf_op jit(solution)/shard_map/ppermute | solution.py:49
  160.9 14.1 %project.2 = (f32[1024,512]{1,0:T(8,128)}, bf16[512,2048]{1,0:T(8,128)(2,1)}, f32[512,2048]{1,0:T(8,128)}) custom-call(s32[2]{0:T(128)S(1)} %pad_add_fusion.3.info, bf16[512,512]{1,0:T(8,128)(2,1)} %get-tuple-element.255.chosen_ref, bf16[512,2048]{1,0:T(8,128)(2,1)} %all-gather.2.cloned.1.call-done.embed_ref, f32[1,2048]{1,0:T(1,128)S(1)} %bitcast.191, ...), custom_call_target="tpu_custom_call" | custom-call | flops 1073741824 | bytes 1048576 | tf_op jit(solution)/shard_map/project/pallas_call | solution.py:827
  176.7 5.9 project.3.pair_ref
  182.6 2.5 broadcast_select_fusion
  187.2 20.8 %attention_forward.2 = (bf16[256,2048]{1,0:T(8,128)(2,1)S(1)}, bf16[256,2048]{1,0:T(8,128)(2,1)S(1)}, f32[4,8,256]{2,1,0:T(8,128)S(1)}) custom-call(s32[5]{0:T(128)S(1)} %stack.84.info, f32[512,2048]{1,0:T(8,128)} %get-tuple-element.263.query_ref, f32[1024,512]{1,0:T(8,128)S(1)} %copy-done.7, f32[1024,128]{1,0:T(8,128)S(1)} %copy-done.20, ...), custom_call_target="tpu_custom_call" | custom-call | flops 21474836480 | bytes 8388608 | tf_op jit(solution)/shard_map/attention_forward/pallas_call | solution.py:256
  209.1 6.7 %output_project.2 = (f32[256,2048]{1,0:T(8,128)}, bf16[256,2048]{1,0:T(8,128)(2,1)S(1)}) custom-call(bf16[256,2048]{1,0:T(8,128)(2,1)S(1)} %get-tuple-element.264.rows_ref, bf16[512,2048]{1,0:T(8,128)(2,1)} %get-tuple-element.265.embedded_ref, f32[1,2048]{1,0:T(1,128)S(1)} %bitcast.187, bf16[1024,2048]{1,0:T(8,128)(2,1)} %near_ref.8, ...), custom_call_target="tpu_custom_call" | custom-call | flops 4294967296 | bytes 12582912 | tf_op jit(solution)/shard_map/output_project/pallas_call | solution.py:870
  216.5 12.5 %attention_forward.3 = (bf16[256,2048]{1,0:T(8,128)(2,1)S(1)}, bf16[256,2048]{1,0:T(8,128)(2,1)S(1)}, f32[4,8,256]{2,1,0:T(8,128)S(1)}) custom-call(s32[5]{0:T(128)S(1)} %stack.85.info, f32[512,2048]{1,0:T(8,128)} %get-tuple-element.263.query_ref, f32[1024,512]{1,0:T(8,128)S(1)} %copy-done.8, f32[1024,128]{1,0:T(8,128)S(1)} %copy-done.20, ...), custom_call_target="tpu_custom_call" | custom-call | flops 10737418240 | bytes 8388608 | tf_op jit(solution)/shard_map/attention_forward/pallas_call | solution.py:256
  229.0 7.0 %output_project.3 = (f32[256,2048]{1,0:T(8,128)}, bf16[256,2048]{1,0:T(8,128)(2,1)S(1)}) custom-call(bf16[256,2048]{1,0:T(8,128)(2,1)S(1)} %get-tuple-element.269.rows_ref, bf16[512,2048]{1,0:T(8,128)(2,1)} %get-tuple-element.265.embedded_ref, f32[1,2048]{1,0:T(1,128)S(1)} %bitcast.188, bf16[1024,2048]{1,0:T(8,128)(2,1)} %near_ref.8, ...), custom_call_target="tpu_custom_call" | custom-call | flops 4294967296 | bytes 12582912 | tf_op jit(solution)/shard_map/output_project/pallas_call | solution.py:870
  236.1 4.5 collective-permute-start.30
  240.9 47.5 %feed_forward.2 = (bf16[512,2048]{1,0:T(8,128)(2,1)S(1)}, bf16[512,2048]{1,0:T(8,128)(2,1)}) custom-call(s32[2]{0:T(128)S(1)} %pad_add_fusion.info, bf16[256,2048]{1,0:T(8,128)(2,1)S(1)} %get-tuple-element.273.refs_0_, bf16[256,2048]{1,0:T(8,128)(2,1)S(1)} %collective-permute-done.28.refs_1_, bf16[1024,2048]{1,0:T(8,128)(2,1)} %rising_ref.3, ...), custom_call_target="tpu_custom_call" | custom-call | flops 50197430272 | bytes 69206016 | tf_op jit(solution)/shard_map/feed_forward/pallas_call | solution.py:742
  290.3 47.6 %feed_forward.3 = (bf16[512,2048]{1,0:T(8,128)(2,1)S(1)}, bf16[512,2048]{1,0:T(8,128)(2,1)}) custom-call(s32[2]{0:T(128)S(1)} %pad_add_fusion.4.info, bf16[256,2048]{1,0:T(8,128)(2,1)S(1)} %get-tuple-element.277.refs_0_, bf16[256,2048]{1,0:T(8,128)(2,1)S(1)} %collective-permute-done.30.refs_1_, bf16[1024,2048]{1,0:T(8,128)(2,1)} %rising_ref.3, ...), custom_call_target="tpu_custom_call" | custom-call | flops 50197430272 | bytes 69206016 | tf_op jit(solution)/shard_map/feed_forward/pallas_call | solution.py:742
  342.9 7.3 %hidden_backward.2 = (f32[256,2048]{1,0:T(8,128)}, bf16[256,2048]{1,0:T(8,128)(2,1)S(1)}) custom-call(s32[5]{0:T(128)S(1)} %stack.84.info, bf16[256,2048]{1,0:T(8,128)(2,1)S(1)} %get-tuple-element.284.here_ref, bf16[256,2048]{1,0:T(8,128)(2,1)S(1)} %collective-permute-done.29.came_ref, f32[256,2048]{1,0:T(8,128)} %get-tuple-element.275.refs_4_.hidden_ref, ...), custom_call_target="tpu_custom_call" | custom-call | flops 4294967296 | bytes 14680064 | tf_op jit(solution)/shard_map/hidden_backward/pallas_call | solution.py:909
  350.2 34.0 %attention_backward.2 = (bf16[512,2048]{1,0:T(8,128)(2,1)S(1)}, f32[4,1024,128]{2,1,0:T(8,128)}) custom-call(s32[5]{0:T(128)S(1)} %stack.84.info, bf16[256,2048]{1,0:T(8,128)(2,1)S(1)} %copy-done.26, bf16[256,2048]{1,0:T(8,128)(2,1)S(1)} %get-tuple-element.286.grad_ref, f32[4,8,256]{2,1,0:T(8,128)S(1)} %get-tuple-element.287.lse_ref, f32[1024,512]{1,0:T(8,128)} %copy-done.6, ...), custom_call_target="tpu_custom_call" | custom-call | flops 53687091200 | bytes 8388608 | tf_op jit(solution)/shard_map/attention_backward/pallas_call | solution.py:292
  390.5 7.3 %hidden_backward.3 = (f32[256,2048]{1,0:T(8,128)}, bf16[256,2048]{1,0:T(8,128)(2,1)S(1)}) custom-call(s32[5]{0:T(128)S(1)} %stack.85.info, bf16[256,2048]{1,0:T(8,128)(2,1)S(1)} %get-tuple-element.290.here_ref, bf16[256,2048]{1,0:T(8,128)(2,1)S(1)} %collective-permute-done.31.came_ref, f32[256,2048]{1,0:T(8,128)} %get-tuple-element.278.refs_4_.hidden_ref, ...), custom_call_target="tpu_custom_call" | custom-call | flops 4294967296 | bytes 14680064 | tf_op jit(solution)/shard_map/hidden_backward/pallas_call | solution.py:909
  397.8 15.7 %attention_backward.3 = (bf16[512,2048]{1,0:T(8,128)(2,1)}, f32[4,512,128]{2,1,0:T(8,128)S(1)}) custom-call(s32[5]{0:T(128)S(1)} %stack.85.info, bf16[256,2048]{1,0:T(8,128)(2,1)S(1)} %copy-done.24, bf16[256,2048]{1,0:T(8,128)(2,1)S(1)} %get-tuple-element.292.grad_ref, f32[4,8,256]{2,1,0:T(8,128)S(1)} %get-tuple-element.293.lse_ref, ...), custom_call_target="tpu_custom_call", output_to_operand_aliasing={{0}: (9, {})} | custom-call | flops 26843545600 | bytes 8388608 | tf_op jit(solution)/shard_map/attention_backward/pallas_call | solution.py:292
  413.6 6.6 %collective-permute-start.35 = (bf16[4,256,128]{2,1,0:T(8,128)(2,1)S(1)}, bf16[4,256,128]{2,1,0:T(8,128)(2,1)S(1)}, u32[]{:S(2)}, u32[]{:S(2)}) collective-permute-start(bf16[4,256,128]{2,1,0:T(8,128)(2,1)S(1)} %dynamic-slice_convert_fusion.9), channel_id=1, source_target_pairs={{0,1},{1,0},{2,3},{3,2},{4,5},{5,4},{6,7},{7,6},{8,9},{9,8},{10,11... | collective-permute-start | bytes 786440 | tf_op jit(solution)/shard_map/ppermute | solution.py:49
  420.3 6.6 %collective-permute-done.35.short_ref = bf16[4,256,128]{2,1,0:T(8,128)(2,1)S(1)} collective-permute-done((bf16[4,256,128]{2,1,0:T(8,128)(2,1)S(1)}, bf16[4,256,128]{2,1,0:T(8,128)(2,1)S(1)}, u32[]{:S(2)}, u32[]{:S(2)}) %collective-permute-start.35) | collective-permute-done | bytes 262176 | tf_op jit(solution)/shard_map/ppermute | solution.py:49
  427.0 17.0 %embed_backward.1 = (bf16[512,2048]{1,0:T(8,128)(2,1)}, bf16[512,512]{1,0:T(8,128)(2,1)S(1)}) custom-call(s32[6]{0:T(128)S(1)} %stack.87.info, bf16[512,2048]{1,0:T(8,128)(2,1)} %get-tuple-element.303.query_ref, f32[4,512,128]{2,1,0:T(8,128)S(1)} %pad_maximum_fusion.1.own_ref, bf16[4,512,128]{2,1,0:T(8,128)(2,1)S(1)} %collective-permute-done.32.came_ref, ...), custom_call_target="tpu_custom_call" | custom-call | flops 12884901888 | bytes 20971520 | tf_op jit(solution)/shard_map/embed_backward/pallas_call | solution.py:979
  443.9 3.1 convolution_convert_fusion
  450.5 3.1 maximum_select_fusion.4
  455.4 4.4 all-to-all-start.3
  473.9 3.0 convert_add_fusion.1
  476.9 9.1 %all-to-all-done.3 = bf16[32,32,512]{2,1,0:T(8,128)(2,1)} async-done(((bf16[32,32,512]{2,1,0:T(8,128)(2,1)}), bf16[32,32,512]{2,1,0:T(8,128)(2,1)}, u32[]{:S(2)}, u32[]{:S(2)}) %all-to-all-start.3) | async-done | bytes 1048608 | tf_op jit(solution)/shard_map/all_to_all | solution.py:1041
  486.1 3.1 fusion.33
  493.4 15.0 %units_backward.1 = (f32[512,512]{1,0:T(8,128)S(1)}, bf16[512,512]{1,0:T(8,128)(2,1)S(1)}, bf16[512,2560]{1,0:T(8,128)(2,1)}, bf16[2048,512]{1,0:T(8,128)(2,1)S(1)}, f32[8,512]{1,0:T(8,128)S(1)}) custom-call(f32[512,512]{1,0:T(8,128)} %get-tuple-element.310.grad_ref, f32[512,512]{1,0:T(8,128)S(1)} %copy-done.19, bf16[512,512]{1,0:T(8,128)(2,1)S(1)} %copy-done.16, ...), custom_call_target="tpu_custom_call" | custom-call | flops 17716740096 | bytes 16777216 | tf_op jit(solution)/shard_map/units_backward/pallas_call | solution.py:556
  508.4 3.0 constant_dynamic-slice_fusion.14
  517.4 17.9 %slot_backward.2 = (bf16[512,8,512]{2,1,0:T(8,128)(2,1)}, f32[512,1536]{1,0:T(8,128)}, f32[8,512]{1,0:T(8,128)S(1)}) custom-call(bf16[512,8,512]{2,1,0:T(8,128)(2,1)} %pieces_ref.5, bf16[4096,1536]{1,0:T(8,128)(2,1)} %get-tuple-element.301.mixed_ref, f32[512,8,128]{2,1,0:T(8,128)S(1)} %get-tuple-element.302.probs_ref, ...), custom_call_target="tpu_custom_call" | custom-call | flops 1048576 | bytes 2048 | tf_op jit(solution)/shard_map/slot_backward/pallas_call | solution.py:667
  540.5 18.6 %slot_backward.3 = (bf16[512,8,512]{2,1,0:T(8,128)(2,1)}, bf16[512,1664]{1,0:T(8,128)(2,1)S(1)}, f32[8,512]{1,0:T(8,128)}) custom-call(bf16[512,8,512]{2,1,0:T(8,128)(2,1)} %pieces_ref.5, bf16[4096,1536]{1,0:T(8,128)(2,1)} %get-tuple-element.301.mixed_ref, f32[512,8,128]{2,1,0:T(8,128)} %copy-done.3, ...), custom_call_target="tpu_custom_call", output_to_operand_aliasing={{0}: (8, {})} | custom-call | flops 1048576 | bytes 2048 | tf_op jit(solution)/shard_map/slot_backward/pallas_call | solution.py:667
  565.0 9.3 %collective-permute-done.45 = bf16[128,1664]{1,0:T(8,128)(2,1)S(1)} collective-permute-done((bf16[128,1664]{1,0:T(8,128)(2,1)S(1)}, bf16[128,1664]{1,0:T(8,128)(2,1)S(1)}, u32[]{:S(2)}, u32[]{:S(2)}) %collective-permute-start.45) | collective-permute-done | bytes 426016 | tf_op jit(solution)/shard_map/ppermute | solution.py:49
  578.9 2.2 collective-permute-done.46
  (360 shorter events, 128.0 us)
Async XLA Ops:
  7.2 88.8 %all-gather.2.cloned.1.call-start = ((), (), s32[]{:S(2)}) async-start(), calls=%async_computation.4 | async-start | bytes 2162688 | tf_op jit(solution)/shard_map/all_gather | solution.py:1153
  11.2 17.4 %collective-permute-start = (bf16[16,1792]{1,0:T(8,128)(2,1)}, bf16[16,1792]{1,0:T(8,128)(2,1)S(1)}, u32[]{:S(2)}, u32[]{:S(2)}) collective-permute-start(bf16[16,1792]{1,0:T(8,128)(2,1)} %get-tuple-element.485), channel_id=1, source_target_pairs={{0,16},{1,17},{2,18},{3,19},{4,20},{5,21},{6,22},{7,23},{8,24},{9,... | collective-permute-start | bytes 172040 | tf_op jit(solution)/shard_map/ppermute | solution.py:49
  16.8 14.2 %collective-permute-start.2 = (bf16[16,2560]{1,0:T(8,128)(2,1)S(1)}, bf16[16,2560]{1,0:T(8,128)(2,1)S(1)}, u32[]{:S(2)}, u32[]{:S(2)}) collective-permute-start(bf16[16,2560]{1,0:T(8,128)(2,1)S(1)} %constant_dynamic-update-slice_fusion), channel_id=1, source_target_pairs={{0,16},{1,17},{2,18},{3,19},{4,20},{5,21},{6,22},{7,23},{8,24},{9,... | collective-permute-start | bytes 245768 | tf_op jit(solution)/shard_map/ppermute | solution.py:49
  16.8 13.5 %collective-permute-start.4 = (bf16[64,512]{1,0:T(8,128)(2,1)}, bf16[64,512]{1,0:T(8,128)(2,1)S(1)}, u32[]{:S(2)}, u32[]{:S(2)}) collective-permute-start(bf16[64,512]{1,0:T(8,128)(2,1)} %param.31), channel_id=1, source_target_pairs={{0,16},{1,17},{2,18},{3,19},{4,20},{5,21},{6,22},{7,23},{8,24},{9,... | collective-permute-start | bytes 196616 | tf_op jit(solution)/shard_map/ppermute | solution.py:49
  22.3 17.7 %collective-permute-start.6 = (bf16[2048,128]{1,0:T(8,128)(2,1)S(1)}, bf16[2048,128]{1,0:T(8,128)(2,1)S(1)}, u32[]{:S(2)}, u32[]{:S(2)}) collective-permute-start(bf16[2048,128]{1,0:T(8,128)(2,1)S(1)} %constant_dynamic-slice_fusion.25), channel_id=1, source_target_pairs={{0,1},{1,0},{2,3},{3,2},{4,5},{5,4},{6,7},{7,6},{8,9},{9,8},{10,11... | collective-permute-start | bytes 1572872 | tf_op jit(solution)/shard_map/ppermute | solution.py:49
  30.4 8.2 %collective-permute-start.5 = (bf16[128,512]{1,0:T(8,128)(2,1)S(1)}, bf16[128,512]{1,0:T(8,128)(2,1)S(1)}, u32[]{:S(2)}, u32[]{:S(2)}) collective-permute-start(bf16[128,512]{1,0:T(8,128)(2,1)S(1)} %maximum_select_fusion.18), channel_id=1, source_target_pairs={{0,1},{1,0},{2,3},{3,2},{4,5},{5,4},{6,7},{7,6},{8,9},{9,8},{10,11... | collective-permute-start | bytes 393224 | tf_op jit(solution)/shard_map/ppermute | solution.py:49
  31.1 8.2 %collective-permute-start.3 = (bf16[32,2560]{1,0:T(8,128)(2,1)S(1)}, bf16[32,2560]{1,0:T(8,128)(2,1)S(1)}, u32[]{:S(2)}, u32[]{:S(2)}) collective-permute-start(bf16[32,2560]{1,0:T(8,128)(2,1)S(1)} %maximum_select_fusion.16), channel_id=1, source_target_pairs={{0,8},{1,9},{2,10},{3,11},{4,12},{5,13},{6,14},{7,15},{8,0},{9,1},... | collective-permute-start | bytes 491528 | tf_op jit(solution)/shard_map/ppermute | solution.py:49
  47.8 10.4 %collective-permute-start.8 = (bf16[128,1792]{1,0:T(8,128)(2,1)S(1)}, bf16[128,1792]{1,0:T(8,128)(2,1)S(1)}, u32[]{:S(2)}, u32[]{:S(2)}) collective-permute-start(bf16[128,1792]{1,0:T(8,128)(2,1)S(1)} %bitcast.231), channel_id=1, source_target_pairs={{0,4},{1,5},{2,6},{3,7},{4,0},{5,1},{6,2},{7,3},{8,12},{9,13},{10,... | collective-permute-start | bytes 1376264 | tf_op jit(solution)/shard_map/ppermute | solution.py:49
  49.4 11.0 %collective-permute-start.9 = (bf16[64,2560]{1,0:T(8,128)(2,1)}, bf16[64,2560]{1,0:T(8,128)(2,1)}, u32[]{:S(2)}, u32[]{:S(2)}) collective-permute-start(bf16[64,2560]{1,0:T(8,128)(2,1)} %bitcast.16), channel_id=1, source_target_pairs={{0,1},{1,0},{2,3},{3,2},{4,5},{5,4},{6,7},{7,6},{8,9},{9,8},{10,11... | collective-permute-start | bytes 983048 | tf_op jit(solution)/shard_map/ppermute | solution.py:49
  50.9 9.5 %collective-permute-start.10 = (bf16[256,512]{1,0:T(8,128)(2,1)}, bf16[256,512]{1,0:T(8,128)(2,1)}, u32[]{:S(2)}, u32[]{:S(2)}) collective-permute-start(bf16[256,512]{1,0:T(8,128)(2,1)} %bitcast.21), channel_id=1, source_target_pairs={{0,8},{1,9},{2,10},{3,11},{4,12},{5,13},{6,14},{7,15},{8,0},{9,1},... | collective-permute-start | bytes 786440 | tf_op jit(solution)/shard_map/ppermute | solution.py:49
  60.4 8.2 %collective-permute-start.11 = (bf16[256,1792]{1,0:T(8,128)(2,1)S(1)}, bf16[256,1792]{1,0:T(8,128)(2,1)S(1)}, u32[]{:S(2)}, u32[]{:S(2)}) collective-permute-start(bf16[256,1792]{1,0:T(8,128)(2,1)S(1)} %bitcast.207), channel_id=1, source_target_pairs={{0,2},{1,3},{2,0},{3,1},{4,6},{5,7},{6,4},{7,5},{8,10},{9,11},{10,... | collective-permute-start | bytes 2752520 | tf_op jit(solution)/shard_map/ppermute | solution.py:49
  60.6 35.4 %collective-permute-start.14 = (bf16[1024,512]{1,0:T(8,128)(2,1)}, bf16[1024,512]{1,0:T(8,128)(2,1)}, u32[]{:S(2)}, u32[]{:S(2)}) collective-permute-start(bf16[1024,512]{1,0:T(8,128)(2,1)} %dynamic_slice.164), channel_id=1, source_target_pairs={{0,1},{1,0},{2,3},{3,2},{4,5},{5,4},{6,7},{7,6},{8,9},{9,8},{10,11... | collective-permute-start | bytes 3145736 | tf_op jit(solution)/shard_map/ppermute | solution.py:49
  64.4 31.6 %collective-permute-start.12 = (bf16[128,2560]{1,0:T(8,128)(2,1)}, bf16[128,2560]{1,0:T(8,128)(2,1)}, u32[]{:S(2)}, u32[]{:S(2)}) collective-permute-start(bf16[128,2560]{1,0:T(8,128)(2,1)} %bitcast.40.refs_0_), channel_id=1, source_target_pairs={{0,4},{1,5},{2,6},{3,7},{4,0},{5,1},{6,2},{7,3},{8,12},{9,13},{10,... | collective-permute-start | bytes 1966088 | tf_op jit(solution)/shard_map/ppermute | solution.py:49
  65.9 37.7 %collective-permute-start.15 = (bf16[128,2560]{1,0:T(8,128)(2,1)}, bf16[128,2560]{1,0:T(8,128)(2,1)}, u32[]{:S(2)}, u32[]{:S(2)}) collective-permute-start(bf16[128,2560]{1,0:T(8,128)(2,1)} %bitcast.40.refs_0_), channel_id=1, source_target_pairs={{0,2},{1,3},{2,0},{3,1},{4,6},{5,7},{6,4},{7,5},{8,10},{9,11},{10,... | collective-permute-start | bytes 1966088 | tf_op jit(solution)/shard_map/ppermute | solution.py:49
  68.1 27.9 %collective-permute-start.13 = (bf16[512,512]{1,0:T(8,128)(2,1)}, bf16[512,512]{1,0:T(8,128)(2,1)}, u32[]{:S(2)}, u32[]{:S(2)}) collective-permute-start(bf16[512,512]{1,0:T(8,128)(2,1)} %bitcast.43.refs_4_), channel_id=1, source_target_pairs={{0,4},{1,5},{2,6},{3,7},{4,0},{5,1},{6,2},{7,3},{8,12},{9,13},{10,... | collective-permute-start | bytes 1572872 | tf_op jit(solution)/shard_map/ppermute | solution.py:49
  68.6 35.0 %collective-permute-start.17 = (bf16[512,512]{1,0:T(8,128)(2,1)}, bf16[512,512]{1,0:T(8,128)(2,1)}, u32[]{:S(2)}, u32[]{:S(2)}) collective-permute-start(bf16[512,512]{1,0:T(8,128)(2,1)} %bitcast.43.refs_4_), channel_id=1, source_target_pairs={{0,2},{1,3},{2,0},{3,1},{4,6},{5,7},{6,4},{7,5},{8,10},{9,11},{10,... | collective-permute-start | bytes 1572872 | tf_op jit(solution)/shard_map/ppermute | solution.py:49
  103.2 34.7 %collective-permute-start.19 = (bf16[1024,512]{1,0:T(8,128)(2,1)}, bf16[1024,512]{1,0:T(8,128)(2,1)}, u32[]{:S(2)}, u32[]{:S(2)}) collective-permute-start(bf16[1024,512]{1,0:T(8,128)(2,1)} %collective-permute-done.14), channel_id=1, source_target_pairs={{0,4},{1,5},{2,6},{3,7},{4,0},{5,1},{6,2},{7,3},{8,12},{9,13},{10,... | collective-permute-start | bytes 3145736 | tf_op jit(solution)/shard_map/ppermute | solution.py:49
  114.8 30.1 %all-to-all-start.2 = ((bf16[32,32,512]{2,1,0:T(8,128)(2,1)}), bf16[32,32,512]{2,1,0:T(8,128)(2,1)}, u32[]{:S(2)}, u32[]{:S(2)}) async-start(bf16[32,32,512]{2,1,0:T(8,128)(2,1)} %select_convert_fusion.1), calls=%async_computation.2 | async-start | bytes 2097152 | tf_op jit(solution)/shard_map/all_to_all | solution.py:1041
  119.0 40.9 %collective-permute-start.24 = (bf16[2048,128]{1,0:T(8,128)(2,1)}, bf16[2048,128]{1,0:T(8,128)(2,1)}, u32[]{:S(2)}, u32[]{:S(2)}) collective-permute-start(bf16[2048,128]{1,0:T(8,128)(2,1)} %copy-done.9), channel_id=1, source_target_pairs={{0,2},{1,3},{2,0},{3,1},{4,6},{5,7},{6,4},{7,5},{8,10},{9,11},{10,... | collective-permute-start | bytes 1572872 | tf_op jit(solution)/shard_map/ppermute | solution.py:49
  119.4 35.9 %collective-permute-start.22 = (bf16[256,2048]{1,0:T(8,128)(2,1)}, bf16[256,2048]{1,0:T(8,128)(2,1)}, u32[]{:S(2)}, u32[]{:S(2)}) collective-permute-start(bf16[256,2048]{1,0:T(8,128)(2,1)} %constant_dynamic-slice_fusion.24), channel_id=1, source_target_pairs={{0,1},{1,0},{2,3},{3,2},{4,5},{5,4},{6,7},{7,6},{8,9},{9,8},{10,11... | collective-permute-start | bytes 3145736 | tf_op jit(solution)/shard_map/ppermute | solution.py:49
  140.9 14.4 %collective-permute-start.20 = (bf16[1024,512]{1,0:T(8,128)(2,1)}, bf16[1024,512]{1,0:T(8,128)(2,1)}, u32[]{:S(2)}, u32[]{:S(2)}) collective-permute-start(bf16[1024,512]{1,0:T(8,128)(2,1)} %get-tuple-element.478.refs_1_.mid_a), channel_id=1, source_target_pairs={{0,2},{1,3},{2,0},{3,1},{4,6},{5,7},{6,4},{7,5},{8,10},{9,11},{10,... | collective-permute-start | bytes 3145736 | tf_op jit(solution)/shard_map/ppermute | solution.py:49
  140.9 14.4 %collective-permute-start.21 = (bf16[1024,512]{1,0:T(8,128)(2,1)}, bf16[1024,512]{1,0:T(8,128)(2,1)}, u32[]{:S(2)}, u32[]{:S(2)}) collective-permute-start(bf16[1024,512]{1,0:T(8,128)(2,1)} %get-tuple-element.477.refs_2_.mid_b), channel_id=1, source_target_pairs={{0,2},{1,3},{2,0},{3,1},{4,6},{5,7},{6,4},{7,5},{8,10},{9,11},{10,... | collective-permute-start | bytes 3145736 | tf_op jit(solution)/shard_map/ppermute | solution.py:49
  157.4 25.2 %collective-permute-start.25 = (bf16[256,2048]{1,0:T(8,128)(2,1)}, bf16[256,2048]{1,0:T(8,128)(2,1)}, u32[]{:S(2)}, u32[]{:S(2)}) collective-permute-start(bf16[256,2048]{1,0:T(8,128)(2,1)} %collective-permute-done.22), channel_id=1, source_target_pairs={{0,4},{1,5},{2,6},{3,7},{4,0},{5,1},{6,2},{7,3},{8,12},{9,13},{10,... | collective-permute-start | bytes 3145736 | tf_op jit(solution)/shard_map/ppermute | solution.py:49
  159.0 16.1 %collective-permute-start.23 = (bf16[512,512]{1,0:T(8,128)(2,1)}, bf16[512,512]{1,0:T(8,128)(2,1)S(1)}, u32[]{:S(2)}, u32[]{:S(2)}) collective-permute-start(bf16[512,512]{1,0:T(8,128)(2,1)} %get-tuple-element.255.chosen_ref), channel_id=1, source_target_pairs={{0,1},{1,0},{2,3},{3,2},{4,5},{5,4},{6,7},{7,6},{8,9},{9,8},{10,11... | collective-permute-start | bytes 1572872 | tf_op jit(solution)/shard_map/ppermute | solution.py:49
  185.1 23.0 %collective-permute-start.26 = (bf16[256,2048]{1,0:T(8,128)(2,1)S(1)}, bf16[256,2048]{1,0:T(8,128)(2,1)S(1)}, u32[]{:S(2)}, u32[]{:S(2)}) collective-permute-start(bf16[256,2048]{1,0:T(8,128)(2,1)S(1)} %get-tuple-element.476.mid_a), channel_id=1, source_target_pairs={{0,2},{1,3},{2,0},{3,1},{4,6},{5,7},{6,4},{7,5},{8,10},{9,11},{10,... | collective-permute-start | bytes 3145736 | tf_op jit(solution)/shard_map/ppermute | solution.py:49
  185.1 22.9 %collective-permute-start.27 = (bf16[256,2048]{1,0:T(8,128)(2,1)S(1)}, bf16[256,2048]{1,0:T(8,128)(2,1)S(1)}, u32[]{:S(2)}, u32[]{:S(2)}) collective-permute-start(bf16[256,2048]{1,0:T(8,128)(2,1)S(1)} %get-tuple-element.475.mid_b), channel_id=1, source_target_pairs={{0,2},{1,3},{2,0},{3,1},{4,6},{5,7},{6,4},{7,5},{8,10},{9,11},{10,... | collective-permute-start | bytes 3145736 | tf_op jit(solution)/shard_map/ppermute | solution.py:49
  215.8 25.2 %collective-permute-start.28 = (bf16[256,2048]{1,0:T(8,128)(2,1)S(1)}, bf16[256,2048]{1,0:T(8,128)(2,1)S(1)}, u32[]{:S(2)}, u32[]{:S(2)}) collective-permute-start(bf16[256,2048]{1,0:T(8,128)(2,1)S(1)} %get-tuple-element.273.refs_0_), channel_id=1, source_target_pairs={{0,1},{1,0},{2,3},{3,2},{4,5},{5,4},{6,7},{7,6},{8,9},{9,8},{10,11... | collective-permute-start | bytes 3145736 | tf_op jit(solution)/shard_map/ppermute | solution.py:49
  236.1 54.3 %collective-permute-start.30 = (bf16[256,2048]{1,0:T(8,128)(2,1)S(1)}, bf16[256,2048]{1,0:T(8,128)(2,1)S(1)}, u32[]{:S(2)}, u32[]{:S(2)}) collective-permute-start(bf16[256,2048]{1,0:T(8,128)(2,1)S(1)} %get-tuple-element.277.refs_0_), channel_id=1, source_target_pairs={{0,1},{1,0},{2,3},{3,2},{4,5},{5,4},{6,7},{7,6},{8,9},{9,8},{10,11... | collective-permute-start | bytes 3145736 | tf_op jit(solution)/shard_map/ppermute | solution.py:49
  289.6 53.2 %collective-permute-start.29 = (bf16[256,2048]{1,0:T(8,128)(2,1)}, bf16[256,2048]{1,0:T(8,128)(2,1)S(1)}, u32[]{:S(2)}, u32[]{:S(2)}) collective-permute-start(bf16[256,2048]{1,0:T(8,128)(2,1)} %get-tuple-element.471), channel_id=1, source_target_pairs={{0,1},{1,0},{2,3},{3,2},{4,5},{5,4},{6,7},{7,6},{8,9},{9,8},{10,11... | collective-permute-start | bytes 3145736 | tf_op jit(solution)/shard_map/ppermute | solution.py:49
  338.2 46.0 %collective-permute-start.31 = (bf16[256,2048]{1,0:T(8,128)(2,1)S(1)}, bf16[256,2048]{1,0:T(8,128)(2,1)S(1)}, u32[]{:S(2)}, u32[]{:S(2)}) collective-permute-start(bf16[256,2048]{1,0:T(8,128)(2,1)S(1)} %get-tuple-element.473), channel_id=1, source_target_pairs={{0,1},{1,0},{2,3},{3,2},{4,5},{5,4},{6,7},{7,6},{8,9},{9,8},{10,11... | collective-permute-start | bytes 3145736 | tf_op jit(solution)/shard_map/ppermute | solution.py:49
  341.6 125.8 %collective-permute-start.34 = (bf16[512,1024]{1,0:T(8,128)(2,1)}, bf16[512,1024]{1,0:T(8,128)(2,1)}, u32[]{:S(2)}, u32[]{:S(2)}) collective-permute-start(bf16[512,1024]{1,0:T(8,128)(2,1)} %get-tuple-element.468), channel_id=1, source_target_pairs={{0,1},{1,0},{2,3},{3,2},{4,5},{5,4},{6,7},{7,6},{8,9},{9,8},{10,11... | collective-permute-start | bytes 3145736 | tf_op jit(solution)/shard_map/ppermute | solution.py:49
  386.3 27.2 %collective-permute-start.32 = (bf16[4,512,128]{2,1,0:T(8,128)(2,1)S(1)}, bf16[4,512,128]{2,1,0:T(8,128)(2,1)S(1)}, u32[]{:S(2)}, u32[]{:S(2)}) collective-permute-start(bf16[4,512,128]{2,1,0:T(8,128)(2,1)S(1)} %pad_maximum_fusion.2), channel_id=1, source_target_pairs={{0,1},{1,0},{2,3},{3,2},{4,5},{5,4},{6,7},{7,6},{8,9},{9,8},{10,11... | collective-permute-start | bytes 1572872 | tf_op jit(solution)/shard_map/ppermute | solution.py:49
  388.9 78.5 %collective-permute-start.33 = (bf16[512,1024]{1,0:T(8,128)(2,1)}, bf16[512,1024]{1,0:T(8,128)(2,1)}, u32[]{:S(2)}, u32[]{:S(2)}) collective-permute-start(bf16[512,1024]{1,0:T(8,128)(2,1)} %get-tuple-element.466), channel_id=1, source_target_pairs={{0,1},{1,0},{2,3},{3,2},{4,5},{5,4},{6,7},{7,6},{8,9},{9,8},{10,11... | collective-permute-start | bytes 3145736 | tf_op jit(solution)/shard_map/ppermute | solution.py:49
  413.6 13.4 %collective-permute-start.35 = (bf16[4,256,128]{2,1,0:T(8,128)(2,1)S(1)}, bf16[4,256,128]{2,1,0:T(8,128)(2,1)S(1)}, u32[]{:S(2)}, u32[]{:S(2)}) collective-permute-start(bf16[4,256,128]{2,1,0:T(8,128)(2,1)S(1)} %dynamic-slice_convert_fusion.9), channel_id=1, source_target_pairs={{0,1},{1,0},{2,3},{3,2},{4,5},{5,4},{6,7},{7,6},{8,9},{9,8},{10,11... | collective-permute-start | bytes 786440 | tf_op jit(solution)/shard_map/ppermute | solution.py:49
  448.5 25.4 %collective-permute-start.36 = (bf16[256,2048]{1,0:T(8,128)(2,1)}, bf16[256,2048]{1,0:T(8,128)(2,1)}, u32[]{:S(2)}, u32[]{:S(2)}) collective-permute-start(bf16[256,2048]{1,0:T(8,128)(2,1)} %bitcast.56), channel_id=1, source_target_pairs={{0,2},{1,3},{2,0},{3,1},{4,6},{5,7},{6,4},{7,5},{8,10},{9,11},{10,... | collective-permute-start | bytes 3145736 | tf_op jit(solution)/shard_map/ppermute | solution.py:49
  455.4 30.7 %all-to-all-start.3 = ((bf16[32,32,512]{2,1,0:T(8,128)(2,1)}), bf16[32,32,512]{2,1,0:T(8,128)(2,1)}, u32[]{:S(2)}, u32[]{:S(2)}) async-start(bf16[32,32,512]{2,1,0:T(8,128)(2,1)} %bitcast.244), calls=%async_computation.3 | async-start | bytes 2097152 | tf_op jit(solution)/shard_map/all_to_all | solution.py:1041
  490.6 22.9 %collective-permute-start.37 = (bf16[128,2048]{1,0:T(8,128)(2,1)S(1)}, bf16[128,2048]{1,0:T(8,128)(2,1)S(1)}, u32[]{:S(2)}, u32[]{:S(2)}) collective-permute-start(bf16[128,2048]{1,0:T(8,128)(2,1)S(1)} %bitcast.262), channel_id=1, source_target_pairs={{0,1},{1,0},{2,3},{3,2},{4,5},{5,4},{6,7},{7,6},{8,9},{9,8},{10,11... | collective-permute-start | bytes 1572872 | tf_op jit(solution)/shard_map/ppermute | solution.py:49
  511.5 23.9 %collective-permute-start.39 = (bf16[256,2560]{1,0:T(8,128)(2,1)}, bf16[256,2560]{1,0:T(8,128)(2,1)}, u32[]{:S(2)}, u32[]{:S(2)}) collective-permute-start(bf16[256,2560]{1,0:T(8,128)(2,1)} %bitcast.81), channel_id=1, source_target_pairs={{0,2},{1,3},{2,0},{3,1},{4,6},{5,7},{6,4},{7,5},{8,10},{9,11},{10,... | collective-permute-start | bytes 3932168 | tf_op jit(solution)/shard_map/ppermute | solution.py:49
  512.7 22.6 %collective-permute-start.40 = (bf16[1024,512]{1,0:T(8,128)(2,1)}, bf16[1024,512]{1,0:T(8,128)(2,1)S(1)}, u32[]{:S(2)}, u32[]{:S(2)}) collective-permute-start(bf16[1024,512]{1,0:T(8,128)(2,1)} %bitcast.84), channel_id=1, source_target_pairs={{0,2},{1,3},{2,0},{3,1},{4,6},{5,7},{6,4},{7,5},{8,10},{9,11},{10,... | collective-permute-start | bytes 3145736 | tf_op jit(solution)/shard_map/ppermute | solution.py:49
  513.7 21.6 %collective-permute-start.38 = (bf16[64,2048]{1,0:T(8,128)(2,1)S(1)}, bf16[64,2048]{1,0:T(8,128)(2,1)S(1)}, u32[]{:S(2)}, u32[]{:S(2)}) collective-permute-start(bf16[64,2048]{1,0:T(8,128)(2,1)S(1)} %bitcast.271), channel_id=1, source_target_pairs={{0,4},{1,5},{2,6},{3,7},{4,0},{5,1},{6,2},{7,3},{8,12},{9,13},{10,... | collective-permute-start | bytes 786440 | tf_op jit(solution)/shard_map/ppermute | solution.py:49
  537.1 22.2 %collective-permute-start.42 = (bf16[128,2560]{1,0:T(8,128)(2,1)S(1)}, bf16[128,2560]{1,0:T(8,128)(2,1)S(1)}, u32[]{:S(2)}, u32[]{:S(2)}) collective-permute-start(bf16[128,2560]{1,0:T(8,128)(2,1)S(1)} %bitcast.254), channel_id=1, source_target_pairs={{0,1},{1,0},{2,3},{3,2},{4,5},{5,4},{6,7},{7,6},{8,9},{9,8},{10,11... | collective-permute-start | bytes 1966088 | tf_op jit(solution)/shard_map/ppermute | solution.py:49
  538.2 21.1 %collective-permute-start.43 = (bf16[512,512]{1,0:T(8,128)(2,1)S(1)}, bf16[512,512]{1,0:T(8,128)(2,1)S(1)}, u32[]{:S(2)}, u32[]{:S(2)}) collective-permute-start(bf16[512,512]{1,0:T(8,128)(2,1)S(1)} %bitcast.261), channel_id=1, source_target_pairs={{0,4},{1,5},{2,6},{3,7},{4,0},{5,1},{6,2},{7,3},{8,12},{9,13},{10,... | collective-permute-start | bytes 1572872 | tf_op jit(solution)/shard_map/ppermute | solution.py:49
  539.5 19.9 %collective-permute-start.41 = (bf16[32,2048]{1,0:T(8,128)(2,1)S(1)}, bf16[32,2048]{1,0:T(8,128)(2,1)S(1)}, u32[]{:S(2)}, u32[]{:S(2)}) collective-permute-start(bf16[32,2048]{1,0:T(8,128)(2,1)S(1)} %bitcast.282), channel_id=1, source_target_pairs={{0,8},{1,9},{2,10},{3,11},{4,12},{5,13},{6,14},{7,15},{8,0},{9,1},... | collective-permute-start | bytes 393224 | tf_op jit(solution)/shard_map/ppermute | solution.py:49
  559.7 14.7 %collective-permute-start.49 = (bf16[16,2048]{1,0:T(8,128)(2,1)S(1)}, bf16[16,2048]{1,0:T(8,128)(2,1)S(1)}, u32[]{:S(2)}, u32[]{:S(2)}) collective-permute-start(bf16[16,2048]{1,0:T(8,128)(2,1)S(1)} %fusion.51), channel_id=1, source_target_pairs={{0,16},{1,17},{2,18},{3,19},{4,20},{5,21},{6,22},{7,23},{8,24},{9,... | collective-permute-start | bytes 196616 | tf_op jit(solution)/shard_map/ppermute | solution.py:49
  561.1 13.4 %collective-permute-start.50 = (bf16[64,2560]{1,0:T(8,128)(2,1)S(1)}, bf16[64,2560]{1,0:T(8,128)(2,1)S(1)}, u32[]{:S(2)}, u32[]{:S(2)}) collective-permute-start(bf16[64,2560]{1,0:T(8,128)(2,1)S(1)} %bitcast.268), channel_id=1, source_target_pairs={{0,4},{1,5},{2,6},{3,7},{4,0},{5,1},{6,2},{7,3},{8,12},{9,13},{10,... | collective-permute-start | bytes 983048 | tf_op jit(solution)/shard_map/ppermute | solution.py:49
  562.7 11.7 %collective-permute-start.45 = (bf16[128,1664]{1,0:T(8,128)(2,1)S(1)}, bf16[128,1664]{1,0:T(8,128)(2,1)S(1)}, u32[]{:S(2)}, u32[]{:S(2)}) collective-permute-start(bf16[128,1664]{1,0:T(8,128)(2,1)S(1)} %bitcast.265), channel_id=1, source_target_pairs={{0,1},{1,0},{2,3},{3,2},{4,5},{5,4},{6,7},{7,6},{8,9},{9,8},{10,11... | collective-permute-start | bytes 1277960 | tf_op jit(solution)/shard_map/ppermute | solution.py:49
  564.1 10.4 %collective-permute-start.51 = (bf16[256,512]{1,0:T(8,128)(2,1)S(1)}, bf16[256,512]{1,0:T(8,128)(2,1)S(1)}, u32[]{:S(2)}, u32[]{:S(2)}) collective-permute-start(bf16[256,512]{1,0:T(8,128)(2,1)S(1)} %bitcast.272), channel_id=1, source_target_pairs={{0,8},{1,9},{2,10},{3,11},{4,12},{5,13},{6,14},{7,15},{8,0},{9,1},... | collective-permute-start | bytes 786440 | tf_op jit(solution)/shard_map/ppermute | solution.py:49
  583.1 8.3 %collective-permute-start.54 = (bf16[16,2560]{1,0:T(8,128)(2,1)S(1)}, bf16[16,2560]{1,0:T(8,128)(2,1)S(1)}, u32[]{:S(2)}, u32[]{:S(2)}) collective-permute-start(bf16[16,2560]{1,0:T(8,128)(2,1)S(1)} %fusion.50), channel_id=1, source_target_pairs={{0,16},{1,17},{2,18},{3,19},{4,20},{5,21},{6,22},{7,23},{8,24},{9,... | collective-permute-start | bytes 245768 | tf_op jit(solution)/shard_map/ppermute | solution.py:49
  (70 other events, 1115.1 us)
Sparse Core Ops, SparseCore 0:
  24.0 58.4 all-gather.1

commit v5 on v4

--- a/solution.py
+++ b/solution.py
@@ -358,9 +358,14 @@
 
 
 def slot_attention_kernel(
-    pieces_ref, counts_ref, weight_ref, norm_ref, mixed_ref, probs_ref, attended_ref, lead_ref
+    pieces_ref, counts_ref, weight_ref, mixed_ref, probs_ref, attended_ref, lead_ref, norm_ref
 ):
     entries, slots, width = pieces_ref.shape
+
+    @pl.when(pl.program_id(0) == 0)
+    def norms():
+        norm_ref[...] = weight_ref[:, 3 * width : 3 * width + PAIR].astype(jnp.float32).T[:8]
+
     rows = entries * slots
     tall = (entries, slots, width)
     pieces = pieces_ref[...].astype(jnp.float32)
@@ -386,7 +391,7 @@
     lead_ref[...] = pieces[:, 0, :]
 
 
-def slot_attention(pieces, counts, in_weight, norm_rows):
+def slot_attention(pieces, counts, in_weight):
     entries, slots, width = pieces.shape
     part = min(ENTRY_BLOCK, entries)
     whole = lambda shape: pl.BlockSpec(shape, lambda i: (0,) * len(shape))
@@ -399,19 +404,20 @@
             tall,
             pl.BlockSpec((part, 1, PAIR), lambda i: (i, 0, 0)),
             whole(in_weight.shape),
-            whole(norm_rows.shape),
         ],
         out_specs=[
             pl.BlockSpec((part * slots, 3 * width), lambda i: (i, 0)),
             pl.BlockSpec((part, slots, PAIR), lambda i: (i, 0, 0)),
             flat,
             flat,
+            whole((8, width)),
         ],
         out_shape=[
             jax.ShapeDtypeStruct((entries * slots, 3 * width), jnp.bfloat16),
             jax.ShapeDtypeStruct((entries, slots, PAIR), jnp.float32),
             jax.ShapeDtypeStruct((entries, width), jnp.bfloat16),
             jax.ShapeDtypeStruct((entries, width), jnp.float32),
+            jax.ShapeDtypeStruct((8, width), jnp.float32),
         ],
         compiler_params=pltpu.CompilerParams(
             dimension_semantics=("arbitrary",), vmem_limit_bytes=VMEM_LIMIT
@@ -420,7 +426,7 @@
             flops=entries * slots * width, bytes_accessed=entries * slots, transcendentals=0
         ),
         name="slot_attention",
-    )(pieces, counts, in_weight, norm_rows)
+    )(pieces, counts, in_weight)
 
 
 def gelu_of(value):
@@ -430,6 +436,19 @@
 
 def gelu_slope(value, cdf):
     return cdf + value * (jnp.exp(-0.5 * value * value) * np.float32((2 * np.pi) ** -0.5))
+
+
+def place_parts(split, places, wholes, parts):
+    @pl.when(pl.program_id(0) == 0)
+    def join():
+        core, side = places[0], places[1]
+        for index, whole in enumerate(wholes):
+            for at, part in enumerate(parts[4 * index : 4 * index + 4]):
+                rows = part.shape[0] // split
+                place = 2 * (side if at % 2 == 0 else 1 - side) + (core if at < 2 else 1 - core)
+                for group in range(split):
+                    start = pl.multiple_of((4 * group + place) * rows, rows)
+                    whole[pl.ds(start, rows), :] = part[group * rows : (group + 1) * rows, :]
 
 
 def units_forward_kernel(
@@ -441,17 +460,7 @@
     else:
         wide_weight_ref, reduce_ref = refs[11:]
 
-        @pl.when(pl.program_id(0) == 0)
-        def join():
-            core = places[0]
-            for whole, parts in ((wide_weight_ref, weights[:4]), (reduce_ref, weights[4:])):
-                rows = parts[0].shape[0] // split
-                for at, part in enumerate(parts):
-                    side = places[1] if at % 2 == 0 else 1 - places[1]
-                    place = 2 * side + (core if at < 2 else 1 - core)
-                    for group in range(split):
-                        start = pl.multiple_of((4 * group + place) * rows, rows)
-                        whole[pl.ds(start, rows), :] = part[group * rows : (group + 1) * rows, :]
+        place_parts(split, places, (wide_weight_ref, reduce_ref), weights)
 
     width = lead_ref.shape[1]
     hidden = lead_ref[...] + matmul(attended_ref[...], wide_weight_ref[:, :width])
@@ -501,11 +510,14 @@
     )(places.astype(jnp.int32), attended, lead, *weights, norm_rows)
 
 
-def units_backward_kernel(
-    grad_ref, hidden_ref, attended_ref, wide_weight_ref, reduce_ref, norm_ref,
-    hidden_grad_ref, attended_grad_ref, wide_ref, reduce_grad_ref, norm_grad_ref,
-    wide_total, reduce_total,
-):
+def units_backward_kernel(split, places, grad_ref, hidden_ref, attended_ref, *refs):
+    *weights, norm_ref, hidden_grad_ref, attended_grad_ref, norm_grad_ref = refs[: 12 if split else 6]
+    if split:
+        *sums, wide_total, reduce_total, wide_weight_ref, reduce_ref = refs[12:]
+        place_parts(split, places, (wide_weight_ref, reduce_ref), weights)
+    else:
+        wide_weight_ref, reduce_ref = weights
+        *sums, wide_total, reduce_total = refs[6:]
     step_at = pl.program_id(0)
     width = hidden_ref.shape[1]
     units = reduce_ref.shape[0]
@@ -542,31 +554,47 @@
 
     @pl.when(step_at == pl.num_programs(0) - 1)
     def finish():
-        wide_ref[...] = to_low(wide_total[...])
-        reduce_grad_ref[...] = to_low(reduce_total[...])
-
-
-def units_backward(grad, hidden, attended, wide_weight, reduce_weight, norm_rows):
+        if not split:
+            sums[0][...] = to_low(wide_total[...])
+            sums[1][...] = to_low(reduce_total[...])
+            return
+        core = places[0]
+        for total, halves in ((wide_total, sums[:2]), (reduce_total, sums[2:])):
+            rows = halves[0].shape[0] // (2 * split)
+            for half, place in zip(halves, (core, 1 - core)):
+                for group in range(2 * split):
+                    start = pl.multiple_of((2 * group + place) * rows, rows)
+                    half[group * rows : (group + 1) * rows, :] = to_low(total[pl.ds(start, rows), :])
+
+
+def units_backward(groups, places, grad, hidden, attended, wide_weight, reduce_weight, norm_rows):
     entries, width = attended.shape
     part = min(UNIT_ROWS, entries)
-    units = reduce_weight.shape[0]
-    whole = lambda shape: pl.BlockSpec(shape, lambda i: (0,) * len(shape))
-    flat = pl.BlockSpec((part, width), lambda i: (i, 0))
+    split = groups if len(wide_weight) == 4 else 0
+    weights = [*wide_weight, *reduce_weight]
+    units = reduce_weight[0].shape[0] * len(reduce_weight)
+    whole = lambda shape: pl.BlockSpec(shape, lambda i, s: (0,) * len(shape))
+    flat = pl.BlockSpec((part, width), lambda i, s: (i, 0))
     wide = (width, width + units)
+    tall = (units, width)
+    half = lambda shape: (shape[0] // 2, shape[1])
+    sums = [half(wide)] * 2 + [half(tall)] * 2 if split else [wide, tall]
     return pl.pallas_call(
-        units_backward_kernel,
-        grid=(entries // part,),
-        in_specs=[flat, flat, flat]
-        + [whole(x.shape) for x in (wide_weight, reduce_weight, norm_rows)],
-        out_specs=[flat, flat, whole(wide), whole((units, width)), whole((8, width))],
+        functools.partial(units_backward_kernel, split),
+        grid_spec=pltpu.PrefetchScalarGridSpec(
+            num_scalar_prefetch=1,
+            grid=(entries // part,),
+            in_specs=[flat, flat, flat] + [fixed(x.shape) for x in (*weights, norm_rows)],
+            out_specs=[flat, flat, whole((8, width))] + [whole(x) for x in sums],
+            scratch_shapes=[pltpu.VMEM(wide, jnp.float32), pltpu.VMEM(tall, jnp.float32)]
+            + [pltpu.VMEM(x, jnp.bfloat16) for x in (wide, tall)] * bool(split),
+        ),
         out_shape=[
             jax.ShapeDtypeStruct((entries, width), jnp.float32),
             jax.ShapeDtypeStruct((entries, width), jnp.bfloat16),
-            jax.ShapeDtypeStruct(wide, jnp.bfloat16),
-            jax.ShapeDtypeStruct((units, width), jnp.bfloat16),
             jax.ShapeDtypeStruct((8, width), jnp.float32),
-        ],
-        scratch_shapes=[pltpu.VMEM(wide, jnp.float32), pltpu.VMEM((units, width), jnp.float32)],
+        ]
+        + [jax.ShapeDtypeStruct(x, jnp.bfloat16) for x in sums],
         compiler_params=pltpu.CompilerParams(
             dimension_semantics=("arbitrary",), vmem_limit_bytes=VMEM_LIMIT
         ),
@@ -574,7 +602,7 @@
             flops=6 * entries * width * (2 * width + 5 * units), bytes_accessed=16 << 20, transcendentals=0
         ),
         name="units_backward",
-    )(grad, hidden, attended, wide_weight, reduce_weight, norm_rows)
+    )(places.astype(jnp.int32), grad, hidden, attended, *weights, norm_rows)
 
 
 def slot_backward_kernel(
@@ -1148,12 +1176,10 @@
     in_came = send(0, bits - 1)
     in_weight = join(0, in_came, bits - 1)
     small = gather_join(
-        in_held[:, in_width:], in_came[:, in_width:], late_y[-1], late_y[:-1], me
+        in_held[:, in_width + PAIR :], in_came[:, in_width + PAIR :], late_y[-1], late_y[:-1], me
     )
     embed_full = lax.all_gather(embed_weight, ("dp", "mp"), axis=0, tiled=True)
-    norm_rows = small[:, :8].astype(jnp.float32).T
-    digit_at = PAIR
-    all_digits = small[:, digit_at : digit_at + digit_width].reshape(devices, 2, 2 * block)
+    all_digits = small[:, :digit_width].reshape(devices, 2, 2 * block)
     all_digits = all_digits.astype(jnp.int32)
     asked = all_digits[:, 0] * PAIR + all_digits[:, 1]
 
@@ -1166,8 +1192,8 @@
     other_base = (1 - mp_index) * kv_local
     head_order = [mp_index * kv_local, mp_index * kv_local + 1, other_base + core, other_base + 1 - core]
 
-    slot_mixed, slot_probs, hyper_attended, lead_rows = slot_attention(
-        pieces, count_rows, in_weight, norm_rows
+    slot_mixed, slot_probs, hyper_attended, lead_rows, norm_rows = slot_attention(
+        pieces, count_rows, in_weight
     )
     asked, _ = lax.optimization_barrier((asked, hyper_attended))
     hyper_attended, embed_full, later_came, query_near = lax.optimization_barrier(
@@ -1190,8 +1216,9 @@
     query_far_row = swap(query_near, 4, devices)
     output_slice, _ = lax.optimization_barrier((output_slice, query_near))
     output_near = swap(output_slice, 1, devices)
+    places = jnp.stack([core, side])
     pooled, hyper_hidden = units_forward(
-        devices // 8, jnp.stack([core, side]), hyper_attended, lead_rows, *forward_weights, norm_rows
+        devices // 8, places, hyper_attended, lead_rows, *forward_weights, norm_rows
     )
     _, query_far_row = lax.optimization_barrier((pooled, query_far_row))
     present, standing = asked_of_me(asked, me, local_vocab)
@@ -1306,8 +1333,9 @@
     def columns(value, index):
         return lax.dynamic_slice_in_dim(value, index * share, share, 1)
 
-    dense_came = [swap(columns(dense_rows[part], 1 - mp_index), 1, devices) for part in range(2)]
-    pair_grads[0], *dense_came = lax.optimization_barrier((pair_grads[0], *dense_came))
+    leaving = [columns(dense_rows[part], 1 - mp_index) for part in range(2)]
+    _, leaving[0] = lax.optimization_barrier((came_short, leaving[0]))
+    dense_came = [swap(x, 1, devices) for x in leaving]
 
     embedded_grad_low, token_grad = embed_backward(
         jnp.stack([*own_at, *head_order]).astype(jnp.int32), query_grad, pair_own, came_long, came_short, tables, grad_hidden, embedded,
@@ -1322,8 +1350,6 @@
         other_out.append(to_low(kept[block:] + arrived[:block]))
     model_out = ordered_blocks(lead, own_out, other_out)
     embed_grad = to_low(matmul_first(chosen_own, embedded_grad_low))
-    _, later_parts = lax.optimization_barrier((token_grad, later_parts))
-    wide_weight, reduce_weight = [joined(which, later_parts[which - 1]) for which in (1, 2)]
 
     def give_back(turn, total):
         taker = taker_choice(own_rank, own_owner, turn, capacity, devices)
@@ -1342,20 +1368,25 @@
     embed_held = scatter_add(*scatter(embed_grad, back_order, 0))
     embed_held, grad_pooled = lax.optimization_barrier((embed_held, grad_pooled))
     embed_held = scatter_add(*scatter(embed_held, back_order, 1))
-    hidden_grad, attended_grad, wide_grad, reduce_grad, later_norms = units_backward(
-        grad_pooled, hyper_hidden, hyper_attended, wide_weight, reduce_weight, norm_rows
+    hidden_grad, attended_grad, later_norms, *unit_sums = units_backward(
+        devices // 8, places, grad_pooled, hyper_hidden, hyper_attended, *forward_weights, norm_rows
     )
     hidden_grad, embed_held = lax.optimization_barrier((hidden_grad, embed_held))
-    held = [embed_held, wide_grad, reduce_grad]
+    held = [embed_held, *([unit_sums[:2], unit_sums[2:]] if together else unit_sums)]
     turned_order = [back_order[0], back_order[2], back_order[3], back_order[1]] + back_order[4:]
     orders = [back_order, back_order, turned_order]
     ahead = [2, 0, 0]
 
     def depart(at):
-        return [
-            scatter(x, order, at + skip) if at + skip < bits else (x, None)
-            for x, order, skip in zip(held, orders, ahead)
-        ]
+        moving = []
+        for x, order, skip in zip(held, orders, ahead):
+            if at + skip >= bits:
+                moving.append((x, None))
+            elif isinstance(x, list):
+                moving.append((x[0], swap(x[1], 1 << order[0], devices)))
+            else:
+                moving.append(scatter(x, order, at + skip))
+        return moving
 
     def arrive(moving):
         return [x if came is None else scatter_add(x, came) for x, came in moving]

time: 613 us -> 598 us (0.976)
  other arithmetic: 57.8 us -> 45.5 us
  local copies, waits for them, and re-layouts: 40.5 us -> 32.8 us
    select_n x21 -> x15, other arithmetic: 22.4 us -> 9.72 us  [gather_join(): jnp.where(me >> bit & 1 == 1, jnp.concatenate([arrived, held], axis=1), j...]
    unnamed x123 -> x122, local copies, waits for them, and re-layouts: 15.5 us -> 13.5 us
  transfers between devices with their start and end apart: 59 -> 59, of which waited for: 17 -> 17; matrix products, arithmetic and copies ran while one was open for 14% -> 11% of each run, Pallas kernels for 52% -> 54%
where the time goes in v5:
time: 598 us; the launch traced here: 588 us
  Pallas kernels  325 us (54%)
  waiting for transfers between devices  80.8 us (14%)
  starting transfers between devices  75 us (13%)
  other arithmetic  45.5 us (8%)
  local copies, waits for them, and re-layouts  32.8 us (5%)
  between operations  17 us (3%)
  matrix products  12.4 us (2%)
    pallas_call x2, Pallas kernels, feed_forward(): pl.pallas_call(lambda info, *refs: feed_forward_kernel(*refs), grid_spec=...  95.1 us
    ppermute x56, starting transfers between devices, swap(): lax.ppermute(value, ('dp', 'mp'), [(d, d ^ mask) for d in range(devices)])  66.7 us
    ppermute x56, waiting for transfers between devices, swap(): lax.ppermute(value, ('dp', 'mp'), [(d, d ^ mask) for d in range(devices)])  65 us
    pallas_call x2, Pallas kernels, attention_backward(): pl.pallas_call(attention_backward_kernel, grid_spec=pltpu.PrefetchScalarG...  49.8 us
    pallas_call x2, Pallas kernels, slot_backward(): pl.pallas_call(functools.partial(slot_backward_kernel, first, last), grid...  36.8 us
    pallas_call x2, Pallas kernels, attention_forward(): pl.pallas_call(attention_forward_kernel, grid_spec=pltpu.PrefetchScalarGr...  33.4 us
    pallas_call x2, Pallas kernels, project(): pl.pallas_call(functools.partial(project_kernel, more), grid_spec=pltpu.P...  20 us
    pallas_call x1, Pallas kernels, slot_attention(): pl.pallas_call(slot_attention_kernel, grid=(entries // part,), in_specs=[...  19.6 us
  transfers between devices with their start and end apart: 59, of which 17 were waited for; matrix products, arithmetic and copies ran while one was open for 11% of the time, Pallas kernels for 54%

profile of v5, /device:TPU:0, one launch (start us, length us, event | category | flops | bytes accessed | tf_op | source)
XLA Modules:
  0.0 588.2 jit_solution(14871836388912310675)
XLA Ops:
  11.2 4.0 collective-permute-start
  16.8 2.9 collective-permute-start.4
  24.0 2.4 constant_dynamic-slice_fusion.20
  26.4 2.3 dynamic_slice.152
  31.6 3.3 collective-permute-done.1
  35.0 3.6 collective-permute-done.5
  43.2 4.5 collective-permute-done.7
  52.5 5.7 collective-permute-done.8
  62.2 2.3 maximum_select_fusion.3
  66.1 2.1 maximum_select_fusion.4
  72.0 19.6 %slot_attention.1 = (bf16[4096,1536]{1,0:T(8,128)(2,1)}, f32[512,8,128]{2,1,0:T(8,128)S(1)}, bf16[512,512]{1,0:T(8,128)(2,1)S(1)}, f32[512,512]{1,0:T(8,128)S(1)}, f32[8,512]{1,0:T(8,128)S(1)}) custom-call(bf16[512,8,512]{2,1,0:T(8,128)(2,1)} %pieces_ref.5, s32[512,1,128]{2,1,0:T(1,128)S(1)} %broadcast_in_dim.30.counts_ref, bf16[512,1792]{1,0:T(8,128)(2,1)S(1)} %bitcast.160), custom_call_target="tpu_custom_call" | custom-call | flops 2097152 | bytes 4096 | tf_op jit(solution)/shard_map/slot_attention/pallas_call | solution.py:400
  93.4 2.6 collective-permute-done.13.refs_5_
  96.6 5.0 compare_reduce_fusion
  104.7 7.6 %units_forward.1 = (bf16[512,512]{1,0:T(8,128)(2,1)S(1)}, f32[512,512]{1,0:T(8,128)}) custom-call(s32[2]{0:T(128)S(1)} %pad_add_fusion.2.places, bf16[512,512]{1,0:T(8,128)(2,1)S(1)} %copy-done.16, f32[512,512]{1,0:T(8,128)} %copy-done.14, bf16[128,2560]{1,0:T(8,128)(2,1)} %bitcast.39.refs_0_, bf16[128,2560]{1,0:T(8,128)(2,1)} %collective-permute-done.12.refs_1_, ...), custom_call_target="tpu_custom_call" | custom-call | flops 262144 | bytes 262144 | tf_op jit(solution)/shard_map/units_forward/pallas_call | solution.py:490
  114.9 4.0 all-to-all-start.2
  121.2 16.6 %collective-permute-done.19 = bf16[1024,512]{1,0:T(8,128)(2,1)} collective-permute-done((bf16[1024,512]{1,0:T(8,128)(2,1)}, bf16[1024,512]{1,0:T(8,128)(2,1)}, u32[]{:S(2)}, u32[]{:S(2)}) %collective-permute-start.19) | collective-permute-done | bytes 1048608 | tf_op jit(solution)/shard_map/ppermute | solution.py:49
  137.8 3.0 broadcast_select_fusion.2
  142.0 3.1 all-to-all-done.2
  145.1 2.8 fusion.34
  147.8 7.6 %collective-permute-done.22 = bf16[256,2048]{1,0:T(8,128)(2,1)} collective-permute-done((bf16[256,2048]{1,0:T(8,128)(2,1)}, bf16[256,2048]{1,0:T(8,128)(2,1)}, u32[]{:S(2)}, u32[]{:S(2)}) %collective-permute-start.22) | collective-permute-done | bytes 1048608 | tf_op jit(solution)/shard_map/ppermute | solution.py:49
  161.1 14.1 %project.2 = (f32[1024,512]{1,0:T(8,128)}, bf16[512,2048]{1,0:T(8,128)(2,1)}, f32[512,2048]{1,0:T(8,128)}) custom-call(s32[2]{0:T(128)S(1)} %pad_add_fusion.3.info, bf16[512,512]{1,0:T(8,128)(2,1)} %get-tuple-element.250.chosen_ref, bf16[512,2048]{1,0:T(8,128)(2,1)} %all-gather.2.cloned.1.call-done.embed_ref, f32[1,2048]{1,0:T(1,128)S(1)} %bitcast.168, ...), custom_call_target="tpu_custom_call" | custom-call | flops 1073741824 | bytes 1048576 | tf_op jit(solution)/shard_map/project/pallas_call | solution.py:855
  176.9 5.9 %project.3.pair_ref = f32[1024,512]{1,0:T(8,128)S(1)} custom-call(s32[2]{0:T(128)S(1)} %pad_add_fusion.1.info, bf16[512,512]{1,0:T(8,128)(2,1)S(1)} %collective-permute-done.23.chosen_ref, bf16[512,2048]{1,0:T(8,128)(2,1)} %all-gather.2.cloned.1.call-done.embed_ref, f32[1,2048]{1,0:T(1,128)S(1)} %bitcast.169, ...), custom_call_target="tpu_custom_call", output_to_operand_aliasing={{}: (7, {})} | custom-call | flops 1073741824 | bytes 1048576 | tf_op jit(solution)/shard_map/project/pallas_call | solution.py:855
  182.8 2.5 broadcast_select_fusion
  187.5 20.8 %attention_forward.2 = (bf16[256,2048]{1,0:T(8,128)(2,1)S(1)}, bf16[256,2048]{1,0:T(8,128)(2,1)S(1)}, f32[4,8,256]{2,1,0:T(8,128)S(1)}) custom-call(s32[5]{0:T(128)S(1)} %stack.84.info, f32[512,2048]{1,0:T(8,128)} %get-tuple-element.258.query_ref, f32[1024,512]{1,0:T(8,128)S(1)} %copy-done.8, f32[1024,128]{1,0:T(8,128)S(1)} %copy-done.20, ...), custom_call_target="tpu_custom_call" | custom-call | flops 21474836480 | bytes 8388608 | tf_op jit(solution)/shard_map/attention_forward/pallas_call | solution.py:256
  209.4 6.7 %output_project.2 = (f32[256,2048]{1,0:T(8,128)}, bf16[256,2048]{1,0:T(8,128)(2,1)S(1)}) custom-call(bf16[256,2048]{1,0:T(8,128)(2,1)S(1)} %get-tuple-element.259.rows_ref, bf16[512,2048]{1,0:T(8,128)(2,1)} %get-tuple-element.260.embedded_ref, f32[1,2048]{1,0:T(1,128)S(1)} %bitcast.164, bf16[1024,2048]{1,0:T(8,128)(2,1)} %near_ref.8, ...), custom_call_target="tpu_custom_call" | custom-call | flops 4294967296 | bytes 12582912 | tf_op jit(solution)/shard_map/output_project/pallas_call | solution.py:898
  216.8 12.6 %attention_forward.3 = (bf16[256,2048]{1,0:T(8,128)(2,1)S(1)}, bf16[256,2048]{1,0:T(8,128)(2,1)S(1)}, f32[4,8,256]{2,1,0:T(8,128)S(1)}) custom-call(s32[5]{0:T(128)S(1)} %stack.85.info, f32[512,2048]{1,0:T(8,128)} %get-tuple-element.258.query_ref, f32[1024,512]{1,0:T(8,128)S(1)} %copy-done.9, f32[1024,128]{1,0:T(8,128)S(1)} %copy-done.20, ...), custom_call_target="tpu_custom_call" | custom-call | flops 10737418240 | bytes 8388608 | tf_op jit(solution)/shard_map/attention_forward/pallas_call | solution.py:256
  229.4 7.0 %output_project.3 = (f32[256,2048]{1,0:T(8,128)}, bf16[256,2048]{1,0:T(8,128)(2,1)S(1)}) custom-call(bf16[256,2048]{1,0:T(8,128)(2,1)S(1)} %get-tuple-element.264.rows_ref, bf16[512,2048]{1,0:T(8,128)(2,1)} %get-tuple-element.260.embedded_ref, f32[1,2048]{1,0:T(1,128)S(1)} %bitcast.165, bf16[1024,2048]{1,0:T(8,128)(2,1)} %near_ref.8, ...), custom_call_target="tpu_custom_call" | custom-call | flops 4294967296 | bytes 12582912 | tf_op jit(solution)/shard_map/output_project/pallas_call | solution.py:898
  236.5 4.6 collective-permute-start.30
  241.2 47.6 %feed_forward.2 = (bf16[512,2048]{1,0:T(8,128)(2,1)S(1)}, bf16[512,2048]{1,0:T(8,128)(2,1)}) custom-call(s32[2]{0:T(128)S(1)} %pad_add_fusion.info, bf16[256,2048]{1,0:T(8,128)(2,1)S(1)} %get-tuple-element.268.refs_0_, bf16[256,2048]{1,0:T(8,128)(2,1)S(1)} %collective-permute-done.28.refs_1_, bf16[1024,2048]{1,0:T(8,128)(2,1)} %rising_ref.3, ...), custom_call_target="tpu_custom_call" | custom-call | flops 50197430272 | bytes 69206016 | tf_op jit(solution)/shard_map/feed_forward/pallas_call | solution.py:770
  288.8 3.5 dynamic-slice_convert_fusion.3
  294.6 47.5 %feed_forward.3 = (bf16[512,2048]{1,0:T(8,128)(2,1)S(1)}, bf16[512,2048]{1,0:T(8,128)(2,1)}) custom-call(s32[2]{0:T(128)S(1)} %pad_add_fusion.4.info, bf16[256,2048]{1,0:T(8,128)(2,1)S(1)} %get-tuple-element.272.refs_0_, bf16[256,2048]{1,0:T(8,128)(2,1)S(1)} %collective-permute-done.30.refs_1_, bf16[1024,2048]{1,0:T(8,128)(2,1)} %rising_ref.3, ...), custom_call_target="tpu_custom_call" | custom-call | flops 50197430272 | bytes 69206016 | tf_op jit(solution)/shard_map/feed_forward/pallas_call | solution.py:770
  343.1 7.3 %hidden_backward.2 = (f32[256,2048]{1,0:T(8,128)}, bf16[256,2048]{1,0:T(8,128)(2,1)S(1)}) custom-call(s32[5]{0:T(128)S(1)} %stack.84.info, bf16[256,2048]{1,0:T(8,128)(2,1)S(1)} %get-tuple-element.279.here_ref, bf16[256,2048]{1,0:T(8,128)(2,1)S(1)} %collective-permute-done.29.came_ref, f32[256,2048]{1,0:T(8,128)} %get-tuple-element.270.refs_4_.hidden_ref, ...), custom_call_target="tpu_custom_call" | custom-call | flops 4294967296 | bytes 14680064 | tf_op jit(solution)/shard_map/hidden_backward/pallas_call | solution.py:937
  350.5 34.1 %attention_backward.2 = (bf16[512,2048]{1,0:T(8,128)(2,1)S(1)}, f32[4,1024,128]{2,1,0:T(8,128)}) custom-call(s32[5]{0:T(128)S(1)} %stack.84.info, bf16[256,2048]{1,0:T(8,128)(2,1)S(1)} %copy-done.26, bf16[256,2048]{1,0:T(8,128)(2,1)S(1)} %get-tuple-element.281.grad_ref, f32[4,8,256]{2,1,0:T(8,128)S(1)} %get-tuple-element.282.lse_ref, f32[1024,512]{1,0:T(8,128)} %copy-done.7, ...), custom_call_target="tpu_custom_call" | custom-call | flops 53687091200 | bytes 8388608 | tf_op jit(solution)/shard_map/attention_backward/pallas_call | solution.py:292
  386.8 7.3 %hidden_backward.3 = (f32[256,2048]{1,0:T(8,128)}, bf16[256,2048]{1,0:T(8,128)(2,1)S(1)}) custom-call(s32[5]{0:T(128)S(1)} %stack.85.info, bf16[256,2048]{1,0:T(8,128)(2,1)S(1)} %get-tuple-element.285.here_ref, bf16[256,2048]{1,0:T(8,128)(2,1)S(1)} %collective-permute-done.31.came_ref, f32[256,2048]{1,0:T(8,128)} %get-tuple-element.273.refs_4_.hidden_ref, ...), custom_call_target="tpu_custom_call" | custom-call | flops 4294967296 | bytes 14680064 | tf_op jit(solution)/shard_map/hidden_backward/pallas_call | solution.py:937
  394.1 15.7 %attention_backward.3 = (bf16[512,2048]{1,0:T(8,128)(2,1)}, f32[4,512,128]{2,1,0:T(8,128)S(1)}) custom-call(s32[5]{0:T(128)S(1)} %stack.85.info, bf16[256,2048]{1,0:T(8,128)(2,1)S(1)} %copy-done.24, bf16[256,2048]{1,0:T(8,128)(2,1)S(1)} %get-tuple-element.287.grad_ref, f32[4,8,256]{2,1,0:T(8,128)S(1)} %get-tuple-element.288.lse_ref, ...), custom_call_target="tpu_custom_call", output_to_operand_aliasing={{0}: (9, {})} | custom-call | flops 26843545600 | bytes 8388608 | tf_op jit(solution)/shard_map/attention_backward/pallas_call | solution.py:292
  411.8 8.2 %collective-permute-start.33 = (bf16[4,256,128]{2,1,0:T(8,128)(2,1)S(1)}, bf16[4,256,128]{2,1,0:T(8,128)(2,1)S(1)}, u32[]{:S(2)}, u32[]{:S(2)}) collective-permute-start(bf16[4,256,128]{2,1,0:T(8,128)(2,1)S(1)} %dynamic-slice_convert_fusion.9), channel_id=1, source_target_pairs={{0,1},{1,0},{2,3},{3,2},{4,5},{5,4},{6,7},{7,6},{8,9},{9,8},{10,11... | collective-permute-start | bytes 786440 | tf_op jit(solution)/shard_map/ppermute | solution.py:49
  420.2 4.4 collective-permute-done.33.short_ref
  426.6 17.0 %embed_backward.1 = (bf16[512,2048]{1,0:T(8,128)(2,1)}, bf16[512,512]{1,0:T(8,128)(2,1)S(1)}) custom-call(s32[6]{0:T(128)S(1)} %stack.87.info, bf16[512,2048]{1,0:T(8,128)(2,1)} %get-tuple-element.297.query_ref, f32[4,512,128]{2,1,0:T(8,128)S(1)} %pad_maximum_fusion.1.own_ref, bf16[4,512,128]{2,1,0:T(8,128)(2,1)S(1)} %collective-permute-done.32.came_ref, ...), custom_call_target="tpu_custom_call" | custom-call | flops 12884901888 | bytes 20971520 | tf_op jit(solution)/shard_map/embed_backward/pallas_call | solution.py:1007
  445.4 4.3 all-to-all-start.3
  449.7 2.9 convolution_convert_fusion
  460.3 2.9 convert_add_fusion.1
  463.3 12.6 %all-to-all-done.3 = bf16[32,32,512]{2,1,0:T(8,128)(2,1)} async-done(((bf16[32,32,512]{2,1,0:T(8,128)(2,1)}), bf16[32,32,512]{2,1,0:T(8,128)(2,1)}, u32[]{:S(2)}, u32[]{:S(2)}) %all-to-all-start.3) | async-done | bytes 1048608 | tf_op jit(solution)/shard_map/all_to_all | solution.py:1069
  475.9 3.0 fusion.33
  481.9 17.0 %units_backward.1 = (f32[512,512]{1,0:T(8,128)}, bf16[512,512]{1,0:T(8,128)(2,1)S(1)}, f32[8,512]{1,0:T(8,128)S(1)}, bf16[256,2560]{1,0:T(8,128)(2,1)}, bf16[256...) custom-call(s32[2]{0:T(128)S(1)} %pad_add_fusion.2.places, ...), custom_call_target="tpu_custom_call" | custom-call | flops 17716740096 | bytes 16777216 | tf_op jit(solution)/shard_map/units_backward/pallas_call | solution.py:582
  503.7 18.1 %slot_backward.2 = (bf16[512,8,512]{2,1,0:T(8,128)(2,1)}, f32[512,1536]{1,0:T(8,128)}, f32[8,512]{1,0:T(8,128)S(1)}) custom-call(bf16[512,8,512]{2,1,0:T(8,128)(2,1)} %pieces_ref.5, bf16[4096,1536]{1,0:T(8,128)(2,1)} %get-tuple-element.295.mixed_ref, f32[512,8,128]{2,1,0:T(8,128)S(1)} %get-tuple-element.296.probs_ref, ...), custom_call_target="tpu_custom_call" | custom-call | flops 1048576 | bytes 2048 | tf_op jit(solution)/shard_map/slot_backward/pallas_call | solution.py:695
  525.3 18.7 %slot_backward.3 = (bf16[512,8,512]{2,1,0:T(8,128)(2,1)}, bf16[512,1664]{1,0:T(8,128)(2,1)S(1)}, f32[8,512]{1,0:T(8,128)}) custom-call(bf16[512,8,512]{2,1,0:T(8,128)(2,1)} %pieces_ref.5, bf16[4096,1536]{1,0:T(8,128)(2,1)} %get-tuple-element.295.mixed_ref, f32[512,8,128]{2,1,0:T(8,128)} %copy-done.3, ...), custom_call_target="tpu_custom_call", output_to_operand_aliasing={{0}: (8, {})} | custom-call | flops 1048576 | bytes 2048 | tf_op jit(solution)/shard_map/slot_backward/pallas_call | solution.py:695
  550.5 9.1 %collective-permute-done.45 = bf16[128,1664]{1,0:T(8,128)(2,1)S(1)} collective-permute-done((bf16[128,1664]{1,0:T(8,128)(2,1)S(1)}, bf16[128,1664]{1,0:T(8,128)(2,1)S(1)}, u32[]{:S(2)}, u32[]{:S(2)}) %collective-permute-start.45) | collective-permute-done | bytes 426016 | tf_op jit(solution)/shard_map/ppermute | solution.py:49
  564.1 2.3 collective-permute-done.46
  (349 shorter events, 108.5 us)
Async XLA Ops:
  7.2 88.8 %all-gather.2.cloned.1.call-start = ((), (), s32[]{:S(2)}) async-start(), calls=%async_computation.4 | async-start | bytes 2162688 | tf_op jit(solution)/shard_map/all_gather | solution.py:1181
  11.2 17.5 %collective-permute-start = (bf16[16,1792]{1,0:T(8,128)(2,1)}, bf16[16,1792]{1,0:T(8,128)(2,1)S(1)}, u32[]{:S(2)}, u32[]{:S(2)}) collective-permute-start(bf16[16,1792]{1,0:T(8,128)(2,1)} %get-tuple-element.469), channel_id=1, source_target_pairs={{0,16},{1,17},{2,18},{3,19},{4,20},{5,21},{6,22},{7,23},{8,24},{9,... | collective-permute-start | bytes 172040 | tf_op jit(solution)/shard_map/ppermute | solution.py:49
  16.8 14.3 %collective-permute-start.2 = (bf16[16,2560]{1,0:T(8,128)(2,1)S(1)}, bf16[16,2560]{1,0:T(8,128)(2,1)S(1)}, u32[]{:S(2)}, u32[]{:S(2)}) collective-permute-start(bf16[16,2560]{1,0:T(8,128)(2,1)S(1)} %constant_dynamic-update-slice_fusion), channel_id=1, source_target_pairs={{0,16},{1,17},{2,18},{3,19},{4,20},{5,21},{6,22},{7,23},{8,24},{9,... | collective-permute-start | bytes 245768 | tf_op jit(solution)/shard_map/ppermute | solution.py:49
  16.8 13.6 %collective-permute-start.4 = (bf16[64,512]{1,0:T(8,128)(2,1)}, bf16[64,512]{1,0:T(8,128)(2,1)S(1)}, u32[]{:S(2)}, u32[]{:S(2)}) collective-permute-start(bf16[64,512]{1,0:T(8,128)(2,1)} %param.31), channel_id=1, source_target_pairs={{0,16},{1,17},{2,18},{3,19},{4,20},{5,21},{6,22},{7,23},{8,24},{9,... | collective-permute-start | bytes 196616 | tf_op jit(solution)/shard_map/ppermute | solution.py:49
  22.4 17.7 %collective-permute-start.6 = (bf16[2048,128]{1,0:T(8,128)(2,1)S(1)}, bf16[2048,128]{1,0:T(8,128)(2,1)S(1)}, u32[]{:S(2)}, u32[]{:S(2)}) collective-permute-start(bf16[2048,128]{1,0:T(8,128)(2,1)S(1)} %constant_dynamic-slice_fusion.21), channel_id=1, source_target_pairs={{0,1},{1,0},{2,3},{3,2},{4,5},{5,4},{6,7},{7,6},{8,9},{9,8},{10,11... | collective-permute-start | bytes 1572872 | tf_op jit(solution)/shard_map/ppermute | solution.py:49
  30.4 8.2 %collective-permute-start.5 = (bf16[128,512]{1,0:T(8,128)(2,1)S(1)}, bf16[128,512]{1,0:T(8,128)(2,1)S(1)}, u32[]{:S(2)}, u32[]{:S(2)}) collective-permute-start(bf16[128,512]{1,0:T(8,128)(2,1)S(1)} %maximum_select_fusion.11), channel_id=1, source_target_pairs={{0,1},{1,0},{2,3},{3,2},{4,5},{5,4},{6,7},{7,6},{8,9},{9,8},{10,11... | collective-permute-start | bytes 393224 | tf_op jit(solution)/shard_map/ppermute | solution.py:49
  31.1 8.2 %collective-permute-start.3 = (bf16[32,2560]{1,0:T(8,128)(2,1)S(1)}, bf16[32,2560]{1,0:T(8,128)(2,1)S(1)}, u32[]{:S(2)}, u32[]{:S(2)}) collective-permute-start(bf16[32,2560]{1,0:T(8,128)(2,1)S(1)} %maximum_select_fusion.9), channel_id=1, source_target_pairs={{0,8},{1,9},{2,10},{3,11},{4,12},{5,13},{6,14},{7,15},{8,0},{9,1},... | collective-permute-start | bytes 491528 | tf_op jit(solution)/shard_map/ppermute | solution.py:49
  47.9 10.4 %collective-permute-start.8 = (bf16[128,1792]{1,0:T(8,128)(2,1)S(1)}, bf16[128,1792]{1,0:T(8,128)(2,1)S(1)}, u32[]{:S(2)}, u32[]{:S(2)}) collective-permute-start(bf16[128,1792]{1,0:T(8,128)(2,1)S(1)} %bitcast.199), channel_id=1, source_target_pairs={{0,4},{1,5},{2,6},{3,7},{4,0},{5,1},{6,2},{7,3},{8,12},{9,13},{10,... | collective-permute-start | bytes 1376264 | tf_op jit(solution)/shard_map/ppermute | solution.py:49
  49.4 11.0 %collective-permute-start.9 = (bf16[64,2560]{1,0:T(8,128)(2,1)}, bf16[64,2560]{1,0:T(8,128)(2,1)}, u32[]{:S(2)}, u32[]{:S(2)}) collective-permute-start(bf16[64,2560]{1,0:T(8,128)(2,1)} %bitcast.16), channel_id=1, source_target_pairs={{0,1},{1,0},{2,3},{3,2},{4,5},{5,4},{6,7},{7,6},{8,9},{9,8},{10,11... | collective-permute-start | bytes 983048 | tf_op jit(solution)/shard_map/ppermute | solution.py:49
  50.9 9.5 %collective-permute-start.10 = (bf16[256,512]{1,0:T(8,128)(2,1)}, bf16[256,512]{1,0:T(8,128)(2,1)}, u32[]{:S(2)}, u32[]{:S(2)}) collective-permute-start(bf16[256,512]{1,0:T(8,128)(2,1)} %bitcast.21), channel_id=1, source_target_pairs={{0,8},{1,9},{2,10},{3,11},{4,12},{5,13},{6,14},{7,15},{8,0},{9,1},... | collective-permute-start | bytes 786440 | tf_op jit(solution)/shard_map/ppermute | solution.py:49
  60.5 8.2 %collective-permute-start.11 = (bf16[256,1792]{1,0:T(8,128)(2,1)S(1)}, bf16[256,1792]{1,0:T(8,128)(2,1)S(1)}, u32[]{:S(2)}, u32[]{:S(2)}) collective-permute-start(bf16[256,1792]{1,0:T(8,128)(2,1)S(1)} %bitcast.184), channel_id=1, source_target_pairs={{0,2},{1,3},{2,0},{3,1},{4,6},{5,7},{6,4},{7,5},{8,10},{9,11},{10,... | collective-permute-start | bytes 2752520 | tf_op jit(solution)/shard_map/ppermute | solution.py:49
  60.7 35.3 %collective-permute-start.14 = (bf16[1024,512]{1,0:T(8,128)(2,1)}, bf16[1024,512]{1,0:T(8,128)(2,1)}, u32[]{:S(2)}, u32[]{:S(2)}) collective-permute-start(bf16[1024,512]{1,0:T(8,128)(2,1)} %dynamic_slice.152), channel_id=1, source_target_pairs={{0,1},{1,0},{2,3},{3,2},{4,5},{5,4},{6,7},{7,6},{8,9},{9,8},{10,11... | collective-permute-start | bytes 3145736 | tf_op jit(solution)/shard_map/ppermute | solution.py:49
  64.5 31.5 %collective-permute-start.12 = (bf16[128,2560]{1,0:T(8,128)(2,1)}, bf16[128,2560]{1,0:T(8,128)(2,1)}, u32[]{:S(2)}, u32[]{:S(2)}) collective-permute-start(bf16[128,2560]{1,0:T(8,128)(2,1)} %bitcast.39.refs_0_), channel_id=1, source_target_pairs={{0,4},{1,5},{2,6},{3,7},{4,0},{5,1},{6,2},{7,3},{8,12},{9,13},{10,... | collective-permute-start | bytes 1966088 | tf_op jit(solution)/shard_map/ppermute | solution.py:49
  66.1 37.6 %collective-permute-start.15 = (bf16[128,2560]{1,0:T(8,128)(2,1)}, bf16[128,2560]{1,0:T(8,128)(2,1)}, u32[]{:S(2)}, u32[]{:S(2)}) collective-permute-start(bf16[128,2560]{1,0:T(8,128)(2,1)} %bitcast.39.refs_0_), channel_id=1, source_target_pairs={{0,2},{1,3},{2,0},{3,1},{4,6},{5,7},{6,4},{7,5},{8,10},{9,11},{10,... | collective-permute-start | bytes 1966088 | tf_op jit(solution)/shard_map/ppermute | solution.py:49
  68.2 27.8 %collective-permute-start.13 = (bf16[512,512]{1,0:T(8,128)(2,1)}, bf16[512,512]{1,0:T(8,128)(2,1)}, u32[]{:S(2)}, u32[]{:S(2)}) collective-permute-start(bf16[512,512]{1,0:T(8,128)(2,1)} %bitcast.42.refs_4_), channel_id=1, source_target_pairs={{0,4},{1,5},{2,6},{3,7},{4,0},{5,1},{6,2},{7,3},{8,12},{9,13},{10,... | collective-permute-start | bytes 1572872 | tf_op jit(solution)/shard_map/ppermute | solution.py:49
  68.7 34.9 %collective-permute-start.17 = (bf16[512,512]{1,0:T(8,128)(2,1)}, bf16[512,512]{1,0:T(8,128)(2,1)}, u32[]{:S(2)}, u32[]{:S(2)}) collective-permute-start(bf16[512,512]{1,0:T(8,128)(2,1)} %bitcast.42.refs_4_), channel_id=1, source_target_pairs={{0,2},{1,3},{2,0},{3,1},{4,6},{5,7},{6,4},{7,5},{8,10},{9,11},{10,... | collective-permute-start | bytes 1572872 | tf_op jit(solution)/shard_map/ppermute | solution.py:49
  96.0 7.6 %collective-permute-start.16 = (bf16[128,2560]{1,0:T(8,128)(2,1)}, bf16[128,2560]{1,0:T(8,128)(2,1)}, u32[]{:S(2)}, u32[]{:S(2)}) collective-permute-start(bf16[128,2560]{1,0:T(8,128)(2,1)} %collective-permute-done.12.refs_1_), channel_id=1, source_target_pairs={{0,2},{1,3},{2,0},{3,1},{4,6},{5,7},{6,4},{7,5},{8,10},{9,11},{10,... | collective-permute-start | bytes 1966088 | tf_op jit(solution)/shard_map/ppermute | solution.py:49
  103.3 34.5 %collective-permute-start.19 = (bf16[1024,512]{1,0:T(8,128)(2,1)}, bf16[1024,512]{1,0:T(8,128)(2,1)}, u32[]{:S(2)}, u32[]{:S(2)}) collective-permute-start(bf16[1024,512]{1,0:T(8,128)(2,1)} %collective-permute-done.14), channel_id=1, source_target_pairs={{0,4},{1,5},{2,6},{3,7},{4,0},{5,1},{6,2},{7,3},{8,12},{9,13},{10,... | collective-permute-start | bytes 3145736 | tf_op jit(solution)/shard_map/ppermute | solution.py:49
  114.9 30.2 %all-to-all-start.2 = ((bf16[32,32,512]{2,1,0:T(8,128)(2,1)}), bf16[32,32,512]{2,1,0:T(8,128)(2,1)}, u32[]{:S(2)}, u32[]{:S(2)}) async-start(bf16[32,32,512]{2,1,0:T(8,128)(2,1)} %select_convert_fusion.1), calls=%async_computation.2 | async-start | bytes 2097152 | tf_op jit(solution)/shard_map/all_to_all | solution.py:1069
  119.2 40.9 %collective-permute-start.24 = (bf16[2048,128]{1,0:T(8,128)(2,1)}, bf16[2048,128]{1,0:T(8,128)(2,1)}, u32[]{:S(2)}, u32[]{:S(2)}) collective-permute-start(bf16[2048,128]{1,0:T(8,128)(2,1)} %copy-done.10), channel_id=1, source_target_pairs={{0,2},{1,3},{2,0},{3,1},{4,6},{5,7},{6,4},{7,5},{8,10},{9,11},{10,... | collective-permute-start | bytes 1572872 | tf_op jit(solution)/shard_map/ppermute | solution.py:49
  119.5 35.9 %collective-permute-start.22 = (bf16[256,2048]{1,0:T(8,128)(2,1)}, bf16[256,2048]{1,0:T(8,128)(2,1)}, u32[]{:S(2)}, u32[]{:S(2)}) collective-permute-start(bf16[256,2048]{1,0:T(8,128)(2,1)} %constant_dynamic-slice_fusion.20), channel_id=1, source_target_pairs={{0,1},{1,0},{2,3},{3,2},{4,5},{5,4},{6,7},{7,6},{8,9},{9,8},{10,11... | collective-permute-start | bytes 3145736 | tf_op jit(solution)/shard_map/ppermute | solution.py:49
  140.8 14.6 %collective-permute-start.20 = (bf16[1024,512]{1,0:T(8,128)(2,1)}, bf16[1024,512]{1,0:T(8,128)(2,1)}, u32[]{:S(2)}, u32[]{:S(2)}) collective-permute-start(bf16[1024,512]{1,0:T(8,128)(2,1)} %get-tuple-element.462.refs_1_.mid_a), channel_id=1, source_target_pairs={{0,2},{1,3},{2,0},{3,1},{4,6},{5,7},{6,4},{7,5},{8,10},{9,11},{10,... | collective-permute-start | bytes 3145736 | tf_op jit(solution)/shard_map/ppermute | solution.py:49
  140.8 14.6 %collective-permute-start.21 = (bf16[1024,512]{1,0:T(8,128)(2,1)}, bf16[1024,512]{1,0:T(8,128)(2,1)}, u32[]{:S(2)}, u32[]{:S(2)}) collective-permute-start(bf16[1024,512]{1,0:T(8,128)(2,1)} %get-tuple-element.461.refs_2_.mid_b), channel_id=1, source_target_pairs={{0,2},{1,3},{2,0},{3,1},{4,6},{5,7},{6,4},{7,5},{8,10},{9,11},{10,... | collective-permute-start | bytes 3145736 | tf_op jit(solution)/shard_map/ppermute | solution.py:49
  157.5 25.3 %collective-permute-start.25 = (bf16[256,2048]{1,0:T(8,128)(2,1)}, bf16[256,2048]{1,0:T(8,128)(2,1)}, u32[]{:S(2)}, u32[]{:S(2)}) collective-permute-start(bf16[256,2048]{1,0:T(8,128)(2,1)} %collective-permute-done.22), channel_id=1, source_target_pairs={{0,4},{1,5},{2,6},{3,7},{4,0},{5,1},{6,2},{7,3},{8,12},{9,13},{10,... | collective-permute-start | bytes 3145736 | tf_op jit(solution)/shard_map/ppermute | solution.py:49
  159.1 16.1 %collective-permute-start.23 = (bf16[512,512]{1,0:T(8,128)(2,1)}, bf16[512,512]{1,0:T(8,128)(2,1)S(1)}, u32[]{:S(2)}, u32[]{:S(2)}) collective-permute-start(bf16[512,512]{1,0:T(8,128)(2,1)} %get-tuple-element.250.chosen_ref), channel_id=1, source_target_pairs={{0,1},{1,0},{2,3},{3,2},{4,5},{5,4},{6,7},{7,6},{8,9},{9,8},{10,11... | collective-permute-start | bytes 1572872 | tf_op jit(solution)/shard_map/ppermute | solution.py:49
  185.3 23.0 %collective-permute-start.26 = (bf16[256,2048]{1,0:T(8,128)(2,1)S(1)}, bf16[256,2048]{1,0:T(8,128)(2,1)S(1)}, u32[]{:S(2)}, u32[]{:S(2)}) collective-permute-start(bf16[256,2048]{1,0:T(8,128)(2,1)S(1)} %get-tuple-element.460.mid_a), channel_id=1, source_target_pairs={{0,2},{1,3},{2,0},{3,1},{4,6},{5,7},{6,4},{7,5},{8,10},{9,11},{10,... | collective-permute-start | bytes 3145736 | tf_op jit(solution)/shard_map/ppermute | solution.py:49
  185.4 23.0 %collective-permute-start.27 = (bf16[256,2048]{1,0:T(8,128)(2,1)S(1)}, bf16[256,2048]{1,0:T(8,128)(2,1)S(1)}, u32[]{:S(2)}, u32[]{:S(2)}) collective-permute-start(bf16[256,2048]{1,0:T(8,128)(2,1)S(1)} %get-tuple-element.459.mid_b), channel_id=1, source_target_pairs={{0,2},{1,3},{2,0},{3,1},{4,6},{5,7},{6,4},{7,5},{8,10},{9,11},{10,... | collective-permute-start | bytes 3145736 | tf_op jit(solution)/shard_map/ppermute | solution.py:49
  216.1 25.1 %collective-permute-start.28 = (bf16[256,2048]{1,0:T(8,128)(2,1)S(1)}, bf16[256,2048]{1,0:T(8,128)(2,1)S(1)}, u32[]{:S(2)}, u32[]{:S(2)}) collective-permute-start(bf16[256,2048]{1,0:T(8,128)(2,1)S(1)} %get-tuple-element.268.refs_0_), channel_id=1, source_target_pairs={{0,1},{1,0},{2,3},{3,2},{4,5},{5,4},{6,7},{7,6},{8,9},{9,8},{10,11... | collective-permute-start | bytes 3145736 | tf_op jit(solution)/shard_map/ppermute | solution.py:49
  236.5 58.1 %collective-permute-start.30 = (bf16[256,2048]{1,0:T(8,128)(2,1)S(1)}, bf16[256,2048]{1,0:T(8,128)(2,1)S(1)}, u32[]{:S(2)}, u32[]{:S(2)}) collective-permute-start(bf16[256,2048]{1,0:T(8,128)(2,1)S(1)} %get-tuple-element.272.refs_0_), channel_id=1, source_target_pairs={{0,1},{1,0},{2,3},{3,2},{4,5},{5,4},{6,7},{7,6},{8,9},{9,8},{10,11... | collective-permute-start | bytes 3145736 | tf_op jit(solution)/shard_map/ppermute | solution.py:49
  292.3 161.6 %collective-permute-start.35 = (bf16[512,1024]{1,0:T(8,128)(2,1)}, bf16[512,1024]{1,0:T(8,128)(2,1)}, u32[]{:S(2)}, u32[]{:S(2)}) collective-permute-start(bf16[512,1024]{1,0:T(8,128)(2,1)} %get-tuple-element.458), channel_id=1, source_target_pairs={{0,1},{1,0},{2,3},{3,2},{4,5},{5,4},{6,7},{7,6},{8,9},{9,8},{10,11... | collective-permute-start | bytes 3145736 | tf_op jit(solution)/shard_map/ppermute | solution.py:49
  293.2 49.9 %collective-permute-start.29 = (bf16[256,2048]{1,0:T(8,128)(2,1)S(1)}, bf16[256,2048]{1,0:T(8,128)(2,1)S(1)}, u32[]{:S(2)}, u32[]{:S(2)}) collective-permute-start(bf16[256,2048]{1,0:T(8,128)(2,1)S(1)} %get-tuple-element.453), channel_id=1, source_target_pairs={{0,1},{1,0},{2,3},{3,2},{4,5},{5,4},{6,7},{7,6},{8,9},{9,8},{10,11... | collective-permute-start | bytes 3145736 | tf_op jit(solution)/shard_map/ppermute | solution.py:49
  342.3 42.2 %collective-permute-start.31 = (bf16[256,2048]{1,0:T(8,128)(2,1)S(1)}, bf16[256,2048]{1,0:T(8,128)(2,1)S(1)}, u32[]{:S(2)}, u32[]{:S(2)}) collective-permute-start(bf16[256,2048]{1,0:T(8,128)(2,1)S(1)} %get-tuple-element.455), channel_id=1, source_target_pairs={{0,1},{1,0},{2,3},{3,2},{4,5},{5,4},{6,7},{7,6},{8,9},{9,8},{10,11... | collective-permute-start | bytes 3145736 | tf_op jit(solution)/shard_map/ppermute | solution.py:49
  386.7 25.1 %collective-permute-start.32 = (bf16[4,512,128]{2,1,0:T(8,128)(2,1)S(1)}, bf16[4,512,128]{2,1,0:T(8,128)(2,1)S(1)}, u32[]{:S(2)}, u32[]{:S(2)}) collective-permute-start(bf16[4,512,128]{2,1,0:T(8,128)(2,1)S(1)} %pad_maximum_fusion.2), channel_id=1, source_target_pairs={{0,1},{1,0},{2,3},{3,2},{4,5},{5,4},{6,7},{7,6},{8,9},{9,8},{10,11... | collective-permute-start | bytes 1572872 | tf_op jit(solution)/shard_map/ppermute | solution.py:49
  411.8 12.7 %collective-permute-start.33 = (bf16[4,256,128]{2,1,0:T(8,128)(2,1)S(1)}, bf16[4,256,128]{2,1,0:T(8,128)(2,1)S(1)}, u32[]{:S(2)}, u32[]{:S(2)}) collective-permute-start(bf16[4,256,128]{2,1,0:T(8,128)(2,1)S(1)} %dynamic-slice_convert_fusion.9), channel_id=1, source_target_pairs={{0,1},{1,0},{2,3},{3,2},{4,5},{5,4},{6,7},{7,6},{8,9},{9,8},{10,11... | collective-permute-start | bytes 786440 | tf_op jit(solution)/shard_map/ppermute | solution.py:49
  424.5 32.6 %collective-permute-start.34 = (bf16[512,1024]{1,0:T(8,128)(2,1)}, bf16[512,1024]{1,0:T(8,128)(2,1)}, u32[]{:S(2)}, u32[]{:S(2)}) collective-permute-start(bf16[512,1024]{1,0:T(8,128)(2,1)} %get-tuple-element.293), channel_id=1, source_target_pairs={{0,1},{1,0},{2,3},{3,2},{4,5},{5,4},{6,7},{7,6},{8,9},{9,8},{10,11... | collective-permute-start | bytes 3145736 | tf_op jit(solution)/shard_map/ppermute | solution.py:49
  445.4 30.5 %all-to-all-start.3 = ((bf16[32,32,512]{2,1,0:T(8,128)(2,1)}), bf16[32,32,512]{2,1,0:T(8,128)(2,1)}, u32[]{:S(2)}, u32[]{:S(2)}) async-start(bf16[32,32,512]{2,1,0:T(8,128)(2,1)} %bitcast.56), calls=%async_computation.3 | async-start | bytes 2097152 | tf_op jit(solution)/shard_map/all_to_all | solution.py:1069
  480.3 19.3 %collective-permute-start.37 = (bf16[128,2048]{1,0:T(8,128)(2,1)S(1)}, bf16[128,2048]{1,0:T(8,128)(2,1)S(1)}, u32[]{:S(2)}, u32[]{:S(2)}) collective-permute-start(bf16[128,2048]{1,0:T(8,128)(2,1)S(1)} %bitcast.226), channel_id=1, source_target_pairs={{0,1},{1,0},{2,3},{3,2},{4,5},{5,4},{6,7},{7,6},{8,9},{9,8},{10,11... | collective-permute-start | bytes 1572872 | tf_op jit(solution)/shard_map/ppermute | solution.py:49
  498.9 22.9 %collective-permute-start.39 = (bf16[256,2560]{1,0:T(8,128)(2,1)}, bf16[256,2560]{1,0:T(8,128)(2,1)S(1)}, u32[]{:S(2)}, u32[]{:S(2)}) collective-permute-start(bf16[256,2560]{1,0:T(8,128)(2,1)} %get-tuple-element.316), channel_id=1, source_target_pairs={{0,2},{1,3},{2,0},{3,1},{4,6},{5,7},{6,4},{7,5},{8,10},{9,11},{10,... | collective-permute-start | bytes 3932168 | tf_op jit(solution)/shard_map/ppermute | solution.py:49
  499.0 22.8 %collective-permute-start.40 = (bf16[1024,512]{1,0:T(8,128)(2,1)}, bf16[1024,512]{1,0:T(8,128)(2,1)S(1)}, u32[]{:S(2)}, u32[]{:S(2)}) collective-permute-start(bf16[1024,512]{1,0:T(8,128)(2,1)} %get-tuple-element.318), channel_id=1, source_target_pairs={{0,2},{1,3},{2,0},{3,1},{4,6},{5,7},{6,4},{7,5},{8,10},{9,11},{10,... | collective-permute-start | bytes 3145736 | tf_op jit(solution)/shard_map/ppermute | solution.py:49
  499.8 21.9 %collective-permute-start.38 = (bf16[64,2048]{1,0:T(8,128)(2,1)S(1)}, bf16[64,2048]{1,0:T(8,128)(2,1)S(1)}, u32[]{:S(2)}, u32[]{:S(2)}) collective-permute-start(bf16[64,2048]{1,0:T(8,128)(2,1)S(1)} %bitcast.235), channel_id=1, source_target_pairs={{0,4},{1,5},{2,6},{3,7},{4,0},{5,1},{6,2},{7,3},{8,12},{9,13},{10,... | collective-permute-start | bytes 786440 | tf_op jit(solution)/shard_map/ppermute | solution.py:49
  522.3 22.0 %collective-permute-start.42 = (bf16[128,2560]{1,0:T(8,128)(2,1)S(1)}, bf16[128,2560]{1,0:T(8,128)(2,1)S(1)}, u32[]{:S(2)}, u32[]{:S(2)}) collective-permute-start(bf16[128,2560]{1,0:T(8,128)(2,1)S(1)} %bitcast.219), channel_id=1, source_target_pairs={{0,1},{1,0},{2,3},{3,2},{4,5},{5,4},{6,7},{7,6},{8,9},{9,8},{10,11... | collective-permute-start | bytes 1966088 | tf_op jit(solution)/shard_map/ppermute | solution.py:49
  523.4 20.8 %collective-permute-start.43 = (bf16[512,512]{1,0:T(8,128)(2,1)S(1)}, bf16[512,512]{1,0:T(8,128)(2,1)S(1)}, u32[]{:S(2)}, u32[]{:S(2)}) collective-permute-start(bf16[512,512]{1,0:T(8,128)(2,1)S(1)} %bitcast.225), channel_id=1, source_target_pairs={{0,4},{1,5},{2,6},{3,7},{4,0},{5,1},{6,2},{7,3},{8,12},{9,13},{10,... | collective-permute-start | bytes 1572872 | tf_op jit(solution)/shard_map/ppermute | solution.py:49
  524.9 19.3 %collective-permute-start.41 = (bf16[32,2048]{1,0:T(8,128)(2,1)S(1)}, bf16[32,2048]{1,0:T(8,128)(2,1)S(1)}, u32[]{:S(2)}, u32[]{:S(2)}) collective-permute-start(bf16[32,2048]{1,0:T(8,128)(2,1)S(1)} %bitcast.248), channel_id=1, source_target_pairs={{0,8},{1,9},{2,10},{3,11},{4,12},{5,13},{6,14},{7,15},{8,0},{9,1},... | collective-permute-start | bytes 393224 | tf_op jit(solution)/shard_map/ppermute | solution.py:49
  544.6 15.1 %collective-permute-start.49 = (bf16[16,2048]{1,0:T(8,128)(2,1)S(1)}, bf16[16,2048]{1,0:T(8,128)(2,1)S(1)}, u32[]{:S(2)}, u32[]{:S(2)}) collective-permute-start(bf16[16,2048]{1,0:T(8,128)(2,1)S(1)} %fusion.51), channel_id=1, source_target_pairs={{0,16},{1,17},{2,18},{3,19},{4,20},{5,21},{6,22},{7,23},{8,24},{9,... | collective-permute-start | bytes 196616 | tf_op jit(solution)/shard_map/ppermute | solution.py:49
  546.6 13.2 %collective-permute-start.50 = (bf16[64,2560]{1,0:T(8,128)(2,1)S(1)}, bf16[64,2560]{1,0:T(8,128)(2,1)S(1)}, u32[]{:S(2)}, u32[]{:S(2)}) collective-permute-start(bf16[64,2560]{1,0:T(8,128)(2,1)S(1)} %bitcast.232), channel_id=1, source_target_pairs={{0,4},{1,5},{2,6},{3,7},{4,0},{5,1},{6,2},{7,3},{8,12},{9,13},{10,... | collective-permute-start | bytes 983048 | tf_op jit(solution)/shard_map/ppermute | solution.py:49
  547.9 11.7 %collective-permute-start.45 = (bf16[128,1664]{1,0:T(8,128)(2,1)S(1)}, bf16[128,1664]{1,0:T(8,128)(2,1)S(1)}, u32[]{:S(2)}, u32[]{:S(2)}) collective-permute-start(bf16[128,1664]{1,0:T(8,128)(2,1)S(1)} %bitcast.229), channel_id=1, source_target_pairs={{0,1},{1,0},{2,3},{3,2},{4,5},{5,4},{6,7},{7,6},{8,9},{9,8},{10,11... | collective-permute-start | bytes 1277960 | tf_op jit(solution)/shard_map/ppermute | solution.py:49
  549.3 10.4 %collective-permute-start.51 = (bf16[256,512]{1,0:T(8,128)(2,1)S(1)}, bf16[256,512]{1,0:T(8,128)(2,1)S(1)}, u32[]{:S(2)}, u32[]{:S(2)}) collective-permute-start(bf16[256,512]{1,0:T(8,128)(2,1)S(1)} %bitcast.236), channel_id=1, source_target_pairs={{0,8},{1,9},{2,10},{3,11},{4,12},{5,13},{6,14},{7,15},{8,0},{9,1},... | collective-permute-start | bytes 786440 | tf_op jit(solution)/shard_map/ppermute | solution.py:49
  568.6 8.4 %collective-permute-start.54 = (bf16[16,2560]{1,0:T(8,128)(2,1)S(1)}, bf16[16,2560]{1,0:T(8,128)(2,1)S(1)}, u32[]{:S(2)}, u32[]{:S(2)}) collective-permute-start(bf16[16,2560]{1,0:T(8,128)(2,1)S(1)} %fusion.50), channel_id=1, source_target_pairs={{0,16},{1,17},{2,18},{3,19},{4,20},{5,21},{6,22},{7,23},{8,24},{9,... | collective-permute-start | bytes 245768 | tf_op jit(solution)/shard_map/ppermute | solution.py:49
  (70 other events, 1143.3 us)
Sparse Core Ops, SparseCore 0:
  24.1 58.4 all-gather.1

commit v6 on v5

--- a/solution.py
+++ b/solution.py
@@ -18,7 +18,7 @@
 SLOT_PARTS = 2
 UNIT_STEP = 256
 COLUMN_STEP = 256
-UNIT_ROWS = 256
+UNIT_ROWS = 512
 
 
 EPS = 1e-05
@@ -227,15 +227,15 @@
     for_lengths(info[0], rows, pair_ref.shape[0], work)
 
 
-def attention_specs(part, rows, length):
+def attention_specs(part, rows, length, first=0):
     span = (rows, 4 * PAIR)
     return {
         "table_pair": pl.BlockSpec((length, PAIR), lambda g, s: (0, 0)),
         "table": pl.BlockSpec((rows, PAIR), lambda g, s: (s[0], 0)),
-        "pair": pl.BlockSpec((length, PAIR), lambda g, s: (0, g)),
-        "part": pl.BlockSpec(span, lambda g, s: (part, g)),
-        "wide": pl.BlockSpec(span, lambda g, s: (0, g)),
-        "sums": pl.BlockSpec((1, 8, rows), lambda g, s: (g, 0, 0)),
+        "pair": pl.BlockSpec((length, PAIR), lambda g, s: (0, g + first)),
+        "part": pl.BlockSpec(span, lambda g, s: (part, g + first)),
+        "wide": pl.BlockSpec(span, lambda g, s: (0, g + first)),
+        "sums": pl.BlockSpec((1, 8, rows), lambda g, s: (g + first, 0, 0)),
     }
 
 
@@ -281,25 +281,25 @@
     )(info, queries, pair_pre, cosine, sine, cosine, sine)
 
 
-def attention_backward(info, low, grad, sums, pair_pre, tables, part, length, before):
+def attention_backward(info, low, grad, sums, pair_pre, tables, part, length, groups, before):
+    first, count = groups
     cosine, sine = tables
     rows = cosine.shape[0] // BLOCK_PARTS
     heads = low.shape[1] // HEAD_WIDTH
-    spec = attention_specs(part, rows, length)
-    before = [] if before is None else [before]
+    spec = attention_specs(part, rows, length, first)
     half = pltpu.VMEM((length, PAIR), jnp.bfloat16)
     full = pltpu.VMEM((length, PAIR), jnp.float32)
     return pl.pallas_call(
         attention_backward_kernel,
         grid_spec=pltpu.PrefetchScalarGridSpec(
             num_scalar_prefetch=1,
-            grid=(4,),
+            grid=(count,),
             in_specs=[
                 spec["wide"], spec["wide"], spec["sums"], spec["pair"],
                 spec["table_pair"], spec["table_pair"], spec["table"], spec["table"],
             ]
             + [pl.BlockSpec(memory_space=pl.ANY)] * len(before),
-            out_specs=[spec["part"], pl.BlockSpec((1, length, PAIR), lambda g, s: (s[1 + g], 0, 0))],
+            out_specs=[spec["part"], pl.BlockSpec((1, length, PAIR), lambda g, s: (s[1 + g + first], 0, 0))],
             scratch_shapes=[
                 half, half, half, half,
                 pltpu.VMEM((HEAD_WIDTH, length), jnp.bfloat16),
@@ -310,11 +310,11 @@
             jax.ShapeDtypeStruct((2 * rows, low.shape[1]), jnp.bfloat16),
             jax.ShapeDtypeStruct((4, length, PAIR), jnp.float32),
         ],
-        input_output_aliases={9: 0} if before else {},
+        input_output_aliases={9 + at: at for at in range(len(before))},
         compiler_params=pltpu.CompilerParams(
             dimension_semantics=("arbitrary",), vmem_limit_bytes=VMEM_LIMIT
         ),
-        cost_estimate=attention_cost(rows, length, heads, 5),
+        cost_estimate=attention_cost(rows, length, heads, 5 if count == 4 else 0),
         name="attention_backward",
     )(info, low, grad, sums, pair_pre, cosine, sine, cosine, sine, *before)
 
@@ -1296,6 +1296,17 @@
         )
         second_came[part] = (grad_second[:block], swap(grad_second[block:], 1, devices))
 
+    share = upstream.shape[1] // mp_count
+
+    def columns(value, index):
+        return lax.dynamic_slice_in_dim(value, index * share, share, 1)
+
+    leaving_columns = [columns(dense_rows[part], 1 - mp_index) for part in range(2)]
+    dense_came = [None, swap(leaving_columns[1], 1, devices)]
+
+    def pick_block(value, at):
+        return lax.dynamic_slice_in_dim(value, at * block, block, 1)
+
     query_grad = None
     grad_hidden = [None, None]
     pair_grads = [None, None]
@@ -1304,20 +1315,24 @@
         if part == 1:
             here, came, dense_rows[0] = lax.optimization_barrier((here, came, dense_rows[0]))
         else:
-            here, came, query_grad = lax.optimization_barrier((here, came, query_grad))
+            here, came, query_grad, dense_came[1] = lax.optimization_barrier(
+                (here, came, query_grad, dense_came[1])
+            )
         grad_hidden[part], grad_attended = hidden_backward(
             infos[part], here, came, hidden_parts[part], upstream, dense_gain, output_weights
         )
+        taken = (lows[part], grad_attended, sums[part], pair_pre, tables, part, spans[part])
+        if part == 1:
+            query_grad, pair_grads[part] = attention_backward(infos[part], *taken, (0, 4), [])
+            continue
+        query_grad, pair_grads[part] = attention_backward(infos[part], *taken, (0, 2), [query_grad])
+        leaving = to_low(jnp.concatenate([pick_block(pair_grads[1], at) for at in other_at], axis=1))
+        leaving, pair_grads[part] = lax.optimization_barrier((leaving, pair_grads[part]))
+        came_long = swap(leaving, 1, devices)
         query_grad, pair_grads[part] = attention_backward(
-            infos[part], lows[part], grad_attended, sums[part], pair_pre, tables, part, spans[part], query_grad
+            infos[part], *taken, (2, 2), [query_grad, pair_grads[part]]
         )
 
-    def pick_block(value, at):
-        return lax.dynamic_slice_in_dim(value, at * block, block, 1)
-
-    came_long = swap(
-        to_low(jnp.concatenate([pick_block(pair_grads[1], at) for at in other_at], axis=1)), 1, devices
-    )
     pair_grads[0], came_long = lax.optimization_barrier((pair_grads[0], came_long))
     came_short = swap(to_low(pick_block(pair_grads[0], other_at[0])), 1, devices)
     pair_own = jnp.concatenate(
@@ -1328,14 +1343,8 @@
         axis=1,
     )
 
-    share = upstream.shape[1] // mp_count
-
-    def columns(value, index):
-        return lax.dynamic_slice_in_dim(value, index * share, share, 1)
-
-    leaving = [columns(dense_rows[part], 1 - mp_index) for part in range(2)]
-    _, leaving[0] = lax.optimization_barrier((came_short, leaving[0]))
-    dense_came = [swap(x, 1, devices) for x in leaving]
+    _, leaving_columns[0] = lax.optimization_barrier((came_short, leaving_columns[0]))
+    dense_came[0] = swap(leaving_columns[0], 1, devices)
 
     embedded_grad_low, token_grad = embed_backward(
         jnp.stack([*own_at, *head_order]).astype(jnp.int32), query_grad, pair_own, came_long, came_short, tables, grad_hidden, embedded,

time: 598 us -> 592 us (0.990)
  other arithmetic: 45.5 us -> 35.9 us
  local copies, waits for them, and re-layouts: 32.8 us -> 39.6 us
    unnamed x122 -> x146, local copies, waits for them, and re-layouts: 13.5 us -> 17.6 us
    pallas_call x2 -> x3, Pallas kernels: 49.8 us -> 52.2 us  [attention_backward(): pl.pallas_call(attention_backward_kernel, grid_spec=pltpu.PrefetchScalarG...]
  transfers between devices with their start and end apart: 59 -> 59, of which waited for: 17 -> 18; matrix products, arithmetic and copies ran while one was open for 11% -> 9% of each run, Pallas kernels for 54% -> 51%
where the time goes in v6:
time: 592 us; the launch traced here: 582 us
  Pallas kernels  320 us (54%)
  waiting for transfers between devices  84.4 us (14%)
  starting transfers between devices  74.8 us (13%)
  local copies, waits for them, and re-layouts  39.6 us (7%)
  other arithmetic  35.9 us (6%)
  between operations  17.1 us (3%)
  matrix products  10.9 us (2%)
    pallas_call x2, Pallas kernels, feed_forward(): pl.pallas_call(lambda info, *refs: feed_forward_kernel(*refs), grid_spec=...  95.1 us
    ppermute x56, waiting for transfers between devices, swap(): lax.ppermute(value, ('dp', 'mp'), [(d, d ^ mask) for d in range(devices)])  67.2 us
    ppermute x56, starting transfers between devices, swap(): lax.ppermute(value, ('dp', 'mp'), [(d, d ^ mask) for d in range(devices)])  65.7 us
    pallas_call x3, Pallas kernels, attention_backward(): pl.pallas_call(attention_backward_kernel, grid_spec=pltpu.PrefetchScalarG...  52.2 us
    pallas_call x2, Pallas kernels, slot_backward(): pl.pallas_call(functools.partial(slot_backward_kernel, first, last), grid...  36.6 us
    pallas_call x2, Pallas kernels, attention_forward(): pl.pallas_call(attention_forward_kernel, grid_spec=pltpu.PrefetchScalarGr...  33.2 us
    pallas_call x2, Pallas kernels, project(): pl.pallas_call(functools.partial(project_kernel, more), grid_spec=pltpu.P...  19.6 us
    pallas_call x1, Pallas kernels, slot_attention(): pl.pallas_call(slot_attention_kernel, grid=(entries // part,), in_specs=[...  19.4 us
  transfers between devices with their start and end apart: 59, of which 18 were waited for; matrix products, arithmetic and copies ran while one was open for 9% of the time, Pallas kernels for 51%

profile of v6, /device:TPU:0, one launch (start us, length us, event | category | flops | bytes accessed | tf_op | source)
XLA Modules:
  0.0 582.4 jit_solution(14653273657862811980)
XLA Ops:
  11.2 4.0 collective-permute-start
  16.8 2.9 collective-permute-start.4
  24.0 2.3 constant_dynamic-slice_fusion.20
  26.3 2.3 dynamic_slice.152
  31.6 3.3 collective-permute-done.1
  34.9 3.6 collective-permute-done.5
  41.8 4.5 collective-permute-done.7
  51.1 5.8 %collective-permute-done.8 = bf16[128,1792]{1,0:T(8,128)(2,1)S(1)} collective-permute-done((bf16[128,1792]{1,0:T(8,128)(2,1)S(1)}, bf16[128,1792]{1,0:T(8,128)(2,1)S(1)}, u32[]{:S(2)}, u32[]{:S(2)}) %collective-permute-start.8) | collective-permute-done | bytes 458784 | tf_op jit(solution)/shard_map/ppermute | solution.py:49
  65.3 2.6 maximum_select_fusion.1
  67.9 19.4 %slot_attention.1 = (bf16[4096,1536]{1,0:T(8,128)(2,1)}, f32[512,8,128]{2,1,0:T(8,128)S(1)}, bf16[512,512]{1,0:T(8,128)(2,1)S(1)}, f32[512,512]{1,0:T(8,128)S(1)}, f32[8,512]{1,0:T(8,128)S(1)}) custom-call(bf16[512,8,512]{2,1,0:T(8,128)(2,1)} %pieces_ref.5, s32[512,1,128]{2,1,0:T(1,128)S(1)} %broadcast_in_dim.30.counts_ref, bf16[512,1792]{1,0:T(8,128)(2,1)S(1)} %bitcast.160), custom_call_target="tpu_custom_call" | custom-call | flops 2097152 | bytes 4096 | tf_op jit(solution)/shard_map/slot_attention/pallas_call | solution.py:400
  91.6 5.0 compare_reduce_fusion
  100.9 5.8 %units_forward.1 = (bf16[512,512]{1,0:T(8,128)(2,1)S(1)}, f32[512,512]{1,0:T(8,128)}) custom-call(s32[2]{0:T(128)S(1)} %pad_add_fusion.2.places, bf16[512,512]{1,0:T(8,128)(2,1)S(1)} %copy-done.30, f32[512,512]{1,0:T(8,128)} %copy-done.26, bf16[128,2560]{1,0:T(8,128)(2,1)S(1)} %bitcast.165, bf16[128,2560]{1,0:T(8,128)(2,1)S(1)} %collective-permute-done.12.refs_1_, ...), custom_call_target="tpu_custom_call" | custom-call | flops 262144 | bytes 262144 | tf_op jit(solution)/shard_map/units_forward/pallas_call | solution.py:490
  109.3 3.6 all-to-all-start.2
  115.0 17.9 %collective-permute-done.19 = bf16[1024,512]{1,0:T(8,128)(2,1)} collective-permute-done((bf16[1024,512]{1,0:T(8,128)(2,1)}, bf16[1024,512]{1,0:T(8,128)(2,1)}, u32[]{:S(2)}, u32[]{:S(2)}) %collective-permute-start.19) | collective-permute-done | bytes 1048608 | tf_op jit(solution)/shard_map/ppermute | solution.py:49
  135.9 3.2 all-to-all-done.2
  139.1 2.8 fusion.34
  141.9 7.4 %collective-permute-done.22 = bf16[256,2048]{1,0:T(8,128)(2,1)} collective-permute-done((bf16[256,2048]{1,0:T(8,128)(2,1)}, bf16[256,2048]{1,0:T(8,128)(2,1)}, u32[]{:S(2)}, u32[]{:S(2)}) %collective-permute-start.22) | collective-permute-done | bytes 1048608 | tf_op jit(solution)/shard_map/ppermute | solution.py:49
  154.0 13.6 %project.2 = (f32[1024,512]{1,0:T(8,128)}, bf16[512,2048]{1,0:T(8,128)(2,1)}, f32[512,2048]{1,0:T(8,128)}) custom-call(s32[2]{0:T(128)S(1)} %pad_add_fusion.3.info, bf16[512,512]{1,0:T(8,128)(2,1)} %get-tuple-element.255.chosen_ref, bf16[512,2048]{1,0:T(8,128)(2,1)} %all-gather.2.cloned.1.call-done.embed_ref, f32[1,2048]{1,0:T(1,128)S(1)} %bitcast.176, ...), custom_call_target="tpu_custom_call" | custom-call | flops 1073741824 | bytes 1048576 | tf_op jit(solution)/shard_map/project/pallas_call | solution.py:855
  169.2 6.0 %project.3.pair_ref = f32[1024,512]{1,0:T(8,128)S(1)} custom-call(s32[2]{0:T(128)S(1)} %pad_add_fusion.1.info, bf16[512,512]{1,0:T(8,128)(2,1)S(1)} %collective-permute-done.23.chosen_ref, bf16[512,2048]{1,0:T(8,128)(2,1)} %all-gather.2.cloned.1.call-done.embed_ref, f32[1,2048]{1,0:T(1,128)S(1)} %bitcast.177, ...), custom_call_target="tpu_custom_call", output_to_operand_aliasing={{}: (7, {})} | custom-call | flops 1073741824 | bytes 1048576 | tf_op jit(solution)/shard_map/project/pallas_call | solution.py:855
  180.3 20.9 %attention_forward.2 = (bf16[256,2048]{1,0:T(8,128)(2,1)S(1)}, bf16[256,2048]{1,0:T(8,128)(2,1)S(1)}, f32[4,8,256]{2,1,0:T(8,128)S(1)}) custom-call(s32[5]{0:T(128)S(1)} %stack.84.info, f32[512,2048]{1,0:T(8,128)} %get-tuple-element.263.query_ref, f32[1024,512]{1,0:T(8,128)S(1)} %copy-done.4, f32[1024,128]{1,0:T(8,128)S(1)} %copy-done.7, ...), custom_call_target="tpu_custom_call" | custom-call | flops 21474836480 | bytes 8388608 | tf_op jit(solution)/shard_map/attention_forward/pallas_call | solution.py:256
  203.2 6.7 %output_project.2 = (f32[256,2048]{1,0:T(8,128)}, bf16[256,2048]{1,0:T(8,128)(2,1)S(1)}) custom-call(bf16[256,2048]{1,0:T(8,128)(2,1)S(1)} %get-tuple-element.264.rows_ref, bf16[512,2048]{1,0:T(8,128)(2,1)} %get-tuple-element.265.embedded_ref, f32[1,2048]{1,0:T(1,128)S(1)} %bitcast.172, bf16[1024,2048]{1,0:T(8,128)(2,1)} %near_ref.8, ...), custom_call_target="tpu_custom_call" | custom-call | flops 4294967296 | bytes 12582912 | tf_op jit(solution)/shard_map/output_project/pallas_call | solution.py:898
  210.5 12.2 %attention_forward.3 = (bf16[256,2048]{1,0:T(8,128)(2,1)S(1)}, bf16[256,2048]{1,0:T(8,128)(2,1)S(1)}, f32[4,8,256]{2,1,0:T(8,128)S(1)}) custom-call(s32[5]{0:T(128)S(1)} %stack.85.info, f32[512,2048]{1,0:T(8,128)} %get-tuple-element.263.query_ref, f32[1024,512]{1,0:T(8,128)S(1)} %copy-done.5, f32[1024,128]{1,0:T(8,128)S(1)} %copy-done.7, ...), custom_call_target="tpu_custom_call" | custom-call | flops 10737418240 | bytes 8388608 | tf_op jit(solution)/shard_map/attention_forward/pallas_call | solution.py:256
  222.8 6.9 %output_project.3 = (f32[256,2048]{1,0:T(8,128)}, bf16[256,2048]{1,0:T(8,128)(2,1)S(1)}) custom-call(bf16[256,2048]{1,0:T(8,128)(2,1)S(1)} %get-tuple-element.269.rows_ref, bf16[512,2048]{1,0:T(8,128)(2,1)} %get-tuple-element.265.embedded_ref, f32[1,2048]{1,0:T(1,128)S(1)} %bitcast.173, bf16[1024,2048]{1,0:T(8,128)(2,1)} %near_ref.8, ...), custom_call_target="tpu_custom_call" | custom-call | flops 4294967296 | bytes 12582912 | tf_op jit(solution)/shard_map/output_project/pallas_call | solution.py:898
  229.7 4.6 collective-permute-start.30
  235.1 47.5 %feed_forward.2 = (bf16[512,2048]{1,0:T(8,128)(2,1)S(1)}, bf16[512,2048]{1,0:T(8,128)(2,1)}) custom-call(s32[2]{0:T(128)S(1)} %pad_add_fusion.info, bf16[256,2048]{1,0:T(8,128)(2,1)S(1)} %get-tuple-element.273.refs_0_, bf16[256,2048]{1,0:T(8,128)(2,1)S(1)} %collective-permute-done.28.refs_1_, bf16[1024,2048]{1,0:T(8,128)(2,1)} %rising_ref.3, ...), custom_call_target="tpu_custom_call" | custom-call | flops 50197430272 | bytes 69206016 | tf_op jit(solution)/shard_map/feed_forward/pallas_call | solution.py:770
  283.5 47.6 %feed_forward.3 = (bf16[512,2048]{1,0:T(8,128)(2,1)S(1)}, bf16[512,2048]{1,0:T(8,128)(2,1)}) custom-call(s32[2]{0:T(128)S(1)} %pad_add_fusion.4.info, bf16[256,2048]{1,0:T(8,128)(2,1)S(1)} %get-tuple-element.277.refs_0_, bf16[256,2048]{1,0:T(8,128)(2,1)S(1)} %collective-permute-done.30.refs_1_, bf16[1024,2048]{1,0:T(8,128)(2,1)} %rising_ref.3, ...), custom_call_target="tpu_custom_call" | custom-call | flops 50197430272 | bytes 69206016 | tf_op jit(solution)/shard_map/feed_forward/pallas_call | solution.py:770
  336.0 7.3 %hidden_backward.2 = (f32[256,2048]{1,0:T(8,128)}, bf16[256,2048]{1,0:T(8,128)(2,1)S(1)}) custom-call(s32[5]{0:T(128)S(1)} %stack.84.info, bf16[256,2048]{1,0:T(8,128)(2,1)S(1)} %get-tuple-element.284.here_ref, bf16[256,2048]{1,0:T(8,128)(2,1)S(1)} %collective-permute-done.29.came_ref, f32[256,2048]{1,0:T(8,128)} %get-tuple-element.275.refs_4_.hidden_ref, ...), custom_call_target="tpu_custom_call" | custom-call | flops 4294967296 | bytes 14680064 | tf_op jit(solution)/shard_map/hidden_backward/pallas_call | solution.py:937
  343.3 34.1 %attention_backward.3 = (bf16[512,2048]{1,0:T(8,128)(2,1)S(1)}, f32[4,1024,128]{2,1,0:T(8,128)}) custom-call(s32[5]{0:T(128)S(1)} %stack.84.info, bf16[256,2048]{1,0:T(8,128)(2,1)S(1)} %copy-done.38, bf16[256,2048]{1,0:T(8,128)(2,1)S(1)} %get-tuple-element.286.grad_ref, f32[4,8,256]{2,1,0:T(8,128)S(1)} %get-tuple-element.287.lse_ref, f32[1024,512]{1,0:T(8,128)} %copy-done.3, ...), custom_call_target="tpu_custom_call" | custom-call | flops 53687091200 | bytes 8388608 | tf_op jit(solution)/shard_map/attention_backward/pallas_call | solution.py:292
  381.3 7.3 %hidden_backward.3 = (f32[256,2048]{1,0:T(8,128)}, bf16[256,2048]{1,0:T(8,128)(2,1)S(1)}) custom-call(s32[5]{0:T(128)S(1)} %stack.85.info, bf16[256,2048]{1,0:T(8,128)(2,1)S(1)} %get-tuple-element.291.here_ref, bf16[256,2048]{1,0:T(8,128)(2,1)S(1)} %collective-permute-done.31.came_ref, f32[256,2048]{1,0:T(8,128)} %get-tuple-element.278.refs_4_.hidden_ref, ...), custom_call_target="tpu_custom_call" | custom-call | flops 4294967296 | bytes 14680064 | tf_op jit(solution)/shard_map/hidden_backward/pallas_call | solution.py:937
  388.6 8.9 %attention_backward.4 = (bf16[512,2048]{1,0:T(8,128)(2,1)}, f32[4,512,128]{2,1,0:T(8,128)S(1)}) custom-call(s32[5]{0:T(128)S(1)} %stack.85.info, bf16[256,2048]{1,0:T(8,128)(2,1)S(1)} %get-tuple-element.281.low_ref, bf16[256,2048]{1,0:T(8,128)(2,1)S(1)} %get-tuple-element.293.grad_ref, ...), custom_call_target="tpu_custom_call", output_to_operand_aliasing={{0}: (9, {})} | custom-call | bytes 8388608 | tf_op jit(solution)/shard_map/attention_backward/pallas_call | solution.py:292
  398.5 3.4 collective-permute-start.33
  402.1 2.3 constant_dynamic-slice_fusion.17
  404.4 9.1 %attention_backward.5 = (bf16[512,2048]{1,0:T(8,128)(2,1)}, f32[4,512,128]{2,1,0:T(8,128)S(1)}) custom-call(s32[5]{0:T(128)S(1)} %stack.85.info, bf16[256,2048]{1,0:T(8,128)(2,1)S(1)} %copy-done.17, bf16[256,2048]{1,0:T(8,128)(2,1)S(1)} %get-tuple-element.293.grad_ref, ...), custom_call_target="tpu_custom_call", output_to_operand_aliasing={{0}: (9, {}), {1}: (10, {})} | custom-call | bytes 8388608 | tf_op jit(solution)/shard_map/attention_backward/pallas_call | solution.py:292
  413.6 3.1 collective-permute-start.34
  416.9 4.3 collective-permute-done.34.short_ref
  421.2 2.2 collective-permute-start.35
  423.4 16.2 %embed_backward.1 = (bf16[512,2048]{1,0:T(8,128)(2,1)}, bf16[512,512]{1,0:T(8,128)(2,1)S(1)}) custom-call(s32[6]{0:T(128)S(1)} %stack.87.info, bf16[512,2048]{1,0:T(8,128)(2,1)} %get-tuple-element.307.query_ref, f32[4,512,128]{2,1,0:T(8,128)S(1)} %pad_maximum_fusion.1.own_ref, bf16[4,512,128]{2,1,0:T(8,128)(2,1)} %collective-permute-done.33.came_ref, ...), custom_call_target="tpu_custom_call" | custom-call | flops 12884901888 | bytes 20971520 | tf_op jit(solution)/shard_map/embed_backward/pallas_call | solution.py:1007
  441.5 5.4 all-to-all-start.3
  456.2 2.9 convert_add_fusion.1
  459.1 14.0 %all-to-all-done.3 = bf16[32,32,512]{2,1,0:T(8,128)(2,1)} async-done(((bf16[32,32,512]{2,1,0:T(8,128)(2,1)}), bf16[32,32,512]{2,1,0:T(8,128)(2,1)}, u32[]{:S(2)}, u32[]{:S(2)}) %all-to-all-start.3) | async-done | bytes 1048608 | tf_op jit(solution)/shard_map/all_to_all | solution.py:1069
  473.2 3.0 fusion.33
  479.3 13.5 %units_backward.1 = (f32[512,512]{1,0:T(8,128)}, bf16[512,512]{1,0:T(8,128)(2,1)S(1)}, f32[8,512]{1,0:T(8,128)S(1)}, bf16[256,2560]{1,0:T(8,128)(2,1)}, bf16[256...) custom-call(s32[2]{0:T(128)S(1)} %copy-done.36, f32[512,512]{1,0:T(8,128)} %get-tuple-element.314.grad_ref, ...), custom_call_target="tpu_custom_call" | custom-call | flops 17716740096 | bytes 16777216 | tf_op jit(solution)/shard_map/units_backward/pallas_call | solution.py:582
  495.1 2.3 maximum_select_fusion
  498.0 18.0 %slot_backward.2 = (bf16[512,8,512]{2,1,0:T(8,128)(2,1)}, f32[512,1536]{1,0:T(8,128)}, f32[8,512]{1,0:T(8,128)S(1)}) custom-call(bf16[512,8,512]{2,1,0:T(8,128)(2,1)} %pieces_ref.5, bf16[4096,1536]{1,0:T(8,128)(2,1)} %get-tuple-element.305.mixed_ref, f32[512,8,128]{2,1,0:T(8,128)S(1)} %copy-done.11, ...), custom_call_target="tpu_custom_call" | custom-call | flops 1048576 | bytes 2048 | tf_op jit(solution)/shard_map/slot_backward/pallas_call | solution.py:695
  519.6 18.6 %slot_backward.3 = (bf16[512,8,512]{2,1,0:T(8,128)(2,1)}, bf16[512,1664]{1,0:T(8,128)(2,1)S(1)}, f32[8,512]{1,0:T(8,128)}) custom-call(bf16[512,8,512]{2,1,0:T(8,128)(2,1)} %pieces_ref.5, bf16[4096,1536]{1,0:T(8,128)(2,1)} %get-tuple-element.305.mixed_ref, f32[512,8,128]{2,1,0:T(8,128)} %copy-done.10, ...), custom_call_target="tpu_custom_call", output_to_operand_aliasing={{0}: (8, {})} | custom-call | flops 1048576 | bytes 2048 | tf_op jit(solution)/shard_map/slot_backward/pallas_call | solution.py:695
  544.4 9.4 %collective-permute-done.45 = bf16[128,1664]{1,0:T(8,128)(2,1)S(1)} collective-permute-done((bf16[128,1664]{1,0:T(8,128)(2,1)S(1)}, bf16[128,1664]{1,0:T(8,128)(2,1)S(1)}, u32[]{:S(2)}, u32[]{:S(2)}) %collective-permute-start.45) | collective-permute-done | bytes 426016 | tf_op jit(solution)/shard_map/ppermute | solution.py:49
  558.3 2.2 collective-permute-done.46
  565.5 2.1 collective-permute-done.47
  (375 shorter events, 112.8 us)
Async XLA Ops:
  7.2 83.8 %all-gather.2.cloned.1.call-start = ((), (), s32[]{:S(2)}) async-start(), calls=%async_computation.4 | async-start | bytes 2162688 | tf_op jit(solution)/shard_map/all_gather | solution.py:1181
  11.2 17.4 %collective-permute-start = (bf16[16,1792]{1,0:T(8,128)(2,1)}, bf16[16,1792]{1,0:T(8,128)(2,1)S(1)}, u32[]{:S(2)}, u32[]{:S(2)}) collective-permute-start(bf16[16,1792]{1,0:T(8,128)(2,1)} %get-tuple-element.477), channel_id=1, source_target_pairs={{0,16},{1,17},{2,18},{3,19},{4,20},{5,21},{6,22},{7,23},{8,24},{9,... | collective-permute-start | bytes 172040 | tf_op jit(solution)/shard_map/ppermute | solution.py:49
  16.8 14.3 %collective-permute-start.2 = (bf16[16,2560]{1,0:T(8,128)(2,1)S(1)}, bf16[16,2560]{1,0:T(8,128)(2,1)S(1)}, u32[]{:S(2)}, u32[]{:S(2)}) collective-permute-start(bf16[16,2560]{1,0:T(8,128)(2,1)S(1)} %constant_dynamic-update-slice_fusion), channel_id=1, source_target_pairs={{0,16},{1,17},{2,18},{3,19},{4,20},{5,21},{6,22},{7,23},{8,24},{9,... | collective-permute-start | bytes 245768 | tf_op jit(solution)/shard_map/ppermute | solution.py:49
  16.8 13.5 %collective-permute-start.4 = (bf16[64,512]{1,0:T(8,128)(2,1)}, bf16[64,512]{1,0:T(8,128)(2,1)S(1)}, u32[]{:S(2)}, u32[]{:S(2)}) collective-permute-start(bf16[64,512]{1,0:T(8,128)(2,1)} %param.31), channel_id=1, source_target_pairs={{0,16},{1,17},{2,18},{3,19},{4,20},{5,21},{6,22},{7,23},{8,24},{9,... | collective-permute-start | bytes 196616 | tf_op jit(solution)/shard_map/ppermute | solution.py:49
  22.4 16.3 %collective-permute-start.6 = (bf16[2048,128]{1,0:T(8,128)(2,1)S(1)}, bf16[2048,128]{1,0:T(8,128)(2,1)}, u32[]{:S(2)}, u32[]{:S(2)}) collective-permute-start(bf16[2048,128]{1,0:T(8,128)(2,1)S(1)} %constant_dynamic-slice_fusion.21), channel_id=1, source_target_pairs={{0,1},{1,0},{2,3},{3,2},{4,5},{5,4},{6,7},{7,6},{8,9},{9,8},{10,11... | collective-permute-start | bytes 1572872 | tf_op jit(solution)/shard_map/ppermute | solution.py:49
  30.4 8.2 %collective-permute-start.5 = (bf16[128,512]{1,0:T(8,128)(2,1)S(1)}, bf16[128,512]{1,0:T(8,128)(2,1)S(1)}, u32[]{:S(2)}, u32[]{:S(2)}) collective-permute-start(bf16[128,512]{1,0:T(8,128)(2,1)S(1)} %maximum_select_fusion.11), channel_id=1, source_target_pairs={{0,1},{1,0},{2,3},{3,2},{4,5},{5,4},{6,7},{7,6},{8,9},{9,8},{10,11... | collective-permute-start | bytes 393224 | tf_op jit(solution)/shard_map/ppermute | solution.py:49
  31.1 7.6 %collective-permute-start.3 = (bf16[32,2560]{1,0:T(8,128)(2,1)S(1)}, bf16[32,2560]{1,0:T(8,128)(2,1)S(1)}, u32[]{:S(2)}, u32[]{:S(2)}) collective-permute-start(bf16[32,2560]{1,0:T(8,128)(2,1)S(1)} %maximum_select_fusion.9), channel_id=1, source_target_pairs={{0,8},{1,9},{2,10},{3,11},{4,12},{5,13},{6,14},{7,15},{8,0},{9,1},... | collective-permute-start | bytes 491528 | tf_op jit(solution)/shard_map/ppermute | solution.py:49
  46.5 10.5 %collective-permute-start.8 = (bf16[128,1792]{1,0:T(8,128)(2,1)S(1)}, bf16[128,1792]{1,0:T(8,128)(2,1)S(1)}, u32[]{:S(2)}, u32[]{:S(2)}) collective-permute-start(bf16[128,1792]{1,0:T(8,128)(2,1)S(1)} %bitcast.206), channel_id=1, source_target_pairs={{0,4},{1,5},{2,6},{3,7},{4,0},{5,1},{6,2},{7,3},{8,12},{9,13},{10,... | collective-permute-start | bytes 1376264 | tf_op jit(solution)/shard_map/ppermute | solution.py:49
  48.0 9.1 %collective-permute-start.9 = (bf16[64,2560]{1,0:T(8,128)(2,1)S(1)}, bf16[64,2560]{1,0:T(8,128)(2,1)S(1)}, u32[]{:S(2)}, u32[]{:S(2)}) collective-permute-start(bf16[64,2560]{1,0:T(8,128)(2,1)S(1)} %bitcast.212), channel_id=1, source_target_pairs={{0,1},{1,0},{2,3},{3,2},{4,5},{5,4},{6,7},{7,6},{8,9},{9,8},{10,11... | collective-permute-start | bytes 983048 | tf_op jit(solution)/shard_map/ppermute | solution.py:49
  49.5 7.6 %collective-permute-start.10 = (bf16[256,512]{1,0:T(8,128)(2,1)S(1)}, bf16[256,512]{1,0:T(8,128)(2,1)}, u32[]{:S(2)}, u32[]{:S(2)}) collective-permute-start(bf16[256,512]{1,0:T(8,128)(2,1)S(1)} %bitcast.219), channel_id=1, source_target_pairs={{0,8},{1,9},{2,10},{3,11},{4,12},{5,13},{6,14},{7,15},{8,0},{9,1},... | collective-permute-start | bytes 786440 | tf_op jit(solution)/shard_map/ppermute | solution.py:49
  57.4 33.6 %collective-permute-start.14 = (bf16[1024,512]{1,0:T(8,128)(2,1)}, bf16[1024,512]{1,0:T(8,128)(2,1)}, u32[]{:S(2)}, u32[]{:S(2)}) collective-permute-start(bf16[1024,512]{1,0:T(8,128)(2,1)} %dynamic_slice.152), channel_id=1, source_target_pairs={{0,1},{1,0},{2,3},{3,2},{4,5},{5,4},{6,7},{7,6},{8,9},{9,8},{10,11... | collective-permute-start | bytes 3145736 | tf_op jit(solution)/shard_map/ppermute | solution.py:49
  59.0 31.9 %collective-permute-start.12 = (bf16[128,2560]{1,0:T(8,128)(2,1)S(1)}, bf16[128,2560]{1,0:T(8,128)(2,1)S(1)}, u32[]{:S(2)}, u32[]{:S(2)}) collective-permute-start(bf16[128,2560]{1,0:T(8,128)(2,1)S(1)} %bitcast.163), channel_id=1, source_target_pairs={{0,4},{1,5},{2,6},{3,7},{4,0},{5,1},{6,2},{7,3},{8,12},{9,13},{10,... | collective-permute-start | bytes 1966088 | tf_op jit(solution)/shard_map/ppermute | solution.py:49
  60.6 39.2 %collective-permute-start.15 = (bf16[128,2560]{1,0:T(8,128)(2,1)S(1)}, bf16[128,2560]{1,0:T(8,128)(2,1)}, u32[]{:S(2)}, u32[]{:S(2)}) collective-permute-start(bf16[128,2560]{1,0:T(8,128)(2,1)S(1)} %bitcast.164), channel_id=1, source_target_pairs={{0,2},{1,3},{2,0},{3,1},{4,6},{5,7},{6,4},{7,5},{8,10},{9,11},{10,... | collective-permute-start | bytes 1966088 | tf_op jit(solution)/shard_map/ppermute | solution.py:49
  61.8 29.2 %collective-permute-start.13 = (bf16[512,512]{1,0:T(8,128)(2,1)S(1)}, bf16[512,512]{1,0:T(8,128)(2,1)}, u32[]{:S(2)}, u32[]{:S(2)}) collective-permute-start(bf16[512,512]{1,0:T(8,128)(2,1)S(1)} %bitcast.167), channel_id=1, source_target_pairs={{0,4},{1,5},{2,6},{3,7},{4,0},{5,1},{6,2},{7,3},{8,12},{9,13},{10,... | collective-permute-start | bytes 1572872 | tf_op jit(solution)/shard_map/ppermute | solution.py:49
  62.4 37.4 %collective-permute-start.17 = (bf16[512,512]{1,0:T(8,128)(2,1)S(1)}, bf16[512,512]{1,0:T(8,128)(2,1)}, u32[]{:S(2)}, u32[]{:S(2)}) collective-permute-start(bf16[512,512]{1,0:T(8,128)(2,1)S(1)} %bitcast.168), channel_id=1, source_target_pairs={{0,2},{1,3},{2,0},{3,1},{4,6},{5,7},{6,4},{7,5},{8,10},{9,11},{10,... | collective-permute-start | bytes 1572872 | tf_op jit(solution)/shard_map/ppermute | solution.py:49
  91.0 8.8 %collective-permute-start.16 = (bf16[128,2560]{1,0:T(8,128)(2,1)S(1)}, bf16[128,2560]{1,0:T(8,128)(2,1)}, u32[]{:S(2)}, u32[]{:S(2)}) collective-permute-start(bf16[128,2560]{1,0:T(8,128)(2,1)S(1)} %collective-permute-done.12.refs_1_), channel_id=1, source_target_pairs={{0,2},{1,3},{2,0},{3,1},{4,6},{5,7},{6,4},{7,5},{8,10},{9,11},{10,... | collective-permute-start | bytes 1966088 | tf_op jit(solution)/shard_map/ppermute | solution.py:49
  91.1 8.7 %collective-permute-start.18 = (bf16[512,512]{1,0:T(8,128)(2,1)}, bf16[512,512]{1,0:T(8,128)(2,1)}, u32[]{:S(2)}, u32[]{:S(2)}) collective-permute-start(bf16[512,512]{1,0:T(8,128)(2,1)} %collective-permute-done.13.refs_5_), channel_id=1, source_target_pairs={{0,2},{1,3},{2,0},{3,1},{4,6},{5,7},{6,4},{7,5},{8,10},{9,11},{10,... | collective-permute-start | bytes 1572872 | tf_op jit(solution)/shard_map/ppermute | solution.py:49
  98.2 34.7 %collective-permute-start.19 = (bf16[1024,512]{1,0:T(8,128)(2,1)}, bf16[1024,512]{1,0:T(8,128)(2,1)}, u32[]{:S(2)}, u32[]{:S(2)}) collective-permute-start(bf16[1024,512]{1,0:T(8,128)(2,1)} %collective-permute-done.14), channel_id=1, source_target_pairs={{0,4},{1,5},{2,6},{3,7},{4,0},{5,1},{6,2},{7,3},{8,12},{9,13},{10,... | collective-permute-start | bytes 3145736 | tf_op jit(solution)/shard_map/ppermute | solution.py:49
  109.3 29.8 %all-to-all-start.2 = ((bf16[32,32,512]{2,1,0:T(8,128)(2,1)}), bf16[32,32,512]{2,1,0:T(8,128)(2,1)}, u32[]{:S(2)}, u32[]{:S(2)}) async-start(bf16[32,32,512]{2,1,0:T(8,128)(2,1)} %select_convert_fusion.1), calls=%async_computation.2 | async-start | bytes 2097152 | tf_op jit(solution)/shard_map/all_to_all | solution.py:1069
  113.1 40.9 %collective-permute-start.24 = (bf16[2048,128]{1,0:T(8,128)(2,1)}, bf16[2048,128]{1,0:T(8,128)(2,1)}, u32[]{:S(2)}, u32[]{:S(2)}) collective-permute-start(bf16[2048,128]{1,0:T(8,128)(2,1)} %collective-permute-done.6.pair_near), channel_id=1, source_target_pairs={{0,2},{1,3},{2,0},{3,1},{4,6},{5,7},{6,4},{7,5},{8,10},{9,11},{10,... | collective-permute-start | bytes 1572872 | tf_op jit(solution)/shard_map/ppermute | solution.py:49
  113.3 36.0 %collective-permute-start.22 = (bf16[256,2048]{1,0:T(8,128)(2,1)}, bf16[256,2048]{1,0:T(8,128)(2,1)}, u32[]{:S(2)}, u32[]{:S(2)}) collective-permute-start(bf16[256,2048]{1,0:T(8,128)(2,1)} %constant_dynamic-slice_fusion.20), channel_id=1, source_target_pairs={{0,1},{1,0},{2,3},{3,2},{4,5},{5,4},{6,7},{7,6},{8,9},{9,8},{10,11... | collective-permute-start | bytes 3145736 | tf_op jit(solution)/shard_map/ppermute | solution.py:49
  134.6 14.7 %collective-permute-start.20 = (bf16[1024,512]{1,0:T(8,128)(2,1)S(1)}, bf16[1024,512]{1,0:T(8,128)(2,1)}, u32[]{:S(2)}, u32[]{:S(2)}) collective-permute-start(bf16[1024,512]{1,0:T(8,128)(2,1)S(1)} %get-tuple-element.470.refs_1_.mid_a), channel_id=1, source_target_pairs={{0,2},{1,3},{2,0},{3,1},{4,6},{5,7},{6,4},{7,5},{8,10},{9,11},{10,... | collective-permute-start | bytes 3145736 | tf_op jit(solution)/shard_map/ppermute | solution.py:49
  134.6 14.6 %collective-permute-start.21 = (bf16[1024,512]{1,0:T(8,128)(2,1)S(1)}, bf16[1024,512]{1,0:T(8,128)(2,1)}, u32[]{:S(2)}, u32[]{:S(2)}) collective-permute-start(bf16[1024,512]{1,0:T(8,128)(2,1)S(1)} %get-tuple-element.469.refs_2_.mid_b), channel_id=1, source_target_pairs={{0,2},{1,3},{2,0},{3,1},{4,6},{5,7},{6,4},{7,5},{8,10},{9,11},{10,... | collective-permute-start | bytes 3145736 | tf_op jit(solution)/shard_map/ppermute | solution.py:49
  151.4 25.0 %collective-permute-start.25 = (bf16[256,2048]{1,0:T(8,128)(2,1)}, bf16[256,2048]{1,0:T(8,128)(2,1)}, u32[]{:S(2)}, u32[]{:S(2)}) collective-permute-start(bf16[256,2048]{1,0:T(8,128)(2,1)} %collective-permute-done.22), channel_id=1, source_target_pairs={{0,4},{1,5},{2,6},{3,7},{4,0},{5,1},{6,2},{7,3},{8,12},{9,13},{10,... | collective-permute-start | bytes 3145736 | tf_op jit(solution)/shard_map/ppermute | solution.py:49
  153.0 14.6 %collective-permute-start.23 = (bf16[512,512]{1,0:T(8,128)(2,1)}, bf16[512,512]{1,0:T(8,128)(2,1)S(1)}, u32[]{:S(2)}, u32[]{:S(2)}) collective-permute-start(bf16[512,512]{1,0:T(8,128)(2,1)} %get-tuple-element.255.chosen_ref), channel_id=1, source_target_pairs={{0,1},{1,0},{2,3},{3,2},{4,5},{5,4},{6,7},{7,6},{8,9},{9,8},{10,11... | collective-permute-start | bytes 1572872 | tf_op jit(solution)/shard_map/ppermute | solution.py:49
  178.1 24.1 %collective-permute-start.26 = (bf16[256,2048]{1,0:T(8,128)(2,1)S(1)}, bf16[256,2048]{1,0:T(8,128)(2,1)S(1)}, u32[]{:S(2)}, u32[]{:S(2)}) collective-permute-start(bf16[256,2048]{1,0:T(8,128)(2,1)S(1)} %get-tuple-element.468.mid_a), channel_id=1, source_target_pairs={{0,2},{1,3},{2,0},{3,1},{4,6},{5,7},{6,4},{7,5},{8,10},{9,11},{10,... | collective-permute-start | bytes 3145736 | tf_op jit(solution)/shard_map/ppermute | solution.py:49
  178.2 24.0 %collective-permute-start.27 = (bf16[256,2048]{1,0:T(8,128)(2,1)S(1)}, bf16[256,2048]{1,0:T(8,128)(2,1)S(1)}, u32[]{:S(2)}, u32[]{:S(2)}) collective-permute-start(bf16[256,2048]{1,0:T(8,128)(2,1)S(1)} %get-tuple-element.467.mid_b), channel_id=1, source_target_pairs={{0,2},{1,3},{2,0},{3,1},{4,6},{5,7},{6,4},{7,5},{8,10},{9,11},{10,... | collective-permute-start | bytes 3145736 | tf_op jit(solution)/shard_map/ppermute | solution.py:49
  209.9 25.2 %collective-permute-start.28 = (bf16[256,2048]{1,0:T(8,128)(2,1)S(1)}, bf16[256,2048]{1,0:T(8,128)(2,1)S(1)}, u32[]{:S(2)}, u32[]{:S(2)}) collective-permute-start(bf16[256,2048]{1,0:T(8,128)(2,1)S(1)} %get-tuple-element.273.refs_0_), channel_id=1, source_target_pairs={{0,1},{1,0},{2,3},{3,2},{4,5},{5,4},{6,7},{7,6},{8,9},{9,8},{10,11... | collective-permute-start | bytes 3145736 | tf_op jit(solution)/shard_map/ppermute | solution.py:49
  229.7 53.8 %collective-permute-start.30 = (bf16[256,2048]{1,0:T(8,128)(2,1)S(1)}, bf16[256,2048]{1,0:T(8,128)(2,1)S(1)}, u32[]{:S(2)}, u32[]{:S(2)}) collective-permute-start(bf16[256,2048]{1,0:T(8,128)(2,1)S(1)} %get-tuple-element.277.refs_0_), channel_id=1, source_target_pairs={{0,1},{1,0},{2,3},{3,2},{4,5},{5,4},{6,7},{7,6},{8,9},{9,8},{10,11... | collective-permute-start | bytes 3145736 | tf_op jit(solution)/shard_map/ppermute | solution.py:49
  282.8 53.2 %collective-permute-start.29 = (bf16[256,2048]{1,0:T(8,128)(2,1)S(1)}, bf16[256,2048]{1,0:T(8,128)(2,1)S(1)}, u32[]{:S(2)}, u32[]{:S(2)}) collective-permute-start(bf16[256,2048]{1,0:T(8,128)(2,1)S(1)} %get-tuple-element.463), channel_id=1, source_target_pairs={{0,1},{1,0},{2,3},{3,2},{4,5},{5,4},{6,7},{7,6},{8,9},{9,8},{10,11... | collective-permute-start | bytes 3145736 | tf_op jit(solution)/shard_map/ppermute | solution.py:49
  331.2 47.5 %collective-permute-start.31 = (bf16[256,2048]{1,0:T(8,128)(2,1)S(1)}, bf16[256,2048]{1,0:T(8,128)(2,1)S(1)}, u32[]{:S(2)}, u32[]{:S(2)}) collective-permute-start(bf16[256,2048]{1,0:T(8,128)(2,1)S(1)} %get-tuple-element.465), channel_id=1, source_target_pairs={{0,1},{1,0},{2,3},{3,2},{4,5},{5,4},{6,7},{7,6},{8,9},{9,8},{10,11... | collective-permute-start | bytes 3145736 | tf_op jit(solution)/shard_map/ppermute | solution.py:49
  334.7 44.1 %collective-permute-start.32 = (bf16[512,1024]{1,0:T(8,128)(2,1)}, bf16[512,1024]{1,0:T(8,128)(2,1)S(1)}, u32[]{:S(2)}, u32[]{:S(2)}) collective-permute-start(bf16[512,1024]{1,0:T(8,128)(2,1)} %get-tuple-element.462), channel_id=1, source_target_pairs={{0,1},{1,0},{2,3},{3,2},{4,5},{5,4},{6,7},{7,6},{8,9},{9,8},{10,11... | collective-permute-start | bytes 3145736 | tf_op jit(solution)/shard_map/ppermute | solution.py:49
  398.5 15.0 %collective-permute-start.33 = (bf16[4,512,128]{2,1,0:T(8,128)(2,1)}, bf16[4,512,128]{2,1,0:T(8,128)(2,1)}, u32[]{:S(2)}, u32[]{:S(2)}) collective-permute-start(bf16[4,512,128]{2,1,0:T(8,128)(2,1)} %pad_maximum_fusion.2), channel_id=1, source_target_pairs={{0,1},{1,0},{2,3},{3,2},{4,5},{5,4},{6,7},{7,6},{8,9},{9,8},{10,11... | collective-permute-start | bytes 1572872 | tf_op jit(solution)/shard_map/ppermute | solution.py:49
  413.6 7.6 %collective-permute-start.34 = (bf16[4,256,128]{2,1,0:T(8,128)(2,1)S(1)}, bf16[4,256,128]{2,1,0:T(8,128)(2,1)S(1)}, u32[]{:S(2)}, u32[]{:S(2)}) collective-permute-start(bf16[4,256,128]{2,1,0:T(8,128)(2,1)S(1)} %dynamic-slice_convert_fusion.9), channel_id=1, source_target_pairs={{0,1},{1,0},{2,3},{3,2},{4,5},{5,4},{6,7},{7,6},{8,9},{9,8},{10,11... | collective-permute-start | bytes 786440 | tf_op jit(solution)/shard_map/ppermute | solution.py:49
  421.2 32.2 %collective-permute-start.35 = (bf16[512,1024]{1,0:T(8,128)(2,1)}, bf16[512,1024]{1,0:T(8,128)(2,1)}, u32[]{:S(2)}, u32[]{:S(2)}) collective-permute-start(bf16[512,1024]{1,0:T(8,128)(2,1)} %constant_dynamic-slice_fusion.17), channel_id=1, source_target_pairs={{0,1},{1,0},{2,3},{3,2},{4,5},{5,4},{6,7},{7,6},{8,9},{9,8},{10,11... | collective-permute-start | bytes 3145736 | tf_op jit(solution)/shard_map/ppermute | solution.py:49
  441.5 31.7 %all-to-all-start.3 = ((bf16[32,32,512]{2,1,0:T(8,128)(2,1)}), bf16[32,32,512]{2,1,0:T(8,128)(2,1)}, u32[]{:S(2)}, u32[]{:S(2)}) async-start(bf16[32,32,512]{2,1,0:T(8,128)(2,1)} %bitcast.56), calls=%async_computation.3 | async-start | bytes 2097152 | tf_op jit(solution)/shard_map/all_to_all | solution.py:1069
  477.7 15.7 %collective-permute-start.37 = (bf16[128,2048]{1,0:T(8,128)(2,1)S(1)}, bf16[128,2048]{1,0:T(8,128)(2,1)S(1)}, u32[]{:S(2)}, u32[]{:S(2)}) collective-permute-start(bf16[128,2048]{1,0:T(8,128)(2,1)S(1)} %bitcast.236), channel_id=1, source_target_pairs={{0,1},{1,0},{2,3},{3,2},{4,5},{5,4},{6,7},{7,6},{8,9},{9,8},{10,11... | collective-permute-start | bytes 1572872 | tf_op jit(solution)/shard_map/ppermute | solution.py:49
  492.7 23.3 %collective-permute-start.39 = (bf16[256,2560]{1,0:T(8,128)(2,1)}, bf16[256,2560]{1,0:T(8,128)(2,1)S(1)}, u32[]{:S(2)}, u32[]{:S(2)}) collective-permute-start(bf16[256,2560]{1,0:T(8,128)(2,1)} %get-tuple-element.326), channel_id=1, source_target_pairs={{0,2},{1,3},{2,0},{3,1},{4,6},{5,7},{6,4},{7,5},{8,10},{9,11},{10,... | collective-permute-start | bytes 3932168 | tf_op jit(solution)/shard_map/ppermute | solution.py:49
  492.7 23.3 %collective-permute-start.40 = (bf16[1024,512]{1,0:T(8,128)(2,1)}, bf16[1024,512]{1,0:T(8,128)(2,1)S(1)}, u32[]{:S(2)}, u32[]{:S(2)}) collective-permute-start(bf16[1024,512]{1,0:T(8,128)(2,1)} %get-tuple-element.328), channel_id=1, source_target_pairs={{0,2},{1,3},{2,0},{3,1},{4,6},{5,7},{6,4},{7,5},{8,10},{9,11},{10,... | collective-permute-start | bytes 3145736 | tf_op jit(solution)/shard_map/ppermute | solution.py:49
  493.5 22.5 %collective-permute-start.38 = (bf16[64,2048]{1,0:T(8,128)(2,1)S(1)}, bf16[64,2048]{1,0:T(8,128)(2,1)S(1)}, u32[]{:S(2)}, u32[]{:S(2)}) collective-permute-start(bf16[64,2048]{1,0:T(8,128)(2,1)S(1)} %bitcast.246), channel_id=1, source_target_pairs={{0,4},{1,5},{2,6},{3,7},{4,0},{5,1},{6,2},{7,3},{8,12},{9,13},{10,... | collective-permute-start | bytes 786440 | tf_op jit(solution)/shard_map/ppermute | solution.py:49
  516.5 21.9 %collective-permute-start.42 = (bf16[128,2560]{1,0:T(8,128)(2,1)S(1)}, bf16[128,2560]{1,0:T(8,128)(2,1)S(1)}, u32[]{:S(2)}, u32[]{:S(2)}) collective-permute-start(bf16[128,2560]{1,0:T(8,128)(2,1)S(1)} %bitcast.229), channel_id=1, source_target_pairs={{0,1},{1,0},{2,3},{3,2},{4,5},{5,4},{6,7},{7,6},{8,9},{9,8},{10,11... | collective-permute-start | bytes 1966088 | tf_op jit(solution)/shard_map/ppermute | solution.py:49
  517.7 20.7 %collective-permute-start.43 = (bf16[512,512]{1,0:T(8,128)(2,1)S(1)}, bf16[512,512]{1,0:T(8,128)(2,1)S(1)}, u32[]{:S(2)}, u32[]{:S(2)}) collective-permute-start(bf16[512,512]{1,0:T(8,128)(2,1)S(1)} %bitcast.235), channel_id=1, source_target_pairs={{0,4},{1,5},{2,6},{3,7},{4,0},{5,1},{6,2},{7,3},{8,12},{9,13},{10,... | collective-permute-start | bytes 1572872 | tf_op jit(solution)/shard_map/ppermute | solution.py:49
  518.8 19.6 %collective-permute-start.41 = (bf16[32,2048]{1,0:T(8,128)(2,1)S(1)}, bf16[32,2048]{1,0:T(8,128)(2,1)S(1)}, u32[]{:S(2)}, u32[]{:S(2)}) collective-permute-start(bf16[32,2048]{1,0:T(8,128)(2,1)S(1)} %bitcast.259), channel_id=1, source_target_pairs={{0,8},{1,9},{2,10},{3,11},{4,12},{5,13},{6,14},{7,15},{8,0},{9,1},... | collective-permute-start | bytes 393224 | tf_op jit(solution)/shard_map/ppermute | solution.py:49
  538.8 15.1 %collective-permute-start.49 = (bf16[16,2048]{1,0:T(8,128)(2,1)S(1)}, bf16[16,2048]{1,0:T(8,128)(2,1)S(1)}, u32[]{:S(2)}, u32[]{:S(2)}) collective-permute-start(bf16[16,2048]{1,0:T(8,128)(2,1)S(1)} %fusion.51), channel_id=1, source_target_pairs={{0,16},{1,17},{2,18},{3,19},{4,20},{5,21},{6,22},{7,23},{8,24},{9,... | collective-permute-start | bytes 196616 | tf_op jit(solution)/shard_map/ppermute | solution.py:49
  540.4 13.5 %collective-permute-start.50 = (bf16[64,2560]{1,0:T(8,128)(2,1)S(1)}, bf16[64,2560]{1,0:T(8,128)(2,1)S(1)}, u32[]{:S(2)}, u32[]{:S(2)}) collective-permute-start(bf16[64,2560]{1,0:T(8,128)(2,1)S(1)} %bitcast.242), channel_id=1, source_target_pairs={{0,4},{1,5},{2,6},{3,7},{4,0},{5,1},{6,2},{7,3},{8,12},{9,13},{10,... | collective-permute-start | bytes 983048 | tf_op jit(solution)/shard_map/ppermute | solution.py:49
  542.1 11.7 %collective-permute-start.45 = (bf16[128,1664]{1,0:T(8,128)(2,1)S(1)}, bf16[128,1664]{1,0:T(8,128)(2,1)S(1)}, u32[]{:S(2)}, u32[]{:S(2)}) collective-permute-start(bf16[128,1664]{1,0:T(8,128)(2,1)S(1)} %bitcast.239), channel_id=1, source_target_pairs={{0,1},{1,0},{2,3},{3,2},{4,5},{5,4},{6,7},{7,6},{8,9},{9,8},{10,11... | collective-permute-start | bytes 1277960 | tf_op jit(solution)/shard_map/ppermute | solution.py:49
  543.5 10.4 %collective-permute-start.51 = (bf16[256,512]{1,0:T(8,128)(2,1)S(1)}, bf16[256,512]{1,0:T(8,128)(2,1)S(1)}, u32[]{:S(2)}, u32[]{:S(2)}) collective-permute-start(bf16[256,512]{1,0:T(8,128)(2,1)S(1)} %bitcast.247), channel_id=1, source_target_pairs={{0,8},{1,9},{2,10},{3,11},{4,12},{5,13},{6,14},{7,15},{8,0},{9,1},... | collective-permute-start | bytes 786440 | tf_op jit(solution)/shard_map/ppermute | solution.py:49
  562.4 8.4 %collective-permute-start.54 = (bf16[16,2560]{1,0:T(8,128)(2,1)S(1)}, bf16[16,2560]{1,0:T(8,128)(2,1)S(1)}, u32[]{:S(2)}, u32[]{:S(2)}) collective-permute-start(bf16[16,2560]{1,0:T(8,128)(2,1)S(1)} %fusion.50), channel_id=1, source_target_pairs={{0,16},{1,17},{2,18},{3,19},{4,20},{5,21},{6,22},{7,23},{8,24},{9,... | collective-permute-start | bytes 245768 | tf_op jit(solution)/shard_map/ppermute | solution.py:49
  (82 other events, 1046.5 us)
Sparse Core Ops, SparseCore 0:
  24.1 58.1 all-gather.1

commit v7 on v6

--- a/solution.py
+++ b/solution.py
@@ -1412,8 +1412,17 @@
     pieces_grad, input_grad, _ = slots_held
     input_held = input_grad
     moving = depart(SLOT_PARTS)
+    cut = in_width // (2 * PAIR) * PAIR + PAIR
     for at in range(bits):
-        input_held = scatter_add(*scatter(input_held, back_order, at))
+        if at == 1:
+            input_held = [input_held[:, :cut], input_held[:, cut:]]
+        if at in (1, 2):
+            crossing = [back_order, [back_order[0], back_order[2], back_order[1]] + back_order[3:]]
+            input_held = [scatter_add(*scatter(x, order, at)) for x, order in zip(input_held, crossing)]
+            if at == 2:
+                input_held = jnp.concatenate(input_held, axis=1)
+        else:
+            input_held = scatter_add(*scatter(input_held, back_order, at))
         if at > 0:
             _, moving = lax.optimization_barrier((input_held, moving))
             held = arrive(moving)

time: 592 us -> 593 us (level)
    ppermute x56 -> x58, starting transfers between devices: 65.7 us -> 68.2 us  [swap(): lax.ppermute(value, ('dp', 'mp'), [(d, d ^ mask) for d in range(devices)])]
    ppermute x56 -> x58, waiting for transfers between devices: 67.2 us -> 65.4 us  [swap(): lax.ppermute(value, ('dp', 'mp'), [(d, d ^ mask) for d in range(devices)])]
  transfers between devices with their start and end apart: 59 -> 61, of which waited for: 18 -> 17; matrix products, arithmetic and copies ran while one was open for 9% -> 9% of each run, Pallas kernels for 51% -> 51%
where the time goes in v7:
time: 593 us; the launch traced here: 583 us
  Pallas kernels  320 us (54%)
  waiting for transfers between devices  82.6 us (14%)
  starting transfers between devices  77.2 us (13%)
  local copies, waits for them, and re-layouts  39.9 us (7%)
  other arithmetic  35.9 us (6%)
  between operations  17.2 us (3%)
  matrix products  10.9 us (2%)
    pallas_call x2, Pallas kernels, feed_forward(): pl.pallas_call(lambda info, *refs: feed_forward_kernel(*refs), grid_spec=...  95.1 us
    ppermute x58, starting transfers between devices, swap(): lax.ppermute(value, ('dp', 'mp'), [(d, d ^ mask) for d in range(devices)])  68.2 us
    ppermute x58, waiting for transfers between devices, swap(): lax.ppermute(value, ('dp', 'mp'), [(d, d ^ mask) for d in range(devices)])  65.4 us
    pallas_call x3, Pallas kernels, attention_backward(): pl.pallas_call(attention_backward_kernel, grid_spec=pltpu.PrefetchScalarG...  52.2 us
    pallas_call x2, Pallas kernels, slot_backward(): pl.pallas_call(functools.partial(slot_backward_kernel, first, last), grid...  36.6 us
    pallas_call x2, Pallas kernels, attention_forward(): pl.pallas_call(attention_forward_kernel, grid_spec=pltpu.PrefetchScalarGr...  33.2 us
    pallas_call x2, Pallas kernels, project(): pl.pallas_call(functools.partial(project_kernel, more), grid_spec=pltpu.P...  19.6 us
    pallas_call x1, Pallas kernels, slot_attention(): pl.pallas_call(slot_attention_kernel, grid=(entries // part,), in_specs=[...  19.4 us
  transfers between devices with their start and end apart: 61, of which 17 were waited for; matrix products, arithmetic and copies ran while one was open for 9% of the time, Pallas kernels for 51%

profile of v7, /device:TPU:0, one launch (start us, length us, event | category | flops | bytes accessed | tf_op | source)
XLA Modules:
  0.0 583.4 jit_solution(13691972847071361153)
XLA Ops:
  11.2 4.0 collective-permute-start
  16.8 2.9 collective-permute-start.4
  24.0 2.3 constant_dynamic-slice_fusion.22
  26.3 2.3 dynamic_slice.164
  31.6 3.3 collective-permute-done.1
  34.9 3.7 collective-permute-done.5
  41.8 4.5 collective-permute-done.7
  51.1 5.8 collective-permute-done.8
  65.3 2.6 maximum_select_fusion.1
  67.9 19.4 %slot_attention.1 = (bf16[4096,1536]{1,0:T(8,128)(2,1)}, f32[512,8,128]{2,1,0:T(8,128)S(1)}, bf16[512,512]{1,0:T(8,128)(2,1)S(1)}, f32[512,512]{1,0:T(8,128)S(1)}, f32[8,512]{1,0:T(8,128)S(1)}) custom-call(bf16[512,8,512]{2,1,0:T(8,128)(2,1)} %pieces_ref.5, s32[512,1,128]{2,1,0:T(1,128)S(1)} %broadcast_in_dim.30.counts_ref, bf16[512,1792]{1,0:T(8,128)(2,1)S(1)} %bitcast.168), custom_call_target="tpu_custom_call" | custom-call | flops 2097152 | bytes 4096 | tf_op jit(solution)/shard_map/slot_attention/pallas_call | solution.py:400
  91.6 5.0 compare_reduce_fusion
  100.9 5.8 units_forward.1
  109.3 3.6 all-to-all-start.2
  115.0 17.9 %collective-permute-done.19 = bf16[1024,512]{1,0:T(8,128)(2,1)} collective-permute-done((bf16[1024,512]{1,0:T(8,128)(2,1)}, bf16[1024,512]{1,0:T(8,128)(2,1)}, u32[]{:S(2)}, u32[]{:S(2)}) %collective-permute-start.19) | collective-permute-done | bytes 1048608 | tf_op jit(solution)/shard_map/ppermute | solution.py:49
  135.9 3.2 all-to-all-done.2
  139.0 2.8 fusion.34
  141.9 7.4 %collective-permute-done.22 = bf16[256,2048]{1,0:T(8,128)(2,1)} collective-permute-done((bf16[256,2048]{1,0:T(8,128)(2,1)}, bf16[256,2048]{1,0:T(8,128)(2,1)}, u32[]{:S(2)}, u32[]{:S(2)}) %collective-permute-start.22) | collective-permute-done | bytes 1048608 | tf_op jit(solution)/shard_map/ppermute | solution.py:49
  153.9 13.6 %project.2 = (f32[1024,512]{1,0:T(8,128)}, bf16[512,2048]{1,0:T(8,128)(2,1)}, f32[512,2048]{1,0:T(8,128)}) custom-call(s32[2]{0:T(128)S(1)} %pad_add_fusion.3.info, bf16[512,512]{1,0:T(8,128)(2,1)} %get-tuple-element.255.chosen_ref, bf16[512,2048]{1,0:T(8,128)(2,1)} %all-gather.2.cloned.1.call-done.embed_ref, f32[1,2048]{1,0:T(1,128)S(1)} %bitcast.184, ...), custom_call_target="tpu_custom_call" | custom-call | flops 1073741824 | bytes 1048576 | tf_op jit(solution)/shard_map/project/pallas_call | solution.py:855
  169.2 6.0 %project.3.pair_ref = f32[1024,512]{1,0:T(8,128)S(1)} custom-call(s32[2]{0:T(128)S(1)} %pad_add_fusion.1.info, bf16[512,512]{1,0:T(8,128)(2,1)S(1)} %collective-permute-done.23.chosen_ref, bf16[512,2048]{1,0:T(8,128)(2,1)} %all-gather.2.cloned.1.call-done.embed_ref, f32[1,2048]{1,0:T(1,128)S(1)} %bitcast.185, ...), custom_call_target="tpu_custom_call", output_to_operand_aliasing={{}: (7, {})} | custom-call | flops 1073741824 | bytes 1048576 | tf_op jit(solution)/shard_map/project/pallas_call | solution.py:855
  180.3 20.9 %attention_forward.2 = (bf16[256,2048]{1,0:T(8,128)(2,1)S(1)}, bf16[256,2048]{1,0:T(8,128)(2,1)S(1)}, f32[4,8,256]{2,1,0:T(8,128)S(1)}) custom-call(s32[5]{0:T(128)S(1)} %stack.84.info, f32[512,2048]{1,0:T(8,128)} %get-tuple-element.263.query_ref, f32[1024,512]{1,0:T(8,128)S(1)} %copy-done.4, f32[1024,128]{1,0:T(8,128)S(1)} %copy-done.7, ...), custom_call_target="tpu_custom_call" | custom-call | flops 21474836480 | bytes 8388608 | tf_op jit(solution)/shard_map/attention_forward/pallas_call | solution.py:256
  203.2 6.7 %output_project.2 = (f32[256,2048]{1,0:T(8,128)}, bf16[256,2048]{1,0:T(8,128)(2,1)S(1)}) custom-call(bf16[256,2048]{1,0:T(8,128)(2,1)S(1)} %get-tuple-element.264.rows_ref, bf16[512,2048]{1,0:T(8,128)(2,1)} %get-tuple-element.265.embedded_ref, f32[1,2048]{1,0:T(1,128)S(1)} %bitcast.180, bf16[1024,2048]{1,0:T(8,128)(2,1)} %near_ref.8, ...), custom_call_target="tpu_custom_call" | custom-call | flops 4294967296 | bytes 12582912 | tf_op jit(solution)/shard_map/output_project/pallas_call | solution.py:898
  210.5 12.2 %attention_forward.3 = (bf16[256,2048]{1,0:T(8,128)(2,1)S(1)}, bf16[256,2048]{1,0:T(8,128)(2,1)S(1)}, f32[4,8,256]{2,1,0:T(8,128)S(1)}) custom-call(s32[5]{0:T(128)S(1)} %stack.85.info, f32[512,2048]{1,0:T(8,128)} %get-tuple-element.263.query_ref, f32[1024,512]{1,0:T(8,128)S(1)} %copy-done.5, f32[1024,128]{1,0:T(8,128)S(1)} %copy-done.7, ...), custom_call_target="tpu_custom_call" | custom-call | flops 10737418240 | bytes 8388608 | tf_op jit(solution)/shard_map/attention_forward/pallas_call | solution.py:256
  222.8 6.9 %output_project.3 = (f32[256,2048]{1,0:T(8,128)}, bf16[256,2048]{1,0:T(8,128)(2,1)S(1)}) custom-call(bf16[256,2048]{1,0:T(8,128)(2,1)S(1)} %get-tuple-element.269.rows_ref, bf16[512,2048]{1,0:T(8,128)(2,1)} %get-tuple-element.265.embedded_ref, f32[1,2048]{1,0:T(1,128)S(1)} %bitcast.181, bf16[1024,2048]{1,0:T(8,128)(2,1)} %near_ref.8, ...), custom_call_target="tpu_custom_call" | custom-call | flops 4294967296 | bytes 12582912 | tf_op jit(solution)/shard_map/output_project/pallas_call | solution.py:898
  229.7 4.6 collective-permute-start.30
  235.1 47.5 %feed_forward.2 = (bf16[512,2048]{1,0:T(8,128)(2,1)S(1)}, bf16[512,2048]{1,0:T(8,128)(2,1)}) custom-call(s32[2]{0:T(128)S(1)} %pad_add_fusion.info, bf16[256,2048]{1,0:T(8,128)(2,1)S(1)} %get-tuple-element.273.refs_0_, bf16[256,2048]{1,0:T(8,128)(2,1)S(1)} %collective-permute-done.28.refs_1_, bf16[1024,2048]{1,0:T(8,128)(2,1)} %rising_ref.3, ...), custom_call_target="tpu_custom_call" | custom-call | flops 50197430272 | bytes 69206016 | tf_op jit(solution)/shard_map/feed_forward/pallas_call | solution.py:770
  283.5 47.6 %feed_forward.3 = (bf16[512,2048]{1,0:T(8,128)(2,1)S(1)}, bf16[512,2048]{1,0:T(8,128)(2,1)}) custom-call(s32[2]{0:T(128)S(1)} %pad_add_fusion.4.info, bf16[256,2048]{1,0:T(8,128)(2,1)S(1)} %get-tuple-element.277.refs_0_, bf16[256,2048]{1,0:T(8,128)(2,1)S(1)} %collective-permute-done.30.refs_1_, bf16[1024,2048]{1,0:T(8,128)(2,1)} %rising_ref.3, ...), custom_call_target="tpu_custom_call" | custom-call | flops 50197430272 | bytes 69206016 | tf_op jit(solution)/shard_map/feed_forward/pallas_call | solution.py:770
  336.1 7.3 %hidden_backward.2 = (f32[256,2048]{1,0:T(8,128)}, bf16[256,2048]{1,0:T(8,128)(2,1)S(1)}) custom-call(s32[5]{0:T(128)S(1)} %stack.84.info, bf16[256,2048]{1,0:T(8,128)(2,1)S(1)} %get-tuple-element.284.here_ref, bf16[256,2048]{1,0:T(8,128)(2,1)S(1)} %collective-permute-done.29.came_ref, f32[256,2048]{1,0:T(8,128)} %get-tuple-element.275.refs_4_.hidden_ref, ...), custom_call_target="tpu_custom_call" | custom-call | flops 4294967296 | bytes 14680064 | tf_op jit(solution)/shard_map/hidden_backward/pallas_call | solution.py:937
  343.4 34.1 %attention_backward.3 = (bf16[512,2048]{1,0:T(8,128)(2,1)S(1)}, f32[4,1024,128]{2,1,0:T(8,128)}) custom-call(s32[5]{0:T(128)S(1)} %stack.84.info, bf16[256,2048]{1,0:T(8,128)(2,1)S(1)} %copy-done.38, bf16[256,2048]{1,0:T(8,128)(2,1)S(1)} %get-tuple-element.286.grad_ref, f32[4,8,256]{2,1,0:T(8,128)S(1)} %get-tuple-element.287.lse_ref, f32[1024,512]{1,0:T(8,128)} %copy-done.3, ...), custom_call_target="tpu_custom_call" | custom-call | flops 53687091200 | bytes 8388608 | tf_op jit(solution)/shard_map/attention_backward/pallas_call | solution.py:292
  381.3 7.3 %hidden_backward.3 = (f32[256,2048]{1,0:T(8,128)}, bf16[256,2048]{1,0:T(8,128)(2,1)S(1)}) custom-call(s32[5]{0:T(128)S(1)} %stack.85.info, bf16[256,2048]{1,0:T(8,128)(2,1)S(1)} %get-tuple-element.291.here_ref, bf16[256,2048]{1,0:T(8,128)(2,1)S(1)} %collective-permute-done.31.came_ref, f32[256,2048]{1,0:T(8,128)} %get-tuple-element.278.refs_4_.hidden_ref, ...), custom_call_target="tpu_custom_call" | custom-call | flops 4294967296 | bytes 14680064 | tf_op jit(solution)/shard_map/hidden_backward/pallas_call | solution.py:937
  388.6 8.9 %attention_backward.4 = (bf16[512,2048]{1,0:T(8,128)(2,1)}, f32[4,512,128]{2,1,0:T(8,128)S(1)}) custom-call(s32[5]{0:T(128)S(1)} %stack.85.info, bf16[256,2048]{1,0:T(8,128)(2,1)S(1)} %get-tuple-element.281.low_ref, bf16[256,2048]{1,0:T(8,128)(2,1)S(1)} %get-tuple-element.293.grad_ref, ...), custom_call_target="tpu_custom_call", output_to_operand_aliasing={{0}: (9, {})} | custom-call | bytes 8388608 | tf_op jit(solution)/shard_map/attention_backward/pallas_call | solution.py:292
  398.6 3.5 collective-permute-start.33
  402.2 2.4 constant_dynamic-slice_fusion.19
  404.6 9.1 %attention_backward.5 = (bf16[512,2048]{1,0:T(8,128)(2,1)}, f32[4,512,128]{2,1,0:T(8,128)S(1)}) custom-call(s32[5]{0:T(128)S(1)} %stack.85.info, bf16[256,2048]{1,0:T(8,128)(2,1)S(1)} %copy-done.17, bf16[256,2048]{1,0:T(8,128)(2,1)S(1)} %get-tuple-element.293.grad_ref, ...), custom_call_target="tpu_custom_call", output_to_operand_aliasing={{0}: (9, {}), {1}: (10, {})} | custom-call | bytes 8388608 | tf_op jit(solution)/shard_map/attention_backward/pallas_call | solution.py:292
  413.8 3.1 collective-permute-start.34
  417.1 4.3 collective-permute-done.34.short_ref
  423.6 16.2 %embed_backward.1 = (bf16[512,2048]{1,0:T(8,128)(2,1)}, bf16[512,512]{1,0:T(8,128)(2,1)S(1)}) custom-call(s32[6]{0:T(128)S(1)} %stack.87.info, bf16[512,2048]{1,0:T(8,128)(2,1)} %get-tuple-element.307.query_ref, f32[4,512,128]{2,1,0:T(8,128)S(1)} %pad_maximum_fusion.1.own_ref, bf16[4,512,128]{2,1,0:T(8,128)(2,1)} %collective-permute-done.33.came_ref, ...), custom_call_target="tpu_custom_call" | custom-call | flops 12884901888 | bytes 20971520 | tf_op jit(solution)/shard_map/embed_backward/pallas_call | solution.py:1007
  441.6 5.4 all-to-all-start.3
  456.3 2.9 convert_add_fusion.1
  459.3 14.0 %all-to-all-done.3 = bf16[32,32,512]{2,1,0:T(8,128)(2,1)} async-done(((bf16[32,32,512]{2,1,0:T(8,128)(2,1)}), bf16[32,32,512]{2,1,0:T(8,128)(2,1)}, u32[]{:S(2)}, u32[]{:S(2)}) %all-to-all-start.3) | async-done | bytes 1048608 | tf_op jit(solution)/shard_map/all_to_all | solution.py:1069
  473.3 3.0 fusion.33
  479.4 13.4 %units_backward.1 = (f32[512,512]{1,0:T(8,128)}, bf16[512,512]{1,0:T(8,128)(2,1)S(1)}, f32[8,512]{1,0:T(8,128)S(1)}, bf16[256,2560]{1,0:T(8,128)(2,1)}, bf16[256...) custom-call(s32[2]{0:T(128)S(1)} %copy-done.36, f32[512,512]{1,0:T(8,128)} %get-tuple-element.314.grad_ref, ...), custom_call_target="tpu_custom_call" | custom-call | flops 17716740096 | bytes 16777216 | tf_op jit(solution)/shard_map/units_backward/pallas_call | solution.py:582
  495.2 2.3 maximum_select_fusion
  498.1 17.9 %slot_backward.2 = (bf16[512,8,512]{2,1,0:T(8,128)(2,1)}, f32[512,1536]{1,0:T(8,128)}, f32[8,512]{1,0:T(8,128)S(1)}) custom-call(bf16[512,8,512]{2,1,0:T(8,128)(2,1)} %pieces_ref.5, bf16[4096,1536]{1,0:T(8,128)(2,1)} %get-tuple-element.305.mixed_ref, f32[512,8,128]{2,1,0:T(8,128)S(1)} %copy-done.11, ...), custom_call_target="tpu_custom_call" | custom-call | flops 1048576 | bytes 2048 | tf_op jit(solution)/shard_map/slot_backward/pallas_call | solution.py:695
  519.7 18.6 %slot_backward.3 = (bf16[512,8,512]{2,1,0:T(8,128)(2,1)}, bf16[512,1664]{1,0:T(8,128)(2,1)S(1)}, f32[8,512]{1,0:T(8,128)}) custom-call(bf16[512,8,512]{2,1,0:T(8,128)(2,1)} %pieces_ref.5, bf16[4096,1536]{1,0:T(8,128)(2,1)} %get-tuple-element.305.mixed_ref, f32[512,8,128]{2,1,0:T(8,128)} %copy-done.10, ...), custom_call_target="tpu_custom_call", output_to_operand_aliasing={{0}: (8, {})} | custom-call | flops 1048576 | bytes 2048 | tf_op jit(solution)/shard_map/slot_backward/pallas_call | solution.py:695
  545.5 9.1 %collective-permute-done.47 = bf16[128,768]{1,0:T(8,128)(2,1)S(1)} collective-permute-done((bf16[128,768]{1,0:T(8,128)(2,1)S(1)}, bf16[128,768]{1,0:T(8,128)(2,1)S(1)}, u32[]{:S(2)}, u32[]{:S(2)}) %collective-permute-start.47) | collective-permute-done | bytes 196640 | tf_op jit(solution)/shard_map/ppermute | solution.py:49
  563.6 2.1 collective-permute-start.56
  566.8 2.1 collective-permute-start.50
  568.9 4.1 collective-permute-done.57
  (388 shorter events, 112.0 us)
Async XLA Ops:
  7.2 83.8 %all-gather.2.cloned.1.call-start = ((), (), s32[]{:S(2)}) async-start(), calls=%async_computation.4 | async-start | bytes 2162688 | tf_op jit(solution)/shard_map/all_gather | solution.py:1181
  11.2 17.4 %collective-permute-start = (bf16[16,1792]{1,0:T(8,128)(2,1)}, bf16[16,1792]{1,0:T(8,128)(2,1)S(1)}, u32[]{:S(2)}, u32[]{:S(2)}) collective-permute-start(bf16[16,1792]{1,0:T(8,128)(2,1)} %get-tuple-element.477), channel_id=1, source_target_pairs={{0,16},{1,17},{2,18},{3,19},{4,20},{5,21},{6,22},{7,23},{8,24},{9,... | collective-permute-start | bytes 172040 | tf_op jit(solution)/shard_map/ppermute | solution.py:49
  16.8 14.2 %collective-permute-start.2 = (bf16[16,2560]{1,0:T(8,128)(2,1)S(1)}, bf16[16,2560]{1,0:T(8,128)(2,1)S(1)}, u32[]{:S(2)}, u32[]{:S(2)}) collective-permute-start(bf16[16,2560]{1,0:T(8,128)(2,1)S(1)} %constant_dynamic-update-slice_fusion), channel_id=1, source_target_pairs={{0,16},{1,17},{2,18},{3,19},{4,20},{5,21},{6,22},{7,23},{8,24},{9,... | collective-permute-start | bytes 245768 | tf_op jit(solution)/shard_map/ppermute | solution.py:49
  16.8 13.5 %collective-permute-start.4 = (bf16[64,512]{1,0:T(8,128)(2,1)}, bf16[64,512]{1,0:T(8,128)(2,1)S(1)}, u32[]{:S(2)}, u32[]{:S(2)}) collective-permute-start(bf16[64,512]{1,0:T(8,128)(2,1)} %param.31), channel_id=1, source_target_pairs={{0,16},{1,17},{2,18},{3,19},{4,20},{5,21},{6,22},{7,23},{8,24},{9,... | collective-permute-start | bytes 196616 | tf_op jit(solution)/shard_map/ppermute | solution.py:49
  22.4 16.3 %collective-permute-start.6 = (bf16[2048,128]{1,0:T(8,128)(2,1)S(1)}, bf16[2048,128]{1,0:T(8,128)(2,1)}, u32[]{:S(2)}, u32[]{:S(2)}) collective-permute-start(bf16[2048,128]{1,0:T(8,128)(2,1)S(1)} %constant_dynamic-slice_fusion.23), channel_id=1, source_target_pairs={{0,1},{1,0},{2,3},{3,2},{4,5},{5,4},{6,7},{7,6},{8,9},{9,8},{10,11... | collective-permute-start | bytes 1572872 | tf_op jit(solution)/shard_map/ppermute | solution.py:49
  30.3 8.2 %collective-permute-start.5 = (bf16[128,512]{1,0:T(8,128)(2,1)S(1)}, bf16[128,512]{1,0:T(8,128)(2,1)S(1)}, u32[]{:S(2)}, u32[]{:S(2)}) collective-permute-start(bf16[128,512]{1,0:T(8,128)(2,1)S(1)} %maximum_select_fusion.11), channel_id=1, source_target_pairs={{0,1},{1,0},{2,3},{3,2},{4,5},{5,4},{6,7},{7,6},{8,9},{9,8},{10,11... | collective-permute-start | bytes 393224 | tf_op jit(solution)/shard_map/ppermute | solution.py:49
  46.5 10.5 %collective-permute-start.8 = (bf16[128,1792]{1,0:T(8,128)(2,1)S(1)}, bf16[128,1792]{1,0:T(8,128)(2,1)S(1)}, u32[]{:S(2)}, u32[]{:S(2)}) collective-permute-start(bf16[128,1792]{1,0:T(8,128)(2,1)S(1)} %bitcast.214), channel_id=1, source_target_pairs={{0,4},{1,5},{2,6},{3,7},{4,0},{5,1},{6,2},{7,3},{8,12},{9,13},{10,... | collective-permute-start | bytes 1376264 | tf_op jit(solution)/shard_map/ppermute | solution.py:49
  48.0 9.1 %collective-permute-start.9 = (bf16[64,2560]{1,0:T(8,128)(2,1)S(1)}, bf16[64,2560]{1,0:T(8,128)(2,1)S(1)}, u32[]{:S(2)}, u32[]{:S(2)}) collective-permute-start(bf16[64,2560]{1,0:T(8,128)(2,1)S(1)} %bitcast.222), channel_id=1, source_target_pairs={{0,1},{1,0},{2,3},{3,2},{4,5},{5,4},{6,7},{7,6},{8,9},{9,8},{10,11... | collective-permute-start | bytes 983048 | tf_op jit(solution)/shard_map/ppermute | solution.py:49
  49.5 7.6 %collective-permute-start.10 = (bf16[256,512]{1,0:T(8,128)(2,1)S(1)}, bf16[256,512]{1,0:T(8,128)(2,1)}, u32[]{:S(2)}, u32[]{:S(2)}) collective-permute-start(bf16[256,512]{1,0:T(8,128)(2,1)S(1)} %bitcast.231), channel_id=1, source_target_pairs={{0,8},{1,9},{2,10},{3,11},{4,12},{5,13},{6,14},{7,15},{8,0},{9,1},... | collective-permute-start | bytes 786440 | tf_op jit(solution)/shard_map/ppermute | solution.py:49
  57.4 33.6 %collective-permute-start.14 = (bf16[1024,512]{1,0:T(8,128)(2,1)}, bf16[1024,512]{1,0:T(8,128)(2,1)}, u32[]{:S(2)}, u32[]{:S(2)}) collective-permute-start(bf16[1024,512]{1,0:T(8,128)(2,1)} %dynamic_slice.164), channel_id=1, source_target_pairs={{0,1},{1,0},{2,3},{3,2},{4,5},{5,4},{6,7},{7,6},{8,9},{9,8},{10,11... | collective-permute-start | bytes 3145736 | tf_op jit(solution)/shard_map/ppermute | solution.py:49
  59.0 31.9 %collective-permute-start.12 = (bf16[128,2560]{1,0:T(8,128)(2,1)S(1)}, bf16[128,2560]{1,0:T(8,128)(2,1)S(1)}, u32[]{:S(2)}, u32[]{:S(2)}) collective-permute-start(bf16[128,2560]{1,0:T(8,128)(2,1)S(1)} %bitcast.171), channel_id=1, source_target_pairs={{0,4},{1,5},{2,6},{3,7},{4,0},{5,1},{6,2},{7,3},{8,12},{9,13},{10,... | collective-permute-start | bytes 1966088 | tf_op jit(solution)/shard_map/ppermute | solution.py:49
  60.6 39.2 %collective-permute-start.15 = (bf16[128,2560]{1,0:T(8,128)(2,1)S(1)}, bf16[128,2560]{1,0:T(8,128)(2,1)}, u32[]{:S(2)}, u32[]{:S(2)}) collective-permute-start(bf16[128,2560]{1,0:T(8,128)(2,1)S(1)} %bitcast.172), channel_id=1, source_target_pairs={{0,2},{1,3},{2,0},{3,1},{4,6},{5,7},{6,4},{7,5},{8,10},{9,11},{10,... | collective-permute-start | bytes 1966088 | tf_op jit(solution)/shard_map/ppermute | solution.py:49
  61.8 29.2 %collective-permute-start.13 = (bf16[512,512]{1,0:T(8,128)(2,1)S(1)}, bf16[512,512]{1,0:T(8,128)(2,1)}, u32[]{:S(2)}, u32[]{:S(2)}) collective-permute-start(bf16[512,512]{1,0:T(8,128)(2,1)S(1)} %bitcast.175), channel_id=1, source_target_pairs={{0,4},{1,5},{2,6},{3,7},{4,0},{5,1},{6,2},{7,3},{8,12},{9,13},{10,... | collective-permute-start | bytes 1572872 | tf_op jit(solution)/shard_map/ppermute | solution.py:49
  62.4 37.4 %collective-permute-start.17 = (bf16[512,512]{1,0:T(8,128)(2,1)S(1)}, bf16[512,512]{1,0:T(8,128)(2,1)}, u32[]{:S(2)}, u32[]{:S(2)}) collective-permute-start(bf16[512,512]{1,0:T(8,128)(2,1)S(1)} %bitcast.176), channel_id=1, source_target_pairs={{0,2},{1,3},{2,0},{3,1},{4,6},{5,7},{6,4},{7,5},{8,10},{9,11},{10,... | collective-permute-start | bytes 1572872 | tf_op jit(solution)/shard_map/ppermute | solution.py:49
  91.0 8.8 %collective-permute-start.16 = (bf16[128,2560]{1,0:T(8,128)(2,1)S(1)}, bf16[128,2560]{1,0:T(8,128)(2,1)}, u32[]{:S(2)}, u32[]{:S(2)}) collective-permute-start(bf16[128,2560]{1,0:T(8,128)(2,1)S(1)} %collective-permute-done.12.refs_1_), channel_id=1, source_target_pairs={{0,2},{1,3},{2,0},{3,1},{4,6},{5,7},{6,4},{7,5},{8,10},{9,11},{10,... | collective-permute-start | bytes 1966088 | tf_op jit(solution)/shard_map/ppermute | solution.py:49
  91.1 8.7 %collective-permute-start.18 = (bf16[512,512]{1,0:T(8,128)(2,1)}, bf16[512,512]{1,0:T(8,128)(2,1)}, u32[]{:S(2)}, u32[]{:S(2)}) collective-permute-start(bf16[512,512]{1,0:T(8,128)(2,1)} %collective-permute-done.13.refs_5_), channel_id=1, source_target_pairs={{0,2},{1,3},{2,0},{3,1},{4,6},{5,7},{6,4},{7,5},{8,10},{9,11},{10,... | collective-permute-start | bytes 1572872 | tf_op jit(solution)/shard_map/ppermute | solution.py:49
  98.2 34.7 %collective-permute-start.19 = (bf16[1024,512]{1,0:T(8,128)(2,1)}, bf16[1024,512]{1,0:T(8,128)(2,1)}, u32[]{:S(2)}, u32[]{:S(2)}) collective-permute-start(bf16[1024,512]{1,0:T(8,128)(2,1)} %collective-permute-done.14), channel_id=1, source_target_pairs={{0,4},{1,5},{2,6},{3,7},{4,0},{5,1},{6,2},{7,3},{8,12},{9,13},{10,... | collective-permute-start | bytes 3145736 | tf_op jit(solution)/shard_map/ppermute | solution.py:49
  109.3 29.8 %all-to-all-start.2 = ((bf16[32,32,512]{2,1,0:T(8,128)(2,1)}), bf16[32,32,512]{2,1,0:T(8,128)(2,1)}, u32[]{:S(2)}, u32[]{:S(2)}) async-start(bf16[32,32,512]{2,1,0:T(8,128)(2,1)} %select_convert_fusion.1), calls=%async_computation.2 | async-start | bytes 2097152 | tf_op jit(solution)/shard_map/all_to_all | solution.py:1069
  113.1 40.9 %collective-permute-start.24 = (bf16[2048,128]{1,0:T(8,128)(2,1)}, bf16[2048,128]{1,0:T(8,128)(2,1)}, u32[]{:S(2)}, u32[]{:S(2)}) collective-permute-start(bf16[2048,128]{1,0:T(8,128)(2,1)} %collective-permute-done.6.pair_near), channel_id=1, source_target_pairs={{0,2},{1,3},{2,0},{3,1},{4,6},{5,7},{6,4},{7,5},{8,10},{9,11},{10,... | collective-permute-start | bytes 1572872 | tf_op jit(solution)/shard_map/ppermute | solution.py:49
  113.3 36.0 %collective-permute-start.22 = (bf16[256,2048]{1,0:T(8,128)(2,1)}, bf16[256,2048]{1,0:T(8,128)(2,1)}, u32[]{:S(2)}, u32[]{:S(2)}) collective-permute-start(bf16[256,2048]{1,0:T(8,128)(2,1)} %constant_dynamic-slice_fusion.22), channel_id=1, source_target_pairs={{0,1},{1,0},{2,3},{3,2},{4,5},{5,4},{6,7},{7,6},{8,9},{9,8},{10,11... | collective-permute-start | bytes 3145736 | tf_op jit(solution)/shard_map/ppermute | solution.py:49
  134.6 14.7 %collective-permute-start.20 = (bf16[1024,512]{1,0:T(8,128)(2,1)S(1)}, bf16[1024,512]{1,0:T(8,128)(2,1)}, u32[]{:S(2)}, u32[]{:S(2)}) collective-permute-start(bf16[1024,512]{1,0:T(8,128)(2,1)S(1)} %get-tuple-element.470.refs_1_.mid_a), channel_id=1, source_target_pairs={{0,2},{1,3},{2,0},{3,1},{4,6},{5,7},{6,4},{7,5},{8,10},{9,11},{10,... | collective-permute-start | bytes 3145736 | tf_op jit(solution)/shard_map/ppermute | solution.py:49
  134.6 14.6 %collective-permute-start.21 = (bf16[1024,512]{1,0:T(8,128)(2,1)S(1)}, bf16[1024,512]{1,0:T(8,128)(2,1)}, u32[]{:S(2)}, u32[]{:S(2)}) collective-permute-start(bf16[1024,512]{1,0:T(8,128)(2,1)S(1)} %get-tuple-element.469.refs_2_.mid_b), channel_id=1, source_target_pairs={{0,2},{1,3},{2,0},{3,1},{4,6},{5,7},{6,4},{7,5},{8,10},{9,11},{10,... | collective-permute-start | bytes 3145736 | tf_op jit(solution)/shard_map/ppermute | solution.py:49
  151.4 25.0 %collective-permute-start.25 = (bf16[256,2048]{1,0:T(8,128)(2,1)}, bf16[256,2048]{1,0:T(8,128)(2,1)}, u32[]{:S(2)}, u32[]{:S(2)}) collective-permute-start(bf16[256,2048]{1,0:T(8,128)(2,1)} %collective-permute-done.22), channel_id=1, source_target_pairs={{0,4},{1,5},{2,6},{3,7},{4,0},{5,1},{6,2},{7,3},{8,12},{9,13},{10,... | collective-permute-start | bytes 3145736 | tf_op jit(solution)/shard_map/ppermute | solution.py:49
  153.0 14.6 %collective-permute-start.23 = (bf16[512,512]{1,0:T(8,128)(2,1)}, bf16[512,512]{1,0:T(8,128)(2,1)S(1)}, u32[]{:S(2)}, u32[]{:S(2)}) collective-permute-start(bf16[512,512]{1,0:T(8,128)(2,1)} %get-tuple-element.255.chosen_ref), channel_id=1, source_target_pairs={{0,1},{1,0},{2,3},{3,2},{4,5},{5,4},{6,7},{7,6},{8,9},{9,8},{10,11... | collective-permute-start | bytes 1572872 | tf_op jit(solution)/shard_map/ppermute | solution.py:49
  178.1 24.1 %collective-permute-start.26 = (bf16[256,2048]{1,0:T(8,128)(2,1)S(1)}, bf16[256,2048]{1,0:T(8,128)(2,1)S(1)}, u32[]{:S(2)}, u32[]{:S(2)}) collective-permute-start(bf16[256,2048]{1,0:T(8,128)(2,1)S(1)} %get-tuple-element.468.mid_a), channel_id=1, source_target_pairs={{0,2},{1,3},{2,0},{3,1},{4,6},{5,7},{6,4},{7,5},{8,10},{9,11},{10,... | collective-permute-start | bytes 3145736 | tf_op jit(solution)/shard_map/ppermute | solution.py:49
  178.2 24.0 %collective-permute-start.27 = (bf16[256,2048]{1,0:T(8,128)(2,1)S(1)}, bf16[256,2048]{1,0:T(8,128)(2,1)S(1)}, u32[]{:S(2)}, u32[]{:S(2)}) collective-permute-start(bf16[256,2048]{1,0:T(8,128)(2,1)S(1)} %get-tuple-element.467.mid_b), channel_id=1, source_target_pairs={{0,2},{1,3},{2,0},{3,1},{4,6},{5,7},{6,4},{7,5},{8,10},{9,11},{10,... | collective-permute-start | bytes 3145736 | tf_op jit(solution)/shard_map/ppermute | solution.py:49
  209.9 25.2 %collective-permute-start.28 = (bf16[256,2048]{1,0:T(8,128)(2,1)S(1)}, bf16[256,2048]{1,0:T(8,128)(2,1)S(1)}, u32[]{:S(2)}, u32[]{:S(2)}) collective-permute-start(bf16[256,2048]{1,0:T(8,128)(2,1)S(1)} %get-tuple-element.273.refs_0_), channel_id=1, source_target_pairs={{0,1},{1,0},{2,3},{3,2},{4,5},{5,4},{6,7},{7,6},{8,9},{9,8},{10,11... | collective-permute-start | bytes 3145736 | tf_op jit(solution)/shard_map/ppermute | solution.py:49
  229.7 53.8 %collective-permute-start.30 = (bf16[256,2048]{1,0:T(8,128)(2,1)S(1)}, bf16[256,2048]{1,0:T(8,128)(2,1)S(1)}, u32[]{:S(2)}, u32[]{:S(2)}) collective-permute-start(bf16[256,2048]{1,0:T(8,128)(2,1)S(1)} %get-tuple-element.277.refs_0_), channel_id=1, source_target_pairs={{0,1},{1,0},{2,3},{3,2},{4,5},{5,4},{6,7},{7,6},{8,9},{9,8},{10,11... | collective-permute-start | bytes 3145736 | tf_op jit(solution)/shard_map/ppermute | solution.py:49
  282.8 53.2 %collective-permute-start.29 = (bf16[256,2048]{1,0:T(8,128)(2,1)S(1)}, bf16[256,2048]{1,0:T(8,128)(2,1)S(1)}, u32[]{:S(2)}, u32[]{:S(2)}) collective-permute-start(bf16[256,2048]{1,0:T(8,128)(2,1)S(1)} %get-tuple-element.463), channel_id=1, source_target_pairs={{0,1},{1,0},{2,3},{3,2},{4,5},{5,4},{6,7},{7,6},{8,9},{9,8},{10,11... | collective-permute-start | bytes 3145736 | tf_op jit(solution)/shard_map/ppermute | solution.py:49
  331.3 47.5 %collective-permute-start.31 = (bf16[256,2048]{1,0:T(8,128)(2,1)S(1)}, bf16[256,2048]{1,0:T(8,128)(2,1)S(1)}, u32[]{:S(2)}, u32[]{:S(2)}) collective-permute-start(bf16[256,2048]{1,0:T(8,128)(2,1)S(1)} %get-tuple-element.465), channel_id=1, source_target_pairs={{0,1},{1,0},{2,3},{3,2},{4,5},{5,4},{6,7},{7,6},{8,9},{9,8},{10,11... | collective-permute-start | bytes 3145736 | tf_op jit(solution)/shard_map/ppermute | solution.py:49
  334.8 44.0 %collective-permute-start.32 = (bf16[512,1024]{1,0:T(8,128)(2,1)}, bf16[512,1024]{1,0:T(8,128)(2,1)S(1)}, u32[]{:S(2)}, u32[]{:S(2)}) collective-permute-start(bf16[512,1024]{1,0:T(8,128)(2,1)} %get-tuple-element.462), channel_id=1, source_target_pairs={{0,1},{1,0},{2,3},{3,2},{4,5},{5,4},{6,7},{7,6},{8,9},{9,8},{10,11... | collective-permute-start | bytes 3145736 | tf_op jit(solution)/shard_map/ppermute | solution.py:49
  398.6 15.1 %collective-permute-start.33 = (bf16[4,512,128]{2,1,0:T(8,128)(2,1)}, bf16[4,512,128]{2,1,0:T(8,128)(2,1)}, u32[]{:S(2)}, u32[]{:S(2)}) collective-permute-start(bf16[4,512,128]{2,1,0:T(8,128)(2,1)} %pad_maximum_fusion.2), channel_id=1, source_target_pairs={{0,1},{1,0},{2,3},{3,2},{4,5},{5,4},{6,7},{7,6},{8,9},{9,8},{10,11... | collective-permute-start | bytes 1572872 | tf_op jit(solution)/shard_map/ppermute | solution.py:49
  413.8 7.6 %collective-permute-start.34 = (bf16[4,256,128]{2,1,0:T(8,128)(2,1)S(1)}, bf16[4,256,128]{2,1,0:T(8,128)(2,1)S(1)}, u32[]{:S(2)}, u32[]{:S(2)}) collective-permute-start(bf16[4,256,128]{2,1,0:T(8,128)(2,1)S(1)} %dynamic-slice_convert_fusion.8), channel_id=1, source_target_pairs={{0,1},{1,0},{2,3},{3,2},{4,5},{5,4},{6,7},{7,6},{8,9},{9,8},{10,11... | collective-permute-start | bytes 786440 | tf_op jit(solution)/shard_map/ppermute | solution.py:49
  421.4 32.1 %collective-permute-start.35 = (bf16[512,1024]{1,0:T(8,128)(2,1)}, bf16[512,1024]{1,0:T(8,128)(2,1)}, u32[]{:S(2)}, u32[]{:S(2)}) collective-permute-start(bf16[512,1024]{1,0:T(8,128)(2,1)} %constant_dynamic-slice_fusion.19), channel_id=1, source_target_pairs={{0,1},{1,0},{2,3},{3,2},{4,5},{5,4},{6,7},{7,6},{8,9},{9,8},{10,11... | collective-permute-start | bytes 3145736 | tf_op jit(solution)/shard_map/ppermute | solution.py:49
  441.6 31.7 %all-to-all-start.3 = ((bf16[32,32,512]{2,1,0:T(8,128)(2,1)}), bf16[32,32,512]{2,1,0:T(8,128)(2,1)}, u32[]{:S(2)}, u32[]{:S(2)}) async-start(bf16[32,32,512]{2,1,0:T(8,128)(2,1)} %bitcast.56), calls=%async_computation.3 | async-start | bytes 2097152 | tf_op jit(solution)/shard_map/all_to_all | solution.py:1069
  477.8 15.6 %collective-permute-start.37 = (bf16[128,2048]{1,0:T(8,128)(2,1)S(1)}, bf16[128,2048]{1,0:T(8,128)(2,1)S(1)}, u32[]{:S(2)}, u32[]{:S(2)}) collective-permute-start(bf16[128,2048]{1,0:T(8,128)(2,1)S(1)} %bitcast.248), channel_id=1, source_target_pairs={{0,1},{1,0},{2,3},{3,2},{4,5},{5,4},{6,7},{7,6},{8,9},{9,8},{10,11... | collective-permute-start | bytes 1572872 | tf_op jit(solution)/shard_map/ppermute | solution.py:49
  492.8 23.3 %collective-permute-start.39 = (bf16[256,2560]{1,0:T(8,128)(2,1)}, bf16[256,2560]{1,0:T(8,128)(2,1)S(1)}, u32[]{:S(2)}, u32[]{:S(2)}) collective-permute-start(bf16[256,2560]{1,0:T(8,128)(2,1)} %get-tuple-element.326), channel_id=1, source_target_pairs={{0,2},{1,3},{2,0},{3,1},{4,6},{5,7},{6,4},{7,5},{8,10},{9,11},{10,... | collective-permute-start | bytes 3932168 | tf_op jit(solution)/shard_map/ppermute | solution.py:49
  492.8 23.3 %collective-permute-start.40 = (bf16[1024,512]{1,0:T(8,128)(2,1)}, bf16[1024,512]{1,0:T(8,128)(2,1)S(1)}, u32[]{:S(2)}, u32[]{:S(2)}) collective-permute-start(bf16[1024,512]{1,0:T(8,128)(2,1)} %get-tuple-element.328), channel_id=1, source_target_pairs={{0,2},{1,3},{2,0},{3,1},{4,6},{5,7},{6,4},{7,5},{8,10},{9,11},{10,... | collective-permute-start | bytes 3145736 | tf_op jit(solution)/shard_map/ppermute | solution.py:49
  493.6 22.4 %collective-permute-start.38 = (bf16[64,2048]{1,0:T(8,128)(2,1)S(1)}, bf16[64,2048]{1,0:T(8,128)(2,1)S(1)}, u32[]{:S(2)}, u32[]{:S(2)}) collective-permute-start(bf16[64,2048]{1,0:T(8,128)(2,1)S(1)} %bitcast.258), channel_id=1, source_target_pairs={{0,4},{1,5},{2,6},{3,7},{4,0},{5,1},{6,2},{7,3},{8,12},{9,13},{10,... | collective-permute-start | bytes 786440 | tf_op jit(solution)/shard_map/ppermute | solution.py:49
  516.6 21.9 %collective-permute-start.42 = (bf16[128,2560]{1,0:T(8,128)(2,1)S(1)}, bf16[128,2560]{1,0:T(8,128)(2,1)S(1)}, u32[]{:S(2)}, u32[]{:S(2)}) collective-permute-start(bf16[128,2560]{1,0:T(8,128)(2,1)S(1)} %bitcast.241), channel_id=1, source_target_pairs={{0,1},{1,0},{2,3},{3,2},{4,5},{5,4},{6,7},{7,6},{8,9},{9,8},{10,11... | collective-permute-start | bytes 1966088 | tf_op jit(solution)/shard_map/ppermute | solution.py:49
  517.7 20.8 %collective-permute-start.43 = (bf16[512,512]{1,0:T(8,128)(2,1)S(1)}, bf16[512,512]{1,0:T(8,128)(2,1)S(1)}, u32[]{:S(2)}, u32[]{:S(2)}) collective-permute-start(bf16[512,512]{1,0:T(8,128)(2,1)S(1)} %bitcast.247), channel_id=1, source_target_pairs={{0,4},{1,5},{2,6},{3,7},{4,0},{5,1},{6,2},{7,3},{8,12},{9,13},{10,... | collective-permute-start | bytes 1572872 | tf_op jit(solution)/shard_map/ppermute | solution.py:49
  518.9 19.6 %collective-permute-start.41 = (bf16[32,2048]{1,0:T(8,128)(2,1)S(1)}, bf16[32,2048]{1,0:T(8,128)(2,1)S(1)}, u32[]{:S(2)}, u32[]{:S(2)}) collective-permute-start(bf16[32,2048]{1,0:T(8,128)(2,1)S(1)} %bitcast.271), channel_id=1, source_target_pairs={{0,8},{1,9},{2,10},{3,11},{4,12},{5,13},{6,14},{7,15},{8,0},{9,1},... | collective-permute-start | bytes 393224 | tf_op jit(solution)/shard_map/ppermute | solution.py:49
  538.9 17.3 %collective-permute-start.51 = (bf16[16,2048]{1,0:T(8,128)(2,1)S(1)}, bf16[16,2048]{1,0:T(8,128)(2,1)S(1)}, u32[]{:S(2)}, u32[]{:S(2)}) collective-permute-start(bf16[16,2048]{1,0:T(8,128)(2,1)S(1)} %fusion.51), channel_id=1, source_target_pairs={{0,16},{1,17},{2,18},{3,19},{4,20},{5,21},{6,22},{7,23},{8,24},{9,... | collective-permute-start | bytes 196616 | tf_op jit(solution)/shard_map/ppermute | solution.py:49
  540.5 15.7 %collective-permute-start.52 = (bf16[64,2560]{1,0:T(8,128)(2,1)S(1)}, bf16[64,2560]{1,0:T(8,128)(2,1)S(1)}, u32[]{:S(2)}, u32[]{:S(2)}) collective-permute-start(bf16[64,2560]{1,0:T(8,128)(2,1)S(1)} %bitcast.253), channel_id=1, source_target_pairs={{0,4},{1,5},{2,6},{3,7},{4,0},{5,1},{6,2},{7,3},{8,12},{9,13},{10,... | collective-permute-start | bytes 983048 | tf_op jit(solution)/shard_map/ppermute | solution.py:49
  541.8 14.4 %collective-permute-start.53 = (bf16[256,512]{1,0:T(8,128)(2,1)S(1)}, bf16[256,512]{1,0:T(8,128)(2,1)S(1)}, u32[]{:S(2)}, u32[]{:S(2)}) collective-permute-start(bf16[256,512]{1,0:T(8,128)(2,1)S(1)} %bitcast.257), channel_id=1, source_target_pairs={{0,8},{1,9},{2,10},{3,11},{4,12},{5,13},{6,14},{7,15},{8,0},{9,1},... | collective-permute-start | bytes 786440 | tf_op jit(solution)/shard_map/ppermute | solution.py:49
  543.5 11.1 %collective-permute-start.47 = (bf16[128,768]{1,0:T(8,128)(2,1)S(1)}, bf16[128,768]{1,0:T(8,128)(2,1)S(1)}, u32[]{:S(2)}, u32[]{:S(2)}) collective-permute-start(bf16[128,768]{1,0:T(8,128)(2,1)S(1)} %bitcast.266), channel_id=1, source_target_pairs={{0,4},{1,5},{2,6},{3,7},{4,0},{5,1},{6,2},{7,3},{8,12},{9,13},{10,... | collective-permute-start | bytes 589832 | tf_op jit(solution)/shard_map/ppermute | solution.py:49
  544.7 11.5 %collective-permute-start.45 = (bf16[128,896]{1,0:T(8,128)(2,1)S(1)}, bf16[128,896]{1,0:T(8,128)(2,1)S(1)}, u32[]{:S(2)}, u32[]{:S(2)}) collective-permute-start(bf16[128,896]{1,0:T(8,128)(2,1)S(1)} %bitcast.264), channel_id=1, source_target_pairs={{0,1},{1,0},{2,3},{3,2},{4,5},{5,4},{6,7},{7,6},{8,9},{9,8},{10,11... | collective-permute-start | bytes 688136 | tf_op jit(solution)/shard_map/ppermute | solution.py:49
  563.6 9.5 %collective-permute-start.56 = (bf16[16,2560]{1,0:T(8,128)(2,1)S(1)}, bf16[16,2560]{1,0:T(8,128)(2,1)S(1)}, u32[]{:S(2)}, u32[]{:S(2)}) collective-permute-start(bf16[16,2560]{1,0:T(8,128)(2,1)S(1)} %fusion.50), channel_id=1, source_target_pairs={{0,16},{1,17},{2,18},{3,19},{4,20},{5,21},{6,22},{7,23},{8,24},{9,... | collective-permute-start | bytes 245768 | tf_op jit(solution)/shard_map/ppermute | solution.py:49
  (84 other events, 1060.7 us)
Sparse Core Ops, SparseCore 0:
  24.1 58.1 all-gather.1
